TPU v7x, 256 devices: a whole 4x4x8 slice. The times are simulated.
256 devices in a mesh: seq: 32 (over z, x_lo, core), head: 8 (over y, x_hi).
Axes of the slice: x: 4 (x_hi: 2, x_lo: 2; x = x_hi * 2 + x_lo), y: 4, z: 8, core: 2. Of those that a mesh axis runs over, the one named last changes fastest.
Arguments:
- queries: bfloat16 [8192, 3072], P('seq', 'head'), may hold values from -6 to 6
- key_states: bfloat16 [8192, 3072], P('seq', 'head'), may hold values from -6 to 6
- value_states: bfloat16 [8192, 3072], P('seq', 'head'), may hold values from -6 to 6
- block_list: int32 [32, 27], P('seq'), may hold values from -1 to 31, as said below
- text_slots: int32 [2], replicated, may hold values from 0 to 31, as said below
- out_weight: bfloat16 [3072, 3072], P('head'), may hold values from -0.15625 to 0.15625
Outputs:
- mixed: bfloat16 [8192, 3072], P('seq', 'head')
Inputs may be any that keep to these rules, and one draw needn't show every extreme that they name: `block_list`: video tiles are numbered slab by slab in a grid of 4 x 4 tiles a frame slab, the last slab possibly partial, and occupy the slots that are not text slots in increasing order of their numbers. Row i lists, in a fixed order of the 27 offsets in -1..1 along the three dimensions, the slots of the existing video tiles next to or equal to the video tile in slot i, with -1 where the tile does not exist; rows of text slots are all -1. `text_slots`: the distinct slots of the text tiles in increasing order; the last slot is always one of them; no row of block_list names them.
All inputs are finite; a program needn't handle non-finite values.
Results may differ from a plain program's by a relative error of at most 0.0057.
Values may be sent and summed in bfloat16 or wider, within the bound.
No kernel may reach another device: no remote copies, remote signals or barrier semaphores. Data moves between devices by JAX's collectives and lax.ppermute only.
A program may use at most 128 MiB of HBM per device.

v0:
```python
import math

import jax
import jax.numpy as jnp
from jax import lax
from jax.sharding import PartitionSpec as P

HD = 128
TILE = 256


def attend_listed(collected, key_lists, queries_split, score_scale):
    head_count = queries_split.shape[1]
    tile_count = queries_split.shape[0] // TILE
    all_tiles = collected.reshape(2, -1, TILE, head_count, HD)
    query_tiles = queries_split.reshape(tile_count, TILE, head_count, HD)

    def one_tile(operands):
        query_tile, listed = operands
        present = listed >= 0
        chosen = jnp.where(present, listed, 0)
        picked = all_tiles[:, chosen].reshape(2, -1, head_count, HD)
        scores = (
            jnp.einsum("qhd,khd->hqk", query_tile, picked[0], preferred_element_type=jnp.float32)
            * score_scale
        )
        wanted = jnp.repeat(present, TILE)
        scores = jnp.where(wanted[None, None, :], scores, -jnp.inf)
        peak = jnp.max(scores, axis=-1, keepdims=True)
        weights = jnp.exp(scores - peak)
        total = jnp.sum(weights, axis=-1)
        weighted = jnp.einsum(
            "hqk,khd->qhd",
            weights.astype(jnp.bfloat16),
            picked[1],
            preferred_element_type=jnp.float32,
        )
        return (weighted / total.T[..., None]).astype(jnp.bfloat16)

    return lax.map(one_tile, (query_tiles, key_lists))


def per_device(queries, key_states, value_states, block_list, text_slots, out_weight):
    row_count, feat_width = queries.shape
    head_count = feat_width // HD
    score_scale = 1.0 / math.sqrt(HD)
    key_lists = jnp.concatenate([block_list, text_slots[None, :]], axis=1)
    queries_split = queries.reshape(row_count, head_count, HD)
    stacked = jnp.stack([key_states, value_states])
    collected = lax.all_gather(stacked, "seq", axis=1, tiled=True)
    attended = attend_listed(collected, key_lists, queries_split, score_scale).reshape(
        row_count, feat_width
    )
    mixed_cols = lax.psum_scatter(
        lax.dot_general(
            out_weight, attended, (((0,), (1,)), ((), ())), preferred_element_type=jnp.float32
        ),
        "head",
        scatter_dimension=0,
        tiled=True,
    )
    return mixed_cols.T.astype(jnp.bfloat16)


def solution(mesh):
    return jax.shard_map(
        per_device,
        mesh=mesh,
        in_specs=(
            P("seq", "head"),
            P("seq", "head"),
            P("seq", "head"),
            P("seq", None),
            P(),
            P("head", None),
        ),
        out_specs=P("seq", "head"),
        check_vma=False,
    )
```

profile of v0, /device:TPU:2, one launch (start us, length us, event | category | flops | bytes accessed | tf_op | source)
XLA Modules:
  0.0 280.0 jit_solution(3612928401344774634)
XLA Ops:
  6.5 0.0 copy-start
  6.5 0.0 all-gather.2.cloned.1.call-start
  6.5 1.9 pad_maximum_fusion
  8.5 0.0 all-gather.2.cloned.1.call-update
  8.5 0.0 reduce-scatter.2.cloned.1.call-start
  8.6 0.8 compare_bitcast_fusion
  9.3 0.1 broadcast_in_dim.38
  9.4 1.1 copy.14
  10.5 0.8 fusion.15
  11.2 80.7 %all-gather.2.cloned.1.call-done = bf16[2,8192,384]{2,1,0:T(8,128)(2,1)} async-done(((bf16[2,256,384]{2,1,0:T(8,128)(2,1)}), bf16[2,8192,384]{2,1,0:T(8,128)(2,1)}) %all-gather.2.cloned.1.call-update) | async-done | bytes 12582928 | tf_op jit(solution)/shard_map/all_gather | solution.py:50
  91.9 32.1 %reshape.59 = bf16[2,32,256,3,128]{4,3,2,1,0:T(4,128)(2,1)} reshape(bf16[2,8192,384]{2,1,0:T(8,128)(2,1)} %all-gather.2.cloned.1.call-done) | data formatting | bytes 25165824 | tf_op jit(solution)/shard_map/reshape | solution.py:15
  124.1 12.8 %copy.11 = bf16[2,32,256,3,128]{4,2,3,1,0:T(8,128)(2,1)} copy(bf16[2,32,256,3,128]{4,3,2,1,0:T(4,128)(2,1)} %reshape.59) | data formatting | bytes 25165824 | tf_op jit(solution)/shard_map/reshape | solution.py:15
  136.9 11.0 %gather_fusion = bf16[29,2,256,3,128]{4,2,3,1,0:T(8,128)(2,1)} fusion(bf16[2,32,256,3,128]{4,2,3,1,0:T(8,128)(2,1)} %copy.11, s32[1024]{0:T(1024)S(1)} %pad_clamp_fusion), kind=kCustom, calls=%fused_computation | custom fusion | bytes 22806644 | tf_op jit(solution)/shard_map/while/body/eval_jaxpr/gather | solution.py:22
  147.9 5.0 %fusion.18 = (bf16[1,29,256,3,128]{4,2,3,0,1:T(8,128)(2,1)S(1)}, bf16[1,29,256,3,128]{4,2,3,0,1:T(8,128)(2,1)S(1)}) fusion(bf16[2,29,256,3,128]{4,2,3,0,1:T(8,128)(2,1)} %bitcast.46), kind=kLoop, calls=%fused_computation.23 | loop fusion | bytes 22806528 | tf_op jit(solution)/shard_map/while/body/eval_jaxpr/slice | solution.py:24
  152.8 2.9 %copy.13 = bf16[1,29,256,3,128]{4,2,1,3,0:T(8,128)(2,1)} copy(bf16[1,29,256,3,128]{4,2,3,0,1:T(8,128)(2,1)S(1)} %get-tuple-element.13) | data formatting | bytes 11403264 | tf_op jit(solution)/shard_map/while/body/eval_jaxpr/slice | solution.py:24
  155.8 2.9 %copy.12 = bf16[1,29,256,3,128]{4,2,1,3,0:T(8,128)(2,1)} copy(bf16[1,29,256,3,128]{4,2,3,0,1:T(8,128)(2,1)S(1)} %get-tuple-element.14) | data formatting | bytes 11403264 | tf_op jit(solution)/shard_map/while/body/eval_jaxpr/slice | solution.py:35
  158.6 8.4 %bitcast_reduce_fusion = (f32[3,256]{1,0:T(4,128)S(1)}, f32[3,7424,256]{2,1,0:T(8,128)S(1)}) fusion(pred[7424]{0:T(1024)(128)(4,1)S(1)} %broadcast_in_dim.39, bf16[7424,3,128]{2,0,1:T(8,128)(2,1)} %bitcast.47, bf16[256,3,128]{0,2,1:T(8,128)(2,1)S(1)} %bitcast.49), kind=kOutput, calls=%fused_computation.2 | convolution fusion | flops 1476721920 | bytes 28715264 | tf_op jit(solution)/shard_map/while/body/eval_jaxpr/qhd,khd->hqk/dot_general | solution.py:24
  167.0 6.4 %fusion.1 = f32[3,256]{1,0:T(4,128)S(1)} fusion(f32[3,7424,256]{2,1,0:T(8,128)S(1)} %get-tuple-element.22, f32[3,256]{1,0:T(4,128)S(1)} %get-tuple-element.20, pred[7424]{0:T(1024)(128)(4,1)S(1)} %broadcast_in_dim.39), kind=kLoop, calls=%fused_computation.5 | loop fusion | flops 22805760 | bytes 22820096 | tf_op jit(solution)/shard_map/while/body/eval_jaxpr/reduce_sum | solution.py:31
  173.5 11.6 %fusion.12 = bf16[256,3,128]{0,2,1:T(8,128)(2,1)S(1)} fusion(bf16[7424,3,128]{2,0,1:T(8,128)(2,1)} %bitcast.48, f32[3,7424,256]{2,1,0:T(8,128)S(1)} %get-tuple-element.22, f32[3,256]{1,0:T(4,128)S(1)} %get-tuple-element.20, pred[7424]{0:T(1024)(128)(4,1)S(1)} %broadcast_in_dim.39, f32[256,3]{0,1:T(4,128)S(1)} %bitcast.53), kind=kOutput, calls=%fused_computation.12 | convolution fusion | flops 1482620928 | bytes 28718336 | tf_op jit(solution)/shard_map/while/body/eval_jaxpr/hqk,khd->qhd/dot_general | solution.py:32
  185.0 0.0 copy-done
  185.0 2.7 convolution_bitcast_fusion
  187.7 0.0 reduce-scatter.2.cloned.1.call-update
  187.7 83.7 %reduce-scatter.2.cloned.1.call-done = f32[384,256]{0,1:T(8,128)} async-done(((f32[3072,256]{0,1:T(8,128)}), f32[384,256]{0,1:T(8,128)}) %reduce-scatter.2.cloned.1.call-update) | async-done | bytes 393232 | tf_op jit(solution)/shard_map/reduce_scatter | solution.py:54
  271.5 1.7 convert_bitcast_fusion
  (2 shorter events, 0.0 us)
Async XLA Ops:
  6.5 178.5 %copy-start = (bf16[384,3072]{1,0:T(8,128)(2,1)S(1)}, bf16[384,3072]{1,0:T(8,128)(2,1)}, u32[]{:S(2)}) copy-start(bf16[384,3072]{1,0:T(8,128)(2,1)} %param.11) | copy-start | bytes 7077892
  6.5 85.4 %all-gather.2.cloned.1.call-start = ((), (), s32[]{:S(2)}) async-start(), calls=%async_computation.1 | async-start | bytes 12976128 | tf_op jit(solution)/shard_map/all_gather | solution.py:50
  8.5 263.0 %reduce-scatter.2.cloned.1.call-start = ((), (), s32[]{:S(2)}) async-start(), calls=%async_computation.2 | async-start | bytes 3538944 | tf_op jit(solution)/shard_map/reduce_scatter | solution.py:54
Sparse Core Ops, SparseCore 0:
  9.2 82.7 all-gather.1
  187.9 83.5 reduce-scatter.1
where the time goes:
time: 282 us; the launch traced here: 280 us
  waiting for transfers between devices  164 us (58%)
  local copies, waits for them, and re-layouts  67.8 us (24%)
  matrix products  22.6 us (8%)
  between operations  13.5 us (5%)
  other arithmetic  11.6 us (4%)
    reduce_scatter x1, waiting for transfers between devices, per_device(): lax.psum_scatter(lax.dot_general(out_weight, attended, (((0,), (1,)), (()...  83.7 us
    all_gather x1, waiting for transfers between devices, per_device(): collected = lax.all_gather(stacked, 'seq', axis=1, tiled=True)  80.7 us
    reshape x2, local copies, waits for them, and re-layouts, attend_listed(): all_tiles = collected.reshape(2, -1, TILE, head_count, HD)  44.9 us
    dot_general x1, matrix products, one_tile(): jnp.einsum('hqk,khd->qhd', weights.astype(jnp.bfloat16), picked[1], prefe...  11.6 us
    gather x1, local copies, waits for them, and re-layouts, one_tile(): picked = all_tiles[:, chosen].reshape(2, -1, head_count, HD)  11 us
    dot_general x1, matrix products, one_tile(): jnp.einsum('qhd,khd->hqk', query_tile, picked[0], preferred_element_type=...  8.4 us
    slice x2, local copies, waits for them, and re-layouts, one_tile(): picked[0]  7.87 us
    reduce_sum x1, other arithmetic, one_tile(): total = jnp.sum(weights, axis=-1)  6.43 us
  transfers between devices with their start and end apart: 2, of which 2 were waited for; matrix products, arithmetic and copies ran while one was open for 1% of the time, Pallas kernels for 0%

commit v1 on v0

v1 whole, which is shorter than its diff:
```python
import functools
import math

import jax
import jax.numpy as jnp
from jax import lax
from jax.experimental import pallas as pl
from jax.experimental.pallas import tpu as pltpu
from jax.sharding import PartitionSpec as P

HD = 128
TILE = 256
GROUP = 4
PART_ROWS = 16
LOWEST = -1e30
LOG2E = math.log2(math.e)


def write_part(ref, index, outs, sums):
    heads = len(outs)
    for h in range(heads):
        ref[index, h * HD:(h + 1) * HD, :] = outs[h].astype(jnp.bfloat16)
    rows = jnp.concatenate(sums + [jnp.zeros((8 - heads, TILE), jnp.float32)], axis=0)
    high = rows.astype(jnp.bfloat16).astype(jnp.float32)
    middle = (rows - high).astype(jnp.bfloat16).astype(jnp.float32)
    low = rows - high - middle
    block = jnp.concatenate([high, middle], axis=0).astype(jnp.bfloat16)
    last = jnp.concatenate([low, jnp.zeros_like(low)], axis=0).astype(jnp.bfloat16)
    base = heads * HD
    ref[index, base:base + 16, :] = block
    ref[index, base + 16:base + 32, :] = last


def read_sums(ref, index, heads):
    base = heads * HD
    block = ref[index, base:base + 16, :].astype(jnp.float32)
    last = ref[index, base + 16:base + 32, :].astype(jnp.float32)
    return block[0:8] + block[8:16] + last[0:8]


def merged(ref_a, index_a, ref_b, index_b, heads):
    sums_a = read_sums(ref_a, index_a, heads)
    sums_b = read_sums(ref_b, index_b, heads)
    top = jnp.maximum(sums_a, sums_b)
    weight_a = jnp.exp2(sums_a - top)
    weight_b = jnp.exp2(sums_b - top)
    total = weight_a + weight_b
    scale_a = weight_a / total
    scale_b = weight_b / total
    sums = top + jnp.log2(total)
    outs = []
    for h in range(heads):
        part_a = ref_a[index_a, h * HD:(h + 1) * HD, :].astype(jnp.float32)
        part_b = ref_b[index_b, h * HD:(h + 1) * HD, :].astype(jnp.float32)
        outs.append(part_a * scale_a[h:h + 1] + part_b * scale_b[h:h + 1])
    return outs, [sums[h:h + 1] for h in range(heads)]


def attend_kernel(factor, need_ref, q_ref, kv_ref, out_ref, acc_ref, peak_ref, total_ref):
    tiles = q_ref.shape[0]
    heads = q_ref.shape[2] // HD
    keys = kv_ref.shape[0]
    acc_ref[...] = jnp.zeros_like(acc_ref)
    peak_ref[...] = jnp.full_like(peak_ref, LOWEST)
    total_ref[...] = jnp.zeros_like(total_ref)

    def visit(step, carry):
        z = step // tiles
        t = step % tiles

        @pl.when(need_ref[t, z] > 0)
        def _():
            for h in range(heads):
                cols = slice(h * HD, (h + 1) * HD)
                query = q_ref[t, :, cols]
                key = kv_ref[z, 0:TILE, cols]
                value = kv_ref[z, TILE:2 * TILE, cols]
                scores = lax.dot_general(
                    key, query, (((1,), (1,)), ((), ())), preferred_element_type=jnp.float32
                )
                row = t * heads + h
                old = peak_ref[row]
                peak = jnp.maximum(old, jnp.max(scores, axis=0, keepdims=True) * factor)
                weights = jnp.exp2(scores * factor - peak)
                shrink = jnp.exp2(old - peak)
                peak_ref[row] = peak
                total_ref[row] = total_ref[row] * shrink + jnp.sum(weights, axis=0, keepdims=True)
                acc_ref[row] = acc_ref[row] * shrink + lax.dot_general(
                    value,
                    weights.astype(jnp.bfloat16),
                    (((0,), (0,)), ((), ())),
                    preferred_element_type=jnp.float32,
                )

        return carry

    lax.fori_loop(0, keys * tiles, visit, 0)
    for t in range(tiles):
        outs, sums = [], []
        for h in range(heads):
            row = t * heads + h
            total = total_ref[row]
            held = total > 0.0
            safe = jnp.where(held, total, 1.0)
            outs.append(acc_ref[row] / safe)
            sums.append(jnp.where(held, peak_ref[row] + jnp.log2(safe), LOWEST))
        write_part(out_ref, t, outs, sums)


def merge_kernel(mine_ref, other_ref, keep_ref, send_ref):
    heads = mine_ref.shape[1] // HD
    outs, sums = merged(mine_ref, 2, other_ref, 1, heads)
    write_part(send_ref, 0, outs, sums)
    outs, sums = merged(mine_ref, 0, other_ref, 0, heads)
    write_part(keep_ref, 0, outs, sums)


def project_kernel(keep_ref, other_ref, weight_ref, out_ref, held_ref):
    heads = keep_ref.shape[1] // HD
    outs, _ = merged(keep_ref, 0, other_ref, 0, heads)
    for h in range(heads):
        held_ref[h * HD:(h + 1) * HD, :] = outs[h].astype(jnp.bfloat16)
    shares, _, width = out_ref.shape
    attended = held_ref[...].T
    for j in range(shares):
        out_ref[j] = jnp.dot(
            attended, weight_ref[:, j * width:(j + 1) * width], preferred_element_type=jnp.float32
        ).astype(jnp.bfloat16)


def vmem_specs(count):
    return [pl.BlockSpec(memory_space=pltpu.VMEM)] * count


def per_device(seq_size, head_size, queries, key_states, value_states, block_list, text_slots, out_weight):
    width = queries.shape[1]
    heads = width // HD
    planes = seq_size // GROUP
    me = lax.axis_index("seq")
    swap_core = [(s, s ^ 1) for s in range(seq_size)]
    swap_chip = [(s, s ^ 2) for s in range(seq_size)]
    z_groups = [[z * GROUP + d for z in range(planes)] for d in range(GROUP)]

    both = jnp.concatenate([key_states, value_states], axis=0)
    held = lax.all_gather(both, "seq", axis_index_groups=z_groups, axis=0, tiled=False)

    lists = jnp.concatenate([block_list, lax.ppermute(block_list, "seq", swap_core)], axis=0)
    lists = jnp.concatenate([lists, lax.ppermute(lists, "seq", swap_chip)], axis=0)
    tiles = jnp.stack([queries, lax.ppermute(queries, "seq", swap_core)])
    tiles = jnp.concatenate([tiles, lax.ppermute(tiles, "seq", swap_chip)], axis=0)

    lists = jnp.concatenate([lists, jnp.broadcast_to(text_slots[None, :], (GROUP, text_slots.shape[0]))], axis=1)
    slots = jnp.arange(planes, dtype=jnp.int32) * GROUP + me % GROUP
    need = jnp.any(lists[:, None, :] == slots[None, :, None], axis=2).astype(jnp.int32)

    part_rows = width + 2 * PART_ROWS
    part = jax.ShapeDtypeStruct((1, part_rows, TILE), jnp.bfloat16)
    parts = pl.pallas_call(
        functools.partial(attend_kernel, LOG2E / math.sqrt(HD)),
        out_shape=jax.ShapeDtypeStruct((GROUP, part_rows, TILE), jnp.bfloat16),
        in_specs=[pl.BlockSpec(memory_space=pltpu.SMEM)] + vmem_specs(2),
        out_specs=pl.BlockSpec(memory_space=pltpu.VMEM),
        scratch_shapes=[
            pltpu.VMEM((GROUP * heads, HD, TILE), jnp.float32),
            pltpu.VMEM((GROUP * heads, 1, TILE), jnp.float32),
            pltpu.VMEM((GROUP * heads, 1, TILE), jnp.float32),
        ],
        compiler_params=pltpu.CompilerParams(vmem_limit_bytes=32 * 1024 * 1024),
        name="attend",
    )(need, tiles, held)

    other = lax.ppermute(jnp.stack([parts[1], parts[3]]), "seq", swap_core)
    keep, send = pl.pallas_call(
        merge_kernel,
        out_shape=(part, part),
        in_specs=vmem_specs(2),
        out_specs=tuple(vmem_specs(2)),
        compiler_params=pltpu.CompilerParams(vmem_limit_bytes=32 * 1024 * 1024),
        name="merge",
    )(parts, other)
    other = lax.ppermute(send, "seq", swap_chip)
    shares = pl.pallas_call(
        project_kernel,
        out_shape=jax.ShapeDtypeStruct((head_size, TILE, width), jnp.bfloat16),
        in_specs=vmem_specs(3),
        out_specs=pl.BlockSpec(memory_space=pltpu.VMEM),
        scratch_shapes=[pltpu.VMEM((width, TILE), jnp.bfloat16)],
        compiler_params=pltpu.CompilerParams(vmem_limit_bytes=32 * 1024 * 1024),
        name="project",
    )(keep, other, out_weight)
    shares = lax.all_to_all(shares, "head", 0, 0, tiled=False)
    return jnp.sum(shares.astype(jnp.float32), axis=0).astype(jnp.bfloat16)


def solution(mesh):
    return jax.shard_map(
        functools.partial(per_device, mesh.shape["seq"], mesh.shape["head"]),
        mesh=mesh,
        in_specs=(
            P("seq", "head"),
            P("seq", "head"),
            P("seq", "head"),
            P("seq", None),
            P(),
            P("head", None),
        ),
        out_specs=P("seq", "head"),
        check_vma=False,
    )
```

time: 282 us -> 126 us (0.45)
  the two profiles are of different devices: /device:TPU:2 before, /device:TPU:32 now
where the time goes in v1:
time: 126 us
  waiting for transfers between devices  48.4 us (38%)
  blocking collectives  28.8 us (23%)
  Pallas kernels  16.9 us (13%)
  between operations  13.5 us (11%)
  starting transfers between devices  9.34 us (7%)
  other arithmetic  6.33 us (5%)
  local copies, waits for them, and re-layouts  2.65 us (2%)
    all_gather x1, waiting for transfers between devices, per_device(): lax.all_gather(both, 'seq', axis_index_groups=z_groups, axis=0, tiled=False)  31.2 us
    all_to_all x1, blocking collectives, per_device(): shares = lax.all_to_all(shares, 'head', 0, 0, tiled=False)  28.8 us
    pallas_call x1, Pallas kernels, per_device(): pl.pallas_call(functools.partial(attend_kernel, LOG2E / math.sqrt(HD)), o...  15.4 us
    ppermute x1, waiting for transfers between devices, per_device(): lax.ppermute(tiles, 'seq', swap_chip)  8.72 us
    ppermute x1, starting transfers between devices, per_device(): other = lax.ppermute(send, 'seq', swap_chip)  6.54 us
    ppermute x1, waiting for transfers between devices, per_device(): other = lax.ppermute(send, 'seq', swap_chip)  5.55 us
  transfers between devices with their start and end apart: 7, of which 5 were waited for; matrix products, arithmetic and copies ran while one was open for 3% of the time, Pallas kernels for 0%

profile of v1, /device:TPU:32, one launch (start us, length us, event | category | flops | bytes accessed | tf_op | source)
XLA Modules:
  0.0 125.8 jit_solution(6431257981909300883)
XLA Ops:
  6.5 0.0 all-gather.3.cloned.1.call-start
  6.5 1.8 %pad_maximum_fusion.3 = bf16[512,384]{1,0:T(8,128)(2,1)} fusion(bf16[256,384]{1,0:T(8,128)(2,1)} %param.8, bf16[256,384]{1,0:T(8,128)(2,1)} %param.7), kind=kLoop, calls=%fused_computation.3 | loop fusion | flops 786432 | bytes 786432 | tf_op jit(solution)/shard_map/concatenate | solution.py:144
  8.3 0.0 all-gather.3.cloned.1.call-update
  8.4 0.1 collective-permute-start.2
  8.5 0.5 collective-permute-start
  9.0 1.1 collective-permute-done
  10.1 0.7 pad_add_fusion
  10.8 1.5 %collective-permute-start.1 = (s32[2,27]{1,0:T(2,128)S(1)}, s32[2,27]{1,0:T(2,128)S(1)}, u32[]{:S(2)}, u32[]{:S(2)}) collective-permute-start(s32[2,27]{1,0:T(2,128)S(1)} %pad_add_fusion), channel_id=1, source_target_pairs={{0,16},{8,24},{16,0},{24,8},{32,48},{40,56},{48,32},{56,40},{64,80... | collective-permute-start | bytes 656 | tf_op jit(solution)/shard_map/ppermute | solution.py:148
  12.3 0.0 collective-permute-done.2
  12.3 1.0 pad_maximum_fusion.2
  13.2 0.6 collective-permute-start.3
  13.9 0.7 pad.12.clone
  14.6 0.0 collective-permute-done.1
  14.6 0.7 add_add_fusion
  15.3 0.2 compare_reduce_fusion
  15.5 8.7 %collective-permute-done.3 = bf16[2,256,384]{2,1,0:T(8,128)(2,1)S(1)} collective-permute-done((bf16[2,256,384]{2,1,0:T(8,128)(2,1)S(1)}, bf16[2,256,384]{2,1,0:T(8,128)(2,1)S(1)}, u32[]{:S(2)}, u32[]{:S(2)}) %collective-permute-start.3) | collective-permute-done | bytes 393248 | tf_op jit(solution)/shard_map/ppermute | solution.py:150
  24.2 1.0 pad_maximum_fusion.q_ref
  25.2 31.2 %all-gather.3.cloned.1.call-done = bf16[4096,384]{1,0:T(8,128)(2,1)} async-done(((bf16[512,384]{1,0:T(8,128)(2,1)}), bf16[4096,384]{1,0:T(8,128)(2,1)}) %all-gather.3.cloned.1.call-update) | async-done | bytes 3145744 | tf_op jit(solution)/shard_map/all_gather | solution.py:145
  56.4 0.0 copy-start
  56.4 1.9 %copy-done = bf16[4096,384]{1,0:T(8,128)(2,1)S(1)} copy-done((bf16[4096,384]{1,0:T(8,128)(2,1)S(1)}, bf16[4096,384]{1,0:T(8,128)(2,1)}, u32[]{:S(2)}) %copy-start) | copy-done | bytes 3145752
  58.3 15.4 %attend.1.mine_ref = bf16[4,416,256]{2,1,0:T(8,128)(2,1)S(1)} custom-call(s32[4,8]{1,0:T(4,128)S(1)} %convert_element_type.2.need_ref, bf16[4,256,384]{2,1,0:T(8,128)(2,1)S(1)} %pad_maximum_fusion.q_ref, bf16[8,512,384]{2,1,0:T(8,128)(2,1)S(1)} %bitcast.3), custom_call_target="tpu_custom_call" | custom-call | tf_op jit(solution)/shard_map/attend/pallas_call | solution.py:158
  73.8 0.0 copy-start.1
  73.9 0.1 collective-permute-start.4
  74.0 1.8 %collective-permute-done.4.other_ref = bf16[2,416,256]{2,1,0:T(8,128)(2,1)S(1)} collective-permute-done((bf16[2,416,256]{2,1,0:T(8,128)(2,1)S(1)}, bf16[2,416,256]{2,1,0:T(8,128)(2,1)S(1)}, u32[]{:S(2)}, u32[]{:S(2)}) %collective-permute-start.4) | collective-permute-done | bytes 426016 | tf_op jit(solution)/shard_map/ppermute | solution.py:172
  75.7 0.2 merge.1
  75.9 6.5 %collective-permute-start.5 = (bf16[1,416,256]{2,1,0:T(8,128)(2,1)S(1)}, bf16[1,416,256]{2,1,0:T(8,128)(2,1)S(1)}, u32[]{:S(2)}, u32[]{:S(2)}) collective-permute-start(bf16[1,416,256]{2,1,0:T(8,128)(2,1)S(1)} %get-tuple-element.8), channel_id=1, source_target_pairs={{0,16},{8,24},{16,0},{24,8},{32,48},{40,56},{48,32},{56,40},{64,80... | collective-permute-start | bytes 638984 | tf_op jit(solution)/shard_map/ppermute | solution.py:181
  82.5 5.6 %collective-permute-done.5.other_ref = bf16[1,416,256]{2,1,0:T(8,128)(2,1)S(1)} collective-permute-done((bf16[1,416,256]{2,1,0:T(8,128)(2,1)S(1)}, bf16[1,416,256]{2,1,0:T(8,128)(2,1)S(1)}, u32[]{:S(2)}, u32[]{:S(2)}) %collective-permute-start.5) | collective-permute-done | bytes 213024 | tf_op jit(solution)/shard_map/ppermute | solution.py:181
  88.0 0.0 copy-done.1
  88.0 1.2 project.1
  89.3 28.8 %all_to_all.5 = bf16[8,256,384]{2,1,0:T(8,128)(2,1)S(1)} all-to-all(bf16[8,256,384]{2,1,0:T(8,128)(2,1)S(1)} %project.1), channel_id=1, replica_groups=mesh['seq'=32,'head'=8] {'head'}, dimensions={0} | all-to-all | bytes 3145728 | tf_op jit(solution)/shard_map/all_to_all | solution.py:191
  118.1 0.9 reduce_sum.12
  (4 shorter events, 0.1 us)
Async XLA Ops:
  6.5 49.9 %all-gather.3.cloned.1.call-start = ((), (), s32[]{:S(2)}) async-start(), calls=%async_computation.1 | async-start | bytes 3538944 | tf_op jit(solution)/shard_map/all_gather | solution.py:145
  8.4 3.9 %collective-permute-start.2 = (bf16[256,384]{1,0:T(8,128)(2,1)}, bf16[256,384]{1,0:T(8,128)(2,1)S(1)}, u32[]{:S(2)}, u32[]{:S(2)}) collective-permute-start(bf16[256,384]{1,0:T(8,128)(2,1)} %param.6), channel_id=1, source_target_pairs={{0,8},{8,0},{16,24},{24,16},{32,40},{40,32},{48,56},{56,48},{64,72... | collective-permute-start | bytes 589832 | tf_op jit(solution)/shard_map/ppermute | solution.py:149
  8.5 1.6 %collective-permute-start = (s32[1,27]{1,0:T(1,128)}, s32[1,27]{1,0:T(1,128)S(1)}, u32[]{:S(2)}, u32[]{:S(2)}) collective-permute-start(s32[1,27]{1,0:T(1,128)} %param.9), channel_id=1, source_target_pairs={{0,8},{8,0},{16,24},{24,16},{32,40},{40,32},{48,56},{56,48},{64,72... | collective-permute-start | bytes 332 | tf_op jit(solution)/shard_map/ppermute | solution.py:147
  10.8 3.8 %collective-permute-start.1 = (s32[2,27]{1,0:T(2,128)S(1)}, s32[2,27]{1,0:T(2,128)S(1)}, u32[]{:S(2)}, u32[]{:S(2)}) collective-permute-start(s32[2,27]{1,0:T(2,128)S(1)} %pad_add_fusion), channel_id=1, source_target_pairs={{0,16},{8,24},{16,0},{24,8},{32,48},{40,56},{48,32},{56,40},{64,80... | collective-permute-start | bytes 656 | tf_op jit(solution)/shard_map/ppermute | solution.py:148
  13.2 11.0 %collective-permute-start.3 = (bf16[2,256,384]{2,1,0:T(8,128)(2,1)S(1)}, bf16[2,256,384]{2,1,0:T(8,128)(2,1)S(1)}, u32[]{:S(2)}, u32[]{:S(2)}) collective-permute-start(bf16[2,256,384]{2,1,0:T(8,128)(2,1)S(1)} %pad_maximum_fusion.2), channel_id=1, source_target_pairs={{0,16},{8,24},{16,0},{24,8},{32,48},{40,56},{48,32},{56,40},{64,80... | collective-permute-start | bytes 1179656 | tf_op jit(solution)/shard_map/ppermute | solution.py:150
  56.4 1.9 %copy-start = (bf16[4096,384]{1,0:T(8,128)(2,1)S(1)}, bf16[4096,384]{1,0:T(8,128)(2,1)}, u32[]{:S(2)}) copy-start(bf16[4096,384]{1,0:T(8,128)(2,1)} %all-gather.3.cloned.1.call-done) | copy-start | bytes 9437188
  73.8 14.3 %copy-start.1 = (bf16[384,3072]{1,0:T(8,128)(2,1)S(1)}, bf16[384,3072]{1,0:T(8,128)(2,1)}, u32[]{:S(2)}) copy-start(bf16[384,3072]{1,0:T(8,128)(2,1)} %weight_ref.1) | copy-start | bytes 7077892
  73.9 1.9 %collective-permute-start.4 = (bf16[2,416,256]{2,1,0:T(8,128)(2,1)S(1)}, bf16[2,416,256]{2,1,0:T(8,128)(2,1)S(1)}, u32[]{:S(2)}, u32[]{:S(2)}) collective-permute-start(bf16[2,416,256]{2,1,0:T(8,128)(2,1)S(1)} %pad_maximum_fusion.1), channel_id=1, source_target_pairs={{0,8},{8,0},{16,24},{24,16},{32,40},{40,32},{48,56},{56,48},{64,72... | collective-permute-start | bytes 1277960 | tf_op jit(solution)/shard_map/ppermute | solution.py:172
  75.9 12.1 %collective-permute-start.5 = (bf16[1,416,256]{2,1,0:T(8,128)(2,1)S(1)}, bf16[1,416,256]{2,1,0:T(8,128)(2,1)S(1)}, u32[]{:S(2)}, u32[]{:S(2)}) collective-permute-start(bf16[1,416,256]{2,1,0:T(8,128)(2,1)S(1)} %get-tuple-element.8), channel_id=1, source_target_pairs={{0,16},{8,24},{16,0},{24,8},{32,48},{40,56},{48,32},{56,40},{64,80... | collective-permute-start | bytes 638984 | tf_op jit(solution)/shard_map/ppermute | solution.py:181
Sparse Core Ops, SparseCore 0:
  9.1 47.2 all-gather.2

commit v2 on v0

v2 whole, which is shorter than its diff:
```python
import functools
import math

import jax
import jax.numpy as jnp
from jax import lax
from jax.experimental import pallas as pl
from jax.experimental.pallas import tpu as pltpu
from jax.sharding import PartitionSpec as P

HD = 128
TILE = 256
GROUP = 4
PART_ROWS = 16
LOWEST = -1e30
LOG2E = math.log2(math.e)


def pack_part(ref, index, outs, sums):
    heads = len(outs)
    for h in range(heads):
        ref[index, h * HD:(h + 1) * HD, :] = outs[h].astype(jnp.bfloat16)
    rows = jnp.concatenate(sums + [jnp.zeros((8 - heads, TILE), jnp.float32)], axis=0)
    high = rows.astype(jnp.bfloat16).astype(jnp.float32)
    middle = (rows - high).astype(jnp.bfloat16).astype(jnp.float32)
    low = rows - high - middle
    base = heads * HD
    ref[index, base:base + 16, :] = jnp.concatenate([high, middle], axis=0).astype(jnp.bfloat16)
    ref[index, base + 16:base + 32, :] = jnp.concatenate([low, jnp.zeros_like(low)], axis=0).astype(jnp.bfloat16)


def unpack_sums(ref, index, heads):
    base = heads * HD
    block = ref[index, base:base + 16, :].astype(jnp.float32)
    last = ref[index, base + 16:base + 32, :].astype(jnp.float32)
    return block[0:8] + block[8:16] + last[0:8]


def merged(mine_ref, mine_sum_ref, mine, other_ref, other, heads):
    others = unpack_sums(other_ref, other, heads)
    outs, sums = [], []
    for h in range(heads):
        rows = slice(h * HD, (h + 1) * HD)
        own_sum = mine_sum_ref[mine, h:h + 1, :]
        other_sum = others[h:h + 1]
        top = jnp.maximum(own_sum, other_sum)
        own_weight = jnp.exp2(own_sum - top)
        other_weight = jnp.exp2(other_sum - top)
        total = own_weight + other_weight
        outs.append(
            mine_ref[mine, rows, :] * (own_weight / total)
            + other_ref[other, rows, :].astype(jnp.float32) * (other_weight / total)
        )
        sums.append(top + jnp.log2(total))
    return outs, sums


def visit_shards(factor, need_ref, first, q_refs, shards, acc_ref, peak_ref, total_ref):
    heads = q_refs[0].shape[1] // HD
    for j, (k_ref, v_ref) in enumerate(shards):
        for t, q_ref in enumerate(q_refs):

            @pl.when(need_ref[t, first + j] > 0)
            def _():
                for h in range(heads):
                    cols = slice(h * HD, (h + 1) * HD)
                    scores = lax.dot_general(
                        k_ref[:, cols],
                        q_ref[0:TILE, cols],
                        (((1,), (1,)), ((), ())),
                        preferred_element_type=jnp.float32,
                    )
                    row = t * heads + h
                    old = peak_ref[row]
                    peak = jnp.maximum(old, jnp.max(scores, axis=0, keepdims=True) * factor)
                    weights = jnp.exp2(scores * factor - peak)
                    shrink = jnp.exp2(old - peak)
                    peak_ref[row] = peak
                    total_ref[row] = total_ref[row] * shrink + jnp.sum(weights, axis=0, keepdims=True)
                    acc_ref[row] = acc_ref[row] * shrink + lax.dot_general(
                        v_ref[:, cols],
                        weights.astype(jnp.bfloat16),
                        (((0,), (0,)), ((), ())),
                        preferred_element_type=jnp.float32,
                    )


def open_kernel(factor, count, need_ref, *refs):
    q_refs, kv_refs, (acc_ref, peak_ref, total_ref) = refs[:GROUP], refs[GROUP:-3], refs[-3:]
    acc_ref[...] = jnp.zeros_like(acc_ref)
    peak_ref[...] = jnp.full_like(peak_ref, LOWEST)
    total_ref[...] = jnp.zeros_like(total_ref)
    shards = list(zip(kv_refs[:count], kv_refs[count:]))
    visit_shards(factor, need_ref, 0, q_refs, shards, acc_ref, peak_ref, total_ref)


def more_kernel(factor, first, count, need_ref, *refs):
    q_refs, kv_refs = refs[:GROUP], refs[GROUP:GROUP + 2 * count]
    held, state = refs[GROUP + 2 * count:-3], refs[-3:]
    for source, target in zip(held, state):
        target[...] = source[...]
    shards = list(zip(kv_refs[:count], kv_refs[count:]))
    visit_shards(factor, need_ref, first, q_refs, shards, *state)


def close_kernel(factor, first, need_ref, *refs):
    q_refs, kv_refs = refs[:GROUP], refs[GROUP:GROUP + 2]
    held = refs[GROUP + 2:GROUP + 5]
    keep_ref, keep_sum_ref, send_ref, acc_ref, peak_ref, total_ref = refs[GROUP + 5:]
    heads = q_refs[0].shape[1] // HD
    for source, target in zip(held, (acc_ref, peak_ref, total_ref)):
        target[...] = source[...]
    visit_shards(factor, need_ref, first, q_refs, [kv_refs], acc_ref, peak_ref, total_ref)
    for t in range(GROUP):
        outs, sums = [], []
        for h in range(heads):
            row = t * heads + h
            total = total_ref[row]
            present = total > 0.0
            safe = jnp.where(present, total, 1.0)
            outs.append(acc_ref[row] * (1.0 / safe))
            sums.append(jnp.where(present, peak_ref[row] + jnp.log2(safe), LOWEST))
        if t % 2:
            pack_part(send_ref, t // 2, outs, sums)
        else:
            for h in range(heads):
                keep_ref[t // 2, h * HD:(h + 1) * HD, :] = outs[h]
                keep_sum_ref[t // 2, h:h + 1, :] = sums[h]


def merge_kernel(mine_ref, mine_sum_ref, other_ref, keep_ref, keep_sum_ref, send_ref):
    heads = mine_ref.shape[1] // HD
    outs, sums = merged(mine_ref, mine_sum_ref, 1, other_ref, 1, heads)
    pack_part(send_ref, 0, outs, sums)
    outs, sums = merged(mine_ref, mine_sum_ref, 0, other_ref, 0, heads)
    for h in range(heads):
        keep_ref[0, h * HD:(h + 1) * HD, :] = outs[h]
        keep_sum_ref[0, h:h + 1, :] = sums[h]


def project_kernel(mine_ref, mine_sum_ref, other_ref, weight_ref, out_ref, held_ref):
    heads = mine_ref.shape[1] // HD
    outs, _ = merged(mine_ref, mine_sum_ref, 0, other_ref, 0, heads)
    for h in range(heads):
        held_ref[:, h * HD:(h + 1) * HD] = outs[h].T.astype(jnp.bfloat16)
    shares, _, width = out_ref.shape
    attended = held_ref[...]
    for j in range(shares):
        out_ref[j] = jnp.dot(
            attended, weight_ref[:, j * width:(j + 1) * width], preferred_element_type=jnp.float32
        ).astype(jnp.bfloat16)


def vmem_specs(count):
    return [pl.BlockSpec(memory_space=pltpu.VMEM)] * count


def attend_cost(blocks):
    return pl.CostEstimate(
        flops=blocks * 4 * TILE * TILE * HD, bytes_accessed=4 << 20, transcendentals=blocks * TILE * TILE
    )


PARAMS = pltpu.CompilerParams(vmem_limit_bytes=32 * 1024 * 1024)


def per_device(seq_size, head_size, queries, key_states, value_states, block_list, text_slots, out_weight):
    width = queries.shape[1]
    heads = width // HD
    planes = seq_size // GROUP
    me = lax.axis_index("seq")
    up = [(s, (s + GROUP) % seq_size) for s in range(seq_size)]
    down = [(s, (s - GROUP) % seq_size) for s in range(seq_size)]

    k_up, k_down, v_up, v_down = [key_states], [key_states], [value_states], [value_states]
    half = planes // 2
    for step in range(half):
        k_up.append(lax.ppermute(k_up[-1], "seq", up))
        if step < half - 1:
            k_down.append(lax.ppermute(k_down[-1], "seq", down))
            v_up.append(lax.ppermute(v_up[-1], "seq", up))
        v_down.append(lax.ppermute(v_down[-1], "seq", down))
        if step == 0:
            listed = jnp.pad(
                block_list.astype(jnp.bfloat16), ((0, PART_ROWS - 1), (0, width - block_list.shape[1]))
            )
            packed = jnp.concatenate([queries, listed], axis=0)
            tiles = [packed] + [
                lax.ppermute(packed, "seq", [(s, s ^ k) for s in range(seq_size)]) for k in range(1, GROUP)
            ]
            lists = jnp.concatenate([t[TILE:TILE + 1, :block_list.shape[1]] for t in tiles], axis=0)
            lists = jnp.concatenate(
                [lists.astype(jnp.int32), jnp.broadcast_to(text_slots[None, :], (GROUP, text_slots.shape[0]))],
                axis=1,
            )
            order = [0] + [sign * i for i in range(1, half) for sign in (-1, 1)] + [half]
            slots = (me + GROUP * jnp.asarray(order, jnp.int32)) % seq_size
            need = jnp.any(lists[:, None, :] == slots[None, :, None], axis=2).astype(jnp.int32)

    rows = GROUP * heads
    state = (
        jax.ShapeDtypeStruct((rows, HD, TILE), jnp.float32),
        jax.ShapeDtypeStruct((rows, 1, TILE), jnp.float32),
        jax.ShapeDtypeStruct((rows, 1, TILE), jnp.float32),
    )
    factor = LOG2E / math.sqrt(HD)
    smem = [pl.BlockSpec(memory_space=pltpu.SMEM)]

    def shards(pairs):
        return [k for k, _ in pairs] + [v for _, v in pairs]

    first = [(key_states, value_states), (k_up[1], v_up[1]), (k_down[1], v_down[1])]
    held = pl.pallas_call(
        functools.partial(open_kernel, factor, 3),
        out_shape=state,
        in_specs=smem + vmem_specs(GROUP + 6),
        out_specs=tuple(vmem_specs(3)),
        compiler_params=PARAMS,
        cost_estimate=attend_cost(27),
        name="attend_near",
    )(need, *tiles, *shards(first))
    second = [pair for i in range(2, half) for pair in ((k_up[i], v_up[i]), (k_down[i], v_down[i]))]
    held = pl.pallas_call(
        functools.partial(more_kernel, factor, 3, len(second)),
        out_shape=state,
        in_specs=smem + vmem_specs(GROUP + 2 * len(second) + 3),
        out_specs=tuple(vmem_specs(3)),
        compiler_params=PARAMS,
        cost_estimate=attend_cost(18),
        name="attend_far",
    )(need, *tiles, *shards(second), *held)
    keep, keep_sum, send = pl.pallas_call(
        functools.partial(close_kernel, factor, planes - 1),
        out_shape=(
            jax.ShapeDtypeStruct((2, width, TILE), jnp.float32),
            jax.ShapeDtypeStruct((2, 8, TILE), jnp.float32),
            jax.ShapeDtypeStruct((2, width + 2 * PART_ROWS, TILE), jnp.bfloat16),
        ),
        in_specs=smem + vmem_specs(GROUP + 5),
        out_specs=tuple(vmem_specs(3)),
        scratch_shapes=[pltpu.VMEM(s.shape, s.dtype) for s in state],
        compiler_params=PARAMS,
        cost_estimate=attend_cost(9),
        name="attend_last",
    )(need, *tiles, k_up[half], v_down[half], *held)

    other = lax.ppermute(send, "seq", [(s, s ^ 1) for s in range(seq_size)])
    keep, keep_sum, send = pl.pallas_call(
        merge_kernel,
        out_shape=(
            jax.ShapeDtypeStruct((1, width, TILE), jnp.float32),
            jax.ShapeDtypeStruct((1, 8, TILE), jnp.float32),
            jax.ShapeDtypeStruct((1, width + 2 * PART_ROWS, TILE), jnp.bfloat16),
        ),
        in_specs=vmem_specs(3),
        out_specs=tuple(vmem_specs(3)),
        compiler_params=PARAMS,
        name="merge",
    )(keep, keep_sum, other)
    other = lax.ppermute(send, "seq", [(s, s ^ 2) for s in range(seq_size)])
    shares = pl.pallas_call(
        project_kernel,
        out_shape=jax.ShapeDtypeStruct((head_size, TILE, width), jnp.bfloat16),
        in_specs=vmem_specs(4),
        out_specs=pl.BlockSpec(memory_space=pltpu.VMEM),
        scratch_shapes=[pltpu.VMEM((TILE, width), jnp.bfloat16)],
        compiler_params=PARAMS,
        name="project",
    )(keep, keep_sum, other, out_weight)
    shares = lax.all_to_all(shares, "head", 0, 0, tiled=False)
    return jnp.sum(shares.astype(jnp.float32), axis=0).astype(jnp.bfloat16)


def solution(mesh):
    return jax.shard_map(
        functools.partial(per_device, mesh.shape["seq"], mesh.shape["head"]),
        mesh=mesh,
        in_specs=(
            P("seq", "head"),
            P("seq", "head"),
            P("seq", "head"),
            P("seq", None),
            P(),
            P("head", None),
        ),
        out_specs=P("seq", "head"),
        check_vma=False,
    )
```

time: 282 us -> 102 us (0.36)
  the two profiles are of different devices: /device:TPU:2 before, /device:TPU:64 now
where the time goes in v2:
time: 102 us; the launch traced here: 101 us
  blocking collectives  29.4 us (29%)
  starting transfers between devices  26.9 us (26%)
  waiting for transfers between devices  19.3 us (19%)
  Pallas kernels  19.1 us (19%)
  other arithmetic  3.43 us (3%)
  local copies, waits for them, and re-layouts  2.59 us (3%)
    all_to_all x1, blocking collectives, per_device(): shares = lax.all_to_all(shares, 'head', 0, 0, tiled=False)  29.4 us
    ppermute x4, starting transfers between devices, per_device(): k_up.append(lax.ppermute(k_up[-1], 'seq', up))  10.5 us
    pallas_call x1, Pallas kernels, per_device(): pl.pallas_call(functools.partial(more_kernel, factor, 3, len(second)), ou...  9.08 us
    ppermute x3, starting transfers between devices, per_device(): k_down.append(lax.ppermute(k_down[-1], 'seq', down))  6.55 us
    ppermute x3, waiting for transfers between devices, per_device(): k_down.append(lax.ppermute(k_down[-1], 'seq', down))  5.83 us
    pallas_call x1, Pallas kernels, per_device(): pl.pallas_call(functools.partial(open_kernel, factor, 3), out_shape=state...  5.78 us
    ppermute x1, waiting for transfers between devices, per_device(): other = lax.ppermute(send, 'seq', [(s, s ^ 2) for s in range(seq_size)])  5.55 us
    ppermute x4, waiting for transfers between devices, per_device(): v_down.append(lax.ppermute(v_down[-1], 'seq', down))  4.11 us
  transfers between devices with their start and end apart: 19, of which 8 were waited for; matrix products, arithmetic and copies ran while one was open for 2% of the time, Pallas kernels for 15%

profile of v2, /device:TPU:64, one launch (start us, length us, event | category | flops | bytes accessed | tf_op | source)
XLA Modules:
  0.0 100.9 jit_solution(10617077931600353058)
XLA Ops:
  0.0 0.7 convert_element_type.13
  0.7 0.9 fusion.1.refs_0_
  1.7 0.2 collective-permute-start.11
  1.9 1.9 %collective-permute-start.3 = (bf16[256,384]{1,0:T(8,128)(2,1)}, bf16[256,384]{1,0:T(8,128)(2,1)S(1)}, u32[]{:S(2)}, u32[]{:S(2)}) collective-permute-start(bf16[256,384]{1,0:T(8,128)(2,1)} %refs_4_.1), channel_id=1, source_target_pairs={{0,32},{8,40},{16,48},{24,56},{32,64},{40,72},{48,80},{56,88},{64,... | collective-permute-start | bytes 589832 | tf_op jit(solution)/shard_map/ppermute | solution.py:178
  3.9 1.5 %collective-permute-start.1 = (bf16[272,384]{1,0:T(8,128)(2,1)S(1)}, bf16[272,384]{1,0:T(8,128)(2,1)S(1)}, u32[]{:S(2)}, u32[]{:S(2)}) collective-permute-start(bf16[272,384]{1,0:T(8,128)(2,1)S(1)} %fusion.1.refs_0_), channel_id=1, source_target_pairs={{0,16},{8,24},{16,0},{24,8},{32,48},{40,56},{48,32},{56,40},{64,80... | collective-permute-start | bytes 626696 | tf_op jit(solution)/shard_map/ppermute | solution.py:189
  5.4 4.3 %collective-permute-done.11.refs_6_ = bf16[256,384]{1,0:T(8,128)(2,1)S(1)} collective-permute-done((bf16[256,384]{1,0:T(8,128)(2,1)}, bf16[256,384]{1,0:T(8,128)(2,1)S(1)}, u32[]{:S(2)}, u32[]{:S(2)}) %collective-permute-start.11) | collective-permute-done | bytes 196640 | tf_op jit(solution)/shard_map/ppermute | solution.py:180
  9.7 0.6 collective-permute-start.2
  10.3 3.1 %collective-permute-start.14 = (bf16[256,384]{1,0:T(8,128)(2,1)}, bf16[256,384]{1,0:T(8,128)(2,1)S(1)}, u32[]{:S(2)}, u32[]{:S(2)}) collective-permute-start(bf16[256,384]{1,0:T(8,128)(2,1)} %refs_7_.1), channel_id=1, source_target_pairs={{0,32},{8,40},{16,48},{24,56},{32,64},{40,72},{48,80},{56,88},{64,... | collective-permute-start | bytes 589832 | tf_op jit(solution)/shard_map/ppermute | solution.py:181
  13.6 3.1 %collective-permute-start.4 = (bf16[256,384]{1,0:T(8,128)(2,1)S(1)}, bf16[256,384]{1,0:T(8,128)(2,1)S(1)}, u32[]{:S(2)}, u32[]{:S(2)}) collective-permute-start(bf16[256,384]{1,0:T(8,128)(2,1)S(1)} %collective-permute-done.3.refs_5_), channel_id=1, source_target_pairs={{0,32},{8,40},{16,48},{24,56},{32,64},{40,72},{48,80},{56,88},{64,... | collective-permute-start | bytes 589832 | tf_op jit(solution)/shard_map/ppermute | solution.py:178
  16.7 0.7 and_select_fusion
  17.4 0.7 pad.6.clone
  18.1 1.1 %collective-permute-done.14.refs_8_ = bf16[256,384]{1,0:T(8,128)(2,1)S(1)} collective-permute-done((bf16[256,384]{1,0:T(8,128)(2,1)}, bf16[256,384]{1,0:T(8,128)(2,1)S(1)}, u32[]{:S(2)}, u32[]{:S(2)}) %collective-permute-start.14) | collective-permute-done | bytes 196640 | tf_op jit(solution)/shard_map/ppermute | solution.py:181
  19.3 3.0 %collective-permute-start.12 = (bf16[256,384]{1,0:T(8,128)(2,1)S(1)}, bf16[256,384]{1,0:T(8,128)(2,1)S(1)}, u32[]{:S(2)}, u32[]{:S(2)}) collective-permute-start(bf16[256,384]{1,0:T(8,128)(2,1)S(1)} %collective-permute-done.11.refs_6_), channel_id=1, source_target_pairs={{0,224},{8,232},{16,240},{24,248},{32,0},{40,8},{48,16},{56,24},{6... | collective-permute-start | bytes 589832 | tf_op jit(solution)/shard_map/ppermute | solution.py:180
  22.3 0.9 collective-permute-done.4.refs_4_
  23.2 2.5 %collective-permute-start.5 = (bf16[256,384]{1,0:T(8,128)(2,1)S(1)}, bf16[256,384]{1,0:T(8,128)(2,1)S(1)}, u32[]{:S(2)}, u32[]{:S(2)}) collective-permute-start(bf16[256,384]{1,0:T(8,128)(2,1)S(1)} %collective-permute-done.4.refs_4_), channel_id=1, source_target_pairs={{0,32},{8,40},{16,48},{24,56},{32,64},{40,72},{48,80},{56,88},{64,... | collective-permute-start | bytes 589832 | tf_op jit(solution)/shard_map/ppermute | solution.py:178
  25.7 1.6 %collective-permute-done.12.refs_5_ = bf16[256,384]{1,0:T(8,128)(2,1)S(1)} collective-permute-done((bf16[256,384]{1,0:T(8,128)(2,1)S(1)}, bf16[256,384]{1,0:T(8,128)(2,1)S(1)}, u32[]{:S(2)}, u32[]{:S(2)}) %collective-permute-start.12) | collective-permute-done | bytes 196640 | tf_op jit(solution)/shard_map/ppermute | solution.py:180
  27.3 3.4 %collective-permute-start.13 = (bf16[256,384]{1,0:T(8,128)(2,1)S(1)}, bf16[256,384]{1,0:T(8,128)(2,1)S(1)}, u32[]{:S(2)}, u32[]{:S(2)}) collective-permute-start(bf16[256,384]{1,0:T(8,128)(2,1)S(1)} %collective-permute-done.12.refs_5_), channel_id=1, source_target_pairs={{0,224},{8,232},{16,240},{24,248},{32,0},{40,8},{48,16},{56,24},{6... | collective-permute-start | bytes 589832 | tf_op jit(solution)/shard_map/ppermute | solution.py:180
  30.7 3.9 %collective-permute-done.9.refs_11_ = bf16[256,384]{1,0:T(8,128)(2,1)S(1)} collective-permute-done((bf16[256,384]{1,0:T(8,128)(2,1)S(1)}, bf16[256,384]{1,0:T(8,128)(2,1)S(1)}, u32[]{:S(2)}, u32[]{:S(2)}) %collective-permute-start.9) | collective-permute-done | bytes 196640 | tf_op jit(solution)/shard_map/ppermute | solution.py:182
  34.6 0.3 collective-permute-start.10
  34.9 3.0 %collective-permute-start.6 = (bf16[256,384]{1,0:T(8,128)(2,1)S(1)}, bf16[256,384]{1,0:T(8,128)(2,1)S(1)}, u32[]{:S(2)}, u32[]{:S(2)}) collective-permute-start(bf16[256,384]{1,0:T(8,128)(2,1)S(1)} %collective-permute-done.5.refs_6_), channel_id=1, source_target_pairs={{0,32},{8,40},{16,48},{24,56},{32,64},{40,72},{48,80},{56,88},{64,... | collective-permute-start | bytes 589832 | tf_op jit(solution)/shard_map/ppermute | solution.py:178
  37.9 0.2 compare_reduce_fusion
  38.2 0.9 copy-done.1
  39.1 0.9 copy-done.2
  40.0 5.8 %attend_near.1 = (f32[12,128,256]{2,1,0:T(8,128)S(1)}, f32[12,1,256]{2,1,0:T(1,128)S(1)}, f32[12,1,256]{2,1,0:T(1,128)S(1)}) custom-call(s32[4,8]{1,0:T(4,128)S(1)} %convert_element_type.15.need_ref, bf16[272,384]{1,0:T(8,128)(2,1)S(1)} %fusion.1.refs_0_, bf16[272,384]{1,0:T(8,128)(2,1)S(1)} %collective-permute-done.refs_1_, ...), custom_call_target="tpu_custom_call" | custom-call | flops 905969664 | bytes 4194304 | tf_op jit(solution)/shard_map/attend_near/pallas_call | solution.py:213
  45.8 9.1 %attend_far.1 = (f32[12,128,256]{2,1,0:T(8,128)S(1)}, f32[12,1,256]{2,1,0:T(1,128)S(1)}, f32[12,1,256]{2,1,0:T(1,128)S(1)}) custom-call(s32[4,8]{1,0:T(4,128)S(1)} %convert_element_type.15.need_ref, bf16[272,384]{1,0:T(8,128)(2,1)S(1)} %fusion.1.refs_0_, bf16[272,384]{1,0:T(8,128)(2,1)S(1)} %collective-permute-done.refs_1_, ...), custom_call_target="tpu_custom_call" | custom-call | flops 603979776 | bytes 4194304 | tf_op jit(solution)/shard_map/attend_far/pallas_call | solution.py:223
  54.9 2.8 %attend_last.1 = (f32[2,384,256]{2,1,0:T(8,128)S(1)}, f32[2,8,256]{2,1,0:T(8,128)S(1)}, bf16[2,416,256]{2,1,0:T(8,128)(2,1)S(1)}) custom-call(s32[4,8]{1,0:T(4,128)S(1)} %convert_element_type.15.need_ref, bf16[272,384]{1,0:T(8,128)(2,1)S(1)} %fusion.1.refs_0_, bf16[272,384]{1,0:T(8,128)(2,1)S(1)} %collective-permute-done.refs_1_, ...), custom_call_target="tpu_custom_call" | custom-call | flops 301989888 | bytes 4194304 | tf_op jit(solution)/shard_map/attend_last/pallas_call | solution.py:232
  57.9 1.8 %collective-permute-done.17.other_ref = bf16[2,416,256]{2,1,0:T(8,128)(2,1)S(1)} collective-permute-done((bf16[2,416,256]{2,1,0:T(8,128)(2,1)S(1)}, bf16[2,416,256]{2,1,0:T(8,128)(2,1)S(1)}, u32[]{:S(2)}, u32[]{:S(2)}) %collective-permute-start.17) | collective-permute-done | bytes 426016 | tf_op jit(solution)/shard_map/ppermute | solution.py:247
  59.8 3.9 %collective-permute-start.18 = (bf16[1,416,256]{2,1,0:T(8,128)(2,1)S(1)}, bf16[1,416,256]{2,1,0:T(8,128)(2,1)S(1)}, u32[]{:S(2)}, u32[]{:S(2)}) collective-permute-start(bf16[1,416,256]{2,1,0:T(8,128)(2,1)S(1)} %get-tuple-element.28), channel_id=1, source_target_pairs={{0,16},{8,24},{16,0},{24,8},{32,48},{40,56},{48,32},{56,40},{64,80... | collective-permute-start | bytes 638984 | tf_op jit(solution)/shard_map/ppermute | solution.py:260
  63.8 5.6 %collective-permute-done.18.other_ref = bf16[1,416,256]{2,1,0:T(8,128)(2,1)S(1)} collective-permute-done((bf16[1,416,256]{2,1,0:T(8,128)(2,1)S(1)}, bf16[1,416,256]{2,1,0:T(8,128)(2,1)S(1)}, u32[]{:S(2)}, u32[]{:S(2)}) %collective-permute-start.18) | collective-permute-done | bytes 213024 | tf_op jit(solution)/shard_map/ppermute | solution.py:260
  69.3 1.3 %project.1 = bf16[8,256,384]{2,1,0:T(8,128)(2,1)S(1)} custom-call(f32[1,384,256]{2,1,0:T(8,128)S(1)} %get-tuple-element.26.mine_ref, f32[1,8,256]{2,1,0:T(8,128)S(1)} %get-tuple-element.27.mine_sum_ref, bf16[1,416,256]{2,1,0:T(8,128)(2,1)S(1)} %collective-permute-done.18.other_ref, bf16[384,3072]{1,0:T(8,128)(2,1)S(1)} %copy-done), custom_call_target="tpu_custom_call" | custom-call | tf_op jit(solution)/shard_map/project/pallas_call | solution.py:261
  70.6 29.4 %all_to_all.5 = bf16[8,256,384]{2,1,0:T(8,128)(2,1)S(1)} all-to-all(bf16[8,256,384]{2,1,0:T(8,128)(2,1)S(1)} %project.1), channel_id=1, replica_groups=mesh['seq'=32,'head'=8] {'head'}, dimensions={0} | all-to-all | bytes 3145728 | tf_op jit(solution)/shard_map/all_to_all | solution.py:270
  100.0 0.9 reduce_sum.12
  (30 shorter events, 0.8 us)
Async XLA Ops:
  1.6 15.1 %collective-permute-start = (bf16[272,384]{1,0:T(8,128)(2,1)S(1)}, bf16[272,384]{1,0:T(8,128)(2,1)S(1)}, u32[]{:S(2)}, u32[]{:S(2)}) collective-permute-start(bf16[272,384]{1,0:T(8,128)(2,1)S(1)} %fusion.1.refs_0_), channel_id=1, source_target_pairs={{0,8},{8,0},{16,24},{24,16},{32,40},{40,32},{48,56},{56,48},{64,72... | collective-permute-start | bytes 626696 | tf_op jit(solution)/shard_map/ppermute | solution.py:189
  1.7 8.0 %collective-permute-start.11 = (bf16[256,384]{1,0:T(8,128)(2,1)}, bf16[256,384]{1,0:T(8,128)(2,1)S(1)}, u32[]{:S(2)}, u32[]{:S(2)}) collective-permute-start(bf16[256,384]{1,0:T(8,128)(2,1)} %refs_4_.1), channel_id=1, source_target_pairs={{0,224},{8,232},{16,240},{24,248},{32,0},{40,8},{48,16},{56,24},{6... | collective-permute-start | bytes 589832 | tf_op jit(solution)/shard_map/ppermute | solution.py:180
  1.9 8.4 %collective-permute-start.3 = (bf16[256,384]{1,0:T(8,128)(2,1)}, bf16[256,384]{1,0:T(8,128)(2,1)S(1)}, u32[]{:S(2)}, u32[]{:S(2)}) collective-permute-start(bf16[256,384]{1,0:T(8,128)(2,1)} %refs_4_.1), channel_id=1, source_target_pairs={{0,32},{8,40},{16,48},{24,56},{32,64},{40,72},{48,80},{56,88},{64,... | collective-permute-start | bytes 589832 | tf_op jit(solution)/shard_map/ppermute | solution.py:178
  3.8 9.8 %collective-permute-start.7 = (bf16[256,384]{1,0:T(8,128)(2,1)}, bf16[256,384]{1,0:T(8,128)(2,1)S(1)}, u32[]{:S(2)}, u32[]{:S(2)}) collective-permute-start(bf16[256,384]{1,0:T(8,128)(2,1)} %refs_7_.1), channel_id=1, source_target_pairs={{0,224},{8,232},{16,240},{24,248},{32,0},{40,8},{48,16},{56,24},{6... | collective-permute-start | bytes 589832 | tf_op jit(solution)/shard_map/ppermute | solution.py:182
  3.9 18.3 %collective-permute-start.1 = (bf16[272,384]{1,0:T(8,128)(2,1)S(1)}, bf16[272,384]{1,0:T(8,128)(2,1)S(1)}, u32[]{:S(2)}, u32[]{:S(2)}) collective-permute-start(bf16[272,384]{1,0:T(8,128)(2,1)S(1)} %fusion.1.refs_0_), channel_id=1, source_target_pairs={{0,16},{8,24},{16,0},{24,8},{32,48},{40,56},{48,32},{56,40},{64,80... | collective-permute-start | bytes 626696 | tf_op jit(solution)/shard_map/ppermute | solution.py:189
  9.7 12.6 %collective-permute-start.2 = (bf16[272,384]{1,0:T(8,128)(2,1)S(1)}, bf16[272,384]{1,0:T(8,128)(2,1)S(1)}, u32[]{:S(2)}, u32[]{:S(2)}) collective-permute-start(bf16[272,384]{1,0:T(8,128)(2,1)S(1)} %fusion.1.refs_0_), channel_id=1, source_target_pairs={{0,24},{8,16},{16,8},{24,0},{32,56},{40,48},{48,40},{56,32},{64,88... | collective-permute-start | bytes 626696 | tf_op jit(solution)/shard_map/ppermute | solution.py:189
  10.3 9.0 %collective-permute-start.14 = (bf16[256,384]{1,0:T(8,128)(2,1)}, bf16[256,384]{1,0:T(8,128)(2,1)S(1)}, u32[]{:S(2)}, u32[]{:S(2)}) collective-permute-start(bf16[256,384]{1,0:T(8,128)(2,1)} %refs_7_.1), channel_id=1, source_target_pairs={{0,32},{8,40},{16,48},{24,56},{32,64},{40,72},{48,80},{56,88},{64,... | collective-permute-start | bytes 589832 | tf_op jit(solution)/shard_map/ppermute | solution.py:181
  13.6 9.6 %collective-permute-start.4 = (bf16[256,384]{1,0:T(8,128)(2,1)S(1)}, bf16[256,384]{1,0:T(8,128)(2,1)S(1)}, u32[]{:S(2)}, u32[]{:S(2)}) collective-permute-start(bf16[256,384]{1,0:T(8,128)(2,1)S(1)} %collective-permute-done.3.refs_5_), channel_id=1, source_target_pairs={{0,32},{8,40},{16,48},{24,56},{32,64},{40,72},{48,80},{56,88},{64,... | collective-permute-start | bytes 589832 | tf_op jit(solution)/shard_map/ppermute | solution.py:178
  16.7 8.9 %collective-permute-start.8 = (bf16[256,384]{1,0:T(8,128)(2,1)S(1)}, bf16[256,384]{1,0:T(8,128)(2,1)S(1)}, u32[]{:S(2)}, u32[]{:S(2)}) collective-permute-start(bf16[256,384]{1,0:T(8,128)(2,1)S(1)} %collective-permute-done.7.refs_9_), channel_id=1, source_target_pairs={{0,224},{8,232},{16,240},{24,248},{32,0},{40,8},{48,16},{56,24},{6... | collective-permute-start | bytes 589832 | tf_op jit(solution)/shard_map/ppermute | solution.py:182
  19.3 8.0 %collective-permute-start.12 = (bf16[256,384]{1,0:T(8,128)(2,1)S(1)}, bf16[256,384]{1,0:T(8,128)(2,1)S(1)}, u32[]{:S(2)}, u32[]{:S(2)}) collective-permute-start(bf16[256,384]{1,0:T(8,128)(2,1)S(1)} %collective-permute-done.11.refs_6_), channel_id=1, source_target_pairs={{0,224},{8,232},{16,240},{24,248},{32,0},{40,8},{48,16},{56,24},{6... | collective-permute-start | bytes 589832 | tf_op jit(solution)/shard_map/ppermute | solution.py:180
  22.3 8.4 %collective-permute-start.15 = (bf16[256,384]{1,0:T(8,128)(2,1)S(1)}, bf16[256,384]{1,0:T(8,128)(2,1)S(1)}, u32[]{:S(2)}, u32[]{:S(2)}) collective-permute-start(bf16[256,384]{1,0:T(8,128)(2,1)S(1)} %collective-permute-done.14.refs_8_), channel_id=1, source_target_pairs={{0,32},{8,40},{16,48},{24,56},{32,64},{40,72},{48,80},{56,88},{64,... | collective-permute-start | bytes 589832 | tf_op jit(solution)/shard_map/ppermute | solution.py:181
  23.2 11.7 %collective-permute-start.5 = (bf16[256,384]{1,0:T(8,128)(2,1)S(1)}, bf16[256,384]{1,0:T(8,128)(2,1)S(1)}, u32[]{:S(2)}, u32[]{:S(2)}) collective-permute-start(bf16[256,384]{1,0:T(8,128)(2,1)S(1)} %collective-permute-done.4.refs_4_), channel_id=1, source_target_pairs={{0,32},{8,40},{16,48},{24,56},{32,64},{40,72},{48,80},{56,88},{64,... | collective-permute-start | bytes 589832 | tf_op jit(solution)/shard_map/ppermute | solution.py:178
  25.7 9.0 %collective-permute-start.9 = (bf16[256,384]{1,0:T(8,128)(2,1)S(1)}, bf16[256,384]{1,0:T(8,128)(2,1)S(1)}, u32[]{:S(2)}, u32[]{:S(2)}) collective-permute-start(bf16[256,384]{1,0:T(8,128)(2,1)S(1)} %collective-permute-done.8.refs_9_), channel_id=1, source_target_pairs={{0,224},{8,232},{16,240},{24,248},{32,0},{40,8},{48,16},{56,24},{6... | collective-permute-start | bytes 589832 | tf_op jit(solution)/shard_map/ppermute | solution.py:182
  27.3 18.5 %collective-permute-start.13 = (bf16[256,384]{1,0:T(8,128)(2,1)S(1)}, bf16[256,384]{1,0:T(8,128)(2,1)S(1)}, u32[]{:S(2)}, u32[]{:S(2)}) collective-permute-start(bf16[256,384]{1,0:T(8,128)(2,1)S(1)} %collective-permute-done.12.refs_5_), channel_id=1, source_target_pairs={{0,224},{8,232},{16,240},{24,248},{32,0},{40,8},{48,16},{56,24},{6... | collective-permute-start | bytes 589832 | tf_op jit(solution)/shard_map/ppermute | solution.py:180
  30.7 15.1 %collective-permute-start.16 = (bf16[256,384]{1,0:T(8,128)(2,1)S(1)}, bf16[256,384]{1,0:T(8,128)(2,1)S(1)}, u32[]{:S(2)}, u32[]{:S(2)}) collective-permute-start(bf16[256,384]{1,0:T(8,128)(2,1)S(1)} %collective-permute-done.15.refs_8_), channel_id=1, source_target_pairs={{0,32},{8,40},{16,48},{24,56},{32,64},{40,72},{48,80},{56,88},{64,... | collective-permute-start | bytes 589832 | tf_op jit(solution)/shard_map/ppermute | solution.py:181
  34.6 20.3 %collective-permute-start.10 = (bf16[256,384]{1,0:T(8,128)(2,1)S(1)}, bf16[256,384]{1,0:T(8,128)(2,1)S(1)}, u32[]{:S(2)}, u32[]{:S(2)}) collective-permute-start(bf16[256,384]{1,0:T(8,128)(2,1)S(1)} %collective-permute-done.9.refs_11_), channel_id=1, source_target_pairs={{0,224},{8,232},{16,240},{24,248},{32,0},{40,8},{48,16},{56,24},{6... | collective-permute-start | bytes 589832 | tf_op jit(solution)/shard_map/ppermute | solution.py:182
  34.9 20.0 %collective-permute-start.6 = (bf16[256,384]{1,0:T(8,128)(2,1)S(1)}, bf16[256,384]{1,0:T(8,128)(2,1)S(1)}, u32[]{:S(2)}, u32[]{:S(2)}) collective-permute-start(bf16[256,384]{1,0:T(8,128)(2,1)S(1)} %collective-permute-done.5.refs_6_), channel_id=1, source_target_pairs={{0,32},{8,40},{16,48},{24,56},{32,64},{40,72},{48,80},{56,88},{64,... | collective-permute-start | bytes 589832 | tf_op jit(solution)/shard_map/ppermute | solution.py:178
  38.2 0.9 copy-start.1
  39.1 0.9 copy-start.2
  54.9 14.4 %copy-start = (bf16[384,3072]{1,0:T(8,128)(2,1)S(1)}, bf16[384,3072]{1,0:T(8,128)(2,1)}, u32[]{:S(2)}) copy-start(bf16[384,3072]{1,0:T(8,128)(2,1)} %weight_ref.1) | copy-start | bytes 7077892
  57.8 1.9 %collective-permute-start.17 = (bf16[2,416,256]{2,1,0:T(8,128)(2,1)S(1)}, bf16[2,416,256]{2,1,0:T(8,128)(2,1)S(1)}, u32[]{:S(2)}, u32[]{:S(2)}) collective-permute-start(bf16[2,416,256]{2,1,0:T(8,128)(2,1)S(1)} %get-tuple-element.25), channel_id=1, source_target_pairs={{0,8},{8,0},{16,24},{24,16},{32,40},{40,32},{48,56},{56,48},{64,72... | collective-permute-start | bytes 1277960 | tf_op jit(solution)/shard_map/ppermute | solution.py:247
  59.8 9.5 %collective-permute-start.18 = (bf16[1,416,256]{2,1,0:T(8,128)(2,1)S(1)}, bf16[1,416,256]{2,1,0:T(8,128)(2,1)S(1)}, u32[]{:S(2)}, u32[]{:S(2)}) collective-permute-start(bf16[1,416,256]{2,1,0:T(8,128)(2,1)S(1)} %get-tuple-element.28), channel_id=1, source_target_pairs={{0,16},{8,24},{16,0},{24,8},{32,48},{40,56},{48,32},{56,40},{64,80... | collective-permute-start | bytes 638984 | tf_op jit(solution)/shard_map/ppermute | solution.py:260

commit v3 on v2

--- a/solution.py
+++ b/solution.py
@@ -55,62 +55,95 @@
     return outs, sums
 
 
-def visit_shards(factor, need_ref, first, q_refs, shards, acc_ref, peak_ref, total_ref):
-    heads = q_refs[0].shape[1] // HD
-    for j, (k_ref, v_ref) in enumerate(shards):
-        for t, q_ref in enumerate(q_refs):
-
-            @pl.when(need_ref[t, first + j] > 0)
-            def _():
-                for h in range(heads):
-                    cols = slice(h * HD, (h + 1) * HD)
-                    scores = lax.dot_general(
+def transpose_values(v_refs, vt_ref, first):
+    for j, v_ref in enumerate(v_refs):
+        for h in range(v_ref.shape[1] // HD):
+            vt_ref[first + j, h] = v_ref[:, h * HD:(h + 1) * HD].T
+
+
+def visit_group(factor, need_ref, first, q_ref, k_refs, vt_ref, vt_first, state):
+    acc_ref, peak_ref, total_ref = state
+    heads = q_ref.shape[2] // HD
+
+    def visit(t, carry):
+        wanted = [need_ref[t, first + j] for j in range(len(k_refs))]
+
+        @pl.when(sum(wanted[1:], wanted[0]) > 0)
+        def _():
+            shift = [jnp.where(w > 0, 0.0, LOWEST) for w in wanted]
+
+            def scores_of(h):
+                cols = slice(h * HD, (h + 1) * HD)
+                return [
+                    lax.dot_general(
                         k_ref[:, cols],
-                        q_ref[0:TILE, cols],
+                        q_ref[t, :, cols],
                         (((1,), (1,)), ((), ())),
                         preferred_element_type=jnp.float32,
                     )
-                    row = t * heads + h
-                    old = peak_ref[row]
-                    peak = jnp.maximum(old, jnp.max(scores, axis=0, keepdims=True) * factor)
-                    weights = jnp.exp2(scores * factor - peak)
-                    shrink = jnp.exp2(old - peak)
-                    peak_ref[row] = peak
-                    total_ref[row] = total_ref[row] * shrink + jnp.sum(weights, axis=0, keepdims=True)
-                    acc_ref[row] = acc_ref[row] * shrink + lax.dot_general(
-                        v_ref[:, cols],
-                        weights.astype(jnp.bfloat16),
-                        (((0,), (0,)), ((), ())),
-                        preferred_element_type=jnp.float32,
-                    )
-
-
-def open_kernel(factor, count, need_ref, *refs):
-    q_refs, kv_refs, (acc_ref, peak_ref, total_ref) = refs[:GROUP], refs[GROUP:-3], refs[-3:]
+                    for k_ref in k_refs
+                ]
+
+            following = scores_of(0)
+            for h in range(heads):
+                scores = following
+                if h + 1 < heads:
+                    following = scores_of(h + 1)
+                row = t * heads + h
+                old = peak_ref[row]
+                peak = old
+                for part, low in zip(scores, shift):
+                    peak = jnp.maximum(peak, jnp.max(part, axis=0, keepdims=True) * factor + low)
+                weights = [jnp.exp2(part * factor - (peak - low)) for part, low in zip(scores, shift)]
+                shrink = jnp.exp2(old - peak)
+                sums = [jnp.sum(w, axis=0, keepdims=True) for w in weights]
+                dots = [
+                    jnp.dot(vt_ref[vt_first + j, h], w.astype(jnp.bfloat16), preferred_element_type=jnp.float32)
+                    for j, w in enumerate(weights)
+                ]
+                peak_ref[row] = peak
+                total_ref[row] = total_ref[row] * shrink + sum(sums[1:], sums[0])
+                acc_ref[row] = acc_ref[row] * shrink + sum(dots[1:], dots[0])
+
+        return carry
+
+    lax.fori_loop(0, q_ref.shape[0], visit, 0)
+
+
+def near_kernel(factor, count, need_ref, *refs):
+    q_refs, k_refs, v_refs = refs[:GROUP], refs[GROUP:GROUP + count], refs[GROUP + count:GROUP + 2 * count]
+    stacked_ref, acc_ref, peak_ref, total_ref, vt_ref = refs[GROUP + 2 * count:]
     acc_ref[...] = jnp.zeros_like(acc_ref)
     peak_ref[...] = jnp.full_like(peak_ref, LOWEST)
     total_ref[...] = jnp.zeros_like(total_ref)
-    shards = list(zip(kv_refs[:count], kv_refs[count:]))
-    visit_shards(factor, need_ref, 0, q_refs, shards, acc_ref, peak_ref, total_ref)
-
-
-def more_kernel(factor, first, count, need_ref, *refs):
-    q_refs, kv_refs = refs[:GROUP], refs[GROUP:GROUP + 2 * count]
-    held, state = refs[GROUP + 2 * count:-3], refs[-3:]
-    for source, target in zip(held, state):
-        target[...] = source[...]
-    shards = list(zip(kv_refs[:count], kv_refs[count:]))
-    visit_shards(factor, need_ref, first, q_refs, shards, *state)
-
-
-def close_kernel(factor, first, need_ref, *refs):
-    q_refs, kv_refs = refs[:GROUP], refs[GROUP:GROUP + 2]
-    held = refs[GROUP + 2:GROUP + 5]
-    keep_ref, keep_sum_ref, send_ref, acc_ref, peak_ref, total_ref = refs[GROUP + 5:]
-    heads = q_refs[0].shape[1] // HD
+    for t, q_ref in enumerate(q_refs):
+        stacked_ref[t] = q_ref[0:TILE, :]
+    transpose_values(v_refs, vt_ref, 0)
+    visit_group(factor, need_ref, 0, stacked_ref, k_refs, vt_ref, 0, (acc_ref, peak_ref, total_ref))
+
+
+def far_kernel(factor, groups, need_ref, stacked_ref, *refs):
+    count = sum(groups)
+    k_refs, v_refs = refs[:count], refs[count:2 * count]
+    held = refs[2 * count:2 * count + 3]
+    keep_ref, keep_sum_ref, send_ref, acc_ref, peak_ref, total_ref, vt_ref = refs[2 * count + 3:]
+    heads = stacked_ref.shape[2] // HD
     for source, target in zip(held, (acc_ref, peak_ref, total_ref)):
         target[...] = source[...]
-    visit_shards(factor, need_ref, first, q_refs, [kv_refs], acc_ref, peak_ref, total_ref)
+    transpose_values(v_refs, vt_ref, 0)
+    begin = 0
+    for size in groups:
+        visit_group(
+            factor,
+            need_ref,
+            GROUP - 1 + begin,
+            stacked_ref,
+            k_refs[begin:begin + size],
+            vt_ref,
+            begin,
+            (acc_ref, peak_ref, total_ref),
+        )
+        begin += size
     for t in range(GROUP):
         outs, sums = [], []
         for h in range(heads):
@@ -193,7 +226,7 @@
                 [lists.astype(jnp.int32), jnp.broadcast_to(text_slots[None, :], (GROUP, text_slots.shape[0]))],
                 axis=1,
             )
-            order = [0] + [sign * i for i in range(1, half) for sign in (-1, 1)] + [half]
+            order = [0, -1, 1, -3, 3, 4, -2, 2]
             slots = (me + GROUP * jnp.asarray(order, jnp.int32)) % seq_size
             need = jnp.any(lists[:, None, :] == slots[None, :, None], axis=2).astype(jnp.int32)
 
@@ -209,40 +242,36 @@
     def shards(pairs):
         return [k for k, _ in pairs] + [v for _, v in pairs]
 
-    first = [(key_states, value_states), (k_up[1], v_up[1]), (k_down[1], v_down[1])]
-    held = pl.pallas_call(
-        functools.partial(open_kernel, factor, 3),
-        out_shape=state,
-        in_specs=smem + vmem_specs(GROUP + 6),
-        out_specs=tuple(vmem_specs(3)),
+    def vt_scratch(count):
+        return pltpu.VMEM((count, heads, HD, TILE), jnp.bfloat16)
+
+    near = [(key_states, value_states), (k_up[1], v_up[1]), (k_down[1], v_down[1])]
+    stacked = jax.ShapeDtypeStruct((GROUP, TILE, width), jnp.bfloat16)
+    stacked, *held = pl.pallas_call(
+        functools.partial(near_kernel, factor, len(near)),
+        out_shape=(stacked,) + state,
+        in_specs=smem + vmem_specs(GROUP + 2 * len(near)),
+        out_specs=tuple(vmem_specs(4)),
+        scratch_shapes=[vt_scratch(len(near))],
         compiler_params=PARAMS,
         cost_estimate=attend_cost(27),
         name="attend_near",
-    )(need, *tiles, *shards(first))
-    second = [pair for i in range(2, half) for pair in ((k_up[i], v_up[i]), (k_down[i], v_down[i]))]
-    held = pl.pallas_call(
-        functools.partial(more_kernel, factor, 3, len(second)),
-        out_shape=state,
-        in_specs=smem + vmem_specs(GROUP + 2 * len(second) + 3),
-        out_specs=tuple(vmem_specs(3)),
-        compiler_params=PARAMS,
-        cost_estimate=attend_cost(18),
-        name="attend_far",
-    )(need, *tiles, *shards(second), *held)
+    )(need, *tiles, *shards(near))
+    far = [(k_up[3], v_up[3]), (k_down[3], v_down[3]), (k_up[4], v_down[4]), (k_up[2], v_up[2]), (k_down[2], v_down[2])]
     keep, keep_sum, send = pl.pallas_call(
-        functools.partial(close_kernel, factor, planes - 1),
+        functools.partial(far_kernel, factor, (3, 2)),
         out_shape=(
             jax.ShapeDtypeStruct((2, width, TILE), jnp.float32),
             jax.ShapeDtypeStruct((2, 8, TILE), jnp.float32),
             jax.ShapeDtypeStruct((2, width + 2 * PART_ROWS, TILE), jnp.bfloat16),
         ),
-        in_specs=smem + vmem_specs(GROUP + 5),
+        in_specs=smem + vmem_specs(1 + 2 * len(far) + 3),
         out_specs=tuple(vmem_specs(3)),
-        scratch_shapes=[pltpu.VMEM(s.shape, s.dtype) for s in state],
+        scratch_shapes=[pltpu.VMEM(s.shape, s.dtype) for s in state] + [vt_scratch(len(far))],
         compiler_params=PARAMS,
-        cost_estimate=attend_cost(9),
-        name="attend_last",
-    )(need, *tiles, k_up[half], v_down[half], *held)
+        cost_estimate=attend_cost(27),
+        name="attend_far",
+    )(need, stacked, *shards(far), *held)
 
     other = lax.ppermute(send, "seq", [(s, s ^ 1) for s in range(seq_size)])
     keep, keep_sum, send = pl.pallas_call(

time: 102 us -> 91.2 us (0.89)
  the two profiles are of different devices: /device:TPU:64 before, /device:TPU:2 now
where the time goes in v3:
time: 91.2 us; the launch traced here: 90.3 us
  blocking collectives  28.7 us (31%)
  starting transfers between devices  26.4 us (29%)
  waiting for transfers between devices  18.5 us (20%)
  Pallas kernels  10.6 us (12%)
  other arithmetic  3.43 us (4%)
  local copies, waits for them, and re-layouts  2.59 us (3%)
    all_to_all x1, blocking collectives, per_device(): shares = lax.all_to_all(shares, 'head', 0, 0, tiled=False)  28.7 us
    ppermute x4, starting transfers between devices, per_device(): v_down.append(lax.ppermute(v_down[-1], 'seq', down))  11.6 us
    ppermute x3, starting transfers between devices, per_device(): k_down.append(lax.ppermute(k_down[-1], 'seq', down))  7.79 us
    ppermute x4, waiting for transfers between devices, per_device(): k_up.append(lax.ppermute(k_up[-1], 'seq', up))  6.82 us
    ppermute x1, waiting for transfers between devices, per_device(): other = lax.ppermute(send, 'seq', [(s, s ^ 2) for s in range(seq_size)])  5.68 us
    pallas_call x1, Pallas kernels, per_device(): pl.pallas_call(functools.partial(far_kernel, factor, (3, 2)), out_shape=(...  4.72 us
    pallas_call x1, Pallas kernels, per_device(): pl.pallas_call(functools.partial(near_kernel, factor, len(near)), out_sha...  4.48 us
    ppermute x4, waiting for transfers between devices, per_device(): v_down.append(lax.ppermute(v_down[-1], 'seq', down))  3.37 us
  transfers between devices with their start and end apart: 19, of which 7 were waited for; matrix products, arithmetic and copies ran while one was open for 2% of the time, Pallas kernels for 5%

profile of v3, /device:TPU:2, one launch (start us, length us, event | category | flops | bytes accessed | tf_op | source)
XLA Modules:
  0.0 90.3 jit_solution(12744035873813010627)
XLA Ops:
  0.0 0.7 convert_element_type.13
  0.7 0.9 %fusion.1.refs_0_ = bf16[272,384]{1,0:T(8,128)(2,1)S(1)} fusion(bf16[1,27]{1,0:T(2,128)(2,1)S(1)} %convert_element_type.13, bf16[256,384]{1,0:T(8,128)(2,1)} %param.7), kind=kLoop, calls=%fused_computation.2 | loop fusion | flops 626688 | bytes 405558 | tf_op jit(solution)/shard_map/concatenate | solution.py:220
  1.7 2.0 %collective-permute-start.3 = (bf16[256,384]{1,0:T(8,128)(2,1)}, bf16[256,384]{1,0:T(8,128)(2,1)S(1)}, u32[]{:S(2)}, u32[]{:S(2)}) collective-permute-start(bf16[256,384]{1,0:T(8,128)(2,1)} %refs_4_.1), channel_id=1, source_target_pairs={{0,32},{8,40},{16,48},{24,56},{32,64},{40,72},{48,80},{56,88},{64,... | collective-permute-start | bytes 589832 | tf_op jit(solution)/shard_map/ppermute | solution.py:211
  3.7 4.0 %collective-permute-start.4 = (bf16[256,384]{1,0:T(8,128)(2,1)}, bf16[256,384]{1,0:T(8,128)(2,1)S(1)}, u32[]{:S(2)}, u32[]{:S(2)}) collective-permute-start(bf16[256,384]{1,0:T(8,128)(2,1)} %refs_4_.1), channel_id=1, source_target_pairs={{0,224},{8,232},{16,240},{24,248},{32,0},{40,8},{48,16},{56,24},{6... | collective-permute-start | bytes 589832 | tf_op jit(solution)/shard_map/ppermute | solution.py:213
  7.7 1.9 %collective-permute-start.6 = (bf16[256,384]{1,0:T(8,128)(2,1)}, bf16[256,384]{1,0:T(8,128)(2,1)S(1)}, u32[]{:S(2)}, u32[]{:S(2)}) collective-permute-start(bf16[256,384]{1,0:T(8,128)(2,1)} %refs_7_.1), channel_id=1, source_target_pairs={{0,224},{8,232},{16,240},{24,248},{32,0},{40,8},{48,16},{56,24},{6... | collective-permute-start | bytes 589832 | tf_op jit(solution)/shard_map/ppermute | solution.py:215
  9.7 0.5 collective-permute-start.1
  10.2 3.1 %collective-permute-done.3.refs_5_ = bf16[256,384]{1,0:T(8,128)(2,1)S(1)} collective-permute-done((bf16[256,384]{1,0:T(8,128)(2,1)}, bf16[256,384]{1,0:T(8,128)(2,1)S(1)}, u32[]{:S(2)}, u32[]{:S(2)}) %collective-permute-start.3) | collective-permute-done | bytes 196640 | tf_op jit(solution)/shard_map/ppermute | solution.py:211
  13.6 3.4 %collective-permute-done.6.refs_9_ = bf16[256,384]{1,0:T(8,128)(2,1)S(1)} collective-permute-done((bf16[256,384]{1,0:T(8,128)(2,1)}, bf16[256,384]{1,0:T(8,128)(2,1)S(1)}, u32[]{:S(2)}, u32[]{:S(2)}) %collective-permute-start.6) | collective-permute-done | bytes 196640 | tf_op jit(solution)/shard_map/ppermute | solution.py:215
  16.9 0.3 collective-permute-start.7
  17.2 3.3 %collective-permute-start.14 = (bf16[256,384]{1,0:T(8,128)(2,1)S(1)}, bf16[256,384]{1,0:T(8,128)(2,1)S(1)}, u32[]{:S(2)}, u32[]{:S(2)}) collective-permute-start(bf16[256,384]{1,0:T(8,128)(2,1)S(1)} %collective-permute-done.6.refs_9_), channel_id=1, source_target_pairs={{0,224},{8,232},{16,240},{24,248},{32,0},{40,8},{48,16},{56,24},{6... | collective-permute-start | bytes 589832 | tf_op jit(solution)/shard_map/ppermute | solution.py:215
  20.5 0.7 and_select_fusion
  21.2 0.7 pad.6.clone
  21.9 0.9 collective-permute-done.5.refs_8_
  22.8 1.2 %collective-permute-start.9 = (bf16[256,384]{1,0:T(8,128)(2,1)S(1)}, bf16[256,384]{1,0:T(8,128)(2,1)S(1)}, u32[]{:S(2)}, u32[]{:S(2)}) collective-permute-start(bf16[256,384]{1,0:T(8,128)(2,1)S(1)} %collective-permute-done.4.refs_6_), channel_id=1, source_target_pairs={{0,224},{8,232},{16,240},{24,248},{32,0},{40,8},{48,16},{56,24},{6... | collective-permute-start | bytes 589832 | tf_op jit(solution)/shard_map/ppermute | solution.py:213
  24.0 0.9 collective-permute-start.12
  24.8 1.6 %collective-permute-done.7.refs_3_ = bf16[256,384]{1,0:T(8,128)(2,1)S(1)} collective-permute-done((bf16[256,384]{1,0:T(8,128)(2,1)S(1)}, bf16[256,384]{1,0:T(8,128)(2,1)S(1)}, u32[]{:S(2)}, u32[]{:S(2)}) %collective-permute-start.7) | collective-permute-done | bytes 196640 | tf_op jit(solution)/shard_map/ppermute | solution.py:211
  26.4 3.2 %collective-permute-start.15 = (bf16[256,384]{1,0:T(8,128)(2,1)S(1)}, bf16[256,384]{1,0:T(8,128)(2,1)S(1)}, u32[]{:S(2)}, u32[]{:S(2)}) collective-permute-start(bf16[256,384]{1,0:T(8,128)(2,1)S(1)} %collective-permute-done.14.refs_9_), channel_id=1, source_target_pairs={{0,224},{8,232},{16,240},{24,248},{32,0},{40,8},{48,16},{56,24},{6... | collective-permute-start | bytes 589832 | tf_op jit(solution)/shard_map/ppermute | solution.py:215
  29.7 2.6 %collective-permute-start.10 = (bf16[256,384]{1,0:T(8,128)(2,1)S(1)}, bf16[256,384]{1,0:T(8,128)(2,1)S(1)}, u32[]{:S(2)}, u32[]{:S(2)}) collective-permute-start(bf16[256,384]{1,0:T(8,128)(2,1)S(1)} %collective-permute-done.9.refs_4_), channel_id=1, source_target_pairs={{0,224},{8,232},{16,240},{24,248},{32,0},{40,8},{48,16},{56,24},{6... | collective-permute-start | bytes 589832 | tf_op jit(solution)/shard_map/ppermute | solution.py:213
  32.3 1.0 %collective-permute-start.13 = (bf16[256,384]{1,0:T(8,128)(2,1)S(1)}, bf16[256,384]{1,0:T(8,128)(2,1)S(1)}, u32[]{:S(2)}, u32[]{:S(2)}) collective-permute-start(bf16[256,384]{1,0:T(8,128)(2,1)S(1)} %collective-permute-done.12.refs_8_), channel_id=1, source_target_pairs={{0,32},{8,40},{16,48},{24,56},{32,64},{40,72},{48,80},{56,88},{64,... | collective-permute-start | bytes 589832 | tf_op jit(solution)/shard_map/ppermute | solution.py:214
  33.3 2.1 %collective-permute-done.8.refs_0_ = bf16[256,384]{1,0:T(8,128)(2,1)S(1)} collective-permute-done((bf16[256,384]{1,0:T(8,128)(2,1)S(1)}, bf16[256,384]{1,0:T(8,128)(2,1)S(1)}, u32[]{:S(2)}, u32[]{:S(2)}) %collective-permute-start.8) | collective-permute-done | bytes 196640 | tf_op jit(solution)/shard_map/ppermute | solution.py:211
  35.4 0.2 collective-permute-start.11
  35.6 3.1 %collective-permute-start.16 = (bf16[256,384]{1,0:T(8,128)(2,1)S(1)}, bf16[256,384]{1,0:T(8,128)(2,1)S(1)}, u32[]{:S(2)}, u32[]{:S(2)}) collective-permute-start(bf16[256,384]{1,0:T(8,128)(2,1)S(1)} %collective-permute-done.15.refs_6_), channel_id=1, source_target_pairs={{0,224},{8,232},{16,240},{24,248},{32,0},{40,8},{48,16},{56,24},{6... | collective-permute-start | bytes 589832 | tf_op jit(solution)/shard_map/ppermute | solution.py:215
  39.0 0.9 %copy-done.1 = bf16[256,384]{1,0:T(8,128)(2,1)S(1)} copy-done((bf16[256,384]{1,0:T(8,128)(2,1)S(1)}, bf16[256,384]{1,0:T(8,128)(2,1)}, u32[]{:S(2)}) %copy-start.1) | copy-done | bytes 196632
  39.9 0.9 %copy-done.2 = bf16[256,384]{1,0:T(8,128)(2,1)S(1)} copy-done((bf16[256,384]{1,0:T(8,128)(2,1)S(1)}, bf16[256,384]{1,0:T(8,128)(2,1)}, u32[]{:S(2)}) %copy-start.2) | copy-done | bytes 196632
  40.8 4.5 %attend_near.1 = (bf16[4,256,384]{2,1,0:T(8,128)(2,1)S(1)}, f32[12,128,256]{2,1,0:T(8,128)S(1)}, f32[12,1,256]{2,1,0:T(1,128)S(1)}, f32[12,1,256]{2,1,0:T(1,128)S(1)}) custom-call(s32[4,8]{1,0:T(4,128)S(1)} %convert_element_type.15.need_ref, bf16[272,384]{1,0:T(8,128)(2,1)S(1)} %fusion.1.refs_0_, bf16[272,384]{1,0:T(8,128)(2,1)S(1)} %collective-permute-done.refs_1_, ...), custom_call_target="tpu_custom_call" | custom-call | flops 905969664 | bytes 4194304 | tf_op jit(solution)/shard_map/attend_near/pallas_call | solution.py:250
  45.4 4.7 %attend_far.1 = (f32[2,384,256]{2,1,0:T(8,128)S(1)}, f32[2,8,256]{2,1,0:T(8,128)S(1)}, bf16[2,416,256]{2,1,0:T(8,128)(2,1)S(1)}) custom-call(s32[4,8]{1,0:T(4,128)S(1)} %convert_element_type.15.need_ref, bf16[4,256,384]{2,1,0:T(8,128)(2,1)S(1)} %get-tuple-element.15.stacked_ref, bf16[256,384]{1,0:T(8,128)(2,1)S(1)} %collective-permute-done.8.refs_0_, ...), custom_call_target="tpu_custom_call" | custom-call | flops 905969664 | bytes 4194304 | tf_op jit(solution)/shard_map/attend_far/pallas_call | solution.py:261
  50.2 1.8 %collective-permute-done.17.other_ref = bf16[2,416,256]{2,1,0:T(8,128)(2,1)S(1)} collective-permute-done((bf16[2,416,256]{2,1,0:T(8,128)(2,1)S(1)}, bf16[2,416,256]{2,1,0:T(8,128)(2,1)S(1)}, u32[]{:S(2)}, u32[]{:S(2)}) %collective-permute-start.17) | collective-permute-done | bytes 426016 | tf_op jit(solution)/shard_map/ppermute | solution.py:276
  52.1 1.7 %collective-permute-start.18 = (bf16[1,416,256]{2,1,0:T(8,128)(2,1)S(1)}, bf16[1,416,256]{2,1,0:T(8,128)(2,1)S(1)}, u32[]{:S(2)}, u32[]{:S(2)}) collective-permute-start(bf16[1,416,256]{2,1,0:T(8,128)(2,1)S(1)} %get-tuple-element.24), channel_id=1, source_target_pairs={{0,16},{8,24},{16,0},{24,8},{32,48},{40,56},{48,32},{56,40},{64,80... | collective-permute-start | bytes 638984 | tf_op jit(solution)/shard_map/ppermute | solution.py:289
  53.8 5.7 %collective-permute-done.18.other_ref = bf16[1,416,256]{2,1,0:T(8,128)(2,1)S(1)} collective-permute-done((bf16[1,416,256]{2,1,0:T(8,128)(2,1)S(1)}, bf16[1,416,256]{2,1,0:T(8,128)(2,1)S(1)}, u32[]{:S(2)}, u32[]{:S(2)}) %collective-permute-start.18) | collective-permute-done | bytes 213024 | tf_op jit(solution)/shard_map/ppermute | solution.py:289
  59.5 1.2 %project.1 = bf16[8,256,384]{2,1,0:T(8,128)(2,1)S(1)} custom-call(f32[1,384,256]{2,1,0:T(8,128)S(1)} %get-tuple-element.22.mine_ref, f32[1,8,256]{2,1,0:T(8,128)S(1)} %get-tuple-element.23.mine_sum_ref, bf16[1,416,256]{2,1,0:T(8,128)(2,1)S(1)} %collective-permute-done.18.other_ref, bf16[384,3072]{1,0:T(8,128)(2,1)S(1)} %copy-done), custom_call_target="tpu_custom_call" | custom-call | tf_op jit(solution)/shard_map/project/pallas_call | solution.py:290
  60.8 28.7 %all_to_all.5 = bf16[8,256,384]{2,1,0:T(8,128)(2,1)S(1)} all-to-all(bf16[8,256,384]{2,1,0:T(8,128)(2,1)S(1)} %project.1), channel_id=1, replica_groups=mesh['seq'=32,'head'=8] {'head'}, dimensions={0} | all-to-all | bytes 3145728 | tf_op jit(solution)/shard_map/all_to_all | solution.py:299
  89.4 0.9 %reduce_sum.12 = bf16[256,384]{1,0:T(8,128)(2,1)} reduce(bf16[8,256,384]{2,1,0:T(8,128)(2,1)S(1)} %all_to_all.5, bf16[]{:T(256)} %constant.24.clone.1), dimensions={0}, to_apply=%region_1.2 | reduce | flops 688128 | bytes 1769474 | tf_op jit(solution)/shard_map/reduce_sum | solution.py:300
  (29 shorter events, 0.9 us)
Async XLA Ops:
  1.6 15.6 %collective-permute-start = (bf16[272,384]{1,0:T(8,128)(2,1)S(1)}, bf16[272,384]{1,0:T(8,128)(2,1)S(1)}, u32[]{:S(2)}, u32[]{:S(2)}) collective-permute-start(bf16[272,384]{1,0:T(8,128)(2,1)S(1)} %fusion.1.refs_0_), channel_id=1, source_target_pairs={{0,8},{8,0},{16,24},{24,16},{32,40},{40,32},{48,56},{56,48},{64,72... | collective-permute-start | bytes 626696 | tf_op jit(solution)/shard_map/ppermute | solution.py:222
  1.7 11.6 %collective-permute-start.3 = (bf16[256,384]{1,0:T(8,128)(2,1)}, bf16[256,384]{1,0:T(8,128)(2,1)S(1)}, u32[]{:S(2)}, u32[]{:S(2)}) collective-permute-start(bf16[256,384]{1,0:T(8,128)(2,1)} %refs_4_.1), channel_id=1, source_target_pairs={{0,32},{8,40},{16,48},{24,56},{32,64},{40,72},{48,80},{56,88},{64,... | collective-permute-start | bytes 589832 | tf_op jit(solution)/shard_map/ppermute | solution.py:211
  3.7 9.6 %collective-permute-start.4 = (bf16[256,384]{1,0:T(8,128)(2,1)}, bf16[256,384]{1,0:T(8,128)(2,1)S(1)}, u32[]{:S(2)}, u32[]{:S(2)}) collective-permute-start(bf16[256,384]{1,0:T(8,128)(2,1)} %refs_4_.1), channel_id=1, source_target_pairs={{0,224},{8,232},{16,240},{24,248},{32,0},{40,8},{48,16},{56,24},{6... | collective-permute-start | bytes 589832 | tf_op jit(solution)/shard_map/ppermute | solution.py:213
  7.7 9.2 %collective-permute-start.6 = (bf16[256,384]{1,0:T(8,128)(2,1)}, bf16[256,384]{1,0:T(8,128)(2,1)S(1)}, u32[]{:S(2)}, u32[]{:S(2)}) collective-permute-start(bf16[256,384]{1,0:T(8,128)(2,1)} %refs_7_.1), channel_id=1, source_target_pairs={{0,224},{8,232},{16,240},{24,248},{32,0},{40,8},{48,16},{56,24},{6... | collective-permute-start | bytes 589832 | tf_op jit(solution)/shard_map/ppermute | solution.py:215
  9.7 14.3 %collective-permute-start.1 = (bf16[272,384]{1,0:T(8,128)(2,1)S(1)}, bf16[272,384]{1,0:T(8,128)(2,1)S(1)}, u32[]{:S(2)}, u32[]{:S(2)}) collective-permute-start(bf16[272,384]{1,0:T(8,128)(2,1)S(1)} %fusion.1.refs_0_), channel_id=1, source_target_pairs={{0,16},{8,24},{16,0},{24,8},{32,48},{40,56},{48,32},{56,40},{64,80... | collective-permute-start | bytes 626696 | tf_op jit(solution)/shard_map/ppermute | solution.py:222
  13.3 11.5 %collective-permute-start.2 = (bf16[272,384]{1,0:T(8,128)(2,1)S(1)}, bf16[272,384]{1,0:T(8,128)(2,1)S(1)}, u32[]{:S(2)}, u32[]{:S(2)}) collective-permute-start(bf16[272,384]{1,0:T(8,128)(2,1)S(1)} %fusion.1.refs_0_), channel_id=1, source_target_pairs={{0,24},{8,16},{16,8},{24,0},{32,56},{40,48},{48,40},{56,32},{64,88... | collective-permute-start | bytes 626696 | tf_op jit(solution)/shard_map/ppermute | solution.py:222
  13.3 9.4 %collective-permute-start.5 = (bf16[256,384]{1,0:T(8,128)(2,1)}, bf16[256,384]{1,0:T(8,128)(2,1)S(1)}, u32[]{:S(2)}, u32[]{:S(2)}) collective-permute-start(bf16[256,384]{1,0:T(8,128)(2,1)} %refs_7_.1), channel_id=1, source_target_pairs={{0,32},{8,40},{16,48},{24,56},{32,64},{40,72},{48,80},{56,88},{64,... | collective-permute-start | bytes 589832 | tf_op jit(solution)/shard_map/ppermute | solution.py:214
  16.9 9.5 %collective-permute-start.7 = (bf16[256,384]{1,0:T(8,128)(2,1)S(1)}, bf16[256,384]{1,0:T(8,128)(2,1)S(1)}, u32[]{:S(2)}, u32[]{:S(2)}) collective-permute-start(bf16[256,384]{1,0:T(8,128)(2,1)S(1)} %collective-permute-done.3.refs_5_), channel_id=1, source_target_pairs={{0,32},{8,40},{16,48},{24,56},{32,64},{40,72},{48,80},{56,88},{64,... | collective-permute-start | bytes 589832 | tf_op jit(solution)/shard_map/ppermute | solution.py:211
  17.2 9.2 %collective-permute-start.14 = (bf16[256,384]{1,0:T(8,128)(2,1)S(1)}, bf16[256,384]{1,0:T(8,128)(2,1)S(1)}, u32[]{:S(2)}, u32[]{:S(2)}) collective-permute-start(bf16[256,384]{1,0:T(8,128)(2,1)S(1)} %collective-permute-done.6.refs_9_), channel_id=1, source_target_pairs={{0,224},{8,232},{16,240},{24,248},{32,0},{40,8},{48,16},{56,24},{6... | collective-permute-start | bytes 589832 | tf_op jit(solution)/shard_map/ppermute | solution.py:215
  22.8 6.9 %collective-permute-start.9 = (bf16[256,384]{1,0:T(8,128)(2,1)S(1)}, bf16[256,384]{1,0:T(8,128)(2,1)S(1)}, u32[]{:S(2)}, u32[]{:S(2)}) collective-permute-start(bf16[256,384]{1,0:T(8,128)(2,1)S(1)} %collective-permute-done.4.refs_6_), channel_id=1, source_target_pairs={{0,224},{8,232},{16,240},{24,248},{32,0},{40,8},{48,16},{56,24},{6... | collective-permute-start | bytes 589832 | tf_op jit(solution)/shard_map/ppermute | solution.py:213
  24.0 8.3 %collective-permute-start.12 = (bf16[256,384]{1,0:T(8,128)(2,1)S(1)}, bf16[256,384]{1,0:T(8,128)(2,1)S(1)}, u32[]{:S(2)}, u32[]{:S(2)}) collective-permute-start(bf16[256,384]{1,0:T(8,128)(2,1)S(1)} %collective-permute-done.5.refs_8_), channel_id=1, source_target_pairs={{0,32},{8,40},{16,48},{24,56},{32,64},{40,72},{48,80},{56,88},{64,... | collective-permute-start | bytes 589832 | tf_op jit(solution)/shard_map/ppermute | solution.py:214
  26.4 9.0 %collective-permute-start.8 = (bf16[256,384]{1,0:T(8,128)(2,1)S(1)}, bf16[256,384]{1,0:T(8,128)(2,1)S(1)}, u32[]{:S(2)}, u32[]{:S(2)}) collective-permute-start(bf16[256,384]{1,0:T(8,128)(2,1)S(1)} %collective-permute-done.7.refs_3_), channel_id=1, source_target_pairs={{0,32},{8,40},{16,48},{24,56},{32,64},{40,72},{48,80},{56,88},{64,... | collective-permute-start | bytes 589832 | tf_op jit(solution)/shard_map/ppermute | solution.py:211
  26.4 9.2 %collective-permute-start.15 = (bf16[256,384]{1,0:T(8,128)(2,1)S(1)}, bf16[256,384]{1,0:T(8,128)(2,1)S(1)}, u32[]{:S(2)}, u32[]{:S(2)}) collective-permute-start(bf16[256,384]{1,0:T(8,128)(2,1)S(1)} %collective-permute-done.14.refs_9_), channel_id=1, source_target_pairs={{0,224},{8,232},{16,240},{24,248},{32,0},{40,8},{48,16},{56,24},{6... | collective-permute-start | bytes 589832 | tf_op jit(solution)/shard_map/ppermute | solution.py:215
  29.7 15.6 %collective-permute-start.10 = (bf16[256,384]{1,0:T(8,128)(2,1)S(1)}, bf16[256,384]{1,0:T(8,128)(2,1)S(1)}, u32[]{:S(2)}, u32[]{:S(2)}) collective-permute-start(bf16[256,384]{1,0:T(8,128)(2,1)S(1)} %collective-permute-done.9.refs_4_), channel_id=1, source_target_pairs={{0,224},{8,232},{16,240},{24,248},{32,0},{40,8},{48,16},{56,24},{6... | collective-permute-start | bytes 589832 | tf_op jit(solution)/shard_map/ppermute | solution.py:213
  32.3 13.0 %collective-permute-start.13 = (bf16[256,384]{1,0:T(8,128)(2,1)S(1)}, bf16[256,384]{1,0:T(8,128)(2,1)S(1)}, u32[]{:S(2)}, u32[]{:S(2)}) collective-permute-start(bf16[256,384]{1,0:T(8,128)(2,1)S(1)} %collective-permute-done.12.refs_8_), channel_id=1, source_target_pairs={{0,32},{8,40},{16,48},{24,56},{32,64},{40,72},{48,80},{56,88},{64,... | collective-permute-start | bytes 589832 | tf_op jit(solution)/shard_map/ppermute | solution.py:214
  35.4 9.9 %collective-permute-start.11 = (bf16[256,384]{1,0:T(8,128)(2,1)S(1)}, bf16[256,384]{1,0:T(8,128)(2,1)S(1)}, u32[]{:S(2)}, u32[]{:S(2)}) collective-permute-start(bf16[256,384]{1,0:T(8,128)(2,1)S(1)} %collective-permute-done.8.refs_0_), channel_id=1, source_target_pairs={{0,32},{8,40},{16,48},{24,56},{32,64},{40,72},{48,80},{56,88},{64,... | collective-permute-start | bytes 589832 | tf_op jit(solution)/shard_map/ppermute | solution.py:211
  35.6 9.7 %collective-permute-start.16 = (bf16[256,384]{1,0:T(8,128)(2,1)S(1)}, bf16[256,384]{1,0:T(8,128)(2,1)S(1)}, u32[]{:S(2)}, u32[]{:S(2)}) collective-permute-start(bf16[256,384]{1,0:T(8,128)(2,1)S(1)} %collective-permute-done.15.refs_6_), channel_id=1, source_target_pairs={{0,224},{8,232},{16,240},{24,248},{32,0},{40,8},{48,16},{56,24},{6... | collective-permute-start | bytes 589832 | tf_op jit(solution)/shard_map/ppermute | solution.py:215
  38.9 0.9 %copy-start.1 = (bf16[256,384]{1,0:T(8,128)(2,1)S(1)}, bf16[256,384]{1,0:T(8,128)(2,1)}, u32[]{:S(2)}) copy-start(bf16[256,384]{1,0:T(8,128)(2,1)} %refs_4_.1) | copy-start | bytes 589828
  39.9 0.9 %copy-start.2 = (bf16[256,384]{1,0:T(8,128)(2,1)S(1)}, bf16[256,384]{1,0:T(8,128)(2,1)}, u32[]{:S(2)}) copy-start(bf16[256,384]{1,0:T(8,128)(2,1)} %refs_7_.1) | copy-start | bytes 589828
  45.3 14.2 %copy-start = (bf16[384,3072]{1,0:T(8,128)(2,1)S(1)}, bf16[384,3072]{1,0:T(8,128)(2,1)}, u32[]{:S(2)}) copy-start(bf16[384,3072]{1,0:T(8,128)(2,1)} %weight_ref.1) | copy-start | bytes 7077892
  50.1 1.9 %collective-permute-start.17 = (bf16[2,416,256]{2,1,0:T(8,128)(2,1)S(1)}, bf16[2,416,256]{2,1,0:T(8,128)(2,1)S(1)}, u32[]{:S(2)}, u32[]{:S(2)}) collective-permute-start(bf16[2,416,256]{2,1,0:T(8,128)(2,1)S(1)} %get-tuple-element.21), channel_id=1, source_target_pairs={{0,8},{8,0},{16,24},{24,16},{32,40},{40,32},{48,56},{56,48},{64,72... | collective-permute-start | bytes 1277960 | tf_op jit(solution)/shard_map/ppermute | solution.py:276
  52.1 7.4 %collective-permute-start.18 = (bf16[1,416,256]{2,1,0:T(8,128)(2,1)S(1)}, bf16[1,416,256]{2,1,0:T(8,128)(2,1)S(1)}, u32[]{:S(2)}, u32[]{:S(2)}) collective-permute-start(bf16[1,416,256]{2,1,0:T(8,128)(2,1)S(1)} %get-tuple-element.24), channel_id=1, source_target_pairs={{0,16},{8,24},{16,0},{24,8},{32,48},{40,56},{48,32},{56,40},{64,80... | collective-permute-start | bytes 638984 | tf_op jit(solution)/shard_map/ppermute | solution.py:289

commit v4 on v2

--- a/solution.py
+++ b/solution.py
@@ -55,62 +55,118 @@
     return outs, sums
 
 
-def visit_shards(factor, need_ref, first, q_refs, shards, acc_ref, peak_ref, total_ref):
-    heads = q_refs[0].shape[1] // HD
-    for j, (k_ref, v_ref) in enumerate(shards):
-        for t, q_ref in enumerate(q_refs):
-
-            @pl.when(need_ref[t, first + j] > 0)
+def load_shards(need_ref, first, shards, k_ref, vt_ref):
+    for j, (key, value) in enumerate(shards):
+        wanted = need_ref[0, first + j]
+        for t in range(1, need_ref.shape[0]):
+            wanted = wanted + need_ref[t, first + j]
+
+        @pl.when(wanted > 0)
+        def _():
+            k_ref[j] = key[...]
+            for h in range(vt_ref.shape[1]):
+                vt_ref[j, h] = value[:, h * HD:(h + 1) * HD].T
+
+
+def visit_shards(factor, need_ref, first, count, q_ref, k_ref, vt_ref, state):
+    acc_ref, peak_ref, total_ref = state
+    heads = vt_ref.shape[1]
+
+    def take(t, picks):
+        def scores_of(h):
+            cols = slice(h * HD, (h + 1) * HD)
+            return [
+                lax.dot_general(
+                    k_ref[j, :, cols],
+                    q_ref[t, :, cols],
+                    (((1,), (1,)), ((), ())),
+                    preferred_element_type=jnp.float32,
+                )
+                for j in picks
+            ]
+
+        following = scores_of(0)
+        for h in range(heads):
+            scores = following
+            if h + 1 < heads:
+                following = scores_of(h + 1)
+            row = t * heads + h
+            old = peak_ref[row]
+            tops = [jnp.max(part, axis=0, keepdims=True) for part in scores]
+            peak = jnp.maximum(old, functools.reduce(jnp.maximum, tops) * factor)
+            weights = [jnp.exp2(part * factor - peak) for part in scores]
+            shrink = jnp.exp2(old - peak)
+            sums = [jnp.sum(w, axis=0, keepdims=True) for w in weights]
+            dots = [
+                jnp.dot(vt_ref[j, h], w.astype(jnp.bfloat16), preferred_element_type=jnp.float32)
+                for j, w in zip(picks, weights)
+            ]
+            peak_ref[row] = peak
+            total_ref[row] = total_ref[row] * shrink + sum(sums[1:], sums[0])
+            acc_ref[row] = acc_ref[row] * shrink + sum(dots[1:], dots[0])
+
+    def visit(t, carry):
+        picks = [jnp.int32(0)] * count
+        seen = jnp.int32(0)
+        for j in range(count):
+            wanted = need_ref[t, first + j]
+            for i in range(j + 1):
+                picks[i] = jnp.where((wanted > 0) & (seen == i), j, picks[i])
+            seen = seen + wanted
+
+        if count >= 3:
+
+            @pl.when(seen >= 3)
             def _():
-                for h in range(heads):
-                    cols = slice(h * HD, (h + 1) * HD)
-                    scores = lax.dot_general(
-                        k_ref[:, cols],
-                        q_ref[0:TILE, cols],
-                        (((1,), (1,)), ((), ())),
-                        preferred_element_type=jnp.float32,
-                    )
-                    row = t * heads + h
-                    old = peak_ref[row]
-                    peak = jnp.maximum(old, jnp.max(scores, axis=0, keepdims=True) * factor)
-                    weights = jnp.exp2(scores * factor - peak)
-                    shrink = jnp.exp2(old - peak)
-                    peak_ref[row] = peak
-                    total_ref[row] = total_ref[row] * shrink + jnp.sum(weights, axis=0, keepdims=True)
-                    acc_ref[row] = acc_ref[row] * shrink + lax.dot_general(
-                        v_ref[:, cols],
-                        weights.astype(jnp.bfloat16),
-                        (((0,), (0,)), ((), ())),
-                        preferred_element_type=jnp.float32,
-                    )
-
-
-def open_kernel(factor, count, need_ref, *refs):
-    q_refs, kv_refs, (acc_ref, peak_ref, total_ref) = refs[:GROUP], refs[GROUP:-3], refs[-3:]
+                take(t, picks[:3])
+
+        if count >= 2:
+
+            @pl.when(seen == 2)
+            def _():
+                take(t, picks[:2])
+
+        @pl.when((seen == 1) | (seen == 4))
+        def _():
+            take(t, [jnp.where(seen == 4, picks[-1], picks[0])])
+
+        return carry
+
+    lax.fori_loop(0, q_ref.shape[0], visit, 0)
+
+
+def near_kernel(factor, need_ref, *refs):
+    q_refs, (own_ref, k_low, k_high, v_low, v_high) = refs[:GROUP], refs[GROUP:GROUP + 5]
+    stacked_ref, acc_ref, peak_ref, total_ref, k_ref, vt_ref = refs[GROUP + 5:]
     acc_ref[...] = jnp.zeros_like(acc_ref)
     peak_ref[...] = jnp.full_like(peak_ref, LOWEST)
     total_ref[...] = jnp.zeros_like(total_ref)
-    shards = list(zip(kv_refs[:count], kv_refs[count:]))
-    visit_shards(factor, need_ref, 0, q_refs, shards, acc_ref, peak_ref, total_ref)
-
-
-def more_kernel(factor, first, count, need_ref, *refs):
-    q_refs, kv_refs = refs[:GROUP], refs[GROUP:GROUP + 2 * count]
-    held, state = refs[GROUP + 2 * count:-3], refs[-3:]
+    for t, q_ref in enumerate(q_refs):
+        stacked_ref[t] = q_ref[0:TILE, :]
+    shards = [(own_ref.at[0:TILE], own_ref.at[TILE:2 * TILE]), (k_low, v_low), (k_high, v_high)]
+    load_shards(need_ref, 0, shards, k_ref, vt_ref)
+    visit_shards(factor, need_ref, 0, 3, stacked_ref, k_ref, vt_ref, (acc_ref, peak_ref, total_ref))
+
+
+def far_kernel(factor, first, count, need_ref, stacked_ref, *refs):
+    shards = list(zip(refs[:count], refs[count:2 * count]))
+    held, state = refs[2 * count:2 * count + 3], refs[2 * count + 3:2 * count + 6]
+    k_ref, vt_ref = refs[2 * count + 6:]
     for source, target in zip(held, state):
         target[...] = source[...]
-    shards = list(zip(kv_refs[:count], kv_refs[count:]))
-    visit_shards(factor, need_ref, first, q_refs, shards, *state)
-
-
-def close_kernel(factor, first, need_ref, *refs):
-    q_refs, kv_refs = refs[:GROUP], refs[GROUP:GROUP + 2]
-    held = refs[GROUP + 2:GROUP + 5]
-    keep_ref, keep_sum_ref, send_ref, acc_ref, peak_ref, total_ref = refs[GROUP + 5:]
-    heads = q_refs[0].shape[1] // HD
-    for source, target in zip(held, (acc_ref, peak_ref, total_ref)):
+    load_shards(need_ref, first, shards, k_ref, vt_ref)
+    visit_shards(factor, need_ref, first, count, stacked_ref, k_ref, vt_ref, state)
+
+
+def last_kernel(factor, first, need_ref, stacked_ref, *refs):
+    shards = [refs[:2]]
+    keep_ref, keep_sum_ref, send_ref, *state, k_ref, vt_ref = refs[5:]
+    heads = vt_ref.shape[1]
+    for source, target in zip(refs[2:5], state):
         target[...] = source[...]
-    visit_shards(factor, need_ref, first, q_refs, [kv_refs], acc_ref, peak_ref, total_ref)
+    load_shards(need_ref, first, shards, k_ref, vt_ref)
+    visit_shards(factor, need_ref, first, 1, stacked_ref, k_ref, vt_ref, state)
+    acc_ref, peak_ref, total_ref = state
     for t in range(GROUP):
         outs, sums = [], []
         for h in range(heads):
@@ -128,6 +184,11 @@
                 keep_sum_ref[t // 2, h:h + 1, :] = sums[h]
 
 
+def relay_kernel(k_ref, v_ref, after_ref, k_out_ref, v_out_ref):
+    k_out_ref[...] = k_ref[...]
+    v_out_ref[...] = v_ref[...]
+
+
 def merge_kernel(mine_ref, mine_sum_ref, other_ref, keep_ref, keep_sum_ref, send_ref):
     heads = mine_ref.shape[1] // HD
     outs, sums = merged(mine_ref, mine_sum_ref, 1, other_ref, 1, heads)
@@ -174,28 +235,24 @@
 
     k_up, k_down, v_up, v_down = [key_states], [key_states], [value_states], [value_states]
     half = planes // 2
-    for step in range(half):
+    for step in range(half - 1):
         k_up.append(lax.ppermute(k_up[-1], "seq", up))
-        if step < half - 1:
-            k_down.append(lax.ppermute(k_down[-1], "seq", down))
-            v_up.append(lax.ppermute(v_up[-1], "seq", up))
+        k_down.append(lax.ppermute(k_down[-1], "seq", down))
+        v_up.append(lax.ppermute(v_up[-1], "seq", up))
         v_down.append(lax.ppermute(v_down[-1], "seq", down))
-        if step == 0:
-            listed = jnp.pad(
-                block_list.astype(jnp.bfloat16), ((0, PART_ROWS - 1), (0, width - block_list.shape[1]))
-            )
-            packed = jnp.concatenate([queries, listed], axis=0)
-            tiles = [packed] + [
-                lax.ppermute(packed, "seq", [(s, s ^ k) for s in range(seq_size)]) for k in range(1, GROUP)
-            ]
-            lists = jnp.concatenate([t[TILE:TILE + 1, :block_list.shape[1]] for t in tiles], axis=0)
-            lists = jnp.concatenate(
-                [lists.astype(jnp.int32), jnp.broadcast_to(text_slots[None, :], (GROUP, text_slots.shape[0]))],
-                axis=1,
-            )
-            order = [0] + [sign * i for i in range(1, half) for sign in (-1, 1)] + [half]
-            slots = (me + GROUP * jnp.asarray(order, jnp.int32)) % seq_size
-            need = jnp.any(lists[:, None, :] == slots[None, :, None], axis=2).astype(jnp.int32)
+
+    listed = jnp.pad(block_list.astype(jnp.bfloat16), ((0, PART_ROWS - 1), (0, width - block_list.shape[1])))
+    packed = jnp.concatenate([queries, listed], axis=0)
+    tiles = [packed] + [
+        lax.ppermute(packed, "seq", [(s, s ^ k) for s in range(seq_size)]) for k in range(1, GROUP)
+    ]
+    lists = jnp.concatenate([t[TILE:TILE + 1, :block_list.shape[1]] for t in tiles], axis=0)
+    lists = jnp.concatenate(
+        [lists.astype(jnp.int32), jnp.broadcast_to(text_slots[None, :], (GROUP, text_slots.shape[0]))], axis=1
+    )
+    order = [0, -1, 1, -3, 3, -2, 2, 4]
+    slots = (me + GROUP * jnp.asarray(order, jnp.int32)) % seq_size
+    need = jnp.any(lists[:, None, :] == slots[None, :, None], axis=2).astype(jnp.int32)
 
     rows = GROUP * heads
     state = (
@@ -206,43 +263,58 @@
     factor = LOG2E / math.sqrt(HD)
     smem = [pl.BlockSpec(memory_space=pltpu.SMEM)]
 
-    def shards(pairs):
-        return [k for k, _ in pairs] + [v for _, v in pairs]
-
-    first = [(key_states, value_states), (k_up[1], v_up[1]), (k_down[1], v_down[1])]
-    held = pl.pallas_call(
-        functools.partial(open_kernel, factor, 3),
-        out_shape=state,
-        in_specs=smem + vmem_specs(GROUP + 6),
-        out_specs=tuple(vmem_specs(3)),
+    def scratch(count):
+        return [
+            pltpu.VMEM((count, TILE, width), jnp.bfloat16),
+            pltpu.VMEM((count, heads, HD, TILE), jnp.bfloat16),
+        ]
+
+    own = jnp.concatenate([key_states, value_states], axis=0)
+    stacked, *held = pl.pallas_call(
+        functools.partial(near_kernel, factor),
+        out_shape=(jax.ShapeDtypeStruct((GROUP, TILE, width), jnp.bfloat16),) + state,
+        in_specs=smem + vmem_specs(GROUP + 5),
+        out_specs=tuple(vmem_specs(4)),
+        scratch_shapes=scratch(3),
         compiler_params=PARAMS,
         cost_estimate=attend_cost(27),
         name="attend_near",
-    )(need, *tiles, *shards(first))
-    second = [pair for i in range(2, half) for pair in ((k_up[i], v_up[i]), (k_down[i], v_down[i]))]
+    )(need, *tiles, own, k_up[1], k_down[1], v_up[1], v_down[1])
+    shard = jax.ShapeDtypeStruct(key_states.shape, key_states.dtype)
+    k_last, v_last = pl.pallas_call(
+        relay_kernel,
+        out_shape=(shard, shard),
+        in_specs=vmem_specs(3),
+        out_specs=tuple(vmem_specs(2)),
+        compiler_params=PARAMS,
+        name="relay",
+    )(k_up[-1], v_down[-1], held[2])
+    k_last = lax.ppermute(k_last, "seq", up)
+    v_last = lax.ppermute(v_last, "seq", down)
     held = pl.pallas_call(
-        functools.partial(more_kernel, factor, 3, len(second)),
+        functools.partial(far_kernel, factor, 3, 4),
         out_shape=state,
-        in_specs=smem + vmem_specs(GROUP + 2 * len(second) + 3),
+        in_specs=smem + vmem_specs(12),
         out_specs=tuple(vmem_specs(3)),
-        compiler_params=PARAMS,
-        cost_estimate=attend_cost(18),
+        scratch_shapes=scratch(4),
+        compiler_params=PARAMS,
+        cost_estimate=attend_cost(24),
         name="attend_far",
-    )(need, *tiles, *shards(second), *held)
+    )(need, stacked, k_up[3], k_down[3], k_up[2], k_down[2], v_up[3], v_down[3], v_up[2], v_down[2], *held)
     keep, keep_sum, send = pl.pallas_call(
-        functools.partial(close_kernel, factor, planes - 1),
+        functools.partial(last_kernel, factor, 7),
         out_shape=(
             jax.ShapeDtypeStruct((2, width, TILE), jnp.float32),
             jax.ShapeDtypeStruct((2, 8, TILE), jnp.float32),
             jax.ShapeDtypeStruct((2, width + 2 * PART_ROWS, TILE), jnp.bfloat16),
         ),
-        in_specs=smem + vmem_specs(GROUP + 5),
+        in_specs=smem + vmem_specs(6),
         out_specs=tuple(vmem_specs(3)),
-        scratch_shapes=[pltpu.VMEM(s.shape, s.dtype) for s in state],
-        compiler_params=PARAMS,
-        cost_estimate=attend_cost(9),
+        scratch_shapes=[pltpu.VMEM(s.shape, s.dtype) for s in state] + scratch(1),
+        compiler_params=PARAMS,
+        cost_estimate=attend_cost(12),
         name="attend_last",
-    )(need, *tiles, k_up[half], v_down[half], *held)
+    )(need, stacked, k_last, v_last, *held)
 
     other = lax.ppermute(send, "seq", [(s, s ^ 1) for s in range(seq_size)])
     keep, keep_sum, send = pl.pallas_call(

time: 102 us -> 92.8 us (0.910)
  the two profiles are of different devices: /device:TPU:64 before, /device:TPU:2 now
where the time goes in v4:
time: 92.8 us; the launch traced here: 91.3 us
  starting transfers between devices  29.2 us (31%)
  blocking collectives  28.1 us (30%)
  waiting for transfers between devices  17.7 us (19%)
  Pallas kernels  10.9 us (12%)
  other arithmetic  4.49 us (5%)
    all_to_all x1, blocking collectives, per_device(): shares = lax.all_to_all(shares, 'head', 0, 0, tiled=False)  28.1 us
    ppermute x3, starting transfers between devices, per_device(): k_down.append(lax.ppermute(k_down[-1], 'seq', down))  11.1 us
    ppermute x3, starting transfers between devices, per_device(): v_down.append(lax.ppermute(v_down[-1], 'seq', down))  10.5 us
    ppermute x1, waiting for transfers between devices, per_device(): other = lax.ppermute(send, 'seq', [(s, s ^ 2) for s in range(seq_size)])  6.87 us
    ppermute x3, waiting for transfers between devices, per_device(): v_down.append(lax.ppermute(v_down[-1], 'seq', down))  5.25 us
    pallas_call x1, Pallas kernels, per_device(): pl.pallas_call(functools.partial(near_kernel, factor), out_shape=(jax.Sha...  4.26 us
    ppermute x1, starting transfers between devices, per_device(): v_last = lax.ppermute(v_last, 'seq', down)  3.22 us
    pallas_call x1, Pallas kernels, per_device(): pl.pallas_call(functools.partial(last_kernel, factor, 7), out_shape=(jax....  2.62 us
  transfers between devices with their start and end apart: 19, of which 9 were waited for; matrix products, arithmetic and copies ran while one was open for 3% of the time, Pallas kernels for 8%

profile of v4, /device:TPU:2, one launch (start us, length us, event | category | flops | bytes accessed | tf_op | source)
XLA Modules:
  0.0 91.3 jit_solution(486780134638659200)
XLA Ops:
  0.0 0.7 convert_element_type.13
  0.7 0.9 %fusion.1.refs_0_ = bf16[272,384]{1,0:T(8,128)(2,1)S(1)} fusion(bf16[1,27]{1,0:T(2,128)(2,1)S(1)} %convert_element_type.13, bf16[256,384]{1,0:T(8,128)(2,1)} %param.7), kind=kLoop, calls=%fused_computation.3 | loop fusion | flops 626688 | bytes 405558 | tf_op jit(solution)/shard_map/concatenate | solution.py:245
  1.7 2.0 %collective-permute-start.3 = (bf16[256,384]{1,0:T(8,128)(2,1)}, bf16[256,384]{1,0:T(8,128)(2,1)S(1)}, u32[]{:S(2)}, u32[]{:S(2)}) collective-permute-start(bf16[256,384]{1,0:T(8,128)(2,1)} %param.8), channel_id=1, source_target_pairs={{0,32},{8,40},{16,48},{24,56},{32,64},{40,72},{48,80},{56,88},{64,... | collective-permute-start | bytes 589832 | tf_op jit(solution)/shard_map/ppermute | solution.py:239
  3.7 0.5 collective-permute-start.1
  4.2 1.0 %collective-permute-start.2 = (bf16[272,384]{1,0:T(8,128)(2,1)S(1)}, bf16[272,384]{1,0:T(8,128)(2,1)S(1)}, u32[]{:S(2)}, u32[]{:S(2)}) collective-permute-start(bf16[272,384]{1,0:T(8,128)(2,1)S(1)} %fusion.1.refs_0_), channel_id=1, source_target_pairs={{0,24},{8,16},{16,8},{24,0},{32,56},{40,48},{48,40},{56,32},{64,88... | collective-permute-start | bytes 626696 | tf_op jit(solution)/shard_map/ppermute | solution.py:247
  5.2 4.2 %collective-permute-start.4 = (bf16[256,384]{1,0:T(8,128)(2,1)}, bf16[256,384]{1,0:T(8,128)(2,1)S(1)}, u32[]{:S(2)}, u32[]{:S(2)}) collective-permute-start(bf16[256,384]{1,0:T(8,128)(2,1)} %param.8), channel_id=1, source_target_pairs={{0,224},{8,232},{16,240},{24,248},{32,0},{40,8},{48,16},{56,24},{6... | collective-permute-start | bytes 589832 | tf_op jit(solution)/shard_map/ppermute | solution.py:240
  9.4 0.7 pad.8.clone
  10.1 1.1 %pad_maximum_fusion.refs_4_ = bf16[512,384]{1,0:T(8,128)(2,1)S(1)} fusion(bf16[256,384]{1,0:T(8,128)(2,1)} %param.9, bf16[256,384]{1,0:T(8,128)(2,1)} %param.8), kind=kLoop, calls=%fused_computation.2 | loop fusion | flops 786432 | bytes 786432 | tf_op jit(solution)/shard_map/concatenate | solution.py:272
  11.2 2.1 %collective-permute-done.3.refs_5_ = bf16[256,384]{1,0:T(8,128)(2,1)S(1)} collective-permute-done((bf16[256,384]{1,0:T(8,128)(2,1)}, bf16[256,384]{1,0:T(8,128)(2,1)S(1)}, u32[]{:S(2)}, u32[]{:S(2)}) %collective-permute-start.3) | collective-permute-done | bytes 196640 | tf_op jit(solution)/shard_map/ppermute | solution.py:239
  13.3 3.2 %collective-permute-start.6 = (bf16[256,384]{1,0:T(8,128)(2,1)}, bf16[256,384]{1,0:T(8,128)(2,1)S(1)}, u32[]{:S(2)}, u32[]{:S(2)}) collective-permute-start(bf16[256,384]{1,0:T(8,128)(2,1)} %param.9), channel_id=1, source_target_pairs={{0,224},{8,232},{16,240},{24,248},{32,0},{40,8},{48,16},{56,24},{6... | collective-permute-start | bytes 589832 | tf_op jit(solution)/shard_map/ppermute | solution.py:242
  16.6 0.7 and_select_fusion
  17.2 3.5 %collective-permute-done.6.refs_8_ = bf16[256,384]{1,0:T(8,128)(2,1)S(1)} collective-permute-done((bf16[256,384]{1,0:T(8,128)(2,1)}, bf16[256,384]{1,0:T(8,128)(2,1)S(1)}, u32[]{:S(2)}, u32[]{:S(2)}) %collective-permute-start.6) | collective-permute-done | bytes 196640 | tf_op jit(solution)/shard_map/ppermute | solution.py:242
  20.8 3.6 %collective-permute-start.9 = (bf16[256,384]{1,0:T(8,128)(2,1)S(1)}, bf16[256,384]{1,0:T(8,128)(2,1)S(1)}, u32[]{:S(2)}, u32[]{:S(2)}) collective-permute-start(bf16[256,384]{1,0:T(8,128)(2,1)S(1)} %collective-permute-done.6.refs_8_), channel_id=1, source_target_pairs={{0,224},{8,232},{16,240},{24,248},{32,0},{40,8},{48,16},{56,24},{6... | collective-permute-start | bytes 589832 | tf_op jit(solution)/shard_map/ppermute | solution.py:242
  24.4 3.2 %collective-permute-start.13 = (bf16[256,384]{1,0:T(8,128)(2,1)S(1)}, bf16[256,384]{1,0:T(8,128)(2,1)S(1)}, u32[]{:S(2)}, u32[]{:S(2)}) collective-permute-start(bf16[256,384]{1,0:T(8,128)(2,1)S(1)} %collective-permute-done.4.refs_6_), channel_id=1, source_target_pairs={{0,224},{8,232},{16,240},{24,248},{32,0},{40,8},{48,16},{56,24},{6... | collective-permute-start | bytes 589832 | tf_op jit(solution)/shard_map/ppermute | solution.py:240
  27.7 1.7 %collective-permute-done.9.refs_7_ = bf16[256,384]{1,0:T(8,128)(2,1)S(1)} collective-permute-done((bf16[256,384]{1,0:T(8,128)(2,1)S(1)}, bf16[256,384]{1,0:T(8,128)(2,1)S(1)}, u32[]{:S(2)}, u32[]{:S(2)}) %collective-permute-start.9) | collective-permute-done | bytes 196640 | tf_op jit(solution)/shard_map/ppermute | solution.py:242
  29.4 3.7 %collective-permute-start.10 = (bf16[256,384]{1,0:T(8,128)(2,1)S(1)}, bf16[256,384]{1,0:T(8,128)(2,1)S(1)}, u32[]{:S(2)}, u32[]{:S(2)}) collective-permute-start(bf16[256,384]{1,0:T(8,128)(2,1)S(1)} %collective-permute-done.9.refs_7_), channel_id=1, source_target_pairs={{0,224},{8,232},{16,240},{24,248},{32,0},{40,8},{48,16},{56,24},{6... | collective-permute-start | bytes 589832 | tf_op jit(solution)/shard_map/ppermute | solution.py:242
  33.1 0.2 collective-permute-done.7.refs_2_
  33.3 0.2 compare_reduce_fusion
  33.6 3.7 %collective-permute-start.14 = (bf16[256,384]{1,0:T(8,128)(2,1)S(1)}, bf16[256,384]{1,0:T(8,128)(2,1)S(1)}, u32[]{:S(2)}, u32[]{:S(2)}) collective-permute-start(bf16[256,384]{1,0:T(8,128)(2,1)S(1)} %collective-permute-done.13.refs_3_), channel_id=1, source_target_pairs={{0,224},{8,232},{16,240},{24,248},{32,0},{40,8},{48,16},{56,24},{6... | collective-permute-start | bytes 589832 | tf_op jit(solution)/shard_map/ppermute | solution.py:240
  37.3 0.2 collective-permute-done.15.refs_6_
  37.5 4.3 %attend_near.1 = (bf16[4,256,384]{2,1,0:T(8,128)(2,1)S(1)}, f32[12,128,256]{2,1,0:T(8,128)S(1)}, f32[12,1,256]{2,1,0:T(1,128)S(1)}, f32[12,1,256]{2,1,0:T(1,128)S(1)}) custom-call(s32[4,8]{1,0:T(4,128)S(1)} %convert_element_type.15.need_ref, bf16[272,384]{1,0:T(8,128)(2,1)S(1)} %fusion.1.refs_0_, bf16[272,384]{1,0:T(8,128)(2,1)S(1)} %collective-permute-done.refs_1_, ...), custom_call_target="tpu_custom_call" | custom-call | flops 905969664 | bytes 4194304 | tf_op jit(solution)/shard_map/attend_near/pallas_call | solution.py:273
  41.9 3.2 %collective-permute-start.12 = (bf16[256,384]{1,0:T(8,128)(2,1)S(1)}, bf16[256,384]{1,0:T(8,128)(2,1)S(1)}, u32[]{:S(2)}, u32[]{:S(2)}) collective-permute-start(bf16[256,384]{1,0:T(8,128)(2,1)S(1)} %get-tuple-element.23), channel_id=1, source_target_pairs={{0,224},{8,232},{16,240},{24,248},{32,0},{40,8},{48,16},{56,24},{6... | collective-permute-start | bytes 589832 | tf_op jit(solution)/shard_map/ppermute | solution.py:293
  45.1 1.2 %collective-permute-done.16.refs_4_ = bf16[256,384]{1,0:T(8,128)(2,1)S(1)} collective-permute-done((bf16[256,384]{1,0:T(8,128)(2,1)S(1)}, bf16[256,384]{1,0:T(8,128)(2,1)S(1)}, u32[]{:S(2)}, u32[]{:S(2)}) %collective-permute-start.16) | collective-permute-done | bytes 196640 | tf_op jit(solution)/shard_map/ppermute | solution.py:241
  46.3 2.6 %attend_far.1 = (f32[12,128,256]{2,1,0:T(8,128)S(1)}, f32[12,1,256]{2,1,0:T(1,128)S(1)}, f32[12,1,256]{2,1,0:T(1,128)S(1)}) custom-call(s32[4,8]{1,0:T(4,128)S(1)} %convert_element_type.15.need_ref, bf16[4,256,384]{2,1,0:T(8,128)(2,1)S(1)} %get-tuple-element.20.stacked_ref, bf16[256,384]{1,0:T(8,128)(2,1)S(1)} %collective-permute-done.8.k_ref.refs_0_, ...), custom_call_target="tpu_custom_call" | custom-call | flops 805306368 | bytes 4194304 | tf_op jit(solution)/shard_map/attend_far/pallas_call | solution.py:294
  49.0 2.6 %attend_last.1 = (f32[2,384,256]{2,1,0:T(8,128)S(1)}, f32[2,8,256]{2,1,0:T(8,128)S(1)}, bf16[2,416,256]{2,1,0:T(8,128)(2,1)S(1)}) custom-call(s32[4,8]{1,0:T(4,128)S(1)} %convert_element_type.15.need_ref, bf16[4,256,384]{2,1,0:T(8,128)(2,1)S(1)} %get-tuple-element.20.stacked_ref, bf16[256,384]{1,0:T(8,128)(2,1)S(1)} %collective-permute-done.11.refs_0_, ...), custom_call_target="tpu_custom_call" | custom-call | flops 402653184 | bytes 4194304 | tf_op jit(solution)/shard_map/attend_last/pallas_call | solution.py:304
  51.7 1.8 %collective-permute-done.17.other_ref = bf16[2,416,256]{2,1,0:T(8,128)(2,1)S(1)} collective-permute-done((bf16[2,416,256]{2,1,0:T(8,128)(2,1)S(1)}, bf16[2,416,256]{2,1,0:T(8,128)(2,1)S(1)}, u32[]{:S(2)}, u32[]{:S(2)}) %collective-permute-start.17) | collective-permute-done | bytes 426016 | tf_op jit(solution)/shard_map/ppermute | solution.py:319
  53.4 0.2 merge.1
  53.6 0.5 collective-permute-start.18
  54.1 6.9 %collective-permute-done.18.other_ref = bf16[1,416,256]{2,1,0:T(8,128)(2,1)S(1)} collective-permute-done((bf16[1,416,256]{2,1,0:T(8,128)(2,1)S(1)}, bf16[1,416,256]{2,1,0:T(8,128)(2,1)S(1)}, u32[]{:S(2)}, u32[]{:S(2)}) %collective-permute-start.18) | collective-permute-done | bytes 213024 | tf_op jit(solution)/shard_map/ppermute | solution.py:332
  61.0 1.3 %project.1 = bf16[8,256,384]{2,1,0:T(8,128)(2,1)S(1)} custom-call(f32[1,384,256]{2,1,0:T(8,128)S(1)} %get-tuple-element.32.mine_ref, f32[1,8,256]{2,1,0:T(8,128)S(1)} %get-tuple-element.33.mine_sum_ref, bf16[1,416,256]{2,1,0:T(8,128)(2,1)S(1)} %collective-permute-done.18.other_ref, bf16[384,3072]{1,0:T(8,128)(2,1)S(1)} %copy-done), custom_call_target="tpu_custom_call" | custom-call | tf_op jit(solution)/shard_map/project/pallas_call | solution.py:333
  62.3 28.1 %all_to_all.5 = bf16[8,256,384]{2,1,0:T(8,128)(2,1)S(1)} all-to-all(bf16[8,256,384]{2,1,0:T(8,128)(2,1)S(1)} %project.1), channel_id=1, replica_groups=mesh['seq'=32,'head'=8] {'head'}, dimensions={0} | all-to-all | bytes 3145728 | tf_op jit(solution)/shard_map/all_to_all | solution.py:342
  90.4 0.9 %reduce_sum.12 = bf16[256,384]{1,0:T(8,128)(2,1)} reduce(bf16[8,256,384]{2,1,0:T(8,128)(2,1)S(1)} %all_to_all.5, bf16[]{:T(256)} %constant.24.clone.1), dimensions={0}, to_apply=%region_1.2 | reduce | flops 688128 | bytes 1769474 | tf_op jit(solution)/shard_map/reduce_sum | solution.py:343
  (28 shorter events, 0.5 us)
Async XLA Ops:
  1.6 11.7 %collective-permute-start = (bf16[272,384]{1,0:T(8,128)(2,1)S(1)}, bf16[272,384]{1,0:T(8,128)(2,1)S(1)}, u32[]{:S(2)}, u32[]{:S(2)}) collective-permute-start(bf16[272,384]{1,0:T(8,128)(2,1)S(1)} %fusion.1.refs_0_), channel_id=1, source_target_pairs={{0,8},{8,0},{16,24},{24,16},{32,40},{40,32},{48,56},{56,48},{64,72... | collective-permute-start | bytes 626696 | tf_op jit(solution)/shard_map/ppermute | solution.py:247
  1.7 11.6 %collective-permute-start.3 = (bf16[256,384]{1,0:T(8,128)(2,1)}, bf16[256,384]{1,0:T(8,128)(2,1)S(1)}, u32[]{:S(2)}, u32[]{:S(2)}) collective-permute-start(bf16[256,384]{1,0:T(8,128)(2,1)} %param.8), channel_id=1, source_target_pairs={{0,32},{8,40},{16,48},{24,56},{32,64},{40,72},{48,80},{56,88},{64,... | collective-permute-start | bytes 589832 | tf_op jit(solution)/shard_map/ppermute | solution.py:239
  3.7 23.9 %collective-permute-start.1 = (bf16[272,384]{1,0:T(8,128)(2,1)S(1)}, bf16[272,384]{1,0:T(8,128)(2,1)S(1)}, u32[]{:S(2)}, u32[]{:S(2)}) collective-permute-start(bf16[272,384]{1,0:T(8,128)(2,1)S(1)} %fusion.1.refs_0_), channel_id=1, source_target_pairs={{0,16},{8,24},{16,0},{24,8},{32,48},{40,56},{48,32},{56,40},{64,80... | collective-permute-start | bytes 626696 | tf_op jit(solution)/shard_map/ppermute | solution.py:247
  4.2 23.4 %collective-permute-start.2 = (bf16[272,384]{1,0:T(8,128)(2,1)S(1)}, bf16[272,384]{1,0:T(8,128)(2,1)S(1)}, u32[]{:S(2)}, u32[]{:S(2)}) collective-permute-start(bf16[272,384]{1,0:T(8,128)(2,1)S(1)} %fusion.1.refs_0_), channel_id=1, source_target_pairs={{0,24},{8,16},{16,8},{24,0},{32,56},{40,48},{48,40},{56,32},{64,88... | collective-permute-start | bytes 626696 | tf_op jit(solution)/shard_map/ppermute | solution.py:247
  5.2 19.2 %collective-permute-start.4 = (bf16[256,384]{1,0:T(8,128)(2,1)}, bf16[256,384]{1,0:T(8,128)(2,1)S(1)}, u32[]{:S(2)}, u32[]{:S(2)}) collective-permute-start(bf16[256,384]{1,0:T(8,128)(2,1)} %param.8), channel_id=1, source_target_pairs={{0,224},{8,232},{16,240},{24,248},{32,0},{40,8},{48,16},{56,24},{6... | collective-permute-start | bytes 589832 | tf_op jit(solution)/shard_map/ppermute | solution.py:240
  13.3 11.0 %collective-permute-start.5 = (bf16[256,384]{1,0:T(8,128)(2,1)}, bf16[256,384]{1,0:T(8,128)(2,1)S(1)}, u32[]{:S(2)}, u32[]{:S(2)}) collective-permute-start(bf16[256,384]{1,0:T(8,128)(2,1)} %param.9), channel_id=1, source_target_pairs={{0,32},{8,40},{16,48},{24,56},{32,64},{40,72},{48,80},{56,88},{64,... | collective-permute-start | bytes 589832 | tf_op jit(solution)/shard_map/ppermute | solution.py:241
  13.3 7.4 %collective-permute-start.6 = (bf16[256,384]{1,0:T(8,128)(2,1)}, bf16[256,384]{1,0:T(8,128)(2,1)S(1)}, u32[]{:S(2)}, u32[]{:S(2)}) collective-permute-start(bf16[256,384]{1,0:T(8,128)(2,1)} %param.9), channel_id=1, source_target_pairs={{0,224},{8,232},{16,240},{24,248},{32,0},{40,8},{48,16},{56,24},{6... | collective-permute-start | bytes 589832 | tf_op jit(solution)/shard_map/ppermute | solution.py:242
  20.8 8.6 %collective-permute-start.9 = (bf16[256,384]{1,0:T(8,128)(2,1)S(1)}, bf16[256,384]{1,0:T(8,128)(2,1)S(1)}, u32[]{:S(2)}, u32[]{:S(2)}) collective-permute-start(bf16[256,384]{1,0:T(8,128)(2,1)S(1)} %collective-permute-done.6.refs_8_), channel_id=1, source_target_pairs={{0,224},{8,232},{16,240},{24,248},{32,0},{40,8},{48,16},{56,24},{6... | collective-permute-start | bytes 589832 | tf_op jit(solution)/shard_map/ppermute | solution.py:242
  24.4 8.9 %collective-permute-start.7 = (bf16[256,384]{1,0:T(8,128)(2,1)S(1)}, bf16[256,384]{1,0:T(8,128)(2,1)S(1)}, u32[]{:S(2)}, u32[]{:S(2)}) collective-permute-start(bf16[256,384]{1,0:T(8,128)(2,1)S(1)} %collective-permute-done.3.refs_5_), channel_id=1, source_target_pairs={{0,32},{8,40},{16,48},{24,56},{32,64},{40,72},{48,80},{56,88},{64,... | collective-permute-start | bytes 589832 | tf_op jit(solution)/shard_map/ppermute | solution.py:239
  24.4 9.2 %collective-permute-start.13 = (bf16[256,384]{1,0:T(8,128)(2,1)S(1)}, bf16[256,384]{1,0:T(8,128)(2,1)S(1)}, u32[]{:S(2)}, u32[]{:S(2)}) collective-permute-start(bf16[256,384]{1,0:T(8,128)(2,1)S(1)} %collective-permute-done.4.refs_6_), channel_id=1, source_target_pairs={{0,224},{8,232},{16,240},{24,248},{32,0},{40,8},{48,16},{56,24},{6... | collective-permute-start | bytes 589832 | tf_op jit(solution)/shard_map/ppermute | solution.py:240
  27.6 9.9 %collective-permute-start.15 = (bf16[256,384]{1,0:T(8,128)(2,1)S(1)}, bf16[256,384]{1,0:T(8,128)(2,1)S(1)}, u32[]{:S(2)}, u32[]{:S(2)}) collective-permute-start(bf16[256,384]{1,0:T(8,128)(2,1)S(1)} %collective-permute-done.5.refs_7_), channel_id=1, source_target_pairs={{0,32},{8,40},{16,48},{24,56},{32,64},{40,72},{48,80},{56,88},{64,... | collective-permute-start | bytes 589832 | tf_op jit(solution)/shard_map/ppermute | solution.py:241
  29.4 12.4 %collective-permute-start.10 = (bf16[256,384]{1,0:T(8,128)(2,1)S(1)}, bf16[256,384]{1,0:T(8,128)(2,1)S(1)}, u32[]{:S(2)}, u32[]{:S(2)}) collective-permute-start(bf16[256,384]{1,0:T(8,128)(2,1)S(1)} %collective-permute-done.9.refs_7_), channel_id=1, source_target_pairs={{0,224},{8,232},{16,240},{24,248},{32,0},{40,8},{48,16},{56,24},{6... | collective-permute-start | bytes 589832 | tf_op jit(solution)/shard_map/ppermute | solution.py:242
  33.3 8.5 %collective-permute-start.8 = (bf16[256,384]{1,0:T(8,128)(2,1)S(1)}, bf16[256,384]{1,0:T(8,128)(2,1)S(1)}, u32[]{:S(2)}, u32[]{:S(2)}) collective-permute-start(bf16[256,384]{1,0:T(8,128)(2,1)S(1)} %collective-permute-done.7.refs_2_), channel_id=1, source_target_pairs={{0,32},{8,40},{16,48},{24,56},{32,64},{40,72},{48,80},{56,88},{64,... | collective-permute-start | bytes 589832 | tf_op jit(solution)/shard_map/ppermute | solution.py:239
  33.6 11.5 %collective-permute-start.14 = (bf16[256,384]{1,0:T(8,128)(2,1)S(1)}, bf16[256,384]{1,0:T(8,128)(2,1)S(1)}, u32[]{:S(2)}, u32[]{:S(2)}) collective-permute-start(bf16[256,384]{1,0:T(8,128)(2,1)S(1)} %collective-permute-done.13.refs_3_), channel_id=1, source_target_pairs={{0,224},{8,232},{16,240},{24,248},{32,0},{40,8},{48,16},{56,24},{6... | collective-permute-start | bytes 589832 | tf_op jit(solution)/shard_map/ppermute | solution.py:240
  37.5 8.8 %collective-permute-start.16 = (bf16[256,384]{1,0:T(8,128)(2,1)S(1)}, bf16[256,384]{1,0:T(8,128)(2,1)S(1)}, u32[]{:S(2)}, u32[]{:S(2)}) collective-permute-start(bf16[256,384]{1,0:T(8,128)(2,1)S(1)} %collective-permute-done.15.refs_6_), channel_id=1, source_target_pairs={{0,32},{8,40},{16,48},{24,56},{32,64},{40,72},{48,80},{56,88},{64,... | collective-permute-start | bytes 589832 | tf_op jit(solution)/shard_map/ppermute | solution.py:241
  41.8 7.1 %collective-permute-start.11 = (bf16[256,384]{1,0:T(8,128)(2,1)S(1)}, bf16[256,384]{1,0:T(8,128)(2,1)S(1)}, u32[]{:S(2)}, u32[]{:S(2)}) collective-permute-start(bf16[256,384]{1,0:T(8,128)(2,1)S(1)} %get-tuple-element.22), channel_id=1, source_target_pairs={{0,32},{8,40},{16,48},{24,56},{32,64},{40,72},{48,80},{56,88},{64,... | collective-permute-start | bytes 589832 | tf_op jit(solution)/shard_map/ppermute | solution.py:292
  41.9 7.0 %collective-permute-start.12 = (bf16[256,384]{1,0:T(8,128)(2,1)S(1)}, bf16[256,384]{1,0:T(8,128)(2,1)S(1)}, u32[]{:S(2)}, u32[]{:S(2)}) collective-permute-start(bf16[256,384]{1,0:T(8,128)(2,1)S(1)} %get-tuple-element.23), channel_id=1, source_target_pairs={{0,224},{8,232},{16,240},{24,248},{32,0},{40,8},{48,16},{56,24},{6... | collective-permute-start | bytes 589832 | tf_op jit(solution)/shard_map/ppermute | solution.py:293
  49.0 12.1 %copy-start = (bf16[384,3072]{1,0:T(8,128)(2,1)S(1)}, bf16[384,3072]{1,0:T(8,128)(2,1)}, u32[]{:S(2)}) copy-start(bf16[384,3072]{1,0:T(8,128)(2,1)} %weight_ref.1) | copy-start | bytes 7077892
  51.6 1.9 %collective-permute-start.17 = (bf16[2,416,256]{2,1,0:T(8,128)(2,1)S(1)}, bf16[2,416,256]{2,1,0:T(8,128)(2,1)S(1)}, u32[]{:S(2)}, u32[]{:S(2)}) collective-permute-start(bf16[2,416,256]{2,1,0:T(8,128)(2,1)S(1)} %get-tuple-element.31), channel_id=1, source_target_pairs={{0,8},{8,0},{16,24},{24,16},{32,40},{40,32},{48,56},{56,48},{64,72... | collective-permute-start | bytes 1277960 | tf_op jit(solution)/shard_map/ppermute | solution.py:319
  53.6 7.4 %collective-permute-start.18 = (bf16[1,416,256]{2,1,0:T(8,128)(2,1)S(1)}, bf16[1,416,256]{2,1,0:T(8,128)(2,1)S(1)}, u32[]{:S(2)}, u32[]{:S(2)}) collective-permute-start(bf16[1,416,256]{2,1,0:T(8,128)(2,1)S(1)} %get-tuple-element.34), channel_id=1, source_target_pairs={{0,16},{8,24},{16,0},{24,8},{32,48},{40,56},{48,32},{56,40},{64,80... | collective-permute-start | bytes 638984 | tf_op jit(solution)/shard_map/ppermute | solution.py:332

commit v5 on v4

--- a/solution.py
+++ b/solution.py
@@ -53,6 +53,10 @@
         )
         sums.append(top + jnp.log2(total))
     return outs, sums
+
+
+def halves(ref):
+    return ref.at[0:TILE], ref.at[TILE:2 * TILE]
 
 
 def load_shards(need_ref, first, shards, k_ref, vt_ref):
@@ -136,22 +140,21 @@
 
 
 def near_kernel(factor, need_ref, *refs):
-    q_refs, (own_ref, k_low, k_high, v_low, v_high) = refs[:GROUP], refs[GROUP:GROUP + 5]
-    stacked_ref, acc_ref, peak_ref, total_ref, k_ref, vt_ref = refs[GROUP + 5:]
+    q_refs, kv_refs = refs[:GROUP], refs[GROUP:GROUP + 3]
+    stacked_ref, acc_ref, peak_ref, total_ref, k_ref, vt_ref = refs[GROUP + 3:]
     acc_ref[...] = jnp.zeros_like(acc_ref)
     peak_ref[...] = jnp.full_like(peak_ref, LOWEST)
     total_ref[...] = jnp.zeros_like(total_ref)
     for t, q_ref in enumerate(q_refs):
         stacked_ref[t] = q_ref[0:TILE, :]
-    shards = [(own_ref.at[0:TILE], own_ref.at[TILE:2 * TILE]), (k_low, v_low), (k_high, v_high)]
-    load_shards(need_ref, 0, shards, k_ref, vt_ref)
+    load_shards(need_ref, 0, [halves(ref) for ref in kv_refs], k_ref, vt_ref)
     visit_shards(factor, need_ref, 0, 3, stacked_ref, k_ref, vt_ref, (acc_ref, peak_ref, total_ref))
 
 
 def far_kernel(factor, first, count, need_ref, stacked_ref, *refs):
-    shards = list(zip(refs[:count], refs[count:2 * count]))
-    held, state = refs[2 * count:2 * count + 3], refs[2 * count + 3:2 * count + 6]
-    k_ref, vt_ref = refs[2 * count + 6:]
+    shards = [halves(ref) for ref in refs[:count]]
+    held, state = refs[count:count + 3], refs[count + 3:count + 6]
+    k_ref, vt_ref = refs[count + 6:]
     for source, target in zip(held, state):
         target[...] = source[...]
     load_shards(need_ref, first, shards, k_ref, vt_ref)
@@ -184,9 +187,9 @@
                 keep_sum_ref[t // 2, h:h + 1, :] = sums[h]
 
 
-def relay_kernel(k_ref, v_ref, after_ref, k_out_ref, v_out_ref):
-    k_out_ref[...] = k_ref[...]
-    v_out_ref[...] = v_ref[...]
+def relay_kernel(low_ref, high_ref, after_ref, k_out_ref, v_out_ref):
+    k_out_ref[...] = low_ref[0:TILE]
+    v_out_ref[...] = high_ref[TILE:2 * TILE]
 
 
 def merge_kernel(mine_ref, mine_sum_ref, other_ref, keep_ref, keep_sum_ref, send_ref):
@@ -233,13 +236,12 @@
     up = [(s, (s + GROUP) % seq_size) for s in range(seq_size)]
     down = [(s, (s - GROUP) % seq_size) for s in range(seq_size)]
 
-    k_up, k_down, v_up, v_down = [key_states], [key_states], [value_states], [value_states]
+    own = jnp.concatenate([key_states, value_states], axis=0)
+    kv_up, kv_down = [own], [own]
     half = planes // 2
     for step in range(half - 1):
-        k_up.append(lax.ppermute(k_up[-1], "seq", up))
-        k_down.append(lax.ppermute(k_down[-1], "seq", down))
-        v_up.append(lax.ppermute(v_up[-1], "seq", up))
-        v_down.append(lax.ppermute(v_down[-1], "seq", down))
+        kv_up.append(lax.ppermute(kv_up[-1], "seq", up))
+        kv_down.append(lax.ppermute(kv_down[-1], "seq", down))
 
     listed = jnp.pad(block_list.astype(jnp.bfloat16), ((0, PART_ROWS - 1), (0, width - block_list.shape[1])))
     packed = jnp.concatenate([queries, listed], axis=0)
@@ -269,17 +271,16 @@
             pltpu.VMEM((count, heads, HD, TILE), jnp.bfloat16),
         ]
 
-    own = jnp.concatenate([key_states, value_states], axis=0)
     stacked, *held = pl.pallas_call(
         functools.partial(near_kernel, factor),
         out_shape=(jax.ShapeDtypeStruct((GROUP, TILE, width), jnp.bfloat16),) + state,
-        in_specs=smem + vmem_specs(GROUP + 5),
+        in_specs=smem + vmem_specs(GROUP + 3),
         out_specs=tuple(vmem_specs(4)),
         scratch_shapes=scratch(3),
         compiler_params=PARAMS,
         cost_estimate=attend_cost(27),
         name="attend_near",
-    )(need, *tiles, own, k_up[1], k_down[1], v_up[1], v_down[1])
+    )(need, *tiles, own, kv_up[1], kv_down[1])
     shard = jax.ShapeDtypeStruct(key_states.shape, key_states.dtype)
     k_last, v_last = pl.pallas_call(
         relay_kernel,
@@ -288,19 +289,19 @@
         out_specs=tuple(vmem_specs(2)),
         compiler_params=PARAMS,
         name="relay",
-    )(k_up[-1], v_down[-1], held[2])
+    )(kv_up[-1], kv_down[-1], held[2])
     k_last = lax.ppermute(k_last, "seq", up)
     v_last = lax.ppermute(v_last, "seq", down)
     held = pl.pallas_call(
         functools.partial(far_kernel, factor, 3, 4),
         out_shape=state,
-        in_specs=smem + vmem_specs(12),
+        in_specs=smem + vmem_specs(8),
         out_specs=tuple(vmem_specs(3)),
         scratch_shapes=scratch(4),
         compiler_params=PARAMS,
         cost_estimate=attend_cost(24),
         name="attend_far",
-    )(need, stacked, k_up[3], k_down[3], k_up[2], k_down[2], v_up[3], v_down[3], v_up[2], v_down[2], *held)
+    )(need, stacked, kv_up[3], kv_down[3], kv_up[2], kv_down[2], *held)
     keep, keep_sum, send = pl.pallas_call(
         functools.partial(last_kernel, factor, 7),
         out_shape=(

time: 92.8 us -> 98.1 us (1.057); the launches traced: 91.3 us -> 97.8 us
  waiting for transfers between devices: 17.7 us -> 34.8 us
  starting transfers between devices: 29.2 us -> 17.7 us
  local copies, waits for them, and re-layouts: 0.74 us -> 2.64 us
  other arithmetic: 4.49 us -> 3.43 us
    ppermute x12 -> x6, starting transfers between devices: 23.6 us -> 12.6 us  [the longest x3 10.5 us: per_device(): kv_down.append(lax.ppermute(kv_down[-1], 'seq', down))]
    ppermute x3, waiting for transfers between devices: 0.01 us -> 8.31 us  [per_device(): lax.ppermute(packed, 'seq', [(s, s ^ k) for s in range(seq_size)])]
    ppermute x12 -> x6, waiting for transfers between devices: 9.06 us -> 13.3 us  [the longest x3 13.3 us: per_device(): kv_up.append(lax.ppermute(kv_up[-1], 'seq', up))]
    ppermute x1, waiting for transfers between devices: 0.01 us -> 3.41 us  [per_device(): k_last = lax.ppermute(k_last, 'seq', up)]
    concatenate x1 -> x0, other arithmetic: 1.06 us -> none  [per_device(): own = jnp.concatenate([key_states, value_states], axis=0)]
  transfers between devices with their start and end apart: 19 -> 13, of which waited for: 9 -> 8; matrix products, arithmetic and copies ran while one was open for 3% -> 3% of each run, Pallas kernels for 8% -> 7%
where the time goes in v5:
time: 98.1 us; the launch traced here: 97.8 us
  waiting for transfers between devices  34.8 us (35%)
  blocking collectives  28.1 us (29%)
  starting transfers between devices  17.7 us (18%)
  Pallas kernels  11 us (11%)
  other arithmetic  3.43 us (3%)
  local copies, waits for them, and re-layouts  2.64 us (3%)
    all_to_all x1, blocking collectives, per_device(): shares = lax.all_to_all(shares, 'head', 0, 0, tiled=False)  28.1 us
    ppermute x3, waiting for transfers between devices, per_device(): kv_up.append(lax.ppermute(kv_up[-1], 'seq', up))  13.3 us
    ppermute x3, starting transfers between devices, per_device(): kv_down.append(lax.ppermute(kv_down[-1], 'seq', down))  10.5 us
    ppermute x3, waiting for transfers between devices, per_device(): lax.ppermute(packed, 'seq', [(s, s ^ k) for s in range(seq_size)])  8.31 us
    ppermute x1, waiting for transfers between devices, per_device(): other = lax.ppermute(send, 'seq', [(s, s ^ 2) for s in range(seq_size)])  7.28 us
    pallas_call x1, Pallas kernels, per_device(): pl.pallas_call(functools.partial(near_kernel, factor), out_shape=(jax.Sha...  4.08 us
    ppermute x1, waiting for transfers between devices, per_device(): k_last = lax.ppermute(k_last, 'seq', up)  3.41 us
    ppermute x1, starting transfers between devices, per_device(): v_last = lax.ppermute(v_last, 'seq', down)  3.03 us
  transfers between devices with their start and end apart: 13, of which 8 were waited for; matrix products, arithmetic and copies ran while one was open for 3% of the time, Pallas kernels for 7%

profile of v5, /device:TPU:2, one launch (start us, length us, event | category | flops | bytes accessed | tf_op | source)
XLA Modules:
  0.0 97.8 jit_solution(2669229520961834203)
XLA Ops:
  0.0 0.9 constant_dynamic-update-slice_fusion.1
  0.9 1.0 constant_dynamic-update-slice_fusion.refs_4_
  1.9 2.0 %collective-permute-start.3 = (bf16[512,384]{1,0:T(8,128)(2,1)S(1)}, bf16[512,384]{1,0:T(8,128)(2,1)S(1)}, u32[]{:S(2)}, u32[]{:S(2)}) collective-permute-start(bf16[512,384]{1,0:T(8,128)(2,1)S(1)} %constant_dynamic-update-slice_fusion.refs_4_), channel_id=1, source_target_pairs={{0,32},{8,40},{16,48},{24,56},{32,64},{40,72},{48,80},{56,88},{64,... | collective-permute-start | bytes 1179656 | tf_op jit(solution)/shard_map/ppermute | solution.py:243
  3.9 4.0 %collective-permute-start.4 = (bf16[512,384]{1,0:T(8,128)(2,1)S(1)}, bf16[512,384]{1,0:T(8,128)(2,1)S(1)}, u32[]{:S(2)}, u32[]{:S(2)}) collective-permute-start(bf16[512,384]{1,0:T(8,128)(2,1)S(1)} %constant_dynamic-update-slice_fusion.refs_4_), channel_id=1, source_target_pairs={{0,224},{8,232},{16,240},{24,248},{32,0},{40,8},{48,16},{56,24},{6... | collective-permute-start | bytes 1179656 | tf_op jit(solution)/shard_map/ppermute | solution.py:244
  7.9 0.7 convert_element_type.13
  8.6 8.4 %collective-permute-done.3.refs_5_ = bf16[512,384]{1,0:T(8,128)(2,1)S(1)} collective-permute-done((bf16[512,384]{1,0:T(8,128)(2,1)S(1)}, bf16[512,384]{1,0:T(8,128)(2,1)S(1)}, u32[]{:S(2)}, u32[]{:S(2)}) %collective-permute-start.3) | collective-permute-done | bytes 393248 | tf_op jit(solution)/shard_map/ppermute | solution.py:243
  17.0 3.2 %collective-permute-start.7 = (bf16[512,384]{1,0:T(8,128)(2,1)S(1)}, bf16[512,384]{1,0:T(8,128)(2,1)S(1)}, u32[]{:S(2)}, u32[]{:S(2)}) collective-permute-start(bf16[512,384]{1,0:T(8,128)(2,1)S(1)} %collective-permute-done.4.refs_6_), channel_id=1, source_target_pairs={{0,224},{8,232},{16,240},{24,248},{32,0},{40,8},{48,16},{56,24},{6... | collective-permute-start | bytes 1179656 | tf_op jit(solution)/shard_map/ppermute | solution.py:244
  20.2 0.9 fusion.1.refs_0_
  21.2 0.1 collective-permute-start
  21.3 0.6 collective-permute-start.1
  21.9 1.2 %collective-permute-start.2 = (bf16[272,384]{1,0:T(8,128)(2,1)S(1)}, bf16[272,384]{1,0:T(8,128)(2,1)S(1)}, u32[]{:S(2)}, u32[]{:S(2)}) collective-permute-start(bf16[272,384]{1,0:T(8,128)(2,1)S(1)} %fusion.1.refs_0_), channel_id=1, source_target_pairs={{0,24},{8,16},{16,8},{24,0},{32,56},{40,48},{48,40},{56,32},{64,88... | collective-permute-start | bytes 626696 | tf_op jit(solution)/shard_map/ppermute | solution.py:249
  23.1 0.7 pad.6.clone
  23.9 0.7 and_select_fusion
  24.5 4.8 %collective-permute-done.1.refs_2_ = bf16[272,384]{1,0:T(8,128)(2,1)S(1)} collective-permute-done((bf16[272,384]{1,0:T(8,128)(2,1)S(1)}, bf16[272,384]{1,0:T(8,128)(2,1)S(1)}, u32[]{:S(2)}, u32[]{:S(2)}) %collective-permute-start.1) | collective-permute-done | bytes 208928 | tf_op jit(solution)/shard_map/ppermute | solution.py:249
  29.3 3.5 %collective-permute-done.2.refs_3_ = bf16[272,384]{1,0:T(8,128)(2,1)S(1)} collective-permute-done((bf16[272,384]{1,0:T(8,128)(2,1)S(1)}, bf16[272,384]{1,0:T(8,128)(2,1)S(1)}, u32[]{:S(2)}, u32[]{:S(2)}) %collective-permute-start.2) | collective-permute-done | bytes 208928 | tf_op jit(solution)/shard_map/ppermute | solution.py:249
  33.0 3.2 %collective-permute-start.8 = (bf16[512,384]{1,0:T(8,128)(2,1)S(1)}, bf16[512,384]{1,0:T(8,128)(2,1)S(1)}, u32[]{:S(2)}, u32[]{:S(2)}) collective-permute-start(bf16[512,384]{1,0:T(8,128)(2,1)S(1)} %collective-permute-done.7.refs_3_), channel_id=1, source_target_pairs={{0,224},{8,232},{16,240},{24,248},{32,0},{40,8},{48,16},{56,24},{6... | collective-permute-start | bytes 1179656 | tf_op jit(solution)/shard_map/ppermute | solution.py:244
  36.2 0.2 compare_reduce_fusion
  36.4 4.1 %attend_near.1 = (bf16[4,256,384]{2,1,0:T(8,128)(2,1)S(1)}, f32[12,128,256]{2,1,0:T(8,128)S(1)}, f32[12,1,256]{2,1,0:T(1,128)S(1)}, f32[12,1,256]{2,1,0:T(1,128)S(1)}) custom-call(s32[4,8]{1,0:T(4,128)S(1)} %convert_element_type.15.need_ref, bf16[272,384]{1,0:T(8,128)(2,1)S(1)} %fusion.1.refs_0_, bf16[272,384]{1,0:T(8,128)(2,1)S(1)} %collective-permute-done.refs_1_, ...), custom_call_target="tpu_custom_call" | custom-call | flops 905969664 | bytes 4194304 | tf_op jit(solution)/shard_map/attend_near/pallas_call | solution.py:274
  40.5 5.0 %collective-permute-done.6.low_ref.refs_0_ = bf16[512,384]{1,0:T(8,128)(2,1)S(1)} collective-permute-done((bf16[512,384]{1,0:T(8,128)(2,1)S(1)}, bf16[512,384]{1,0:T(8,128)(2,1)S(1)}, u32[]{:S(2)}, u32[]{:S(2)}) %collective-permute-start.6) | collective-permute-done | bytes 393248 | tf_op jit(solution)/shard_map/ppermute | solution.py:243
  45.5 3.0 %collective-permute-start.10 = (bf16[256,384]{1,0:T(8,128)(2,1)S(1)}, bf16[256,384]{1,0:T(8,128)(2,1)S(1)}, u32[]{:S(2)}, u32[]{:S(2)}) collective-permute-start(bf16[256,384]{1,0:T(8,128)(2,1)S(1)} %get-tuple-element.23), channel_id=1, source_target_pairs={{0,224},{8,232},{16,240},{24,248},{32,0},{40,8},{48,16},{56,24},{6... | collective-permute-start | bytes 589832 | tf_op jit(solution)/shard_map/ppermute | solution.py:294
  48.6 2.8 %attend_far.1 = (f32[12,128,256]{2,1,0:T(8,128)S(1)}, f32[12,1,256]{2,1,0:T(1,128)S(1)}, f32[12,1,256]{2,1,0:T(1,128)S(1)}) custom-call(s32[4,8]{1,0:T(4,128)S(1)} %convert_element_type.15.need_ref, bf16[4,256,384]{2,1,0:T(8,128)(2,1)S(1)} %get-tuple-element.20.stacked_ref, bf16[512,384]{1,0:T(8,128)(2,1)S(1)} %collective-permute-done.6.low_ref.refs_0_, ...), custom_call_target="tpu_custom_call" | custom-call | flops 805306368 | bytes 4194304 | tf_op jit(solution)/shard_map/attend_far/pallas_call | solution.py:295
  51.4 0.7 collective-permute-done.10.refs_1_
  52.0 3.4 %collective-permute-done.9.refs_0_ = bf16[256,384]{1,0:T(8,128)(2,1)S(1)} collective-permute-done((bf16[256,384]{1,0:T(8,128)(2,1)S(1)}, bf16[256,384]{1,0:T(8,128)(2,1)S(1)}, u32[]{:S(2)}, u32[]{:S(2)}) %collective-permute-start.9) | collective-permute-done | bytes 196640 | tf_op jit(solution)/shard_map/ppermute | solution.py:293
  55.5 2.6 %attend_last.1 = (f32[2,384,256]{2,1,0:T(8,128)S(1)}, f32[2,8,256]{2,1,0:T(8,128)S(1)}, bf16[2,416,256]{2,1,0:T(8,128)(2,1)S(1)}) custom-call(s32[4,8]{1,0:T(4,128)S(1)} %convert_element_type.15.need_ref, bf16[4,256,384]{2,1,0:T(8,128)(2,1)S(1)} %get-tuple-element.20.stacked_ref, bf16[256,384]{1,0:T(8,128)(2,1)S(1)} %collective-permute-done.9.refs_0_, ...), custom_call_target="tpu_custom_call" | custom-call | flops 402653184 | bytes 4194304 | tf_op jit(solution)/shard_map/attend_last/pallas_call | solution.py:305
  58.1 0.1 collective-permute-start.11
  58.2 1.8 %collective-permute-done.11.other_ref = bf16[2,416,256]{2,1,0:T(8,128)(2,1)S(1)} collective-permute-done((bf16[2,416,256]{2,1,0:T(8,128)(2,1)S(1)}, bf16[2,416,256]{2,1,0:T(8,128)(2,1)S(1)}, u32[]{:S(2)}, u32[]{:S(2)}) %collective-permute-start.11) | collective-permute-done | bytes 426016 | tf_op jit(solution)/shard_map/ppermute | solution.py:320
  59.9 0.2 merge.1
  60.1 0.1 collective-permute-start.12
  60.2 7.3 %collective-permute-done.12.other_ref = bf16[1,416,256]{2,1,0:T(8,128)(2,1)S(1)} collective-permute-done((bf16[1,416,256]{2,1,0:T(8,128)(2,1)S(1)}, bf16[1,416,256]{2,1,0:T(8,128)(2,1)S(1)}, u32[]{:S(2)}, u32[]{:S(2)}) %collective-permute-start.12) | collective-permute-done | bytes 213024 | tf_op jit(solution)/shard_map/ppermute | solution.py:333
  67.5 1.3 %project.1 = bf16[8,256,384]{2,1,0:T(8,128)(2,1)S(1)} custom-call(f32[1,384,256]{2,1,0:T(8,128)S(1)} %get-tuple-element.32.mine_ref, f32[1,8,256]{2,1,0:T(8,128)S(1)} %get-tuple-element.33.mine_sum_ref, bf16[1,416,256]{2,1,0:T(8,128)(2,1)S(1)} %collective-permute-done.12.other_ref, bf16[384,3072]{1,0:T(8,128)(2,1)S(1)} %copy-done), custom_call_target="tpu_custom_call" | custom-call | tf_op jit(solution)/shard_map/project/pallas_call | solution.py:334
  68.8 28.1 %all_to_all.5 = bf16[8,256,384]{2,1,0:T(8,128)(2,1)S(1)} all-to-all(bf16[8,256,384]{2,1,0:T(8,128)(2,1)S(1)} %project.1), channel_id=1, replica_groups=mesh['seq'=32,'head'=8] {'head'}, dimensions={0} | all-to-all | bytes 3145728 | tf_op jit(solution)/shard_map/all_to_all | solution.py:343
  96.9 0.9 reduce_sum.12
  (17 shorter events, 0.2 us)
Async XLA Ops:
  1.9 15.0 %collective-permute-start.3 = (bf16[512,384]{1,0:T(8,128)(2,1)S(1)}, bf16[512,384]{1,0:T(8,128)(2,1)S(1)}, u32[]{:S(2)}, u32[]{:S(2)}) collective-permute-start(bf16[512,384]{1,0:T(8,128)(2,1)S(1)} %constant_dynamic-update-slice_fusion.refs_4_), channel_id=1, source_target_pairs={{0,32},{8,40},{16,48},{24,56},{32,64},{40,72},{48,80},{56,88},{64,... | collective-permute-start | bytes 1179656 | tf_op jit(solution)/shard_map/ppermute | solution.py:243
  3.9 13.1 %collective-permute-start.4 = (bf16[512,384]{1,0:T(8,128)(2,1)S(1)}, bf16[512,384]{1,0:T(8,128)(2,1)S(1)}, u32[]{:S(2)}, u32[]{:S(2)}) collective-permute-start(bf16[512,384]{1,0:T(8,128)(2,1)S(1)} %constant_dynamic-update-slice_fusion.refs_4_), channel_id=1, source_target_pairs={{0,224},{8,232},{16,240},{24,248},{32,0},{40,8},{48,16},{56,24},{6... | collective-permute-start | bytes 1179656 | tf_op jit(solution)/shard_map/ppermute | solution.py:244
  17.0 15.9 %collective-permute-start.5 = (bf16[512,384]{1,0:T(8,128)(2,1)S(1)}, bf16[512,384]{1,0:T(8,128)(2,1)S(1)}, u32[]{:S(2)}, u32[]{:S(2)}) collective-permute-start(bf16[512,384]{1,0:T(8,128)(2,1)S(1)} %collective-permute-done.3.refs_5_), channel_id=1, source_target_pairs={{0,32},{8,40},{16,48},{24,56},{32,64},{40,72},{48,80},{56,88},{64,... | collective-permute-start | bytes 1179656 | tf_op jit(solution)/shard_map/ppermute | solution.py:243
  17.0 16.0 %collective-permute-start.7 = (bf16[512,384]{1,0:T(8,128)(2,1)S(1)}, bf16[512,384]{1,0:T(8,128)(2,1)S(1)}, u32[]{:S(2)}, u32[]{:S(2)}) collective-permute-start(bf16[512,384]{1,0:T(8,128)(2,1)S(1)} %collective-permute-done.4.refs_6_), channel_id=1, source_target_pairs={{0,224},{8,232},{16,240},{24,248},{32,0},{40,8},{48,16},{56,24},{6... | collective-permute-start | bytes 1179656 | tf_op jit(solution)/shard_map/ppermute | solution.py:244
  21.2 3.4 %collective-permute-start = (bf16[272,384]{1,0:T(8,128)(2,1)S(1)}, bf16[272,384]{1,0:T(8,128)(2,1)S(1)}, u32[]{:S(2)}, u32[]{:S(2)}) collective-permute-start(bf16[272,384]{1,0:T(8,128)(2,1)S(1)} %fusion.1.refs_0_), channel_id=1, source_target_pairs={{0,8},{8,0},{16,24},{24,16},{32,40},{40,32},{48,56},{56,48},{64,72... | collective-permute-start | bytes 626696 | tf_op jit(solution)/shard_map/ppermute | solution.py:249
  21.3 8.1 %collective-permute-start.1 = (bf16[272,384]{1,0:T(8,128)(2,1)S(1)}, bf16[272,384]{1,0:T(8,128)(2,1)S(1)}, u32[]{:S(2)}, u32[]{:S(2)}) collective-permute-start(bf16[272,384]{1,0:T(8,128)(2,1)S(1)} %fusion.1.refs_0_), channel_id=1, source_target_pairs={{0,16},{8,24},{16,0},{24,8},{32,48},{40,56},{48,32},{56,40},{64,80... | collective-permute-start | bytes 626696 | tf_op jit(solution)/shard_map/ppermute | solution.py:249
  21.9 11.0 %collective-permute-start.2 = (bf16[272,384]{1,0:T(8,128)(2,1)S(1)}, bf16[272,384]{1,0:T(8,128)(2,1)S(1)}, u32[]{:S(2)}, u32[]{:S(2)}) collective-permute-start(bf16[272,384]{1,0:T(8,128)(2,1)S(1)} %fusion.1.refs_0_), channel_id=1, source_target_pairs={{0,24},{8,16},{16,8},{24,0},{32,56},{40,48},{48,40},{56,32},{64,88... | collective-permute-start | bytes 626696 | tf_op jit(solution)/shard_map/ppermute | solution.py:249
  32.9 12.6 %collective-permute-start.6 = (bf16[512,384]{1,0:T(8,128)(2,1)S(1)}, bf16[512,384]{1,0:T(8,128)(2,1)S(1)}, u32[]{:S(2)}, u32[]{:S(2)}) collective-permute-start(bf16[512,384]{1,0:T(8,128)(2,1)S(1)} %collective-permute-done.5.refs_2_), channel_id=1, source_target_pairs={{0,32},{8,40},{16,48},{24,56},{32,64},{40,72},{48,80},{56,88},{64,... | collective-permute-start | bytes 1179656 | tf_op jit(solution)/shard_map/ppermute | solution.py:243
  33.0 12.5 %collective-permute-start.8 = (bf16[512,384]{1,0:T(8,128)(2,1)S(1)}, bf16[512,384]{1,0:T(8,128)(2,1)S(1)}, u32[]{:S(2)}, u32[]{:S(2)}) collective-permute-start(bf16[512,384]{1,0:T(8,128)(2,1)S(1)} %collective-permute-done.7.refs_3_), channel_id=1, source_target_pairs={{0,224},{8,232},{16,240},{24,248},{32,0},{40,8},{48,16},{56,24},{6... | collective-permute-start | bytes 1179656 | tf_op jit(solution)/shard_map/ppermute | solution.py:244
  45.5 6.5 %collective-permute-start.10 = (bf16[256,384]{1,0:T(8,128)(2,1)S(1)}, bf16[256,384]{1,0:T(8,128)(2,1)S(1)}, u32[]{:S(2)}, u32[]{:S(2)}) collective-permute-start(bf16[256,384]{1,0:T(8,128)(2,1)S(1)} %get-tuple-element.23), channel_id=1, source_target_pairs={{0,224},{8,232},{16,240},{24,248},{32,0},{40,8},{48,16},{56,24},{6... | collective-permute-start | bytes 589832 | tf_op jit(solution)/shard_map/ppermute | solution.py:294
  48.5 6.9 %collective-permute-start.9 = (bf16[256,384]{1,0:T(8,128)(2,1)S(1)}, bf16[256,384]{1,0:T(8,128)(2,1)S(1)}, u32[]{:S(2)}, u32[]{:S(2)}) collective-permute-start(bf16[256,384]{1,0:T(8,128)(2,1)S(1)} %get-tuple-element.22), channel_id=1, source_target_pairs={{0,32},{8,40},{16,48},{24,56},{32,64},{40,72},{48,80},{56,88},{64,... | collective-permute-start | bytes 589832 | tf_op jit(solution)/shard_map/ppermute | solution.py:293
  55.5 12.1 %copy-start = (bf16[384,3072]{1,0:T(8,128)(2,1)S(1)}, bf16[384,3072]{1,0:T(8,128)(2,1)}, u32[]{:S(2)}) copy-start(bf16[384,3072]{1,0:T(8,128)(2,1)} %weight_ref.1) | copy-start | bytes 7077892
  58.1 1.9 %collective-permute-start.11 = (bf16[2,416,256]{2,1,0:T(8,128)(2,1)S(1)}, bf16[2,416,256]{2,1,0:T(8,128)(2,1)S(1)}, u32[]{:S(2)}, u32[]{:S(2)}) collective-permute-start(bf16[2,416,256]{2,1,0:T(8,128)(2,1)S(1)} %get-tuple-element.31), channel_id=1, source_target_pairs={{0,8},{8,0},{16,24},{24,16},{32,40},{40,32},{48,56},{56,48},{64,72... | collective-permute-start | bytes 1277960 | tf_op jit(solution)/shard_map/ppermute | solution.py:320
  60.1 7.4 %collective-permute-start.12 = (bf16[1,416,256]{2,1,0:T(8,128)(2,1)S(1)}, bf16[1,416,256]{2,1,0:T(8,128)(2,1)S(1)}, u32[]{:S(2)}, u32[]{:S(2)}) collective-permute-start(bf16[1,416,256]{2,1,0:T(8,128)(2,1)S(1)} %get-tuple-element.34), channel_id=1, source_target_pairs={{0,16},{8,24},{16,0},{24,8},{32,48},{40,56},{48,32},{56,40},{64,80... | collective-permute-start | bytes 638984 | tf_op jit(solution)/shard_map/ppermute | solution.py:333

commit v6 on v4

--- a/solution.py
+++ b/solution.py
@@ -135,9 +135,25 @@
     lax.fori_loop(0, q_ref.shape[0], visit, 0)
 
 
-def near_kernel(factor, need_ref, *refs):
+def list_wanted(seq_size, order, place_ref, q_refs, need_ref):
+    slots = [lax.rem(place_ref[0] + (GROUP * plane + seq_size), seq_size) for plane in order]
+    for t, q_ref in enumerate(q_refs):
+        row = q_ref[TILE:TILE + PART_ROWS, 0:HD].astype(jnp.float32)
+        bits = jnp.zeros_like(row)
+        for j, slot in enumerate(slots):
+            bits = bits + jnp.where(row == slot.astype(jnp.float32), float(1 << j), 0.0)
+        code = jnp.sum(bits).astype(jnp.int32)
+        for j, slot in enumerate(slots):
+            wanted = (code >> j) & 1
+            for i in range(1, place_ref.shape[0]):
+                wanted = jnp.where(slot == place_ref[i], 1, wanted)
+            need_ref[t, j] = wanted
+
+
+def near_kernel(factor, seq_size, order, place_ref, *refs):
     q_refs, (own_ref, k_low, k_high, v_low, v_high) = refs[:GROUP], refs[GROUP:GROUP + 5]
-    stacked_ref, acc_ref, peak_ref, total_ref, k_ref, vt_ref = refs[GROUP + 5:]
+    need_ref, stacked_ref, acc_ref, peak_ref, total_ref, k_ref, vt_ref = refs[GROUP + 5:]
+    list_wanted(seq_size, order, place_ref, q_refs, need_ref)
     acc_ref[...] = jnp.zeros_like(acc_ref)
     peak_ref[...] = jnp.full_like(peak_ref, LOWEST)
     total_ref[...] = jnp.zeros_like(total_ref)
@@ -241,18 +257,15 @@
         v_up.append(lax.ppermute(v_up[-1], "seq", up))
         v_down.append(lax.ppermute(v_down[-1], "seq", down))
 
-    listed = jnp.pad(block_list.astype(jnp.bfloat16), ((0, PART_ROWS - 1), (0, width - block_list.shape[1])))
-    packed = jnp.concatenate([queries, listed], axis=0)
+    listed = jnp.pad(
+        block_list, ((0, PART_ROWS - 1), (0, width - block_list.shape[1])), constant_values=-1
+    )
+    packed = jnp.concatenate([queries, listed.astype(jnp.bfloat16)], axis=0)
     tiles = [packed] + [
         lax.ppermute(packed, "seq", [(s, s ^ k) for s in range(seq_size)]) for k in range(1, GROUP)
     ]
-    lists = jnp.concatenate([t[TILE:TILE + 1, :block_list.shape[1]] for t in tiles], axis=0)
-    lists = jnp.concatenate(
-        [lists.astype(jnp.int32), jnp.broadcast_to(text_slots[None, :], (GROUP, text_slots.shape[0]))], axis=1
-    )
-    order = [0, -1, 1, -3, 3, -2, 2, 4]
-    slots = (me + GROUP * jnp.asarray(order, jnp.int32)) % seq_size
-    need = jnp.any(lists[:, None, :] == slots[None, :, None], axis=2).astype(jnp.int32)
+    order = (0, -1, 1, -3, 3, -2, 2, 4)
+    place = jnp.concatenate([me.astype(jnp.int32)[None], text_slots])
 
     rows = GROUP * heads
     state = (
@@ -270,16 +283,20 @@
         ]
 
     own = jnp.concatenate([key_states, value_states], axis=0)
-    stacked, *held = pl.pallas_call(
-        functools.partial(near_kernel, factor),
-        out_shape=(jax.ShapeDtypeStruct((GROUP, TILE, width), jnp.bfloat16),) + state,
+    need, stacked, *held = pl.pallas_call(
+        functools.partial(near_kernel, factor, seq_size, order),
+        out_shape=(
+            jax.ShapeDtypeStruct((GROUP, len(order)), jnp.int32),
+            jax.ShapeDtypeStruct((GROUP, TILE, width), jnp.bfloat16),
+        )
+        + state,
         in_specs=smem + vmem_specs(GROUP + 5),
-        out_specs=tuple(vmem_specs(4)),
+        out_specs=tuple(smem + vmem_specs(4)),
         scratch_shapes=scratch(3),
         compiler_params=PARAMS,
         cost_estimate=attend_cost(27),
         name="attend_near",
-    )(need, *tiles, own, k_up[1], k_down[1], v_up[1], v_down[1])
+    )(place, *tiles, own, k_up[1], k_down[1], v_up[1], v_down[1])
     shard = jax.ShapeDtypeStruct(key_states.shape, key_states.dtype)
     k_last, v_last = pl.pallas_call(
         relay_kernel,

time: 92.8 us -> 87.6 us (0.944)
  waiting for transfers between devices: 17.7 us -> 13.9 us
  starting transfers between devices: 29.2 us -> 25.6 us
  Pallas kernels: 10.9 us -> 13.7 us
    pallas_call x1, Pallas kernels: 2.6 us -> 4.63 us  [per_device(): pl.pallas_call(functools.partial(far_kernel, factor, 3, 4), out_shape=sta...]
    ppermute x3, waiting for transfers between devices: 5.25 us -> 3.59 us  [per_device(): v_down.append(lax.ppermute(v_down[-1], 'seq', down))]
    ppermute x3, starting transfers between devices: 10.5 us -> 8.92 us  [per_device(): v_down.append(lax.ppermute(v_down[-1], 'seq', down))]
    ppermute x3, waiting for transfers between devices: 2.33 us -> 0.76 us  [per_device(): k_up.append(lax.ppermute(k_up[-1], 'seq', up))]
    ppermute x3, starting transfers between devices: 11.1 us -> 10.1 us  [per_device(): k_down.append(lax.ppermute(k_down[-1], 'seq', down))]
  transfers between devices with their start and end apart: 19 -> 19, of which waited for: 9 -> 6; matrix products, arithmetic and copies ran while one was open for 3% -> 4% of each run, Pallas kernels for 8% -> 11%
where the time goes in v6:
time: 87.6 us; the launch traced here: 86.3 us
  blocking collectives  28.6 us (33%)
  starting transfers between devices  25.6 us (29%)
  waiting for transfers between devices  13.9 us (16%)
  Pallas kernels  13.7 us (16%)
  other arithmetic  4.32 us (5%)
    all_to_all x1, blocking collectives, per_device(): shares = lax.all_to_all(shares, 'head', 0, 0, tiled=False)  28.6 us
    ppermute x3, starting transfers between devices, per_device(): k_down.append(lax.ppermute(k_down[-1], 'seq', down))  10.1 us
    ppermute x3, starting transfers between devices, per_device(): v_down.append(lax.ppermute(v_down[-1], 'seq', down))  8.92 us
    ppermute x1, waiting for transfers between devices, per_device(): other = lax.ppermute(send, 'seq', [(s, s ^ 2) for s in range(seq_size)])  7.28 us
    pallas_call x1, Pallas kernels, per_device(): pl.pallas_call(functools.partial(near_kernel, factor, seq_size, order), o...  5 us
    pallas_call x1, Pallas kernels, per_device(): pl.pallas_call(functools.partial(far_kernel, factor, 3, 4), out_shape=sta...  4.63 us
    ppermute x3, waiting for transfers between devices, per_device(): v_down.append(lax.ppermute(v_down[-1], 'seq', down))  3.59 us
    ppermute x1, starting transfers between devices, per_device(): v_last = lax.ppermute(v_last, 'seq', down)  2.93 us
  transfers between devices with their start and end apart: 19, of which 6 were waited for; matrix products, arithmetic and copies ran while one was open for 4% of the time, Pallas kernels for 11%

profile of v6, /device:TPU:2, one launch (start us, length us, event | category | flops | bytes accessed | tf_op | source)
XLA Modules:
  0.0 86.3 jit_solution(6301313298394062191)
XLA Ops:
  0.0 1.9 %collective-permute-start.3 = (bf16[256,384]{1,0:T(8,128)(2,1)}, bf16[256,384]{1,0:T(8,128)(2,1)S(1)}, u32[]{:S(2)}, u32[]{:S(2)}) collective-permute-start(bf16[256,384]{1,0:T(8,128)(2,1)} %param.7), channel_id=1, source_target_pairs={{0,32},{8,40},{16,48},{24,56},{32,64},{40,72},{48,80},{56,88},{64,... | collective-permute-start | bytes 589832 | tf_op jit(solution)/shard_map/ppermute | solution.py:255
  1.9 3.9 %collective-permute-start.4 = (bf16[256,384]{1,0:T(8,128)(2,1)}, bf16[256,384]{1,0:T(8,128)(2,1)S(1)}, u32[]{:S(2)}, u32[]{:S(2)}) collective-permute-start(bf16[256,384]{1,0:T(8,128)(2,1)} %param.7), channel_id=1, source_target_pairs={{0,224},{8,232},{16,240},{24,248},{32,0},{40,8},{48,16},{56,24},{6... | collective-permute-start | bytes 589832 | tf_op jit(solution)/shard_map/ppermute | solution.py:256
  5.9 2.0 %collective-permute-start.6 = (bf16[256,384]{1,0:T(8,128)(2,1)}, bf16[256,384]{1,0:T(8,128)(2,1)S(1)}, u32[]{:S(2)}, u32[]{:S(2)}) collective-permute-start(bf16[256,384]{1,0:T(8,128)(2,1)} %param.8), channel_id=1, source_target_pairs={{0,224},{8,232},{16,240},{24,248},{32,0},{40,8},{48,16},{56,24},{6... | collective-permute-start | bytes 589832 | tf_op jit(solution)/shard_map/ppermute | solution.py:258
  7.9 0.7 convert.5
  8.5 0.9 %fusion.1.refs_0_ = bf16[272,384]{1,0:T(8,128)(2,1)S(1)} fusion(bf16[1,27]{1,0:T(2,128)(2,1)S(1)} %convert.5, bf16[256,384]{1,0:T(8,128)(2,1)} %param.6), kind=kLoop, calls=%fused_computation.3 | loop fusion | flops 626688 | bytes 405558 | tf_op jit(solution)/shard_map/concatenate | solution.py:263
  9.5 0.1 collective-permute-start
  9.6 0.6 collective-permute-start.1
  10.2 0.8 collective-permute-done.3.refs_5_
  11.0 3.6 %collective-permute-done.6.refs_8_ = bf16[256,384]{1,0:T(8,128)(2,1)S(1)} collective-permute-done((bf16[256,384]{1,0:T(8,128)(2,1)}, bf16[256,384]{1,0:T(8,128)(2,1)S(1)}, u32[]{:S(2)}, u32[]{:S(2)}) %collective-permute-start.6) | collective-permute-done | bytes 196640 | tf_op jit(solution)/shard_map/ppermute | solution.py:258
  14.6 3.6 %collective-permute-start.9 = (bf16[256,384]{1,0:T(8,128)(2,1)S(1)}, bf16[256,384]{1,0:T(8,128)(2,1)S(1)}, u32[]{:S(2)}, u32[]{:S(2)}) collective-permute-start(bf16[256,384]{1,0:T(8,128)(2,1)S(1)} %collective-permute-done.6.refs_8_), channel_id=1, source_target_pairs={{0,224},{8,232},{16,240},{24,248},{32,0},{40,8},{48,16},{56,24},{6... | collective-permute-start | bytes 589832 | tf_op jit(solution)/shard_map/ppermute | solution.py:258
  18.1 0.5 collective-permute-done.5.refs_7_
  18.6 0.4 collective-permute-start.2
  19.0 2.5 %collective-permute-start.13 = (bf16[256,384]{1,0:T(8,128)(2,1)S(1)}, bf16[256,384]{1,0:T(8,128)(2,1)S(1)}, u32[]{:S(2)}, u32[]{:S(2)}) collective-permute-start(bf16[256,384]{1,0:T(8,128)(2,1)S(1)} %collective-permute-done.4.refs_6_), channel_id=1, source_target_pairs={{0,224},{8,232},{16,240},{24,248},{32,0},{40,8},{48,16},{56,24},{6... | collective-permute-start | bytes 589832 | tf_op jit(solution)/shard_map/ppermute | solution.py:256
  21.5 1.1 %pad_maximum_fusion.refs_4_ = bf16[512,384]{1,0:T(8,128)(2,1)S(1)} fusion(bf16[256,384]{1,0:T(8,128)(2,1)} %param.8, bf16[256,384]{1,0:T(8,128)(2,1)} %param.7), kind=kLoop, calls=%fused_computation.2 | loop fusion | flops 786432 | bytes 786432 | tf_op jit(solution)/shard_map/concatenate | solution.py:285
  22.5 3.3 %collective-permute-start.10 = (bf16[256,384]{1,0:T(8,128)(2,1)S(1)}, bf16[256,384]{1,0:T(8,128)(2,1)S(1)}, u32[]{:S(2)}, u32[]{:S(2)}) collective-permute-start(bf16[256,384]{1,0:T(8,128)(2,1)S(1)} %collective-permute-done.9.refs_7_), channel_id=1, source_target_pairs={{0,224},{8,232},{16,240},{24,248},{32,0},{40,8},{48,16},{56,24},{6... | collective-permute-start | bytes 589832 | tf_op jit(solution)/shard_map/ppermute | solution.py:258
  25.9 0.7 pad_add_fusion.place_ref
  26.6 0.1 collective-permute-done.13.refs_3_
  26.7 3.7 %collective-permute-start.14 = (bf16[256,384]{1,0:T(8,128)(2,1)S(1)}, bf16[256,384]{1,0:T(8,128)(2,1)S(1)}, u32[]{:S(2)}, u32[]{:S(2)}) collective-permute-start(bf16[256,384]{1,0:T(8,128)(2,1)S(1)} %collective-permute-done.13.refs_3_), channel_id=1, source_target_pairs={{0,224},{8,232},{16,240},{24,248},{32,0},{40,8},{48,16},{56,24},{6... | collective-permute-start | bytes 589832 | tf_op jit(solution)/shard_map/ppermute | solution.py:256
  30.4 5.0 %attend_near.1 = (s32[4,8]{1,0:T(4,128)S(1)}, bf16[4,256,384]{2,1,0:T(8,128)(2,1)S(1)}, f32[12,128,256]{2,1,0:T(8,128)S(1)}, f32[12,1,256]{2,1,0:T(1,128)S(1)}, f32[12,1,256]{2,1,0:T(1,128)S(1)}) custom-call(s32[3]{0:T(128)S(1)} %pad_add_fusion.place_ref, bf16[272,384]{1,0:T(8,128)(2,1)S(1)} %fusion.1.refs_0_, ...), custom_call_target="tpu_custom_call" | custom-call | flops 905969664 | bytes 4194304 | tf_op jit(solution)/shard_map/attend_near/pallas_call | solution.py:286
  35.5 0.4 collective-permute-start.11
  35.8 2.9 %collective-permute-start.12 = (bf16[256,384]{1,0:T(8,128)(2,1)S(1)}, bf16[256,384]{1,0:T(8,128)(2,1)S(1)}, u32[]{:S(2)}, u32[]{:S(2)}) collective-permute-start(bf16[256,384]{1,0:T(8,128)(2,1)S(1)} %get-tuple-element.25), channel_id=1, source_target_pairs={{0,224},{8,232},{16,240},{24,248},{32,0},{40,8},{48,16},{56,24},{6... | collective-permute-start | bytes 589832 | tf_op jit(solution)/shard_map/ppermute | solution.py:310
  38.8 4.6 %attend_far.1 = (f32[12,128,256]{2,1,0:T(8,128)S(1)}, f32[12,1,256]{2,1,0:T(1,128)S(1)}, f32[12,1,256]{2,1,0:T(1,128)S(1)}) custom-call(s32[4,8]{1,0:T(4,128)S(1)} %get-tuple-element.21.need_ref, bf16[4,256,384]{2,1,0:T(8,128)(2,1)S(1)} %get-tuple-element.22.stacked_ref, bf16[256,384]{1,0:T(8,128)(2,1)S(1)} %collective-permute-done.8.k_ref.refs_0_, ...), custom_call_target="tpu_custom_call" | custom-call | flops 805306368 | bytes 4194304 | tf_op jit(solution)/shard_map/attend_far/pallas_call | solution.py:311
  43.4 0.0 copy-start
  43.4 2.6 %attend_last.1 = (f32[2,384,256]{2,1,0:T(8,128)S(1)}, f32[2,8,256]{2,1,0:T(8,128)S(1)}, bf16[2,416,256]{2,1,0:T(8,128)(2,1)S(1)}) custom-call(s32[4,8]{1,0:T(4,128)S(1)} %get-tuple-element.21.need_ref, bf16[4,256,384]{2,1,0:T(8,128)(2,1)S(1)} %get-tuple-element.22.stacked_ref, bf16[256,384]{1,0:T(8,128)(2,1)S(1)} %collective-permute-done.11.refs_0_, ...), custom_call_target="tpu_custom_call" | custom-call | flops 402653184 | bytes 4194304 | tf_op jit(solution)/shard_map/attend_last/pallas_call | solution.py:321
  46.1 0.1 collective-permute-start.17
  46.2 1.8 %collective-permute-done.17.other_ref = bf16[2,416,256]{2,1,0:T(8,128)(2,1)S(1)} collective-permute-done((bf16[2,416,256]{2,1,0:T(8,128)(2,1)S(1)}, bf16[2,416,256]{2,1,0:T(8,128)(2,1)S(1)}, u32[]{:S(2)}, u32[]{:S(2)}) %collective-permute-start.17) | collective-permute-done | bytes 426016 | tf_op jit(solution)/shard_map/ppermute | solution.py:336
  47.9 0.2 merge.1
  48.1 0.1 collective-permute-start.18
  48.2 7.3 %collective-permute-done.18.other_ref = bf16[1,416,256]{2,1,0:T(8,128)(2,1)S(1)} collective-permute-done((bf16[1,416,256]{2,1,0:T(8,128)(2,1)S(1)}, bf16[1,416,256]{2,1,0:T(8,128)(2,1)S(1)}, u32[]{:S(2)}, u32[]{:S(2)}) %collective-permute-start.18) | collective-permute-done | bytes 213024 | tf_op jit(solution)/shard_map/ppermute | solution.py:349
  55.5 1.3 %project.1 = bf16[8,256,384]{2,1,0:T(8,128)(2,1)S(1)} custom-call(f32[1,384,256]{2,1,0:T(8,128)S(1)} %get-tuple-element.34.mine_ref, f32[1,8,256]{2,1,0:T(8,128)S(1)} %get-tuple-element.35.mine_sum_ref, bf16[1,416,256]{2,1,0:T(8,128)(2,1)S(1)} %collective-permute-done.18.other_ref, bf16[384,3072]{1,0:T(8,128)(2,1)S(1)} %copy-done), custom_call_target="tpu_custom_call" | custom-call | tf_op jit(solution)/shard_map/project/pallas_call | solution.py:350
  56.8 28.6 %all_to_all.5 = bf16[8,256,384]{2,1,0:T(8,128)(2,1)S(1)} all-to-all(bf16[8,256,384]{2,1,0:T(8,128)(2,1)S(1)} %project.1), channel_id=1, replica_groups=mesh['seq'=32,'head'=8] {'head'}, dimensions={0} | all-to-all | bytes 3145728 | tf_op jit(solution)/shard_map/all_to_all | solution.py:359
  85.3 0.9 %reduce_sum.12 = bf16[256,384]{1,0:T(8,128)(2,1)} reduce(bf16[8,256,384]{2,1,0:T(8,128)(2,1)S(1)} %all_to_all.5, bf16[]{:T(256)} %constant.11.clone.1), dimensions={0}, to_apply=%region_0.1 | reduce | flops 688128 | bytes 1769474 | tf_op jit(solution)/shard_map/reduce_sum | solution.py:360
  (20 shorter events, 0.1 us)
Async XLA Ops:
  0.0 11.0 %collective-permute-start.3 = (bf16[256,384]{1,0:T(8,128)(2,1)}, bf16[256,384]{1,0:T(8,128)(2,1)S(1)}, u32[]{:S(2)}, u32[]{:S(2)}) collective-permute-start(bf16[256,384]{1,0:T(8,128)(2,1)} %param.7), channel_id=1, source_target_pairs={{0,32},{8,40},{16,48},{24,56},{32,64},{40,72},{48,80},{56,88},{64,... | collective-permute-start | bytes 589832 | tf_op jit(solution)/shard_map/ppermute | solution.py:255
  1.9 16.2 %collective-permute-start.4 = (bf16[256,384]{1,0:T(8,128)(2,1)}, bf16[256,384]{1,0:T(8,128)(2,1)S(1)}, u32[]{:S(2)}, u32[]{:S(2)}) collective-permute-start(bf16[256,384]{1,0:T(8,128)(2,1)} %param.7), channel_id=1, source_target_pairs={{0,224},{8,232},{16,240},{24,248},{32,0},{40,8},{48,16},{56,24},{6... | collective-permute-start | bytes 589832 | tf_op jit(solution)/shard_map/ppermute | solution.py:256
  5.9 8.7 %collective-permute-start.6 = (bf16[256,384]{1,0:T(8,128)(2,1)}, bf16[256,384]{1,0:T(8,128)(2,1)S(1)}, u32[]{:S(2)}, u32[]{:S(2)}) collective-permute-start(bf16[256,384]{1,0:T(8,128)(2,1)} %param.8), channel_id=1, source_target_pairs={{0,224},{8,232},{16,240},{24,248},{32,0},{40,8},{48,16},{56,24},{6... | collective-permute-start | bytes 589832 | tf_op jit(solution)/shard_map/ppermute | solution.py:258
  9.5 9.5 %collective-permute-start = (bf16[272,384]{1,0:T(8,128)(2,1)S(1)}, bf16[272,384]{1,0:T(8,128)(2,1)S(1)}, u32[]{:S(2)}, u32[]{:S(2)}) collective-permute-start(bf16[272,384]{1,0:T(8,128)(2,1)S(1)} %fusion.1.refs_0_), channel_id=1, source_target_pairs={{0,8},{8,0},{16,24},{24,16},{32,40},{40,32},{48,56},{56,48},{64,72... | collective-permute-start | bytes 626696 | tf_op jit(solution)/shard_map/ppermute | solution.py:265
  9.6 11.9 %collective-permute-start.1 = (bf16[272,384]{1,0:T(8,128)(2,1)S(1)}, bf16[272,384]{1,0:T(8,128)(2,1)S(1)}, u32[]{:S(2)}, u32[]{:S(2)}) collective-permute-start(bf16[272,384]{1,0:T(8,128)(2,1)S(1)} %fusion.1.refs_0_), channel_id=1, source_target_pairs={{0,16},{8,24},{16,0},{24,8},{32,48},{40,56},{48,32},{56,40},{64,80... | collective-permute-start | bytes 626696 | tf_op jit(solution)/shard_map/ppermute | solution.py:265
  11.0 7.6 %collective-permute-start.5 = (bf16[256,384]{1,0:T(8,128)(2,1)}, bf16[256,384]{1,0:T(8,128)(2,1)S(1)}, u32[]{:S(2)}, u32[]{:S(2)}) collective-permute-start(bf16[256,384]{1,0:T(8,128)(2,1)} %param.8), channel_id=1, source_target_pairs={{0,32},{8,40},{16,48},{24,56},{32,64},{40,72},{48,80},{56,88},{64,... | collective-permute-start | bytes 589832 | tf_op jit(solution)/shard_map/ppermute | solution.py:257
  14.6 8.0 %collective-permute-start.9 = (bf16[256,384]{1,0:T(8,128)(2,1)S(1)}, bf16[256,384]{1,0:T(8,128)(2,1)S(1)}, u32[]{:S(2)}, u32[]{:S(2)}) collective-permute-start(bf16[256,384]{1,0:T(8,128)(2,1)S(1)} %collective-permute-done.6.refs_8_), channel_id=1, source_target_pairs={{0,224},{8,232},{16,240},{24,248},{32,0},{40,8},{48,16},{56,24},{6... | collective-permute-start | bytes 589832 | tf_op jit(solution)/shard_map/ppermute | solution.py:258
  18.1 7.7 %collective-permute-start.7 = (bf16[256,384]{1,0:T(8,128)(2,1)S(1)}, bf16[256,384]{1,0:T(8,128)(2,1)S(1)}, u32[]{:S(2)}, u32[]{:S(2)}) collective-permute-start(bf16[256,384]{1,0:T(8,128)(2,1)S(1)} %collective-permute-done.3.refs_5_), channel_id=1, source_target_pairs={{0,32},{8,40},{16,48},{24,56},{32,64},{40,72},{48,80},{56,88},{64,... | collective-permute-start | bytes 589832 | tf_op jit(solution)/shard_map/ppermute | solution.py:255
  18.6 11.8 %collective-permute-start.2 = (bf16[272,384]{1,0:T(8,128)(2,1)S(1)}, bf16[272,384]{1,0:T(8,128)(2,1)S(1)}, u32[]{:S(2)}, u32[]{:S(2)}) collective-permute-start(bf16[272,384]{1,0:T(8,128)(2,1)S(1)} %fusion.1.refs_0_), channel_id=1, source_target_pairs={{0,24},{8,16},{16,8},{24,0},{32,56},{40,48},{48,40},{56,32},{64,88... | collective-permute-start | bytes 626696 | tf_op jit(solution)/shard_map/ppermute | solution.py:265
  19.0 7.7 %collective-permute-start.13 = (bf16[256,384]{1,0:T(8,128)(2,1)S(1)}, bf16[256,384]{1,0:T(8,128)(2,1)S(1)}, u32[]{:S(2)}, u32[]{:S(2)}) collective-permute-start(bf16[256,384]{1,0:T(8,128)(2,1)S(1)} %collective-permute-done.4.refs_6_), channel_id=1, source_target_pairs={{0,224},{8,232},{16,240},{24,248},{32,0},{40,8},{48,16},{56,24},{6... | collective-permute-start | bytes 589832 | tf_op jit(solution)/shard_map/ppermute | solution.py:256
  21.5 8.9 %collective-permute-start.15 = (bf16[256,384]{1,0:T(8,128)(2,1)S(1)}, bf16[256,384]{1,0:T(8,128)(2,1)S(1)}, u32[]{:S(2)}, u32[]{:S(2)}) collective-permute-start(bf16[256,384]{1,0:T(8,128)(2,1)S(1)} %collective-permute-done.5.refs_7_), channel_id=1, source_target_pairs={{0,32},{8,40},{16,48},{24,56},{32,64},{40,72},{48,80},{56,88},{64,... | collective-permute-start | bytes 589832 | tf_op jit(solution)/shard_map/ppermute | solution.py:257
  22.5 12.8 %collective-permute-start.10 = (bf16[256,384]{1,0:T(8,128)(2,1)S(1)}, bf16[256,384]{1,0:T(8,128)(2,1)S(1)}, u32[]{:S(2)}, u32[]{:S(2)}) collective-permute-start(bf16[256,384]{1,0:T(8,128)(2,1)S(1)} %collective-permute-done.9.refs_7_), channel_id=1, source_target_pairs={{0,224},{8,232},{16,240},{24,248},{32,0},{40,8},{48,16},{56,24},{6... | collective-permute-start | bytes 589832 | tf_op jit(solution)/shard_map/ppermute | solution.py:258
  25.9 9.5 %collective-permute-start.8 = (bf16[256,384]{1,0:T(8,128)(2,1)S(1)}, bf16[256,384]{1,0:T(8,128)(2,1)S(1)}, u32[]{:S(2)}, u32[]{:S(2)}) collective-permute-start(bf16[256,384]{1,0:T(8,128)(2,1)S(1)} %collective-permute-done.7.refs_2_), channel_id=1, source_target_pairs={{0,32},{8,40},{16,48},{24,56},{32,64},{40,72},{48,80},{56,88},{64,... | collective-permute-start | bytes 589832 | tf_op jit(solution)/shard_map/ppermute | solution.py:255
  26.7 12.1 %collective-permute-start.14 = (bf16[256,384]{1,0:T(8,128)(2,1)S(1)}, bf16[256,384]{1,0:T(8,128)(2,1)S(1)}, u32[]{:S(2)}, u32[]{:S(2)}) collective-permute-start(bf16[256,384]{1,0:T(8,128)(2,1)S(1)} %collective-permute-done.13.refs_3_), channel_id=1, source_target_pairs={{0,224},{8,232},{16,240},{24,248},{32,0},{40,8},{48,16},{56,24},{6... | collective-permute-start | bytes 589832 | tf_op jit(solution)/shard_map/ppermute | solution.py:256
  30.4 8.4 %collective-permute-start.16 = (bf16[256,384]{1,0:T(8,128)(2,1)S(1)}, bf16[256,384]{1,0:T(8,128)(2,1)S(1)}, u32[]{:S(2)}, u32[]{:S(2)}) collective-permute-start(bf16[256,384]{1,0:T(8,128)(2,1)S(1)} %collective-permute-done.15.refs_6_), channel_id=1, source_target_pairs={{0,32},{8,40},{16,48},{24,56},{32,64},{40,72},{48,80},{56,88},{64,... | collective-permute-start | bytes 589832 | tf_op jit(solution)/shard_map/ppermute | solution.py:257
  35.5 8.0 %collective-permute-start.11 = (bf16[256,384]{1,0:T(8,128)(2,1)S(1)}, bf16[256,384]{1,0:T(8,128)(2,1)S(1)}, u32[]{:S(2)}, u32[]{:S(2)}) collective-permute-start(bf16[256,384]{1,0:T(8,128)(2,1)S(1)} %get-tuple-element.24), channel_id=1, source_target_pairs={{0,32},{8,40},{16,48},{24,56},{32,64},{40,72},{48,80},{56,88},{64,... | collective-permute-start | bytes 589832 | tf_op jit(solution)/shard_map/ppermute | solution.py:309
  35.8 7.6 %collective-permute-start.12 = (bf16[256,384]{1,0:T(8,128)(2,1)S(1)}, bf16[256,384]{1,0:T(8,128)(2,1)S(1)}, u32[]{:S(2)}, u32[]{:S(2)}) collective-permute-start(bf16[256,384]{1,0:T(8,128)(2,1)S(1)} %get-tuple-element.25), channel_id=1, source_target_pairs={{0,224},{8,232},{16,240},{24,248},{32,0},{40,8},{48,16},{56,24},{6... | collective-permute-start | bytes 589832 | tf_op jit(solution)/shard_map/ppermute | solution.py:310
  43.4 12.1 %copy-start = (bf16[384,3072]{1,0:T(8,128)(2,1)S(1)}, bf16[384,3072]{1,0:T(8,128)(2,1)}, u32[]{:S(2)}) copy-start(bf16[384,3072]{1,0:T(8,128)(2,1)} %weight_ref.1) | copy-start | bytes 7077892
  46.1 1.9 %collective-permute-start.17 = (bf16[2,416,256]{2,1,0:T(8,128)(2,1)S(1)}, bf16[2,416,256]{2,1,0:T(8,128)(2,1)S(1)}, u32[]{:S(2)}, u32[]{:S(2)}) collective-permute-start(bf16[2,416,256]{2,1,0:T(8,128)(2,1)S(1)} %get-tuple-element.33), channel_id=1, source_target_pairs={{0,8},{8,0},{16,24},{24,16},{32,40},{40,32},{48,56},{56,48},{64,72... | collective-permute-start | bytes 1277960 | tf_op jit(solution)/shard_map/ppermute | solution.py:336
  48.1 7.4 %collective-permute-start.18 = (bf16[1,416,256]{2,1,0:T(8,128)(2,1)S(1)}, bf16[1,416,256]{2,1,0:T(8,128)(2,1)S(1)}, u32[]{:S(2)}, u32[]{:S(2)}) collective-permute-start(bf16[1,416,256]{2,1,0:T(8,128)(2,1)S(1)} %get-tuple-element.36), channel_id=1, source_target_pairs={{0,16},{8,24},{16,0},{24,8},{32,48},{40,56},{48,32},{56,40},{64,80... | collective-permute-start | bytes 638984 | tf_op jit(solution)/shard_map/ppermute | solution.py:349

commit v7 on v6

--- a/solution.py
+++ b/solution.py
@@ -114,21 +114,17 @@
                 picks[i] = jnp.where((wanted > 0) & (seen == i), j, picks[i])
             seen = seen + wanted
 
-        if count >= 3:
-
-            @pl.when(seen >= 3)
-            def _():
-                take(t, picks[:3])
-
-        if count >= 2:
-
-            @pl.when(seen == 2)
-            def _():
-                take(t, picks[:2])
+        @pl.when(seen >= 3)
+        def _():
+            take(t, picks[:3])
+
+        @pl.when((seen == 2) | (seen == 5))
+        def _():
+            take(t, [jnp.where(seen == 5, late, early) for late, early in zip(picks[-2:], picks[:2])])
 
         @pl.when((seen == 1) | (seen == 4))
         def _():
-            take(t, [jnp.where(seen == 4, picks[-1], picks[0])])
+            take(t, [jnp.where(seen == 4, picks[min(3, count - 1)], picks[0])])
 
         return carry
 
@@ -166,22 +162,13 @@
 
 def far_kernel(factor, first, count, need_ref, stacked_ref, *refs):
     shards = list(zip(refs[:count], refs[count:2 * count]))
-    held, state = refs[2 * count:2 * count + 3], refs[2 * count + 3:2 * count + 6]
-    k_ref, vt_ref = refs[2 * count + 6:]
+    held = refs[2 * count:2 * count + 3]
+    keep_ref, keep_sum_ref, send_ref, *state, k_ref, vt_ref = refs[2 * count + 3:]
+    heads = vt_ref.shape[1]
     for source, target in zip(held, state):
         target[...] = source[...]
     load_shards(need_ref, first, shards, k_ref, vt_ref)
     visit_shards(factor, need_ref, first, count, stacked_ref, k_ref, vt_ref, state)
-
-
-def last_kernel(factor, first, need_ref, stacked_ref, *refs):
-    shards = [refs[:2]]
-    keep_ref, keep_sum_ref, send_ref, *state, k_ref, vt_ref = refs[5:]
-    heads = vt_ref.shape[1]
-    for source, target in zip(refs[2:5], state):
-        target[...] = source[...]
-    load_shards(need_ref, first, shards, k_ref, vt_ref)
-    visit_shards(factor, need_ref, first, 1, stacked_ref, k_ref, vt_ref, state)
     acc_ref, peak_ref, total_ref = state
     for t in range(GROUP):
         outs, sums = [], []
@@ -200,11 +187,6 @@
                 keep_sum_ref[t // 2, h:h + 1, :] = sums[h]
 
 
-def relay_kernel(k_ref, v_ref, after_ref, k_out_ref, v_out_ref):
-    k_out_ref[...] = k_ref[...]
-    v_out_ref[...] = v_ref[...]
-
-
 def merge_kernel(mine_ref, mine_sum_ref, other_ref, keep_ref, keep_sum_ref, send_ref):
     heads = mine_ref.shape[1] // HD
     outs, sums = merged(mine_ref, mine_sum_ref, 1, other_ref, 1, heads)
@@ -251,10 +233,11 @@
 
     k_up, k_down, v_up, v_down = [key_states], [key_states], [value_states], [value_states]
     half = planes // 2
-    for step in range(half - 1):
+    for step in range(half):
         k_up.append(lax.ppermute(k_up[-1], "seq", up))
-        k_down.append(lax.ppermute(k_down[-1], "seq", down))
-        v_up.append(lax.ppermute(v_up[-1], "seq", up))
+        if step < half - 1:
+            k_down.append(lax.ppermute(k_down[-1], "seq", down))
+            v_up.append(lax.ppermute(v_up[-1], "seq", up))
         v_down.append(lax.ppermute(v_down[-1], "seq", down))
 
     listed = jnp.pad(
@@ -264,7 +247,7 @@
     tiles = [packed] + [
         lax.ppermute(packed, "seq", [(s, s ^ k) for s in range(seq_size)]) for k in range(1, GROUP)
     ]
-    order = (0, -1, 1, -3, 3, -2, 2, 4)
+    order = (0, -1, 1, -3, 3, 4, -2, 2)
     place = jnp.concatenate([me.astype(jnp.int32)[None], text_slots])
 
     rows = GROUP * heads
@@ -297,41 +280,21 @@
         cost_estimate=attend_cost(27),
         name="attend_near",
     )(place, *tiles, own, k_up[1], k_down[1], v_up[1], v_down[1])
-    shard = jax.ShapeDtypeStruct(key_states.shape, key_states.dtype)
-    k_last, v_last = pl.pallas_call(
-        relay_kernel,
-        out_shape=(shard, shard),
-        in_specs=vmem_specs(3),
-        out_specs=tuple(vmem_specs(2)),
-        compiler_params=PARAMS,
-        name="relay",
-    )(k_up[-1], v_down[-1], held[2])
-    k_last = lax.ppermute(k_last, "seq", up)
-    v_last = lax.ppermute(v_last, "seq", down)
-    held = pl.pallas_call(
-        functools.partial(far_kernel, factor, 3, 4),
-        out_shape=state,
-        in_specs=smem + vmem_specs(12),
-        out_specs=tuple(vmem_specs(3)),
-        scratch_shapes=scratch(4),
-        compiler_params=PARAMS,
-        cost_estimate=attend_cost(24),
-        name="attend_far",
-    )(need, stacked, k_up[3], k_down[3], k_up[2], k_down[2], v_up[3], v_down[3], v_up[2], v_down[2], *held)
+    far = [(k_up[3], v_up[3]), (k_down[3], v_down[3]), (k_up[4], v_down[4]), (k_up[2], v_up[2]), (k_down[2], v_down[2])]
     keep, keep_sum, send = pl.pallas_call(
-        functools.partial(last_kernel, factor, 7),
+        functools.partial(far_kernel, factor, 3, len(far)),
         out_shape=(
             jax.ShapeDtypeStruct((2, width, TILE), jnp.float32),
             jax.ShapeDtypeStruct((2, 8, TILE), jnp.float32),
             jax.ShapeDtypeStruct((2, width + 2 * PART_ROWS, TILE), jnp.bfloat16),
         ),
-        in_specs=smem + vmem_specs(6),
+        in_specs=smem + vmem_specs(1 + 2 * len(far) + 3),
         out_specs=tuple(vmem_specs(3)),
-        scratch_shapes=[pltpu.VMEM(s.shape, s.dtype) for s in state] + scratch(1),
+        scratch_shapes=[pltpu.VMEM(s.shape, s.dtype) for s in state] + scratch(len(far)),
         compiler_params=PARAMS,
-        cost_estimate=attend_cost(12),
-        name="attend_last",
-    )(need, stacked, k_last, v_last, *held)
+        cost_estimate=attend_cost(27),
+        name="attend_far",
+    )(need, stacked, *[k for k, _ in far], *[v for _, v in far], *held)
 
     other = lax.ppermute(send, "seq", [(s, s ^ 1) for s in range(seq_size)])
     keep, keep_sum, send = pl.pallas_call(

time: 87.6 us -> 86.7 us (0.990)
  waiting for transfers between devices: 13.9 us -> 17.7 us
  starting transfers between devices: 25.6 us -> 23 us
  Pallas kernels: 13.7 us -> 11.8 us
    ppermute x3, starting transfers between devices: 10.1 us -> 3.13 us  [per_device(): k_down.append(lax.ppermute(k_down[-1], 'seq', down))]
    ppermute x3 -> x4, starting transfers between devices: 8.92 us -> 14 us  [per_device(): v_down.append(lax.ppermute(v_down[-1], 'seq', down))]
    ppermute x3 -> x4, waiting for transfers between devices: 0.76 us -> 4.98 us  [per_device(): k_up.append(lax.ppermute(k_up[-1], 'seq', up))]
    ppermute x2 -> x0, starting transfers between devices: 3.31 us -> none  [the longest x1 2.93 us: per_device(): v_last = lax.ppermute(v_last, 'seq', down)]
    ppermute x3, starting transfers between devices: 0.01 us -> 3.12 us  [per_device(): v_up.append(lax.ppermute(v_up[-1], 'seq', up))]
    ppermute x3 -> x4, waiting for transfers between devices: 3.59 us -> 0.52 us  [per_device(): v_down.append(lax.ppermute(v_down[-1], 'seq', down))]
    pallas_call x3 -> x1, Pallas kernels: 7.29 us -> 4.25 us  [per_device(): pl.pallas_call(functools.partial(far_kernel, factor, 3, len(far)), out_sh...]
    ppermute x3, waiting for transfers between devices: 0.46 us -> 2.67 us  [per_device(): v_up.append(lax.ppermute(v_up[-1], 'seq', up))]
  transfers between devices with their start and end apart: 19 -> 19, of which waited for: 6 -> 8; matrix products, arithmetic and copies ran while one was open for 4% -> 4% of each run, Pallas kernels for 11% -> 7%
where the time goes in v7:
time: 86.7 us; the launch traced here: 85.2 us
  blocking collectives  28.3 us (33%)
  starting transfers between devices  23 us (27%)
  waiting for transfers between devices  17.7 us (20%)
  Pallas kernels  11.8 us (14%)
  other arithmetic  4.32 us (5%)
    all_to_all x1, blocking collectives, per_device(): shares = lax.all_to_all(shares, 'head', 0, 0, tiled=False)  28.3 us
    ppermute x4, starting transfers between devices, per_device(): v_down.append(lax.ppermute(v_down[-1], 'seq', down))  14 us
    ppermute x1, waiting for transfers between devices, per_device(): other = lax.ppermute(send, 'seq', [(s, s ^ 2) for s in range(seq_size)])  7.28 us
    pallas_call x1, Pallas kernels, per_device(): pl.pallas_call(functools.partial(near_kernel, factor, seq_size, order), o...  6.09 us
    ppermute x4, waiting for transfers between devices, per_device(): k_up.append(lax.ppermute(k_up[-1], 'seq', up))  4.98 us
    pallas_call x1, Pallas kernels, per_device(): pl.pallas_call(functools.partial(far_kernel, factor, 3, len(far)), out_sh...  4.25 us
    ppermute x3, starting transfers between devices, per_device(): k_down.append(lax.ppermute(k_down[-1], 'seq', down))  3.13 us
    ppermute x3, starting transfers between devices, per_device(): v_up.append(lax.ppermute(v_up[-1], 'seq', up))  3.12 us
  transfers between devices with their start and end apart: 19, of which 8 were waited for; matrix products, arithmetic and copies ran while one was open for 4% of the time, Pallas kernels for 7%

profile of v7, /device:TPU:2, one launch (start us, length us, event | category | flops | bytes accessed | tf_op | source)
XLA Modules:
  0.0 85.2 jit_solution(637194266325356248)
XLA Ops:
  0.0 1.9 %collective-permute-start.3 = (bf16[256,384]{1,0:T(8,128)(2,1)}, bf16[256,384]{1,0:T(8,128)(2,1)S(1)}, u32[]{:S(2)}, u32[]{:S(2)}) collective-permute-start(bf16[256,384]{1,0:T(8,128)(2,1)} %param.7), channel_id=1, source_target_pairs={{0,32},{8,40},{16,48},{24,56},{32,64},{40,72},{48,80},{56,88},{64,... | collective-permute-start | bytes 589832 | tf_op jit(solution)/shard_map/ppermute | solution.py:237
  1.9 3.9 %collective-permute-start.6 = (bf16[256,384]{1,0:T(8,128)(2,1)}, bf16[256,384]{1,0:T(8,128)(2,1)S(1)}, u32[]{:S(2)}, u32[]{:S(2)}) collective-permute-start(bf16[256,384]{1,0:T(8,128)(2,1)} %param.8), channel_id=1, source_target_pairs={{0,224},{8,232},{16,240},{24,248},{32,0},{40,8},{48,16},{56,24},{6... | collective-permute-start | bytes 589832 | tf_op jit(solution)/shard_map/ppermute | solution.py:241
  5.9 2.0 %collective-permute-start.4 = (bf16[256,384]{1,0:T(8,128)(2,1)}, bf16[256,384]{1,0:T(8,128)(2,1)S(1)}, u32[]{:S(2)}, u32[]{:S(2)}) collective-permute-start(bf16[256,384]{1,0:T(8,128)(2,1)} %param.7), channel_id=1, source_target_pairs={{0,224},{8,232},{16,240},{24,248},{32,0},{40,8},{48,16},{56,24},{6... | collective-permute-start | bytes 589832 | tf_op jit(solution)/shard_map/ppermute | solution.py:239
  7.9 0.7 convert.5
  8.5 0.9 %fusion.1.refs_0_ = bf16[272,384]{1,0:T(8,128)(2,1)S(1)} fusion(bf16[1,27]{1,0:T(2,128)(2,1)S(1)} %convert.5, bf16[256,384]{1,0:T(8,128)(2,1)} %param.6), kind=kLoop, calls=%fused_computation.3 | loop fusion | flops 626688 | bytes 405558 | tf_op jit(solution)/shard_map/concatenate | solution.py:246
  9.5 0.1 collective-permute-start
  9.7 1.3 %collective-permute-done.3.refs_5_ = bf16[256,384]{1,0:T(8,128)(2,1)S(1)} collective-permute-done((bf16[256,384]{1,0:T(8,128)(2,1)}, bf16[256,384]{1,0:T(8,128)(2,1)S(1)}, u32[]{:S(2)}, u32[]{:S(2)}) %collective-permute-start.3) | collective-permute-done | bytes 196640 | tf_op jit(solution)/shard_map/ppermute | solution.py:237
  11.0 0.5 collective-permute-done.6.refs_8_
  11.5 3.6 %collective-permute-start.14 = (bf16[256,384]{1,0:T(8,128)(2,1)S(1)}, bf16[256,384]{1,0:T(8,128)(2,1)S(1)}, u32[]{:S(2)}, u32[]{:S(2)}) collective-permute-start(bf16[256,384]{1,0:T(8,128)(2,1)S(1)} %collective-permute-done.6.refs_8_), channel_id=1, source_target_pairs={{0,224},{8,232},{16,240},{24,248},{32,0},{40,8},{48,16},{56,24},{6... | collective-permute-start | bytes 589832 | tf_op jit(solution)/shard_map/ppermute | solution.py:241
  15.1 0.5 collective-permute-done.4.refs_6_
  15.6 0.5 collective-permute-start.1
  16.1 2.7 %collective-permute-done.5.refs_7_ = bf16[256,384]{1,0:T(8,128)(2,1)S(1)} collective-permute-done((bf16[256,384]{1,0:T(8,128)(2,1)}, bf16[256,384]{1,0:T(8,128)(2,1)S(1)}, u32[]{:S(2)}, u32[]{:S(2)}) %collective-permute-start.5) | collective-permute-done | bytes 196640 | tf_op jit(solution)/shard_map/ppermute | solution.py:240
  18.8 0.9 %collective-permute-start.9 = (bf16[256,384]{1,0:T(8,128)(2,1)S(1)}, bf16[256,384]{1,0:T(8,128)(2,1)S(1)}, u32[]{:S(2)}, u32[]{:S(2)}) collective-permute-start(bf16[256,384]{1,0:T(8,128)(2,1)S(1)} %collective-permute-done.4.refs_6_), channel_id=1, source_target_pairs={{0,224},{8,232},{16,240},{24,248},{32,0},{40,8},{48,16},{56,24},{6... | collective-permute-start | bytes 589832 | tf_op jit(solution)/shard_map/ppermute | solution.py:239
  19.7 1.1 %collective-permute-start.12 = (bf16[256,384]{1,0:T(8,128)(2,1)S(1)}, bf16[256,384]{1,0:T(8,128)(2,1)S(1)}, u32[]{:S(2)}, u32[]{:S(2)}) collective-permute-start(bf16[256,384]{1,0:T(8,128)(2,1)S(1)} %collective-permute-done.5.refs_7_), channel_id=1, source_target_pairs={{0,32},{8,40},{16,48},{24,56},{32,64},{40,72},{48,80},{56,88},{64,... | collective-permute-start | bytes 589832 | tf_op jit(solution)/shard_map/ppermute | solution.py:240
  20.8 2.2 %collective-permute-done.7.refs_3_ = bf16[256,384]{1,0:T(8,128)(2,1)S(1)} collective-permute-done((bf16[256,384]{1,0:T(8,128)(2,1)S(1)}, bf16[256,384]{1,0:T(8,128)(2,1)S(1)}, u32[]{:S(2)}, u32[]{:S(2)}) %collective-permute-start.7) | collective-permute-done | bytes 196640 | tf_op jit(solution)/shard_map/ppermute | solution.py:237
  23.0 3.2 %collective-permute-start.15 = (bf16[256,384]{1,0:T(8,128)(2,1)S(1)}, bf16[256,384]{1,0:T(8,128)(2,1)S(1)}, u32[]{:S(2)}, u32[]{:S(2)}) collective-permute-start(bf16[256,384]{1,0:T(8,128)(2,1)S(1)} %collective-permute-done.14.refs_9_), channel_id=1, source_target_pairs={{0,224},{8,232},{16,240},{24,248},{32,0},{40,8},{48,16},{56,24},{6... | collective-permute-start | bytes 589832 | tf_op jit(solution)/shard_map/ppermute | solution.py:241
  26.3 1.1 %pad_maximum_fusion.refs_4_ = bf16[512,384]{1,0:T(8,128)(2,1)S(1)} fusion(bf16[256,384]{1,0:T(8,128)(2,1)} %param.8, bf16[256,384]{1,0:T(8,128)(2,1)} %param.7), kind=kLoop, calls=%fused_computation.2 | loop fusion | flops 786432 | bytes 786432 | tf_op jit(solution)/shard_map/concatenate | solution.py:268
  27.3 0.2 collective-permute-start.10
  27.5 1.9 %collective-permute-start.13 = (bf16[256,384]{1,0:T(8,128)(2,1)S(1)}, bf16[256,384]{1,0:T(8,128)(2,1)S(1)}, u32[]{:S(2)}, u32[]{:S(2)}) collective-permute-start(bf16[256,384]{1,0:T(8,128)(2,1)S(1)} %collective-permute-done.12.refs_8_), channel_id=1, source_target_pairs={{0,32},{8,40},{16,48},{24,56},{32,64},{40,72},{48,80},{56,88},{64,... | collective-permute-start | bytes 589832 | tf_op jit(solution)/shard_map/ppermute | solution.py:240
  29.5 1.5 %collective-permute-done.8.refs_0_ = bf16[256,384]{1,0:T(8,128)(2,1)S(1)} collective-permute-done((bf16[256,384]{1,0:T(8,128)(2,1)S(1)}, bf16[256,384]{1,0:T(8,128)(2,1)S(1)}, u32[]{:S(2)}, u32[]{:S(2)}) %collective-permute-start.8) | collective-permute-done | bytes 196640 | tf_op jit(solution)/shard_map/ppermute | solution.py:237
  31.0 3.2 %collective-permute-start.16 = (bf16[256,384]{1,0:T(8,128)(2,1)S(1)}, bf16[256,384]{1,0:T(8,128)(2,1)S(1)}, u32[]{:S(2)}, u32[]{:S(2)}) collective-permute-start(bf16[256,384]{1,0:T(8,128)(2,1)S(1)} %collective-permute-done.15.refs_6_), channel_id=1, source_target_pairs={{0,224},{8,232},{16,240},{24,248},{32,0},{40,8},{48,16},{56,24},{6... | collective-permute-start | bytes 589832 | tf_op jit(solution)/shard_map/ppermute | solution.py:241
  34.2 0.7 pad_add_fusion.place_ref
  34.9 6.1 %attend_near.1 = (s32[4,8]{1,0:T(4,128)S(1)}, bf16[4,256,384]{2,1,0:T(8,128)(2,1)S(1)}, f32[12,128,256]{2,1,0:T(8,128)S(1)}, f32[12,1,256]{2,1,0:T(1,128)S(1)}, f32[12,1,256]{2,1,0:T(1,128)S(1)}) custom-call(s32[3]{0:T(128)S(1)} %pad_add_fusion.place_ref, bf16[272,384]{1,0:T(8,128)(2,1)S(1)} %fusion.1.refs_0_, ...), custom_call_target="tpu_custom_call" | custom-call | flops 905969664 | bytes 4194304 | tf_op jit(solution)/shard_map/attend_near/pallas_call | solution.py:269
  41.1 4.2 %attend_far.1 = (f32[2,384,256]{2,1,0:T(8,128)S(1)}, f32[2,8,256]{2,1,0:T(8,128)S(1)}, bf16[2,416,256]{2,1,0:T(8,128)(2,1)S(1)}) custom-call(s32[4,8]{1,0:T(4,128)S(1)} %get-tuple-element.16.need_ref, bf16[4,256,384]{2,1,0:T(8,128)(2,1)S(1)} %get-tuple-element.17.stacked_ref, bf16[256,384]{1,0:T(8,128)(2,1)S(1)} %collective-permute-done.8.refs_0_, ...), custom_call_target="tpu_custom_call" | custom-call | flops 905969664 | bytes 4194304 | tf_op jit(solution)/shard_map/attend_far/pallas_call | solution.py:284
  45.3 0.1 collective-permute-start.17
  45.4 1.8 %collective-permute-done.17.other_ref = bf16[2,416,256]{2,1,0:T(8,128)(2,1)S(1)} collective-permute-done((bf16[2,416,256]{2,1,0:T(8,128)(2,1)S(1)}, bf16[2,416,256]{2,1,0:T(8,128)(2,1)S(1)}, u32[]{:S(2)}, u32[]{:S(2)}) %collective-permute-start.17) | collective-permute-done | bytes 426016 | tf_op jit(solution)/shard_map/ppermute | solution.py:299
  47.2 0.2 merge.1
  47.4 0.1 collective-permute-start.18
  47.5 7.3 %collective-permute-done.18.other_ref = bf16[1,416,256]{2,1,0:T(8,128)(2,1)S(1)} collective-permute-done((bf16[1,416,256]{2,1,0:T(8,128)(2,1)S(1)}, bf16[1,416,256]{2,1,0:T(8,128)(2,1)S(1)}, u32[]{:S(2)}, u32[]{:S(2)}) %collective-permute-start.18) | collective-permute-done | bytes 213024 | tf_op jit(solution)/shard_map/ppermute | solution.py:312
  54.8 1.2 %project.1 = bf16[8,256,384]{2,1,0:T(8,128)(2,1)S(1)} custom-call(f32[1,384,256]{2,1,0:T(8,128)S(1)} %get-tuple-element.24.mine_ref, f32[1,8,256]{2,1,0:T(8,128)S(1)} %get-tuple-element.25.mine_sum_ref, bf16[1,416,256]{2,1,0:T(8,128)(2,1)S(1)} %collective-permute-done.18.other_ref, bf16[384,3072]{1,0:T(8,128)(2,1)S(1)} %copy-done), custom_call_target="tpu_custom_call" | custom-call | tf_op jit(solution)/shard_map/project/pallas_call | solution.py:313
  56.0 28.3 %all_to_all.5 = bf16[8,256,384]{2,1,0:T(8,128)(2,1)S(1)} all-to-all(bf16[8,256,384]{2,1,0:T(8,128)(2,1)S(1)} %project.1), channel_id=1, replica_groups=mesh['seq'=32,'head'=8] {'head'}, dimensions={0} | all-to-all | bytes 3145728 | tf_op jit(solution)/shard_map/all_to_all | solution.py:322
  84.3 0.9 %reduce_sum.12 = bf16[256,384]{1,0:T(8,128)(2,1)} reduce(bf16[8,256,384]{2,1,0:T(8,128)(2,1)S(1)} %all_to_all.5, bf16[]{:T(256)} %constant.11.clone.1), dimensions={0}, to_apply=%region_0.1 | reduce | flops 688128 | bytes 1769474 | tf_op jit(solution)/shard_map/reduce_sum | solution.py:323
  (18 shorter events, 0.1 us)
Async XLA Ops:
  0.0 11.0 %collective-permute-start.3 = (bf16[256,384]{1,0:T(8,128)(2,1)}, bf16[256,384]{1,0:T(8,128)(2,1)S(1)}, u32[]{:S(2)}, u32[]{:S(2)}) collective-permute-start(bf16[256,384]{1,0:T(8,128)(2,1)} %param.7), channel_id=1, source_target_pairs={{0,32},{8,40},{16,48},{24,56},{32,64},{40,72},{48,80},{56,88},{64,... | collective-permute-start | bytes 589832 | tf_op jit(solution)/shard_map/ppermute | solution.py:237
  1.9 9.6 %collective-permute-start.6 = (bf16[256,384]{1,0:T(8,128)(2,1)}, bf16[256,384]{1,0:T(8,128)(2,1)S(1)}, u32[]{:S(2)}, u32[]{:S(2)}) collective-permute-start(bf16[256,384]{1,0:T(8,128)(2,1)} %param.8), channel_id=1, source_target_pairs={{0,224},{8,232},{16,240},{24,248},{32,0},{40,8},{48,16},{56,24},{6... | collective-permute-start | bytes 589832 | tf_op jit(solution)/shard_map/ppermute | solution.py:241
  5.9 9.7 %collective-permute-start.4 = (bf16[256,384]{1,0:T(8,128)(2,1)}, bf16[256,384]{1,0:T(8,128)(2,1)S(1)}, u32[]{:S(2)}, u32[]{:S(2)}) collective-permute-start(bf16[256,384]{1,0:T(8,128)(2,1)} %param.7), channel_id=1, source_target_pairs={{0,224},{8,232},{16,240},{24,248},{32,0},{40,8},{48,16},{56,24},{6... | collective-permute-start | bytes 589832 | tf_op jit(solution)/shard_map/ppermute | solution.py:239
  9.5 10.2 %collective-permute-start = (bf16[272,384]{1,0:T(8,128)(2,1)S(1)}, bf16[272,384]{1,0:T(8,128)(2,1)S(1)}, u32[]{:S(2)}, u32[]{:S(2)}) collective-permute-start(bf16[272,384]{1,0:T(8,128)(2,1)S(1)} %fusion.1.refs_0_), channel_id=1, source_target_pairs={{0,8},{8,0},{16,24},{24,16},{32,40},{40,32},{48,56},{56,48},{64,72... | collective-permute-start | bytes 626696 | tf_op jit(solution)/shard_map/ppermute | solution.py:248
  9.6 9.2 %collective-permute-start.5 = (bf16[256,384]{1,0:T(8,128)(2,1)}, bf16[256,384]{1,0:T(8,128)(2,1)S(1)}, u32[]{:S(2)}, u32[]{:S(2)}) collective-permute-start(bf16[256,384]{1,0:T(8,128)(2,1)} %param.8), channel_id=1, source_target_pairs={{0,32},{8,40},{16,48},{24,56},{32,64},{40,72},{48,80},{56,88},{64,... | collective-permute-start | bytes 589832 | tf_op jit(solution)/shard_map/ppermute | solution.py:240
  11.0 12.0 %collective-permute-start.7 = (bf16[256,384]{1,0:T(8,128)(2,1)S(1)}, bf16[256,384]{1,0:T(8,128)(2,1)S(1)}, u32[]{:S(2)}, u32[]{:S(2)}) collective-permute-start(bf16[256,384]{1,0:T(8,128)(2,1)S(1)} %collective-permute-done.3.refs_5_), channel_id=1, source_target_pairs={{0,32},{8,40},{16,48},{24,56},{32,64},{40,72},{48,80},{56,88},{64,... | collective-permute-start | bytes 589832 | tf_op jit(solution)/shard_map/ppermute | solution.py:237
  11.5 11.5 %collective-permute-start.14 = (bf16[256,384]{1,0:T(8,128)(2,1)S(1)}, bf16[256,384]{1,0:T(8,128)(2,1)S(1)}, u32[]{:S(2)}, u32[]{:S(2)}) collective-permute-start(bf16[256,384]{1,0:T(8,128)(2,1)S(1)} %collective-permute-done.6.refs_8_), channel_id=1, source_target_pairs={{0,224},{8,232},{16,240},{24,248},{32,0},{40,8},{48,16},{56,24},{6... | collective-permute-start | bytes 589832 | tf_op jit(solution)/shard_map/ppermute | solution.py:241
  15.6 10.7 %collective-permute-start.1 = (bf16[272,384]{1,0:T(8,128)(2,1)S(1)}, bf16[272,384]{1,0:T(8,128)(2,1)S(1)}, u32[]{:S(2)}, u32[]{:S(2)}) collective-permute-start(bf16[272,384]{1,0:T(8,128)(2,1)S(1)} %fusion.1.refs_0_), channel_id=1, source_target_pairs={{0,16},{8,24},{16,0},{24,8},{32,48},{40,56},{48,32},{56,40},{64,80... | collective-permute-start | bytes 626696 | tf_op jit(solution)/shard_map/ppermute | solution.py:248
  18.8 8.5 %collective-permute-start.9 = (bf16[256,384]{1,0:T(8,128)(2,1)S(1)}, bf16[256,384]{1,0:T(8,128)(2,1)S(1)}, u32[]{:S(2)}, u32[]{:S(2)}) collective-permute-start(bf16[256,384]{1,0:T(8,128)(2,1)S(1)} %collective-permute-done.4.refs_6_), channel_id=1, source_target_pairs={{0,224},{8,232},{16,240},{24,248},{32,0},{40,8},{48,16},{56,24},{6... | collective-permute-start | bytes 589832 | tf_op jit(solution)/shard_map/ppermute | solution.py:239
  19.7 7.8 %collective-permute-start.12 = (bf16[256,384]{1,0:T(8,128)(2,1)S(1)}, bf16[256,384]{1,0:T(8,128)(2,1)S(1)}, u32[]{:S(2)}, u32[]{:S(2)}) collective-permute-start(bf16[256,384]{1,0:T(8,128)(2,1)S(1)} %collective-permute-done.5.refs_7_), channel_id=1, source_target_pairs={{0,32},{8,40},{16,48},{24,56},{32,64},{40,72},{48,80},{56,88},{64,... | collective-permute-start | bytes 589832 | tf_op jit(solution)/shard_map/ppermute | solution.py:240
  23.0 8.0 %collective-permute-start.8 = (bf16[256,384]{1,0:T(8,128)(2,1)S(1)}, bf16[256,384]{1,0:T(8,128)(2,1)S(1)}, u32[]{:S(2)}, u32[]{:S(2)}) collective-permute-start(bf16[256,384]{1,0:T(8,128)(2,1)S(1)} %collective-permute-done.7.refs_3_), channel_id=1, source_target_pairs={{0,32},{8,40},{16,48},{24,56},{32,64},{40,72},{48,80},{56,88},{64,... | collective-permute-start | bytes 589832 | tf_op jit(solution)/shard_map/ppermute | solution.py:237
  23.0 8.0 %collective-permute-start.15 = (bf16[256,384]{1,0:T(8,128)(2,1)S(1)}, bf16[256,384]{1,0:T(8,128)(2,1)S(1)}, u32[]{:S(2)}, u32[]{:S(2)}) collective-permute-start(bf16[256,384]{1,0:T(8,128)(2,1)S(1)} %collective-permute-done.14.refs_9_), channel_id=1, source_target_pairs={{0,224},{8,232},{16,240},{24,248},{32,0},{40,8},{48,16},{56,24},{6... | collective-permute-start | bytes 589832 | tf_op jit(solution)/shard_map/ppermute | solution.py:241
  26.3 8.7 %collective-permute-start.2 = (bf16[272,384]{1,0:T(8,128)(2,1)S(1)}, bf16[272,384]{1,0:T(8,128)(2,1)S(1)}, u32[]{:S(2)}, u32[]{:S(2)}) collective-permute-start(bf16[272,384]{1,0:T(8,128)(2,1)S(1)} %fusion.1.refs_0_), channel_id=1, source_target_pairs={{0,24},{8,16},{16,8},{24,0},{32,56},{40,48},{48,40},{56,32},{64,88... | collective-permute-start | bytes 626696 | tf_op jit(solution)/shard_map/ppermute | solution.py:248
  27.3 13.7 %collective-permute-start.10 = (bf16[256,384]{1,0:T(8,128)(2,1)S(1)}, bf16[256,384]{1,0:T(8,128)(2,1)S(1)}, u32[]{:S(2)}, u32[]{:S(2)}) collective-permute-start(bf16[256,384]{1,0:T(8,128)(2,1)S(1)} %collective-permute-done.9.refs_4_), channel_id=1, source_target_pairs={{0,224},{8,232},{16,240},{24,248},{32,0},{40,8},{48,16},{56,24},{6... | collective-permute-start | bytes 589832 | tf_op jit(solution)/shard_map/ppermute | solution.py:239
  27.5 13.5 %collective-permute-start.13 = (bf16[256,384]{1,0:T(8,128)(2,1)S(1)}, bf16[256,384]{1,0:T(8,128)(2,1)S(1)}, u32[]{:S(2)}, u32[]{:S(2)}) collective-permute-start(bf16[256,384]{1,0:T(8,128)(2,1)S(1)} %collective-permute-done.12.refs_8_), channel_id=1, source_target_pairs={{0,32},{8,40},{16,48},{24,56},{32,64},{40,72},{48,80},{56,88},{64,... | collective-permute-start | bytes 589832 | tf_op jit(solution)/shard_map/ppermute | solution.py:240
  31.0 10.1 %collective-permute-start.11 = (bf16[256,384]{1,0:T(8,128)(2,1)S(1)}, bf16[256,384]{1,0:T(8,128)(2,1)S(1)}, u32[]{:S(2)}, u32[]{:S(2)}) collective-permute-start(bf16[256,384]{1,0:T(8,128)(2,1)S(1)} %collective-permute-done.8.refs_0_), channel_id=1, source_target_pairs={{0,32},{8,40},{16,48},{24,56},{32,64},{40,72},{48,80},{56,88},{64,... | collective-permute-start | bytes 589832 | tf_op jit(solution)/shard_map/ppermute | solution.py:237
  31.0 10.1 %collective-permute-start.16 = (bf16[256,384]{1,0:T(8,128)(2,1)S(1)}, bf16[256,384]{1,0:T(8,128)(2,1)S(1)}, u32[]{:S(2)}, u32[]{:S(2)}) collective-permute-start(bf16[256,384]{1,0:T(8,128)(2,1)S(1)} %collective-permute-done.15.refs_6_), channel_id=1, source_target_pairs={{0,224},{8,232},{16,240},{24,248},{32,0},{40,8},{48,16},{56,24},{6... | collective-permute-start | bytes 589832 | tf_op jit(solution)/shard_map/ppermute | solution.py:241
  41.1 13.7 %copy-start = (bf16[384,3072]{1,0:T(8,128)(2,1)S(1)}, bf16[384,3072]{1,0:T(8,128)(2,1)}, u32[]{:S(2)}) copy-start(bf16[384,3072]{1,0:T(8,128)(2,1)} %weight_ref.1) | copy-start | bytes 7077892
  45.3 1.9 %collective-permute-start.17 = (bf16[2,416,256]{2,1,0:T(8,128)(2,1)S(1)}, bf16[2,416,256]{2,1,0:T(8,128)(2,1)S(1)}, u32[]{:S(2)}, u32[]{:S(2)}) collective-permute-start(bf16[2,416,256]{2,1,0:T(8,128)(2,1)S(1)} %get-tuple-element.23), channel_id=1, source_target_pairs={{0,8},{8,0},{16,24},{24,16},{32,40},{40,32},{48,56},{56,48},{64,72... | collective-permute-start | bytes 1277960 | tf_op jit(solution)/shard_map/ppermute | solution.py:299
  47.4 7.4 %collective-permute-start.18 = (bf16[1,416,256]{2,1,0:T(8,128)(2,1)S(1)}, bf16[1,416,256]{2,1,0:T(8,128)(2,1)S(1)}, u32[]{:S(2)}, u32[]{:S(2)}) collective-permute-start(bf16[1,416,256]{2,1,0:T(8,128)(2,1)S(1)} %get-tuple-element.26), channel_id=1, source_target_pairs={{0,16},{8,24},{16,0},{24,8},{32,48},{40,56},{48,32},{56,40},{64,80... | collective-permute-start | bytes 638984 | tf_op jit(solution)/shard_map/ppermute | solution.py:312

commit v8 on v7

--- a/solution.py
+++ b/solution.py
@@ -197,17 +197,29 @@
         keep_sum_ref[0, h:h + 1, :] = sums[h]
 
 
-def project_kernel(mine_ref, mine_sum_ref, other_ref, weight_ref, out_ref, held_ref):
+def finish_kernel(mine_ref, mine_sum_ref, other_ref, out_ref):
     heads = mine_ref.shape[1] // HD
     outs, _ = merged(mine_ref, mine_sum_ref, 0, other_ref, 0, heads)
     for h in range(heads):
-        held_ref[:, h * HD:(h + 1) * HD] = outs[h].T.astype(jnp.bfloat16)
+        out_ref[:, h * HD:(h + 1) * HD] = outs[h].T.astype(jnp.bfloat16)
+
+
+def pick_kernel(side_ref, weight_ref, out_ref):
+    width = weight_ref.shape[0]
+    for j in range(out_ref.shape[1] // width):
+        begin = pl.multiple_of((2 * j + 1 - side_ref[0]) * width, HD)
+        out_ref[:, j * width:(j + 1) * width] = weight_ref[:, pl.ds(begin, width)]
+
+
+def project_kernel(side_ref, mine_ref, other_ref, weight_ref, other_weight_ref, out_ref):
     shares, _, width = out_ref.shape
-    attended = held_ref[...]
     for j in range(shares):
-        out_ref[j] = jnp.dot(
-            attended, weight_ref[:, j * width:(j + 1) * width], preferred_element_type=jnp.float32
-        ).astype(jnp.bfloat16)
+        begin = pl.multiple_of((2 * j + side_ref[0]) * width, HD)
+        mixed = jnp.dot(mine_ref[...], weight_ref[:, pl.ds(begin, width)], preferred_element_type=jnp.float32)
+        mixed = mixed + jnp.dot(
+            other_ref[...], other_weight_ref[:, j * width:(j + 1) * width], preferred_element_type=jnp.float32
+        )
+        out_ref[j] = mixed.astype(jnp.bfloat16)
 
 
 def vmem_specs(count):
@@ -239,6 +251,17 @@
             k_down.append(lax.ppermute(k_down[-1], "seq", down))
             v_up.append(lax.ppermute(v_up[-1], "seq", up))
         v_down.append(lax.ppermute(v_down[-1], "seq", down))
+
+    side = lax.axis_index("head") % 2
+    picked = pl.pallas_call(
+        pick_kernel,
+        out_shape=jax.ShapeDtypeStruct((width, head_size // 2 * width), out_weight.dtype),
+        in_specs=[pl.BlockSpec(memory_space=pltpu.SMEM)] + vmem_specs(1),
+        out_specs=pl.BlockSpec(memory_space=pltpu.VMEM),
+        compiler_params=PARAMS,
+        name="pick",
+    )(side[None], out_weight)
+    other_weight = lax.ppermute(picked, "head", [(h, h ^ 1) for h in range(head_size)])
 
     listed = jnp.pad(
         block_list, ((0, PART_ROWS - 1), (0, width - block_list.shape[1])), constant_values=-1
@@ -310,16 +333,25 @@
         name="merge",
     )(keep, keep_sum, other)
     other = lax.ppermute(send, "seq", [(s, s ^ 2) for s in range(seq_size)])
+    attended = pl.pallas_call(
+        finish_kernel,
+        out_shape=jax.ShapeDtypeStruct((TILE, width), jnp.bfloat16),
+        in_specs=vmem_specs(3),
+        out_specs=pl.BlockSpec(memory_space=pltpu.VMEM),
+        compiler_params=PARAMS,
+        name="finish",
+    )(keep, keep_sum, other)
+    swap_side = [(h, h ^ 1) for h in range(head_size)]
     shares = pl.pallas_call(
         project_kernel,
-        out_shape=jax.ShapeDtypeStruct((head_size, TILE, width), jnp.bfloat16),
-        in_specs=vmem_specs(4),
+        out_shape=jax.ShapeDtypeStruct((head_size // 2, TILE, width), jnp.bfloat16),
+        in_specs=smem + vmem_specs(4),
         out_specs=pl.BlockSpec(memory_space=pltpu.VMEM),
-        scratch_shapes=[pltpu.VMEM((TILE, width), jnp.bfloat16)],
         compiler_params=PARAMS,
         name="project",
-    )(keep, keep_sum, other, out_weight)
-    shares = lax.all_to_all(shares, "head", 0, 0, tiled=False)
+    )(side[None], attended, lax.ppermute(attended, "head", swap_side), out_weight, other_weight)
+    sides = [list(range(k, head_size, 2)) for k in range(2)]
+    shares = lax.all_to_all(shares, "head", 0, 0, axis_index_groups=sides, tiled=True)
     return jnp.sum(shares.astype(jnp.float32), axis=0).astype(jnp.bfloat16)
 
 

time: 86.7 us -> 88.2 us (1.017)
  blocking collectives: 28.3 us -> 15.1 us
  local copies, waits for them, and re-layouts: 0.01 us -> 9.71 us
  starting transfers between devices: 23 us -> 28.2 us
  other arithmetic: 4.32 us -> 2.54 us
  Pallas kernels: 11.8 us -> 13.1 us
  waiting for transfers between devices: 17.7 us -> 18.7 us
    all_to_all x1, blocking collectives: 28.3 us -> 15.1 us  [per_device(): lax.all_to_all(shares, 'head', 0, 0, axis_index_groups=sides, tiled=True)]
    unnamed x2 -> x30, local copies, waits for them, and re-layouts: 0.01 us -> 9.71 us
    ppermute x0 -> x2, waiting for transfers between devices: none -> 4.99 us  [the longest x1 4.98 us: per_device(): lax.ppermute(attended, 'head', swap_side)]
    ppermute x0 -> x2, starting transfers between devices: none -> 4.84 us  [the longest x1 2.72 us: per_device(): lax.ppermute(attended, 'head', swap_side)]
    ppermute x3, waiting for transfers between devices: 2.67 us -> 0.01 us  [per_device(): v_up.append(lax.ppermute(v_up[-1], 'seq', up))]
    ppermute x4, waiting for transfers between devices: 4.98 us -> 2.76 us  [per_device(): k_up.append(lax.ppermute(k_up[-1], 'seq', up))]
    ppermute x4, starting transfers between devices: 14 us -> 11.8 us  [per_device(): v_down.append(lax.ppermute(v_down[-1], 'seq', down))]
    ppermute x3, starting transfers between devices: 3.13 us -> 5.08 us  [per_device(): k_down.append(lax.ppermute(k_down[-1], 'seq', down))]
  transfers between devices with their start and end apart: 19 -> 21, of which waited for: 8 -> 6; matrix products, arithmetic and copies ran while one was open for 4% -> 2% of each run, Pallas kernels for 7% -> 14%
where the time goes in v8:
time: 88.2 us; the launch traced here: 87.6 us
  starting transfers between devices  28.2 us (32%)
  waiting for transfers between devices  18.7 us (21%)
  blocking collectives  15.1 us (17%)
  Pallas kernels  13.1 us (15%)
  local copies, waits for them, and re-layouts  9.71 us (11%)
  other arithmetic  2.54 us (3%)
    all_to_all x1, blocking collectives, per_device(): lax.all_to_all(shares, 'head', 0, 0, axis_index_groups=sides, tiled=True)  15.1 us
    ppermute x4, starting transfers between devices, per_device(): v_down.append(lax.ppermute(v_down[-1], 'seq', down))  11.8 us
    unnamed x30, local copies, waits for them, and re-layouts  9.71 us
    ppermute x1, waiting for transfers between devices, per_device(): other = lax.ppermute(send, 'seq', [(s, s ^ 2) for s in range(seq_size)])  7.28 us
    pallas_call x1, Pallas kernels, per_device(): pl.pallas_call(functools.partial(near_kernel, factor, seq_size, order), o...  6.58 us
    ppermute x3, starting transfers between devices, per_device(): k_down.append(lax.ppermute(k_down[-1], 'seq', down))  5.08 us
    ppermute x1, waiting for transfers between devices, per_device(): lax.ppermute(attended, 'head', swap_side)  4.98 us
    pallas_call x1, Pallas kernels, per_device(): pl.pallas_call(functools.partial(far_kernel, factor, 3, len(far)), out_sh...  4.95 us
  transfers between devices with their start and end apart: 21, of which 6 were waited for; matrix products, arithmetic and copies ran while one was open for 2% of the time, Pallas kernels for 14%

profile of v8, /device:TPU:2, one launch (start us, length us, event | category | flops | bytes accessed | tf_op | source)
XLA Modules:
  0.0 87.6 jit_solution(13708335111754516792)
XLA Ops:
  0.0 1.9 %collective-permute-start.3 = (bf16[256,384]{1,0:T(8,128)(2,1)}, bf16[256,384]{1,0:T(8,128)(2,1)S(1)}, u32[]{:S(2)}, u32[]{:S(2)}) collective-permute-start(bf16[256,384]{1,0:T(8,128)(2,1)} %param.7), channel_id=1, source_target_pairs={{0,32},{8,40},{16,48},{24,56},{32,64},{40,72},{48,80},{56,88},{64,... | collective-permute-start | bytes 589832 | tf_op jit(solution)/shard_map/ppermute | solution.py:249
  1.9 3.9 %collective-permute-start.4 = (bf16[256,384]{1,0:T(8,128)(2,1)}, bf16[256,384]{1,0:T(8,128)(2,1)}, u32[]{:S(2)}, u32[]{:S(2)}) collective-permute-start(bf16[256,384]{1,0:T(8,128)(2,1)} %param.7), channel_id=1, source_target_pairs={{0,224},{8,232},{16,240},{24,248},{32,0},{40,8},{48,16},{56,24},{6... | collective-permute-start | bytes 589832 | tf_op jit(solution)/shard_map/ppermute | solution.py:251
  5.9 2.0 %collective-permute-start.6 = (bf16[256,384]{1,0:T(8,128)(2,1)}, bf16[256,384]{1,0:T(8,128)(2,1)S(1)}, u32[]{:S(2)}, u32[]{:S(2)}) collective-permute-start(bf16[256,384]{1,0:T(8,128)(2,1)} %param.8), channel_id=1, source_target_pairs={{0,224},{8,232},{16,240},{24,248},{32,0},{40,8},{48,16},{56,24},{6... | collective-permute-start | bytes 589832 | tf_op jit(solution)/shard_map/ppermute | solution.py:253
  8.5 0.9 %fusion.1.refs_0_ = bf16[272,384]{1,0:T(8,128)(2,1)S(1)} fusion(bf16[1,27]{1,0:T(2,128)(2,1)S(1)} %convert.5, bf16[256,384]{1,0:T(8,128)(2,1)} %param.6), kind=kLoop, calls=%fused_computation.3 | loop fusion | flops 626688 | bytes 405558 | tf_op jit(solution)/shard_map/concatenate | solution.py:269
  9.6 1.4 %collective-permute-done.3.refs_5_ = bf16[256,384]{1,0:T(8,128)(2,1)S(1)} collective-permute-done((bf16[256,384]{1,0:T(8,128)(2,1)}, bf16[256,384]{1,0:T(8,128)(2,1)S(1)}, u32[]{:S(2)}, u32[]{:S(2)}) %collective-permute-start.3) | collective-permute-done | bytes 196640 | tf_op jit(solution)/shard_map/ppermute | solution.py:249
  12.0 0.7 copy-done.8
  12.6 1.9 %collective-permute-done.6.refs_8_ = bf16[256,384]{1,0:T(8,128)(2,1)S(1)} collective-permute-done((bf16[256,384]{1,0:T(8,128)(2,1)}, bf16[256,384]{1,0:T(8,128)(2,1)S(1)}, u32[]{:S(2)}, u32[]{:S(2)}) %collective-permute-start.6) | collective-permute-done | bytes 196640 | tf_op jit(solution)/shard_map/ppermute | solution.py:253
  14.6 3.6 %collective-permute-start.14 = (bf16[256,384]{1,0:T(8,128)(2,1)S(1)}, bf16[256,384]{1,0:T(8,128)(2,1)S(1)}, u32[]{:S(2)}, u32[]{:S(2)}) collective-permute-start(bf16[256,384]{1,0:T(8,128)(2,1)S(1)} %collective-permute-done.6.refs_8_), channel_id=1, source_target_pairs={{0,224},{8,232},{16,240},{24,248},{32,0},{40,8},{48,16},{56,24},{6... | collective-permute-start | bytes 589832 | tf_op jit(solution)/shard_map/ppermute | solution.py:253
  18.1 0.7 copy-done.10
  20.0 0.7 copy-done.4
  20.7 1.5 %collective-permute-start.12 = (bf16[256,384]{1,0:T(8,128)(2,1)}, bf16[256,384]{1,0:T(8,128)(2,1)}, u32[]{:S(2)}, u32[]{:S(2)}) collective-permute-start(bf16[256,384]{1,0:T(8,128)(2,1)} %collective-permute-done.5.refs_7_), channel_id=1, source_target_pairs={{0,32},{8,40},{16,48},{24,56},{32,64},{40,72},{48,80},{56,88},{64,... | collective-permute-start | bytes 589832 | tf_op jit(solution)/shard_map/ppermute | solution.py:252
  22.3 3.2 %collective-permute-start.15 = (bf16[256,384]{1,0:T(8,128)(2,1)S(1)}, bf16[256,384]{1,0:T(8,128)(2,1)}, u32[]{:S(2)}, u32[]{:S(2)}) collective-permute-start(bf16[256,384]{1,0:T(8,128)(2,1)S(1)} %collective-permute-done.14.refs_9_), channel_id=1, source_target_pairs={{0,224},{8,232},{16,240},{24,248},{32,0},{40,8},{48,16},{56,24},{6... | collective-permute-start | bytes 589832 | tf_op jit(solution)/shard_map/ppermute | solution.py:253
  25.5 1.7 %copy-done = bf16[384,3072]{1,0:T(8,128)(2,1)S(1)} copy-done((bf16[384,3072]{1,0:T(8,128)(2,1)S(1)}, bf16[384,3072]{1,0:T(8,128)(2,1)}, u32[]{:S(2)}) %copy-start) | copy-done | bytes 2359320
  27.3 0.7 copy-done.6
  28.0 2.1 %collective-permute-start.20 = (bf16[384,1536]{1,0:T(8,128)(2,1)S(1)}, bf16[384,1536]{1,0:T(8,128)(2,1)S(1)}, u32[]{:S(2)}, u32[]{:S(2)}) collective-permute-start(bf16[384,1536]{1,0:T(8,128)(2,1)S(1)} %pick.1), channel_id=1, source_target_pairs={{0,1},{1,0},{2,3},{3,2},{4,5},{5,4},{6,7},{7,6},{8,9},{9,8},{10,11... | collective-permute-start | bytes 3538952 | tf_op jit(solution)/shard_map/ppermute | solution.py:264
  30.8 1.5 %collective-permute-start.13 = (bf16[256,384]{1,0:T(8,128)(2,1)}, bf16[256,384]{1,0:T(8,128)(2,1)S(1)}, u32[]{:S(2)}, u32[]{:S(2)}) collective-permute-start(bf16[256,384]{1,0:T(8,128)(2,1)} %collective-permute-done.12.refs_8_), channel_id=1, source_target_pairs={{0,32},{8,40},{16,48},{24,56},{32,64},{40,72},{48,80},{56,88},{64,... | collective-permute-start | bytes 589832 | tf_op jit(solution)/shard_map/ppermute | solution.py:252
  32.2 1.4 %collective-permute-done.8.refs_0_ = bf16[256,384]{1,0:T(8,128)(2,1)} collective-permute-done((bf16[256,384]{1,0:T(8,128)(2,1)S(1)}, bf16[256,384]{1,0:T(8,128)(2,1)}, u32[]{:S(2)}, u32[]{:S(2)}) %collective-permute-start.8) | collective-permute-done | bytes 196640 | tf_op jit(solution)/shard_map/ppermute | solution.py:249
  33.9 3.0 %collective-permute-start.16 = (bf16[256,384]{1,0:T(8,128)(2,1)}, bf16[256,384]{1,0:T(8,128)(2,1)S(1)}, u32[]{:S(2)}, u32[]{:S(2)}) collective-permute-start(bf16[256,384]{1,0:T(8,128)(2,1)} %collective-permute-done.15.refs_6_), channel_id=1, source_target_pairs={{0,224},{8,232},{16,240},{24,248},{32,0},{40,8},{48,16},{56,24},{6... | collective-permute-start | bytes 589832 | tf_op jit(solution)/shard_map/ppermute | solution.py:253
  37.0 0.9 %copy-done.3 = bf16[272,384]{1,0:T(8,128)(2,1)S(1)} copy-done((bf16[272,384]{1,0:T(8,128)(2,1)S(1)}, bf16[272,384]{1,0:T(8,128)(2,1)}, u32[]{:S(2)}) %copy-start.3) | copy-done | bytes 208920
  37.9 0.9 %copy-done.5 = bf16[272,384]{1,0:T(8,128)(2,1)S(1)} copy-done((bf16[272,384]{1,0:T(8,128)(2,1)S(1)}, bf16[272,384]{1,0:T(8,128)(2,1)}, u32[]{:S(2)}) %copy-start.5) | copy-done | bytes 208920
  38.8 0.9 %copy-done.7 = bf16[272,384]{1,0:T(8,128)(2,1)S(1)} copy-done((bf16[272,384]{1,0:T(8,128)(2,1)S(1)}, bf16[272,384]{1,0:T(8,128)(2,1)}, u32[]{:S(2)}) %copy-start.7) | copy-done | bytes 208920
  39.8 0.9 %copy-done.9 = bf16[256,384]{1,0:T(8,128)(2,1)S(1)} copy-done((bf16[256,384]{1,0:T(8,128)(2,1)S(1)}, bf16[256,384]{1,0:T(8,128)(2,1)}, u32[]{:S(2)}) %copy-start.9) | copy-done | bytes 196632
  40.7 0.9 %copy-done.11 = bf16[256,384]{1,0:T(8,128)(2,1)S(1)} copy-done((bf16[256,384]{1,0:T(8,128)(2,1)S(1)}, bf16[256,384]{1,0:T(8,128)(2,1)}, u32[]{:S(2)}) %copy-start.11) | copy-done | bytes 196632
  41.6 6.6 %attend_near.1 = (s32[4,8]{1,0:T(4,128)S(1)}, bf16[4,256,384]{2,1,0:T(8,128)(2,1)S(1)}, f32[12,128,256]{2,1,0:T(8,128)S(1)}, f32[12,1,256]{2,1,0:T(1,128)S(1)}, f32[12,1,256]{2,1,0:T(1,128)S(1)}) custom-call(s32[3]{0:T(128)S(1)} %pad_add_fusion.place_ref, bf16[272,384]{1,0:T(8,128)(2,1)S(1)} %fusion.1.refs_0_, bf16[272,384]{1,0:T(8,128)(2,1)S(1)} %copy-done.3, ...), custom_call_target="tpu_custom_call" | custom-call | flops 905969664 | bytes 4194304 | tf_op jit(solution)/shard_map/attend_near/pallas_call | solution.py:292
  48.2 5.0 %attend_far.1 = (f32[2,384,256]{2,1,0:T(8,128)S(1)}, f32[2,8,256]{2,1,0:T(8,128)S(1)}, bf16[2,416,256]{2,1,0:T(8,128)(2,1)S(1)}) custom-call(s32[4,8]{1,0:T(4,128)S(1)} %get-tuple-element.16.need_ref, bf16[4,256,384]{2,1,0:T(8,128)(2,1)S(1)} %get-tuple-element.17.stacked_ref, bf16[256,384]{1,0:T(8,128)(2,1)} %collective-permute-done.8.refs_0_, ...), custom_call_target="tpu_custom_call" | custom-call | flops 905969664 | bytes 4194304 | tf_op jit(solution)/shard_map/attend_far/pallas_call | solution.py:307
  53.3 1.8 %collective-permute-done.17.other_ref = bf16[2,416,256]{2,1,0:T(8,128)(2,1)S(1)} collective-permute-done((bf16[2,416,256]{2,1,0:T(8,128)(2,1)S(1)}, bf16[2,416,256]{2,1,0:T(8,128)(2,1)S(1)}, u32[]{:S(2)}, u32[]{:S(2)}) %collective-permute-start.17) | collective-permute-done | bytes 426016 | tf_op jit(solution)/shard_map/ppermute | solution.py:322
  55.3 7.3 %collective-permute-done.18.other_ref = bf16[1,416,256]{2,1,0:T(8,128)(2,1)S(1)} collective-permute-done((bf16[1,416,256]{2,1,0:T(8,128)(2,1)S(1)}, bf16[1,416,256]{2,1,0:T(8,128)(2,1)S(1)}, u32[]{:S(2)}, u32[]{:S(2)}) %collective-permute-start.18) | collective-permute-done | bytes 213024 | tf_op jit(solution)/shard_map/ppermute | solution.py:335
  62.8 2.7 %collective-permute-start.19 = (bf16[256,384]{1,0:T(8,128)(2,1)S(1)}, bf16[256,384]{1,0:T(8,128)(2,1)S(1)}, u32[]{:S(2)}, u32[]{:S(2)}) collective-permute-start(bf16[256,384]{1,0:T(8,128)(2,1)S(1)} %finish.1.mine_ref), channel_id=1, source_target_pairs={{0,1},{1,0},{2,3},{3,2},{4,5},{5,4},{6,7},{7,6},{8,9},{9,8},{10,11... | collective-permute-start | bytes 589832 | tf_op jit(solution)/shard_map/ppermute | solution.py:352
  65.5 5.0 %collective-permute-done.19.other_ref = bf16[256,384]{1,0:T(8,128)(2,1)S(1)} collective-permute-done((bf16[256,384]{1,0:T(8,128)(2,1)S(1)}, bf16[256,384]{1,0:T(8,128)(2,1)S(1)}, u32[]{:S(2)}, u32[]{:S(2)}) %collective-permute-start.19) | collective-permute-done | bytes 196640 | tf_op jit(solution)/shard_map/ppermute | solution.py:352
  70.5 1.1 %project.1 = bf16[4,256,384]{2,1,0:T(8,128)(2,1)S(1)} custom-call(s32[1]{0:T(128)} %bitcast.side_ref, bf16[256,384]{1,0:T(8,128)(2,1)S(1)} %finish.1.mine_ref, bf16[256,384]{1,0:T(8,128)(2,1)S(1)} %collective-permute-done.19.other_ref, bf16[384,3072]{1,0:T(8,128)(2,1)S(1)} %copy-done.1, bf16[384,1536]{1,0:T(8,128)(2,1)S(1)} %collective-permute-done.20.other_weight_ref), custom_call_target="tpu_custom_call" | custom-call | tf_op jit(solution)/shard_map/project/pallas_call | solution.py:345
  71.7 15.1 %all_to_all.5 = bf16[4,256,384]{2,1,0:T(8,128)(2,1)S(1)} all-to-all(bf16[4,256,384]{2,1,0:T(8,128)(2,1)S(1)} %project.1), channel_id=1, replica_groups={{0,2,4,6},{1,3,5,7},{8,10,12,14},{9,11,13,15},{16,18,20,22},{17,19,21,2..., dimensions={0} | all-to-all | bytes 1572864 | tf_op jit(solution)/shard_map/all_to_all | solution.py:354
  86.7 0.8 reduce_sum.12
  (52 shorter events, 4.7 us)
Async XLA Ops:
  0.0 11.0 %collective-permute-start.3 = (bf16[256,384]{1,0:T(8,128)(2,1)}, bf16[256,384]{1,0:T(8,128)(2,1)S(1)}, u32[]{:S(2)}, u32[]{:S(2)}) collective-permute-start(bf16[256,384]{1,0:T(8,128)(2,1)} %param.7), channel_id=1, source_target_pairs={{0,32},{8,40},{16,48},{24,56},{32,64},{40,72},{48,80},{56,88},{64,... | collective-permute-start | bytes 589832 | tf_op jit(solution)/shard_map/ppermute | solution.py:249
  1.9 9.6 %collective-permute-start.4 = (bf16[256,384]{1,0:T(8,128)(2,1)}, bf16[256,384]{1,0:T(8,128)(2,1)}, u32[]{:S(2)}, u32[]{:S(2)}) collective-permute-start(bf16[256,384]{1,0:T(8,128)(2,1)} %param.7), channel_id=1, source_target_pairs={{0,224},{8,232},{16,240},{24,248},{32,0},{40,8},{48,16},{56,24},{6... | collective-permute-start | bytes 589832 | tf_op jit(solution)/shard_map/ppermute | solution.py:251
  5.9 8.7 %collective-permute-start.6 = (bf16[256,384]{1,0:T(8,128)(2,1)}, bf16[256,384]{1,0:T(8,128)(2,1)S(1)}, u32[]{:S(2)}, u32[]{:S(2)}) collective-permute-start(bf16[256,384]{1,0:T(8,128)(2,1)} %param.8), channel_id=1, source_target_pairs={{0,224},{8,232},{16,240},{24,248},{32,0},{40,8},{48,16},{56,24},{6... | collective-permute-start | bytes 589832 | tf_op jit(solution)/shard_map/ppermute | solution.py:253
  7.9 10.9 %collective-permute-start.5 = (bf16[256,384]{1,0:T(8,128)(2,1)}, bf16[256,384]{1,0:T(8,128)(2,1)}, u32[]{:S(2)}, u32[]{:S(2)}) collective-permute-start(bf16[256,384]{1,0:T(8,128)(2,1)} %param.8), channel_id=1, source_target_pairs={{0,32},{8,40},{16,48},{24,56},{32,64},{40,72},{48,80},{56,88},{64,... | collective-permute-start | bytes 589832 | tf_op jit(solution)/shard_map/ppermute | solution.py:252
  9.5 9.3 %collective-permute-start = (bf16[272,384]{1,0:T(8,128)(2,1)S(1)}, bf16[272,384]{1,0:T(8,128)(2,1)S(1)}, u32[]{:S(2)}, u32[]{:S(2)}) collective-permute-start(bf16[272,384]{1,0:T(8,128)(2,1)S(1)} %fusion.1.refs_0_), channel_id=1, source_target_pairs={{0,8},{8,0},{16,24},{24,16},{32,40},{40,32},{48,56},{56,48},{64,72... | collective-permute-start | bytes 626696 | tf_op jit(solution)/shard_map/ppermute | solution.py:271
  11.0 9.1 %collective-permute-start.1 = (bf16[272,384]{1,0:T(8,128)(2,1)S(1)}, bf16[272,384]{1,0:T(8,128)(2,1)S(1)}, u32[]{:S(2)}, u32[]{:S(2)}) collective-permute-start(bf16[272,384]{1,0:T(8,128)(2,1)S(1)} %fusion.1.refs_0_), channel_id=1, source_target_pairs={{0,16},{8,24},{16,0},{24,8},{32,48},{40,56},{48,32},{56,40},{64,80... | collective-permute-start | bytes 626696 | tf_op jit(solution)/shard_map/ppermute | solution.py:271
  11.5 10.7 %collective-permute-start.7 = (bf16[256,384]{1,0:T(8,128)(2,1)S(1)}, bf16[256,384]{1,0:T(8,128)(2,1)S(1)}, u32[]{:S(2)}, u32[]{:S(2)}) collective-permute-start(bf16[256,384]{1,0:T(8,128)(2,1)S(1)} %collective-permute-done.3.refs_5_), channel_id=1, source_target_pairs={{0,32},{8,40},{16,48},{24,56},{32,64},{40,72},{48,80},{56,88},{64,... | collective-permute-start | bytes 589832 | tf_op jit(solution)/shard_map/ppermute | solution.py:249
  14.6 7.7 %collective-permute-start.14 = (bf16[256,384]{1,0:T(8,128)(2,1)S(1)}, bf16[256,384]{1,0:T(8,128)(2,1)S(1)}, u32[]{:S(2)}, u32[]{:S(2)}) collective-permute-start(bf16[256,384]{1,0:T(8,128)(2,1)S(1)} %collective-permute-done.6.refs_8_), channel_id=1, source_target_pairs={{0,224},{8,232},{16,240},{24,248},{32,0},{40,8},{48,16},{56,24},{6... | collective-permute-start | bytes 589832 | tf_op jit(solution)/shard_map/ppermute | solution.py:253
  18.8 8.4 %collective-permute-start.2 = (bf16[272,384]{1,0:T(8,128)(2,1)S(1)}, bf16[272,384]{1,0:T(8,128)(2,1)S(1)}, u32[]{:S(2)}, u32[]{:S(2)}) collective-permute-start(bf16[272,384]{1,0:T(8,128)(2,1)S(1)} %fusion.1.refs_0_), channel_id=1, source_target_pairs={{0,24},{8,16},{16,8},{24,0},{32,56},{40,48},{48,40},{56,32},{64,88... | collective-permute-start | bytes 626696 | tf_op jit(solution)/shard_map/ppermute | solution.py:271
  19.5 10.6 %collective-permute-start.9 = (bf16[256,384]{1,0:T(8,128)(2,1)}, bf16[256,384]{1,0:T(8,128)(2,1)S(1)}, u32[]{:S(2)}, u32[]{:S(2)}) collective-permute-start(bf16[256,384]{1,0:T(8,128)(2,1)} %collective-permute-done.4.refs_6_), channel_id=1, source_target_pairs={{0,224},{8,232},{16,240},{24,248},{32,0},{40,8},{48,16},{56,24},{6... | collective-permute-start | bytes 589832 | tf_op jit(solution)/shard_map/ppermute | solution.py:251
  20.7 10.0 %collective-permute-start.12 = (bf16[256,384]{1,0:T(8,128)(2,1)}, bf16[256,384]{1,0:T(8,128)(2,1)}, u32[]{:S(2)}, u32[]{:S(2)}) collective-permute-start(bf16[256,384]{1,0:T(8,128)(2,1)} %collective-permute-done.5.refs_7_), channel_id=1, source_target_pairs={{0,32},{8,40},{16,48},{24,56},{32,64},{40,72},{48,80},{56,88},{64,... | collective-permute-start | bytes 589832 | tf_op jit(solution)/shard_map/ppermute | solution.py:252
  22.2 11.4 %collective-permute-start.8 = (bf16[256,384]{1,0:T(8,128)(2,1)S(1)}, bf16[256,384]{1,0:T(8,128)(2,1)}, u32[]{:S(2)}, u32[]{:S(2)}) collective-permute-start(bf16[256,384]{1,0:T(8,128)(2,1)S(1)} %collective-permute-done.7.refs_3_), channel_id=1, source_target_pairs={{0,32},{8,40},{16,48},{24,56},{32,64},{40,72},{48,80},{56,88},{64,... | collective-permute-start | bytes 589832 | tf_op jit(solution)/shard_map/ppermute | solution.py:249
  22.3 11.7 %collective-permute-start.15 = (bf16[256,384]{1,0:T(8,128)(2,1)S(1)}, bf16[256,384]{1,0:T(8,128)(2,1)}, u32[]{:S(2)}, u32[]{:S(2)}) collective-permute-start(bf16[256,384]{1,0:T(8,128)(2,1)S(1)} %collective-permute-done.14.refs_9_), channel_id=1, source_target_pairs={{0,224},{8,232},{16,240},{24,248},{32,0},{40,8},{48,16},{56,24},{6... | collective-permute-start | bytes 589832 | tf_op jit(solution)/shard_map/ppermute | solution.py:253
  25.5 1.7 %copy-start = (bf16[384,3072]{1,0:T(8,128)(2,1)S(1)}, bf16[384,3072]{1,0:T(8,128)(2,1)}, u32[]{:S(2)}) copy-start(bf16[384,3072]{1,0:T(8,128)(2,1)} %weight_ref.3) | copy-start | bytes 7077892
  27.1 2.9 %copy-start.12 = (bf16[256,384]{1,0:T(8,128)(2,1)S(1)}, bf16[256,384]{1,0:T(8,128)(2,1)}, u32[]{:S(2)}) copy-start(bf16[256,384]{1,0:T(8,128)(2,1)} %param.8) | copy-start | bytes 589828
  27.1 2.9 %copy-start.13 = (bf16[256,384]{1,0:T(8,128)(2,1)S(1)}, bf16[256,384]{1,0:T(8,128)(2,1)}, u32[]{:S(2)}) copy-start(bf16[256,384]{1,0:T(8,128)(2,1)} %param.7) | copy-start | bytes 589828
  27.2 9.7 %copy-start.14 = (s32[2]{0:T(128)S(1)}, s32[2]{0:T(128)}, u32[]{:S(2)}) copy-start(s32[2]{0:T(128)} %param.10) | copy-start | bytes 28
  27.3 0.7 copy-start.6
  28.0 37.6 %collective-permute-start.20 = (bf16[384,1536]{1,0:T(8,128)(2,1)S(1)}, bf16[384,1536]{1,0:T(8,128)(2,1)S(1)}, u32[]{:S(2)}, u32[]{:S(2)}) collective-permute-start(bf16[384,1536]{1,0:T(8,128)(2,1)S(1)} %pick.1), channel_id=1, source_target_pairs={{0,1},{1,0},{2,3},{3,2},{4,5},{5,4},{6,7},{7,6},{8,9},{9,8},{10,11... | collective-permute-start | bytes 3538952 | tf_op jit(solution)/shard_map/ppermute | solution.py:264
  30.1 18.1 %collective-permute-start.10 = (bf16[256,384]{1,0:T(8,128)(2,1)S(1)}, bf16[256,384]{1,0:T(8,128)(2,1)S(1)}, u32[]{:S(2)}, u32[]{:S(2)}) collective-permute-start(bf16[256,384]{1,0:T(8,128)(2,1)S(1)} %collective-permute-done.9.refs_4_), channel_id=1, source_target_pairs={{0,224},{8,232},{16,240},{24,248},{32,0},{40,8},{48,16},{56,24},{6... | collective-permute-start | bytes 589832 | tf_op jit(solution)/shard_map/ppermute | solution.py:251
  30.8 17.5 %collective-permute-start.13 = (bf16[256,384]{1,0:T(8,128)(2,1)}, bf16[256,384]{1,0:T(8,128)(2,1)S(1)}, u32[]{:S(2)}, u32[]{:S(2)}) collective-permute-start(bf16[256,384]{1,0:T(8,128)(2,1)} %collective-permute-done.12.refs_8_), channel_id=1, source_target_pairs={{0,32},{8,40},{16,48},{24,56},{32,64},{40,72},{48,80},{56,88},{64,... | collective-permute-start | bytes 589832 | tf_op jit(solution)/shard_map/ppermute | solution.py:252
  33.6 14.6 %collective-permute-start.11 = (bf16[256,384]{1,0:T(8,128)(2,1)}, bf16[256,384]{1,0:T(8,128)(2,1)S(1)}, u32[]{:S(2)}, u32[]{:S(2)}) collective-permute-start(bf16[256,384]{1,0:T(8,128)(2,1)} %collective-permute-done.8.refs_0_), channel_id=1, source_target_pairs={{0,32},{8,40},{16,48},{24,56},{32,64},{40,72},{48,80},{56,88},{64,... | collective-permute-start | bytes 589832 | tf_op jit(solution)/shard_map/ppermute | solution.py:249
  33.9 14.3 %collective-permute-start.16 = (bf16[256,384]{1,0:T(8,128)(2,1)}, bf16[256,384]{1,0:T(8,128)(2,1)S(1)}, u32[]{:S(2)}, u32[]{:S(2)}) collective-permute-start(bf16[256,384]{1,0:T(8,128)(2,1)} %collective-permute-done.15.refs_6_), channel_id=1, source_target_pairs={{0,224},{8,232},{16,240},{24,248},{32,0},{40,8},{48,16},{56,24},{6... | collective-permute-start | bytes 589832 | tf_op jit(solution)/shard_map/ppermute | solution.py:253
  37.0 0.9 %copy-start.3 = (bf16[272,384]{1,0:T(8,128)(2,1)S(1)}, bf16[272,384]{1,0:T(8,128)(2,1)}, u32[]{:S(2)}) copy-start(bf16[272,384]{1,0:T(8,128)(2,1)} %copy-done.2) | copy-start | bytes 626692
  37.9 0.9 %copy-start.5 = (bf16[272,384]{1,0:T(8,128)(2,1)S(1)}, bf16[272,384]{1,0:T(8,128)(2,1)}, u32[]{:S(2)}) copy-start(bf16[272,384]{1,0:T(8,128)(2,1)} %copy-done.4) | copy-start | bytes 626692
  38.8 0.9 %copy-start.7 = (bf16[272,384]{1,0:T(8,128)(2,1)S(1)}, bf16[272,384]{1,0:T(8,128)(2,1)}, u32[]{:S(2)}) copy-start(bf16[272,384]{1,0:T(8,128)(2,1)} %copy-done.6) | copy-start | bytes 626692
  39.7 0.9 %copy-start.9 = (bf16[256,384]{1,0:T(8,128)(2,1)S(1)}, bf16[256,384]{1,0:T(8,128)(2,1)}, u32[]{:S(2)}) copy-start(bf16[256,384]{1,0:T(8,128)(2,1)} %copy-done.8) | copy-start | bytes 589828
  40.7 0.9 %copy-start.11 = (bf16[256,384]{1,0:T(8,128)(2,1)S(1)}, bf16[256,384]{1,0:T(8,128)(2,1)}, u32[]{:S(2)}) copy-start(bf16[256,384]{1,0:T(8,128)(2,1)} %copy-done.10) | copy-start | bytes 589828
  48.2 22.3 %copy-start.1 = (bf16[384,3072]{1,0:T(8,128)(2,1)S(1)}, bf16[384,3072]{1,0:T(8,128)(2,1)}, u32[]{:S(2)}) copy-start(bf16[384,3072]{1,0:T(8,128)(2,1)} %weight_ref.3) | copy-start | bytes 7077892
  53.2 1.9 %collective-permute-start.17 = (bf16[2,416,256]{2,1,0:T(8,128)(2,1)S(1)}, bf16[2,416,256]{2,1,0:T(8,128)(2,1)S(1)}, u32[]{:S(2)}, u32[]{:S(2)}) collective-permute-start(bf16[2,416,256]{2,1,0:T(8,128)(2,1)S(1)} %get-tuple-element.23), channel_id=1, source_target_pairs={{0,8},{8,0},{16,24},{24,16},{32,40},{40,32},{48,56},{56,48},{64,72... | collective-permute-start | bytes 1277960 | tf_op jit(solution)/shard_map/ppermute | solution.py:322
  55.2 7.4 %collective-permute-start.18 = (bf16[1,416,256]{2,1,0:T(8,128)(2,1)S(1)}, bf16[1,416,256]{2,1,0:T(8,128)(2,1)S(1)}, u32[]{:S(2)}, u32[]{:S(2)}) collective-permute-start(bf16[1,416,256]{2,1,0:T(8,128)(2,1)S(1)} %get-tuple-element.26), channel_id=1, source_target_pairs={{0,16},{8,24},{16,0},{24,8},{32,48},{40,56},{48,32},{56,40},{64,80... | collective-permute-start | bytes 638984 | tf_op jit(solution)/shard_map/ppermute | solution.py:335
  62.8 7.7 %collective-permute-start.19 = (bf16[256,384]{1,0:T(8,128)(2,1)S(1)}, bf16[256,384]{1,0:T(8,128)(2,1)S(1)}, u32[]{:S(2)}, u32[]{:S(2)}) collective-permute-start(bf16[256,384]{1,0:T(8,128)(2,1)S(1)} %finish.1.mine_ref), channel_id=1, source_target_pairs={{0,1},{1,0},{2,3},{3,2},{4,5},{5,4},{6,7},{7,6},{8,9},{9,8},{10,11... | collective-permute-start | bytes 589832 | tf_op jit(solution)/shard_map/ppermute | solution.py:352
  (4 other events, 2.7 us)

commit v9 on v8

--- a/solution.py
+++ b/solution.py
@@ -232,7 +232,7 @@
     )
 
 
-PARAMS = pltpu.CompilerParams(vmem_limit_bytes=32 * 1024 * 1024)
+PARAMS = pltpu.CompilerParams(vmem_limit_bytes=16 * 1024 * 1024)
 
 
 def per_device(seq_size, head_size, queries, key_states, value_states, block_list, text_slots, out_weight):

time: 88.2 us -> 87.7 us (level)
  waiting for transfers between devices: 18.7 us -> 20.1 us
  Pallas kernels: 13.1 us -> 11.8 us
    pallas_call x1, Pallas kernels: 6.58 us -> 5.29 us  [per_device(): pl.pallas_call(functools.partial(near_kernel, factor, seq_size, order), o...]
  transfers between devices with their start and end apart: 21 -> 21, of which waited for: 6 -> 6; matrix products, arithmetic and copies ran while one was open for 2% -> 2% of each run, Pallas kernels for 14% -> 12%
where the time goes in v9:
time: 87.7 us; the launch traced here: 87.2 us
  starting transfers between devices  27.7 us (32%)
  waiting for transfers between devices  20.1 us (23%)
  blocking collectives  15.2 us (17%)
  Pallas kernels  11.8 us (13%)
  local copies, waits for them, and re-layouts  9.71 us (11%)
  other arithmetic  2.54 us (3%)
    all_to_all x1, blocking collectives, per_device(): lax.all_to_all(shares, 'head', 0, 0, axis_index_groups=sides, tiled=True)  15.2 us
    ppermute x4, starting transfers between devices, per_device(): v_down.append(lax.ppermute(v_down[-1], 'seq', down))  11.8 us
    unnamed x30, local copies, waits for them, and re-layouts  9.71 us
    ppermute x1, waiting for transfers between devices, per_device(): other = lax.ppermute(send, 'seq', [(s, s ^ 2) for s in range(seq_size)])  7.82 us
    ppermute x1, waiting for transfers between devices, per_device(): lax.ppermute(attended, 'head', swap_side)  5.78 us
    pallas_call x1, Pallas kernels, per_device(): pl.pallas_call(functools.partial(near_kernel, factor, seq_size, order), o...  5.29 us
    ppermute x3, starting transfers between devices, per_device(): k_down.append(lax.ppermute(k_down[-1], 'seq', down))  5.08 us
    pallas_call x1, Pallas kernels, per_device(): pl.pallas_call(functools.partial(far_kernel, factor, 3, len(far)), out_sh...  4.96 us
  transfers between devices with their start and end apart: 21, of which 6 were waited for; matrix products, arithmetic and copies ran while one was open for 2% of the time, Pallas kernels for 12%

profile of v9, /device:TPU:2, one launch (start us, length us, event | category | flops | bytes accessed | tf_op | source)
XLA Modules:
  0.0 87.2 jit_solution(7382422867303404602)
XLA Ops:
  0.0 1.9 %collective-permute-start.3 = (bf16[256,384]{1,0:T(8,128)(2,1)}, bf16[256,384]{1,0:T(8,128)(2,1)S(1)}, u32[]{:S(2)}, u32[]{:S(2)}) collective-permute-start(bf16[256,384]{1,0:T(8,128)(2,1)} %param.7), channel_id=1, source_target_pairs={{0,32},{8,40},{16,48},{24,56},{32,64},{40,72},{48,80},{56,88},{64,... | collective-permute-start | bytes 589832 | tf_op jit(solution)/shard_map/ppermute | solution.py:249
  1.9 3.9 %collective-permute-start.4 = (bf16[256,384]{1,0:T(8,128)(2,1)}, bf16[256,384]{1,0:T(8,128)(2,1)}, u32[]{:S(2)}, u32[]{:S(2)}) collective-permute-start(bf16[256,384]{1,0:T(8,128)(2,1)} %param.7), channel_id=1, source_target_pairs={{0,224},{8,232},{16,240},{24,248},{32,0},{40,8},{48,16},{56,24},{6... | collective-permute-start | bytes 589832 | tf_op jit(solution)/shard_map/ppermute | solution.py:251
  5.9 2.0 %collective-permute-start.6 = (bf16[256,384]{1,0:T(8,128)(2,1)}, bf16[256,384]{1,0:T(8,128)(2,1)S(1)}, u32[]{:S(2)}, u32[]{:S(2)}) collective-permute-start(bf16[256,384]{1,0:T(8,128)(2,1)} %param.8), channel_id=1, source_target_pairs={{0,224},{8,232},{16,240},{24,248},{32,0},{40,8},{48,16},{56,24},{6... | collective-permute-start | bytes 589832 | tf_op jit(solution)/shard_map/ppermute | solution.py:253
  8.5 0.9 %fusion.1.refs_0_ = bf16[272,384]{1,0:T(8,128)(2,1)S(1)} fusion(bf16[1,27]{1,0:T(2,128)(2,1)S(1)} %convert.5, bf16[256,384]{1,0:T(8,128)(2,1)} %param.6), kind=kLoop, calls=%fused_computation.3 | loop fusion | flops 626688 | bytes 405558 | tf_op jit(solution)/shard_map/concatenate | solution.py:269
  9.6 1.4 %collective-permute-done.3.refs_5_ = bf16[256,384]{1,0:T(8,128)(2,1)S(1)} collective-permute-done((bf16[256,384]{1,0:T(8,128)(2,1)}, bf16[256,384]{1,0:T(8,128)(2,1)S(1)}, u32[]{:S(2)}, u32[]{:S(2)}) %collective-permute-start.3) | collective-permute-done | bytes 196640 | tf_op jit(solution)/shard_map/ppermute | solution.py:249
  12.0 0.7 copy-done.8
  12.6 1.9 %collective-permute-done.6.refs_8_ = bf16[256,384]{1,0:T(8,128)(2,1)S(1)} collective-permute-done((bf16[256,384]{1,0:T(8,128)(2,1)}, bf16[256,384]{1,0:T(8,128)(2,1)S(1)}, u32[]{:S(2)}, u32[]{:S(2)}) %collective-permute-start.6) | collective-permute-done | bytes 196640 | tf_op jit(solution)/shard_map/ppermute | solution.py:253
  14.6 3.6 %collective-permute-start.14 = (bf16[256,384]{1,0:T(8,128)(2,1)S(1)}, bf16[256,384]{1,0:T(8,128)(2,1)S(1)}, u32[]{:S(2)}, u32[]{:S(2)}) collective-permute-start(bf16[256,384]{1,0:T(8,128)(2,1)S(1)} %collective-permute-done.6.refs_8_), channel_id=1, source_target_pairs={{0,224},{8,232},{16,240},{24,248},{32,0},{40,8},{48,16},{56,24},{6... | collective-permute-start | bytes 589832 | tf_op jit(solution)/shard_map/ppermute | solution.py:253
  18.1 0.7 copy-done.10
  20.0 0.7 copy-done.4
  20.7 1.5 %collective-permute-start.12 = (bf16[256,384]{1,0:T(8,128)(2,1)}, bf16[256,384]{1,0:T(8,128)(2,1)}, u32[]{:S(2)}, u32[]{:S(2)}) collective-permute-start(bf16[256,384]{1,0:T(8,128)(2,1)} %collective-permute-done.5.refs_7_), channel_id=1, source_target_pairs={{0,32},{8,40},{16,48},{24,56},{32,64},{40,72},{48,80},{56,88},{64,... | collective-permute-start | bytes 589832 | tf_op jit(solution)/shard_map/ppermute | solution.py:252
  22.3 3.2 %collective-permute-start.15 = (bf16[256,384]{1,0:T(8,128)(2,1)S(1)}, bf16[256,384]{1,0:T(8,128)(2,1)}, u32[]{:S(2)}, u32[]{:S(2)}) collective-permute-start(bf16[256,384]{1,0:T(8,128)(2,1)S(1)} %collective-permute-done.14.refs_9_), channel_id=1, source_target_pairs={{0,224},{8,232},{16,240},{24,248},{32,0},{40,8},{48,16},{56,24},{6... | collective-permute-start | bytes 589832 | tf_op jit(solution)/shard_map/ppermute | solution.py:253
  25.5 1.7 %copy-done = bf16[384,3072]{1,0:T(8,128)(2,1)S(1)} copy-done((bf16[384,3072]{1,0:T(8,128)(2,1)S(1)}, bf16[384,3072]{1,0:T(8,128)(2,1)}, u32[]{:S(2)}) %copy-start) | copy-done | bytes 2359320
  27.3 0.7 copy-done.6
  28.0 2.1 %collective-permute-start.20 = (bf16[384,1536]{1,0:T(8,128)(2,1)S(1)}, bf16[384,1536]{1,0:T(8,128)(2,1)S(1)}, u32[]{:S(2)}, u32[]{:S(2)}) collective-permute-start(bf16[384,1536]{1,0:T(8,128)(2,1)S(1)} %pick.1), channel_id=1, source_target_pairs={{0,1},{1,0},{2,3},{3,2},{4,5},{5,4},{6,7},{7,6},{8,9},{9,8},{10,11... | collective-permute-start | bytes 3538952 | tf_op jit(solution)/shard_map/ppermute | solution.py:264
  30.8 1.5 %collective-permute-start.13 = (bf16[256,384]{1,0:T(8,128)(2,1)}, bf16[256,384]{1,0:T(8,128)(2,1)S(1)}, u32[]{:S(2)}, u32[]{:S(2)}) collective-permute-start(bf16[256,384]{1,0:T(8,128)(2,1)} %collective-permute-done.12.refs_8_), channel_id=1, source_target_pairs={{0,32},{8,40},{16,48},{24,56},{32,64},{40,72},{48,80},{56,88},{64,... | collective-permute-start | bytes 589832 | tf_op jit(solution)/shard_map/ppermute | solution.py:252
  32.2 1.4 %collective-permute-done.8.refs_0_ = bf16[256,384]{1,0:T(8,128)(2,1)} collective-permute-done((bf16[256,384]{1,0:T(8,128)(2,1)S(1)}, bf16[256,384]{1,0:T(8,128)(2,1)}, u32[]{:S(2)}, u32[]{:S(2)}) %collective-permute-start.8) | collective-permute-done | bytes 196640 | tf_op jit(solution)/shard_map/ppermute | solution.py:249
  33.9 3.0 %collective-permute-start.16 = (bf16[256,384]{1,0:T(8,128)(2,1)}, bf16[256,384]{1,0:T(8,128)(2,1)S(1)}, u32[]{:S(2)}, u32[]{:S(2)}) collective-permute-start(bf16[256,384]{1,0:T(8,128)(2,1)} %collective-permute-done.15.refs_6_), channel_id=1, source_target_pairs={{0,224},{8,232},{16,240},{24,248},{32,0},{40,8},{48,16},{56,24},{6... | collective-permute-start | bytes 589832 | tf_op jit(solution)/shard_map/ppermute | solution.py:253
  37.0 0.9 %copy-done.3 = bf16[272,384]{1,0:T(8,128)(2,1)S(1)} copy-done((bf16[272,384]{1,0:T(8,128)(2,1)S(1)}, bf16[272,384]{1,0:T(8,128)(2,1)}, u32[]{:S(2)}) %copy-start.3) | copy-done | bytes 208920
  37.9 0.9 %copy-done.5 = bf16[272,384]{1,0:T(8,128)(2,1)S(1)} copy-done((bf16[272,384]{1,0:T(8,128)(2,1)S(1)}, bf16[272,384]{1,0:T(8,128)(2,1)}, u32[]{:S(2)}) %copy-start.5) | copy-done | bytes 208920
  38.8 0.9 %copy-done.7 = bf16[272,384]{1,0:T(8,128)(2,1)S(1)} copy-done((bf16[272,384]{1,0:T(8,128)(2,1)S(1)}, bf16[272,384]{1,0:T(8,128)(2,1)}, u32[]{:S(2)}) %copy-start.7) | copy-done | bytes 208920
  39.8 0.9 %copy-done.9 = bf16[256,384]{1,0:T(8,128)(2,1)S(1)} copy-done((bf16[256,384]{1,0:T(8,128)(2,1)S(1)}, bf16[256,384]{1,0:T(8,128)(2,1)}, u32[]{:S(2)}) %copy-start.9) | copy-done | bytes 196632
  40.7 0.9 %copy-done.11 = bf16[256,384]{1,0:T(8,128)(2,1)S(1)} copy-done((bf16[256,384]{1,0:T(8,128)(2,1)S(1)}, bf16[256,384]{1,0:T(8,128)(2,1)}, u32[]{:S(2)}) %copy-start.11) | copy-done | bytes 196632
  41.6 5.3 %attend_near.1 = (s32[4,8]{1,0:T(4,128)S(1)}, bf16[4,256,384]{2,1,0:T(8,128)(2,1)S(1)}, f32[12,128,256]{2,1,0:T(8,128)S(1)}, f32[12,1,256]{2,1,0:T(1,128)S(1)}, f32[12,1,256]{2,1,0:T(1,128)S(1)}) custom-call(s32[3]{0:T(128)S(1)} %pad_add_fusion.place_ref, bf16[272,384]{1,0:T(8,128)(2,1)S(1)} %fusion.1.refs_0_, bf16[272,384]{1,0:T(8,128)(2,1)S(1)} %copy-done.3, ...), custom_call_target="tpu_custom_call" | custom-call | flops 905969664 | bytes 4194304 | tf_op jit(solution)/shard_map/attend_near/pallas_call | solution.py:292
  47.0 5.0 %attend_far.1 = (f32[2,384,256]{2,1,0:T(8,128)S(1)}, f32[2,8,256]{2,1,0:T(8,128)S(1)}, bf16[2,416,256]{2,1,0:T(8,128)(2,1)S(1)}) custom-call(s32[4,8]{1,0:T(4,128)S(1)} %get-tuple-element.16.need_ref, bf16[4,256,384]{2,1,0:T(8,128)(2,1)S(1)} %get-tuple-element.17.stacked_ref, bf16[256,384]{1,0:T(8,128)(2,1)} %collective-permute-done.8.refs_0_, ...), custom_call_target="tpu_custom_call" | custom-call | flops 905969664 | bytes 4194304 | tf_op jit(solution)/shard_map/attend_far/pallas_call | solution.py:307
  52.0 1.8 %collective-permute-done.17.other_ref = bf16[2,416,256]{2,1,0:T(8,128)(2,1)S(1)} collective-permute-done((bf16[2,416,256]{2,1,0:T(8,128)(2,1)S(1)}, bf16[2,416,256]{2,1,0:T(8,128)(2,1)S(1)}, u32[]{:S(2)}, u32[]{:S(2)}) %collective-permute-start.17) | collective-permute-done | bytes 426016 | tf_op jit(solution)/shard_map/ppermute | solution.py:322
  54.3 7.8 %collective-permute-done.18.other_ref = bf16[1,416,256]{2,1,0:T(8,128)(2,1)S(1)} collective-permute-done((bf16[1,416,256]{2,1,0:T(8,128)(2,1)S(1)}, bf16[1,416,256]{2,1,0:T(8,128)(2,1)S(1)}, u32[]{:S(2)}, u32[]{:S(2)}) %collective-permute-start.18) | collective-permute-done | bytes 213024 | tf_op jit(solution)/shard_map/ppermute | solution.py:335
  62.3 2.0 %collective-permute-start.19 = (bf16[256,384]{1,0:T(8,128)(2,1)S(1)}, bf16[256,384]{1,0:T(8,128)(2,1)S(1)}, u32[]{:S(2)}, u32[]{:S(2)}) collective-permute-start(bf16[256,384]{1,0:T(8,128)(2,1)S(1)} %finish.1.mine_ref), channel_id=1, source_target_pairs={{0,1},{1,0},{2,3},{3,2},{4,5},{5,4},{6,7},{7,6},{8,9},{9,8},{10,11... | collective-permute-start | bytes 589832 | tf_op jit(solution)/shard_map/ppermute | solution.py:352
  64.2 5.8 %collective-permute-done.19.other_ref = bf16[256,384]{1,0:T(8,128)(2,1)S(1)} collective-permute-done((bf16[256,384]{1,0:T(8,128)(2,1)S(1)}, bf16[256,384]{1,0:T(8,128)(2,1)S(1)}, u32[]{:S(2)}, u32[]{:S(2)}) %collective-permute-start.19) | collective-permute-done | bytes 196640 | tf_op jit(solution)/shard_map/ppermute | solution.py:352
  70.0 1.1 %project.1 = bf16[4,256,384]{2,1,0:T(8,128)(2,1)S(1)} custom-call(s32[1]{0:T(128)} %bitcast.side_ref, bf16[256,384]{1,0:T(8,128)(2,1)S(1)} %finish.1.mine_ref, bf16[256,384]{1,0:T(8,128)(2,1)S(1)} %collective-permute-done.19.other_ref, bf16[384,3072]{1,0:T(8,128)(2,1)S(1)} %copy-done.1, bf16[384,1536]{1,0:T(8,128)(2,1)S(1)} %collective-permute-done.20.other_weight_ref), custom_call_target="tpu_custom_call" | custom-call | tf_op jit(solution)/shard_map/project/pallas_call | solution.py:345
  71.2 15.2 %all_to_all.5 = bf16[4,256,384]{2,1,0:T(8,128)(2,1)S(1)} all-to-all(bf16[4,256,384]{2,1,0:T(8,128)(2,1)S(1)} %project.1), channel_id=1, replica_groups={{0,2,4,6},{1,3,5,7},{8,10,12,14},{9,11,13,15},{16,18,20,22},{17,19,21,2..., dimensions={0} | all-to-all | bytes 1572864 | tf_op jit(solution)/shard_map/all_to_all | solution.py:354
  86.3 0.8 reduce_sum.12
  (52 shorter events, 4.9 us)
Async XLA Ops:
  0.0 11.0 %collective-permute-start.3 = (bf16[256,384]{1,0:T(8,128)(2,1)}, bf16[256,384]{1,0:T(8,128)(2,1)S(1)}, u32[]{:S(2)}, u32[]{:S(2)}) collective-permute-start(bf16[256,384]{1,0:T(8,128)(2,1)} %param.7), channel_id=1, source_target_pairs={{0,32},{8,40},{16,48},{24,56},{32,64},{40,72},{48,80},{56,88},{64,... | collective-permute-start | bytes 589832 | tf_op jit(solution)/shard_map/ppermute | solution.py:249
  1.9 9.6 %collective-permute-start.4 = (bf16[256,384]{1,0:T(8,128)(2,1)}, bf16[256,384]{1,0:T(8,128)(2,1)}, u32[]{:S(2)}, u32[]{:S(2)}) collective-permute-start(bf16[256,384]{1,0:T(8,128)(2,1)} %param.7), channel_id=1, source_target_pairs={{0,224},{8,232},{16,240},{24,248},{32,0},{40,8},{48,16},{56,24},{6... | collective-permute-start | bytes 589832 | tf_op jit(solution)/shard_map/ppermute | solution.py:251
  5.9 8.7 %collective-permute-start.6 = (bf16[256,384]{1,0:T(8,128)(2,1)}, bf16[256,384]{1,0:T(8,128)(2,1)S(1)}, u32[]{:S(2)}, u32[]{:S(2)}) collective-permute-start(bf16[256,384]{1,0:T(8,128)(2,1)} %param.8), channel_id=1, source_target_pairs={{0,224},{8,232},{16,240},{24,248},{32,0},{40,8},{48,16},{56,24},{6... | collective-permute-start | bytes 589832 | tf_op jit(solution)/shard_map/ppermute | solution.py:253
  7.9 10.9 %collective-permute-start.5 = (bf16[256,384]{1,0:T(8,128)(2,1)}, bf16[256,384]{1,0:T(8,128)(2,1)}, u32[]{:S(2)}, u32[]{:S(2)}) collective-permute-start(bf16[256,384]{1,0:T(8,128)(2,1)} %param.8), channel_id=1, source_target_pairs={{0,32},{8,40},{16,48},{24,56},{32,64},{40,72},{48,80},{56,88},{64,... | collective-permute-start | bytes 589832 | tf_op jit(solution)/shard_map/ppermute | solution.py:252
  9.5 9.3 %collective-permute-start = (bf16[272,384]{1,0:T(8,128)(2,1)S(1)}, bf16[272,384]{1,0:T(8,128)(2,1)S(1)}, u32[]{:S(2)}, u32[]{:S(2)}) collective-permute-start(bf16[272,384]{1,0:T(8,128)(2,1)S(1)} %fusion.1.refs_0_), channel_id=1, source_target_pairs={{0,8},{8,0},{16,24},{24,16},{32,40},{40,32},{48,56},{56,48},{64,72... | collective-permute-start | bytes 626696 | tf_op jit(solution)/shard_map/ppermute | solution.py:271
  11.0 9.1 %collective-permute-start.1 = (bf16[272,384]{1,0:T(8,128)(2,1)S(1)}, bf16[272,384]{1,0:T(8,128)(2,1)S(1)}, u32[]{:S(2)}, u32[]{:S(2)}) collective-permute-start(bf16[272,384]{1,0:T(8,128)(2,1)S(1)} %fusion.1.refs_0_), channel_id=1, source_target_pairs={{0,16},{8,24},{16,0},{24,8},{32,48},{40,56},{48,32},{56,40},{64,80... | collective-permute-start | bytes 626696 | tf_op jit(solution)/shard_map/ppermute | solution.py:271
  11.5 10.7 %collective-permute-start.7 = (bf16[256,384]{1,0:T(8,128)(2,1)S(1)}, bf16[256,384]{1,0:T(8,128)(2,1)S(1)}, u32[]{:S(2)}, u32[]{:S(2)}) collective-permute-start(bf16[256,384]{1,0:T(8,128)(2,1)S(1)} %collective-permute-done.3.refs_5_), channel_id=1, source_target_pairs={{0,32},{8,40},{16,48},{24,56},{32,64},{40,72},{48,80},{56,88},{64,... | collective-permute-start | bytes 589832 | tf_op jit(solution)/shard_map/ppermute | solution.py:249
  14.6 7.7 %collective-permute-start.14 = (bf16[256,384]{1,0:T(8,128)(2,1)S(1)}, bf16[256,384]{1,0:T(8,128)(2,1)S(1)}, u32[]{:S(2)}, u32[]{:S(2)}) collective-permute-start(bf16[256,384]{1,0:T(8,128)(2,1)S(1)} %collective-permute-done.6.refs_8_), channel_id=1, source_target_pairs={{0,224},{8,232},{16,240},{24,248},{32,0},{40,8},{48,16},{56,24},{6... | collective-permute-start | bytes 589832 | tf_op jit(solution)/shard_map/ppermute | solution.py:253
  18.8 8.4 %collective-permute-start.2 = (bf16[272,384]{1,0:T(8,128)(2,1)S(1)}, bf16[272,384]{1,0:T(8,128)(2,1)S(1)}, u32[]{:S(2)}, u32[]{:S(2)}) collective-permute-start(bf16[272,384]{1,0:T(8,128)(2,1)S(1)} %fusion.1.refs_0_), channel_id=1, source_target_pairs={{0,24},{8,16},{16,8},{24,0},{32,56},{40,48},{48,40},{56,32},{64,88... | collective-permute-start | bytes 626696 | tf_op jit(solution)/shard_map/ppermute | solution.py:271
  19.5 10.6 %collective-permute-start.9 = (bf16[256,384]{1,0:T(8,128)(2,1)}, bf16[256,384]{1,0:T(8,128)(2,1)S(1)}, u32[]{:S(2)}, u32[]{:S(2)}) collective-permute-start(bf16[256,384]{1,0:T(8,128)(2,1)} %collective-permute-done.4.refs_6_), channel_id=1, source_target_pairs={{0,224},{8,232},{16,240},{24,248},{32,0},{40,8},{48,16},{56,24},{6... | collective-permute-start | bytes 589832 | tf_op jit(solution)/shard_map/ppermute | solution.py:251
  20.7 10.0 %collective-permute-start.12 = (bf16[256,384]{1,0:T(8,128)(2,1)}, bf16[256,384]{1,0:T(8,128)(2,1)}, u32[]{:S(2)}, u32[]{:S(2)}) collective-permute-start(bf16[256,384]{1,0:T(8,128)(2,1)} %collective-permute-done.5.refs_7_), channel_id=1, source_target_pairs={{0,32},{8,40},{16,48},{24,56},{32,64},{40,72},{48,80},{56,88},{64,... | collective-permute-start | bytes 589832 | tf_op jit(solution)/shard_map/ppermute | solution.py:252
  22.2 11.4 %collective-permute-start.8 = (bf16[256,384]{1,0:T(8,128)(2,1)S(1)}, bf16[256,384]{1,0:T(8,128)(2,1)}, u32[]{:S(2)}, u32[]{:S(2)}) collective-permute-start(bf16[256,384]{1,0:T(8,128)(2,1)S(1)} %collective-permute-done.7.refs_3_), channel_id=1, source_target_pairs={{0,32},{8,40},{16,48},{24,56},{32,64},{40,72},{48,80},{56,88},{64,... | collective-permute-start | bytes 589832 | tf_op jit(solution)/shard_map/ppermute | solution.py:249
  22.3 11.7 %collective-permute-start.15 = (bf16[256,384]{1,0:T(8,128)(2,1)S(1)}, bf16[256,384]{1,0:T(8,128)(2,1)}, u32[]{:S(2)}, u32[]{:S(2)}) collective-permute-start(bf16[256,384]{1,0:T(8,128)(2,1)S(1)} %collective-permute-done.14.refs_9_), channel_id=1, source_target_pairs={{0,224},{8,232},{16,240},{24,248},{32,0},{40,8},{48,16},{56,24},{6... | collective-permute-start | bytes 589832 | tf_op jit(solution)/shard_map/ppermute | solution.py:253
  25.5 1.7 %copy-start = (bf16[384,3072]{1,0:T(8,128)(2,1)S(1)}, bf16[384,3072]{1,0:T(8,128)(2,1)}, u32[]{:S(2)}) copy-start(bf16[384,3072]{1,0:T(8,128)(2,1)} %weight_ref.3) | copy-start | bytes 7077892
  27.1 2.9 %copy-start.12 = (bf16[256,384]{1,0:T(8,128)(2,1)S(1)}, bf16[256,384]{1,0:T(8,128)(2,1)}, u32[]{:S(2)}) copy-start(bf16[256,384]{1,0:T(8,128)(2,1)} %param.8) | copy-start | bytes 589828
  27.1 2.9 %copy-start.13 = (bf16[256,384]{1,0:T(8,128)(2,1)S(1)}, bf16[256,384]{1,0:T(8,128)(2,1)}, u32[]{:S(2)}) copy-start(bf16[256,384]{1,0:T(8,128)(2,1)} %param.7) | copy-start | bytes 589828
  27.2 9.7 %copy-start.14 = (s32[2]{0:T(128)S(1)}, s32[2]{0:T(128)}, u32[]{:S(2)}) copy-start(s32[2]{0:T(128)} %param.10) | copy-start | bytes 28
  27.3 0.7 copy-start.6
  28.0 36.3 %collective-permute-start.20 = (bf16[384,1536]{1,0:T(8,128)(2,1)S(1)}, bf16[384,1536]{1,0:T(8,128)(2,1)S(1)}, u32[]{:S(2)}, u32[]{:S(2)}) collective-permute-start(bf16[384,1536]{1,0:T(8,128)(2,1)S(1)} %pick.1), channel_id=1, source_target_pairs={{0,1},{1,0},{2,3},{3,2},{4,5},{5,4},{6,7},{7,6},{8,9},{9,8},{10,11... | collective-permute-start | bytes 3538952 | tf_op jit(solution)/shard_map/ppermute | solution.py:264
  30.1 16.8 %collective-permute-start.10 = (bf16[256,384]{1,0:T(8,128)(2,1)S(1)}, bf16[256,384]{1,0:T(8,128)(2,1)S(1)}, u32[]{:S(2)}, u32[]{:S(2)}) collective-permute-start(bf16[256,384]{1,0:T(8,128)(2,1)S(1)} %collective-permute-done.9.refs_4_), channel_id=1, source_target_pairs={{0,224},{8,232},{16,240},{24,248},{32,0},{40,8},{48,16},{56,24},{6... | collective-permute-start | bytes 589832 | tf_op jit(solution)/shard_map/ppermute | solution.py:251
  30.8 16.2 %collective-permute-start.13 = (bf16[256,384]{1,0:T(8,128)(2,1)}, bf16[256,384]{1,0:T(8,128)(2,1)S(1)}, u32[]{:S(2)}, u32[]{:S(2)}) collective-permute-start(bf16[256,384]{1,0:T(8,128)(2,1)} %collective-permute-done.12.refs_8_), channel_id=1, source_target_pairs={{0,32},{8,40},{16,48},{24,56},{32,64},{40,72},{48,80},{56,88},{64,... | collective-permute-start | bytes 589832 | tf_op jit(solution)/shard_map/ppermute | solution.py:252
  33.6 13.3 %collective-permute-start.11 = (bf16[256,384]{1,0:T(8,128)(2,1)}, bf16[256,384]{1,0:T(8,128)(2,1)S(1)}, u32[]{:S(2)}, u32[]{:S(2)}) collective-permute-start(bf16[256,384]{1,0:T(8,128)(2,1)} %collective-permute-done.8.refs_0_), channel_id=1, source_target_pairs={{0,32},{8,40},{16,48},{24,56},{32,64},{40,72},{48,80},{56,88},{64,... | collective-permute-start | bytes 589832 | tf_op jit(solution)/shard_map/ppermute | solution.py:249
  33.9 13.0 %collective-permute-start.16 = (bf16[256,384]{1,0:T(8,128)(2,1)}, bf16[256,384]{1,0:T(8,128)(2,1)S(1)}, u32[]{:S(2)}, u32[]{:S(2)}) collective-permute-start(bf16[256,384]{1,0:T(8,128)(2,1)} %collective-permute-done.15.refs_6_), channel_id=1, source_target_pairs={{0,224},{8,232},{16,240},{24,248},{32,0},{40,8},{48,16},{56,24},{6... | collective-permute-start | bytes 589832 | tf_op jit(solution)/shard_map/ppermute | solution.py:253
  37.0 0.9 %copy-start.3 = (bf16[272,384]{1,0:T(8,128)(2,1)S(1)}, bf16[272,384]{1,0:T(8,128)(2,1)}, u32[]{:S(2)}) copy-start(bf16[272,384]{1,0:T(8,128)(2,1)} %copy-done.2) | copy-start | bytes 626692
  37.9 0.9 %copy-start.5 = (bf16[272,384]{1,0:T(8,128)(2,1)S(1)}, bf16[272,384]{1,0:T(8,128)(2,1)}, u32[]{:S(2)}) copy-start(bf16[272,384]{1,0:T(8,128)(2,1)} %copy-done.4) | copy-start | bytes 626692
  38.8 0.9 %copy-start.7 = (bf16[272,384]{1,0:T(8,128)(2,1)S(1)}, bf16[272,384]{1,0:T(8,128)(2,1)}, u32[]{:S(2)}) copy-start(bf16[272,384]{1,0:T(8,128)(2,1)} %copy-done.6) | copy-start | bytes 626692
  39.7 0.9 %copy-start.9 = (bf16[256,384]{1,0:T(8,128)(2,1)S(1)}, bf16[256,384]{1,0:T(8,128)(2,1)}, u32[]{:S(2)}) copy-start(bf16[256,384]{1,0:T(8,128)(2,1)} %copy-done.8) | copy-start | bytes 589828
  40.7 0.9 %copy-start.11 = (bf16[256,384]{1,0:T(8,128)(2,1)S(1)}, bf16[256,384]{1,0:T(8,128)(2,1)}, u32[]{:S(2)}) copy-start(bf16[256,384]{1,0:T(8,128)(2,1)} %copy-done.10) | copy-start | bytes 589828
  46.9 23.1 %copy-start.1 = (bf16[384,3072]{1,0:T(8,128)(2,1)S(1)}, bf16[384,3072]{1,0:T(8,128)(2,1)}, u32[]{:S(2)}) copy-start(bf16[384,3072]{1,0:T(8,128)(2,1)} %weight_ref.3) | copy-start | bytes 7077892
  51.9 1.9 %collective-permute-start.17 = (bf16[2,416,256]{2,1,0:T(8,128)(2,1)S(1)}, bf16[2,416,256]{2,1,0:T(8,128)(2,1)S(1)}, u32[]{:S(2)}, u32[]{:S(2)}) collective-permute-start(bf16[2,416,256]{2,1,0:T(8,128)(2,1)S(1)} %get-tuple-element.23), channel_id=1, source_target_pairs={{0,8},{8,0},{16,24},{24,16},{32,40},{40,32},{48,56},{56,48},{64,72... | collective-permute-start | bytes 1277960 | tf_op jit(solution)/shard_map/ppermute | solution.py:322
  54.0 8.1 %collective-permute-start.18 = (bf16[1,416,256]{2,1,0:T(8,128)(2,1)S(1)}, bf16[1,416,256]{2,1,0:T(8,128)(2,1)S(1)}, u32[]{:S(2)}, u32[]{:S(2)}) collective-permute-start(bf16[1,416,256]{2,1,0:T(8,128)(2,1)S(1)} %get-tuple-element.26), channel_id=1, source_target_pairs={{0,16},{8,24},{16,0},{24,8},{32,48},{40,56},{48,32},{56,40},{64,80... | collective-permute-start | bytes 638984 | tf_op jit(solution)/shard_map/ppermute | solution.py:335
  62.3 7.8 %collective-permute-start.19 = (bf16[256,384]{1,0:T(8,128)(2,1)S(1)}, bf16[256,384]{1,0:T(8,128)(2,1)S(1)}, u32[]{:S(2)}, u32[]{:S(2)}) collective-permute-start(bf16[256,384]{1,0:T(8,128)(2,1)S(1)} %finish.1.mine_ref), channel_id=1, source_target_pairs={{0,1},{1,0},{2,3},{3,2},{4,5},{5,4},{6,7},{7,6},{8,9},{9,8},{10,11... | collective-permute-start | bytes 589832 | tf_op jit(solution)/shard_map/ppermute | solution.py:352
  (4 other events, 2.7 us)

commit v10 on v9

--- a/solution.py
+++ b/solution.py
@@ -131,7 +131,7 @@
     lax.fori_loop(0, q_ref.shape[0], visit, 0)
 
 
-def list_wanted(seq_size, order, place_ref, q_refs, need_ref):
+def list_wanted(seq_size, order, place_ref, text_ref, q_refs, need_ref):
     slots = [lax.rem(place_ref[0] + (GROUP * plane + seq_size), seq_size) for plane in order]
     for t, q_ref in enumerate(q_refs):
         row = q_ref[TILE:TILE + PART_ROWS, 0:HD].astype(jnp.float32)
@@ -141,21 +141,21 @@
         code = jnp.sum(bits).astype(jnp.int32)
         for j, slot in enumerate(slots):
             wanted = (code >> j) & 1
-            for i in range(1, place_ref.shape[0]):
-                wanted = jnp.where(slot == place_ref[i], 1, wanted)
+            for i in range(text_ref.shape[0]):
+                wanted = jnp.where(slot == text_ref[i], 1, wanted)
             need_ref[t, j] = wanted
 
 
-def near_kernel(factor, seq_size, order, place_ref, *refs):
-    q_refs, (own_ref, k_low, k_high, v_low, v_high) = refs[:GROUP], refs[GROUP:GROUP + 5]
-    need_ref, stacked_ref, acc_ref, peak_ref, total_ref, k_ref, vt_ref = refs[GROUP + 5:]
-    list_wanted(seq_size, order, place_ref, q_refs, need_ref)
+def near_kernel(factor, seq_size, order, place_ref, text_ref, *refs):
+    q_refs, (k_own, v_own, k_low, k_high, v_low, v_high) = refs[:GROUP], refs[GROUP:GROUP + 6]
+    need_ref, stacked_ref, acc_ref, peak_ref, total_ref, k_ref, vt_ref = refs[GROUP + 6:]
+    list_wanted(seq_size, order, place_ref, text_ref, q_refs, need_ref)
     acc_ref[...] = jnp.zeros_like(acc_ref)
     peak_ref[...] = jnp.full_like(peak_ref, LOWEST)
     total_ref[...] = jnp.zeros_like(total_ref)
     for t, q_ref in enumerate(q_refs):
         stacked_ref[t] = q_ref[0:TILE, :]
-    shards = [(own_ref.at[0:TILE], own_ref.at[TILE:2 * TILE]), (k_low, v_low), (k_high, v_high)]
+    shards = [(k_own, v_own), (k_low, v_low), (k_high, v_high)]
     load_shards(need_ref, 0, shards, k_ref, vt_ref)
     visit_shards(factor, need_ref, 0, 3, stacked_ref, k_ref, vt_ref, (acc_ref, peak_ref, total_ref))
 
@@ -204,21 +204,12 @@
         out_ref[:, h * HD:(h + 1) * HD] = outs[h].T.astype(jnp.bfloat16)
 
 
-def pick_kernel(side_ref, weight_ref, out_ref):
-    width = weight_ref.shape[0]
-    for j in range(out_ref.shape[1] // width):
-        begin = pl.multiple_of((2 * j + 1 - side_ref[0]) * width, HD)
-        out_ref[:, j * width:(j + 1) * width] = weight_ref[:, pl.ds(begin, width)]
-
-
 def project_kernel(side_ref, mine_ref, other_ref, weight_ref, other_weight_ref, out_ref):
     shares, _, width = out_ref.shape
     for j in range(shares):
-        begin = pl.multiple_of((2 * j + side_ref[0]) * width, HD)
-        mixed = jnp.dot(mine_ref[...], weight_ref[:, pl.ds(begin, width)], preferred_element_type=jnp.float32)
-        mixed = mixed + jnp.dot(
-            other_ref[...], other_weight_ref[:, j * width:(j + 1) * width], preferred_element_type=jnp.float32
-        )
+        block = pl.ds(pl.multiple_of((2 * j + side_ref[0]) * width, HD), width)
+        mixed = jnp.dot(mine_ref[...], weight_ref[:, block], preferred_element_type=jnp.float32)
+        mixed = mixed + jnp.dot(other_ref[...], other_weight_ref[:, block], preferred_element_type=jnp.float32)
         out_ref[j] = mixed.astype(jnp.bfloat16)
 
 
@@ -252,16 +243,9 @@
             v_up.append(lax.ppermute(v_up[-1], "seq", up))
         v_down.append(lax.ppermute(v_down[-1], "seq", down))
 
+    swap_side = [(h, h ^ 1) for h in range(head_size)]
     side = lax.axis_index("head") % 2
-    picked = pl.pallas_call(
-        pick_kernel,
-        out_shape=jax.ShapeDtypeStruct((width, head_size // 2 * width), out_weight.dtype),
-        in_specs=[pl.BlockSpec(memory_space=pltpu.SMEM)] + vmem_specs(1),
-        out_specs=pl.BlockSpec(memory_space=pltpu.VMEM),
-        compiler_params=PARAMS,
-        name="pick",
-    )(side[None], out_weight)
-    other_weight = lax.ppermute(picked, "head", [(h, h ^ 1) for h in range(head_size)])
+    other_weight = lax.ppermute(out_weight, "head", swap_side)
 
     listed = jnp.pad(
         block_list, ((0, PART_ROWS - 1), (0, width - block_list.shape[1])), constant_values=-1
@@ -271,7 +255,6 @@
         lax.ppermute(packed, "seq", [(s, s ^ k) for s in range(seq_size)]) for k in range(1, GROUP)
     ]
     order = (0, -1, 1, -3, 3, 4, -2, 2)
-    place = jnp.concatenate([me.astype(jnp.int32)[None], text_slots])
 
     rows = GROUP * heads
     state = (
@@ -288,7 +271,6 @@
             pltpu.VMEM((count, heads, HD, TILE), jnp.bfloat16),
         ]
 
-    own = jnp.concatenate([key_states, value_states], axis=0)
     need, stacked, *held = pl.pallas_call(
         functools.partial(near_kernel, factor, seq_size, order),
         out_shape=(
@@ -296,13 +278,13 @@
             jax.ShapeDtypeStruct((GROUP, TILE, width), jnp.bfloat16),
         )
         + state,
-        in_specs=smem + vmem_specs(GROUP + 5),
+        in_specs=smem * 2 + vmem_specs(GROUP + 6),
         out_specs=tuple(smem + vmem_specs(4)),
         scratch_shapes=scratch(3),
         compiler_params=PARAMS,
         cost_estimate=attend_cost(27),
         name="attend_near",
-    )(place, *tiles, own, k_up[1], k_down[1], v_up[1], v_down[1])
+    )(me[None], text_slots, *tiles, key_states, value_states, k_up[1], k_down[1], v_up[1], v_down[1])
     far = [(k_up[3], v_up[3]), (k_down[3], v_down[3]), (k_up[4], v_down[4]), (k_up[2], v_up[2]), (k_down[2], v_down[2])]
     keep, keep_sum, send = pl.pallas_call(
         functools.partial(far_kernel, factor, 3, len(far)),
@@ -341,7 +323,6 @@
         compiler_params=PARAMS,
         name="finish",
     )(keep, keep_sum, other)
-    swap_side = [(h, h ^ 1) for h in range(head_size)]
     shares = pl.pallas_call(
         project_kernel,
         out_shape=jax.ShapeDtypeStruct((head_size // 2, TILE, width), jnp.bfloat16),

time: 87.7 us -> 142 us (1.62)
  waiting for transfers between devices: 20.1 us -> 66.8 us
  local copies, waits for them, and re-layouts: 9.71 us -> 13.8 us
  starting transfers between devices: 27.7 us -> 29.7 us
    ppermute x3, waiting for transfers between devices: 0.01 us -> 36.6 us  [per_device(): lax.ppermute(packed, 'seq', [(s, s ^ k) for s in range(seq_size)])]
    ppermute x3, starting transfers between devices: 5.08 us -> 12 us  [per_device(): k_down.append(lax.ppermute(k_down[-1], 'seq', down))]
    ppermute x4, waiting for transfers between devices: 2.76 us -> 8.4 us  [per_device(): k_up.append(lax.ppermute(k_up[-1], 'seq', up))]
    unnamed x30 -> x36, local copies, waits for them, and re-layouts: 9.71 us -> 13.8 us
    ppermute x3, starting transfers between devices: 3.01 us -> 0.01 us  [per_device(): v_up.append(lax.ppermute(v_up[-1], 'seq', up))]
    ppermute x3, waiting for transfers between devices: 0.01 us -> 2.85 us  [per_device(): v_up.append(lax.ppermute(v_up[-1], 'seq', up))]
    ppermute x1, starting transfers between devices: 1.97 us -> 0.09 us  [per_device(): lax.ppermute(attended, 'head', swap_side)]
    ppermute x1, waiting for transfers between devices: 5.78 us -> 7.6 us  [per_device(): lax.ppermute(attended, 'head', swap_side)]
  transfers between devices with their start and end apart: 21 -> 21, of which waited for: 6 -> 8; matrix products, arithmetic and copies ran while one was open for 2% -> 1% of each run, Pallas kernels for 12% -> 7%
where the time goes in v10:
time: 142 us; the launch traced here: 141 us
  waiting for transfers between devices  66.8 us (47%)
  starting transfers between devices  29.7 us (21%)
  blocking collectives  15.1 us (11%)
  local copies, waits for them, and re-layouts  13.8 us (10%)
  Pallas kernels  12.7 us (9%)
  other arithmetic  2.43 us (2%)
    ppermute x3, waiting for transfers between devices, per_device(): lax.ppermute(packed, 'seq', [(s, s ^ k) for s in range(seq_size)])  36.6 us
    all_to_all x1, blocking collectives, per_device(): lax.all_to_all(shares, 'head', 0, 0, axis_index_groups=sides, tiled=True)  15.1 us
    unnamed x36, local copies, waits for them, and re-layouts  13.8 us
    ppermute x3, starting transfers between devices, per_device(): k_down.append(lax.ppermute(k_down[-1], 'seq', down))  12 us
    ppermute x4, starting transfers between devices, per_device(): v_down.append(lax.ppermute(v_down[-1], 'seq', down))  11.9 us
    ppermute x4, waiting for transfers between devices, per_device(): k_up.append(lax.ppermute(k_up[-1], 'seq', up))  8.4 us
    ppermute x1, waiting for transfers between devices, per_device(): lax.ppermute(attended, 'head', swap_side)  7.6 us
    ppermute x1, waiting for transfers between devices, per_device(): other = lax.ppermute(send, 'seq', [(s, s ^ 2) for s in range(seq_size)])  7.28 us
  transfers between devices with their start and end apart: 21, of which 8 were waited for; matrix products, arithmetic and copies ran while one was open for 1% of the time, Pallas kernels for 7%

profile of v10, /device:TPU:2, one launch (start us, length us, event | category | flops | bytes accessed | tf_op | source)
XLA Modules:
  0.0 140.7 jit_solution(18418730832481177430)
XLA Ops:
  0.0 2.1 %collective-permute-start.20 = (bf16[384,3072]{1,0:T(8,128)(2,1)}, bf16[384,3072]{1,0:T(8,128)(2,1)}, u32[]{:S(2)}, u32[]{:S(2)}) collective-permute-start(bf16[384,3072]{1,0:T(8,128)(2,1)} %weight_ref.1), channel_id=1, source_target_pairs={{0,1},{1,0},{2,3},{3,2},{4,5},{5,4},{6,7},{7,6},{8,9},{9,8},{10,11... | collective-permute-start | bytes 7077896 | tf_op jit(solution)/shard_map/ppermute | solution.py:248
  2.1 1.9 %collective-permute-start.3 = (bf16[256,384]{1,0:T(8,128)(2,1)}, bf16[256,384]{1,0:T(8,128)(2,1)S(1)}, u32[]{:S(2)}, u32[]{:S(2)}) collective-permute-start(bf16[256,384]{1,0:T(8,128)(2,1)} %refs_4_.1), channel_id=1, source_target_pairs={{0,32},{8,40},{16,48},{24,56},{32,64},{40,72},{48,80},{56,88},{64,... | collective-permute-start | bytes 589832 | tf_op jit(solution)/shard_map/ppermute | solution.py:240
  4.0 3.9 %collective-permute-start.4 = (bf16[256,384]{1,0:T(8,128)(2,1)}, bf16[256,384]{1,0:T(8,128)(2,1)S(1)}, u32[]{:S(2)}, u32[]{:S(2)}) collective-permute-start(bf16[256,384]{1,0:T(8,128)(2,1)} %refs_4_.1), channel_id=1, source_target_pairs={{0,224},{8,232},{16,240},{24,248},{32,0},{40,8},{48,16},{56,24},{6... | collective-permute-start | bytes 589832 | tf_op jit(solution)/shard_map/ppermute | solution.py:242
  8.6 0.9 fusion.1.refs_0_
  9.7 4.3 %collective-permute-done.3.refs_6_ = bf16[256,384]{1,0:T(8,128)(2,1)S(1)} collective-permute-done((bf16[256,384]{1,0:T(8,128)(2,1)}, bf16[256,384]{1,0:T(8,128)(2,1)S(1)}, u32[]{:S(2)}, u32[]{:S(2)}) %collective-permute-start.3) | collective-permute-done | bytes 196640 | tf_op jit(solution)/shard_map/ppermute | solution.py:240
  14.0 2.1 %collective-permute-start.6 = (bf16[256,384]{1,0:T(8,128)(2,1)}, bf16[256,384]{1,0:T(8,128)(2,1)S(1)}, u32[]{:S(2)}, u32[]{:S(2)}) collective-permute-start(bf16[256,384]{1,0:T(8,128)(2,1)} %refs_5_.1), channel_id=1, source_target_pairs={{0,224},{8,232},{16,240},{24,248},{32,0},{40,8},{48,16},{56,24},{6... | collective-permute-start | bytes 589832 | tf_op jit(solution)/shard_map/ppermute | solution.py:244
  16.0 1.4 %collective-permute-start.1 = (bf16[272,384]{1,0:T(8,128)(2,1)S(1)}, bf16[272,384]{1,0:T(8,128)(2,1)S(1)}, u32[]{:S(2)}, u32[]{:S(2)}) collective-permute-start(bf16[272,384]{1,0:T(8,128)(2,1)S(1)} %fusion.1.refs_0_), channel_id=1, source_target_pairs={{0,16},{8,24},{16,0},{24,8},{32,48},{40,56},{48,32},{56,40},{64,80... | collective-permute-start | bytes 626696 | tf_op jit(solution)/shard_map/ppermute | solution.py:255
  17.5 2.4 %collective-permute-done.6.refs_9_ = bf16[256,384]{1,0:T(8,128)(2,1)S(1)} collective-permute-done((bf16[256,384]{1,0:T(8,128)(2,1)}, bf16[256,384]{1,0:T(8,128)(2,1)S(1)}, u32[]{:S(2)}, u32[]{:S(2)}) %collective-permute-start.6) | collective-permute-done | bytes 196640 | tf_op jit(solution)/shard_map/ppermute | solution.py:244
  19.8 3.3 %collective-permute-start.14 = (bf16[256,384]{1,0:T(8,128)(2,1)S(1)}, bf16[256,384]{1,0:T(8,128)(2,1)S(1)}, u32[]{:S(2)}, u32[]{:S(2)}) collective-permute-start(bf16[256,384]{1,0:T(8,128)(2,1)S(1)} %collective-permute-done.6.refs_9_), channel_id=1, source_target_pairs={{0,224},{8,232},{16,240},{24,248},{32,0},{40,8},{48,16},{56,24},{6... | collective-permute-start | bytes 589832 | tf_op jit(solution)/shard_map/ppermute | solution.py:244
  23.8 36.5 %collective-permute-done.1.refs_2_ = bf16[272,384]{1,0:T(8,128)(2,1)S(1)} collective-permute-done((bf16[272,384]{1,0:T(8,128)(2,1)S(1)}, bf16[272,384]{1,0:T(8,128)(2,1)S(1)}, u32[]{:S(2)}, u32[]{:S(2)}) %collective-permute-start.1) | collective-permute-done | bytes 208928 | tf_op jit(solution)/shard_map/ppermute | solution.py:255
  60.4 5.9 %collective-permute-start.9 = (bf16[256,384]{1,0:T(8,128)(2,1)S(1)}, bf16[256,384]{1,0:T(8,128)(2,1)S(1)}, u32[]{:S(2)}, u32[]{:S(2)}) collective-permute-start(bf16[256,384]{1,0:T(8,128)(2,1)S(1)} %collective-permute-done.4.refs_7_), channel_id=1, source_target_pairs={{0,224},{8,232},{16,240},{24,248},{32,0},{40,8},{48,16},{56,24},{6... | collective-permute-start | bytes 589832 | tf_op jit(solution)/shard_map/ppermute | solution.py:242
  67.6 3.3 %collective-permute-start.15 = (bf16[256,384]{1,0:T(8,128)(2,1)S(1)}, bf16[256,384]{1,0:T(8,128)(2,1)S(1)}, u32[]{:S(2)}, u32[]{:S(2)}) collective-permute-start(bf16[256,384]{1,0:T(8,128)(2,1)S(1)} %collective-permute-done.14.refs_9_), channel_id=1, source_target_pairs={{0,224},{8,232},{16,240},{24,248},{32,0},{40,8},{48,16},{56,24},{6... | collective-permute-start | bytes 589832 | tf_op jit(solution)/shard_map/ppermute | solution.py:244
  70.9 2.2 %collective-permute-start.10 = (bf16[256,384]{1,0:T(8,128)(2,1)S(1)}, bf16[256,384]{1,0:T(8,128)(2,1)S(1)}, u32[]{:S(2)}, u32[]{:S(2)}) collective-permute-start(bf16[256,384]{1,0:T(8,128)(2,1)S(1)} %collective-permute-done.9.refs_4_), channel_id=1, source_target_pairs={{0,224},{8,232},{16,240},{24,248},{32,0},{40,8},{48,16},{56,24},{6... | collective-permute-start | bytes 589832 | tf_op jit(solution)/shard_map/ppermute | solution.py:242
  73.1 2.8 %collective-permute-done.12.refs_8_ = bf16[256,384]{1,0:T(8,128)(2,1)S(1)} collective-permute-done((bf16[256,384]{1,0:T(8,128)(2,1)S(1)}, bf16[256,384]{1,0:T(8,128)(2,1)S(1)}, u32[]{:S(2)}, u32[]{:S(2)}) %collective-permute-start.12) | collective-permute-done | bytes 196640 | tf_op jit(solution)/shard_map/ppermute | solution.py:243
  75.9 4.1 %collective-permute-done.8.refs_0_ = bf16[256,384]{1,0:T(8,128)(2,1)S(1)} collective-permute-done((bf16[256,384]{1,0:T(8,128)(2,1)S(1)}, bf16[256,384]{1,0:T(8,128)(2,1)S(1)}, u32[]{:S(2)}, u32[]{:S(2)}) %collective-permute-start.8) | collective-permute-done | bytes 196640 | tf_op jit(solution)/shard_map/ppermute | solution.py:240
  80.1 3.2 %collective-permute-start.16 = (bf16[256,384]{1,0:T(8,128)(2,1)S(1)}, bf16[256,384]{1,0:T(8,128)(2,1)S(1)}, u32[]{:S(2)}, u32[]{:S(2)}) collective-permute-start(bf16[256,384]{1,0:T(8,128)(2,1)S(1)} %collective-permute-done.15.refs_6_), channel_id=1, source_target_pairs={{0,224},{8,232},{16,240},{24,248},{32,0},{40,8},{48,16},{56,24},{6... | collective-permute-start | bytes 589832 | tf_op jit(solution)/shard_map/ppermute | solution.py:244
  83.3 0.9 copy-done.9
  84.2 0.9 copy-done.10
  85.2 0.9 copy-done.12
  86.1 0.9 copy-done.14
  87.0 0.9 copy-done.16
  88.6 5.4 %attend_near.1 = (s32[4,8]{1,0:T(4,128)S(1)}, bf16[4,256,384]{2,1,0:T(8,128)(2,1)S(1)}, f32[12,128,256]{2,1,0:T(8,128)S(1)}, f32[12,1,256]{2,1,0:T(1,128)S(1)}, f32[12,1,256]{2,1,0:T(1,128)S(1)}) custom-call(s32[1]{0:T(128)} %bitcast.1.place_ref, s32[2]{0:T(128)S(1)} %copy-done.17, bf16[272,384]{1,0:T(8,128)(2,1)S(1)} %fusion.1.refs_0_, ...), custom_call_target="tpu_custom_call" | custom-call | flops 905969664 | bytes 4194304 | tf_op jit(solution)/shard_map/attend_near/pallas_call | solution.py:274
  96.7 0.9 copy-done.2
  97.7 0.9 copy-done.4
  98.6 0.9 copy-done.6
  99.5 0.9 copy-done.8
  100.4 4.2 %attend_far.1 = (f32[2,384,256]{2,1,0:T(8,128)S(1)}, f32[2,8,256]{2,1,0:T(8,128)S(1)}, bf16[2,416,256]{2,1,0:T(8,128)(2,1)S(1)}) custom-call(s32[4,8]{1,0:T(4,128)S(1)} %get-tuple-element.16.need_ref, bf16[4,256,384]{2,1,0:T(8,128)(2,1)S(1)} %get-tuple-element.17.stacked_ref, bf16[256,384]{1,0:T(8,128)(2,1)S(1)} %collective-permute-done.8.refs_0_, ...), custom_call_target="tpu_custom_call" | custom-call | flops 905969664 | bytes 4194304 | tf_op jit(solution)/shard_map/attend_far/pallas_call | solution.py:289
  104.8 1.8 %collective-permute-done.17.other_ref = bf16[2,416,256]{2,1,0:T(8,128)(2,1)S(1)} collective-permute-done((bf16[2,416,256]{2,1,0:T(8,128)(2,1)S(1)}, bf16[2,416,256]{2,1,0:T(8,128)(2,1)S(1)}, u32[]{:S(2)}, u32[]{:S(2)}) %collective-permute-start.17) | collective-permute-done | bytes 426016 | tf_op jit(solution)/shard_map/ppermute | solution.py:304
  106.8 7.3 %collective-permute-done.18.other_ref = bf16[1,416,256]{2,1,0:T(8,128)(2,1)S(1)} collective-permute-done((bf16[1,416,256]{2,1,0:T(8,128)(2,1)S(1)}, bf16[1,416,256]{2,1,0:T(8,128)(2,1)S(1)}, u32[]{:S(2)}, u32[]{:S(2)}) %collective-permute-start.18) | collective-permute-done | bytes 213024 | tf_op jit(solution)/shard_map/ppermute | solution.py:317
  114.4 7.6 %collective-permute-done.19.other_ref = bf16[256,384]{1,0:T(8,128)(2,1)S(1)} collective-permute-done((bf16[256,384]{1,0:T(8,128)(2,1)S(1)}, bf16[256,384]{1,0:T(8,128)(2,1)S(1)}, u32[]{:S(2)}, u32[]{:S(2)}) %collective-permute-start.19) | collective-permute-done | bytes 196640 | tf_op jit(solution)/shard_map/ppermute | solution.py:333
  122.0 2.8 %project.1 = bf16[4,256,384]{2,1,0:T(8,128)(2,1)S(1)} custom-call(s32[1]{0:T(128)} %bitcast.side_ref, bf16[256,384]{1,0:T(8,128)(2,1)S(1)} %finish.1.mine_ref, bf16[256,384]{1,0:T(8,128)(2,1)S(1)} %collective-permute-done.19.other_ref, bf16[384,3072]{1,0:T(8,128)(2,1)S(1)} %copy-done, bf16[384,3072]{1,0:T(8,128)(2,1)} %collective-permute-done.20.other_weight_ref), custom_call_target="tpu_custom_call" | custom-call | tf_op jit(solution)/shard_map/project/pallas_call | solution.py:326
  124.8 15.1 %all_to_all.5 = bf16[4,256,384]{2,1,0:T(8,128)(2,1)S(1)} all-to-all(bf16[4,256,384]{2,1,0:T(8,128)(2,1)S(1)} %project.1), channel_id=1, replica_groups={{0,2,4,6},{1,3,5,7},{8,10,12,14},{9,11,13,15},{16,18,20,22},{17,19,21,2..., dimensions={0} | all-to-all | bytes 1572864 | tf_op jit(solution)/shard_map/all_to_all | solution.py:335
  (55 shorter events, 7.7 us)
Async XLA Ops:
  0.0 122.0 %collective-permute-start.20 = (bf16[384,3072]{1,0:T(8,128)(2,1)}, bf16[384,3072]{1,0:T(8,128)(2,1)}, u32[]{:S(2)}, u32[]{:S(2)}) collective-permute-start(bf16[384,3072]{1,0:T(8,128)(2,1)} %weight_ref.1), channel_id=1, source_target_pairs={{0,1},{1,0},{2,3},{3,2},{4,5},{5,4},{6,7},{7,6},{8,9},{9,8},{10,11... | collective-permute-start | bytes 7077896 | tf_op jit(solution)/shard_map/ppermute | solution.py:248
  2.1 11.8 %collective-permute-start.3 = (bf16[256,384]{1,0:T(8,128)(2,1)}, bf16[256,384]{1,0:T(8,128)(2,1)S(1)}, u32[]{:S(2)}, u32[]{:S(2)}) collective-permute-start(bf16[256,384]{1,0:T(8,128)(2,1)} %refs_4_.1), channel_id=1, source_target_pairs={{0,32},{8,40},{16,48},{24,56},{32,64},{40,72},{48,80},{56,88},{64,... | collective-permute-start | bytes 589832 | tf_op jit(solution)/shard_map/ppermute | solution.py:240
  4.0 12.0 %collective-permute-start.4 = (bf16[256,384]{1,0:T(8,128)(2,1)}, bf16[256,384]{1,0:T(8,128)(2,1)S(1)}, u32[]{:S(2)}, u32[]{:S(2)}) collective-permute-start(bf16[256,384]{1,0:T(8,128)(2,1)} %refs_4_.1), channel_id=1, source_target_pairs={{0,224},{8,232},{16,240},{24,248},{32,0},{40,8},{48,16},{56,24},{6... | collective-permute-start | bytes 589832 | tf_op jit(solution)/shard_map/ppermute | solution.py:242
  8.0 9.5 %collective-permute-start.5 = (bf16[256,384]{1,0:T(8,128)(2,1)}, bf16[256,384]{1,0:T(8,128)(2,1)S(1)}, u32[]{:S(2)}, u32[]{:S(2)}) collective-permute-start(bf16[256,384]{1,0:T(8,128)(2,1)} %refs_5_.1), channel_id=1, source_target_pairs={{0,32},{8,40},{16,48},{24,56},{32,64},{40,72},{48,80},{56,88},{64,... | collective-permute-start | bytes 589832 | tf_op jit(solution)/shard_map/ppermute | solution.py:243
  9.6 10.2 %collective-permute-start = (bf16[272,384]{1,0:T(8,128)(2,1)S(1)}, bf16[272,384]{1,0:T(8,128)(2,1)S(1)}, u32[]{:S(2)}, u32[]{:S(2)}) collective-permute-start(bf16[272,384]{1,0:T(8,128)(2,1)S(1)} %fusion.1.refs_0_), channel_id=1, source_target_pairs={{0,8},{8,0},{16,24},{24,16},{32,40},{40,32},{48,56},{56,48},{64,72... | collective-permute-start | bytes 626696 | tf_op jit(solution)/shard_map/ppermute | solution.py:255
  14.0 5.9 %collective-permute-start.6 = (bf16[256,384]{1,0:T(8,128)(2,1)}, bf16[256,384]{1,0:T(8,128)(2,1)S(1)}, u32[]{:S(2)}, u32[]{:S(2)}) collective-permute-start(bf16[256,384]{1,0:T(8,128)(2,1)} %refs_5_.1), channel_id=1, source_target_pairs={{0,224},{8,232},{16,240},{24,248},{32,0},{40,8},{48,16},{56,24},{6... | collective-permute-start | bytes 589832 | tf_op jit(solution)/shard_map/ppermute | solution.py:244
  16.0 44.3 %collective-permute-start.1 = (bf16[272,384]{1,0:T(8,128)(2,1)S(1)}, bf16[272,384]{1,0:T(8,128)(2,1)S(1)}, u32[]{:S(2)}, u32[]{:S(2)}) collective-permute-start(bf16[272,384]{1,0:T(8,128)(2,1)S(1)} %fusion.1.refs_0_), channel_id=1, source_target_pairs={{0,16},{8,24},{16,0},{24,8},{32,48},{40,56},{48,32},{56,40},{64,80... | collective-permute-start | bytes 626696 | tf_op jit(solution)/shard_map/ppermute | solution.py:255
  17.5 49.4 %collective-permute-start.2 = (bf16[272,384]{1,0:T(8,128)(2,1)S(1)}, bf16[272,384]{1,0:T(8,128)(2,1)S(1)}, u32[]{:S(2)}, u32[]{:S(2)}) collective-permute-start(bf16[272,384]{1,0:T(8,128)(2,1)S(1)} %fusion.1.refs_0_), channel_id=1, source_target_pairs={{0,24},{8,16},{16,8},{24,0},{32,56},{40,48},{48,40},{56,32},{64,88... | collective-permute-start | bytes 626696 | tf_op jit(solution)/shard_map/ppermute | solution.py:255
  19.8 47.7 %collective-permute-start.7 = (bf16[256,384]{1,0:T(8,128)(2,1)S(1)}, bf16[256,384]{1,0:T(8,128)(2,1)S(1)}, u32[]{:S(2)}, u32[]{:S(2)}) collective-permute-start(bf16[256,384]{1,0:T(8,128)(2,1)S(1)} %collective-permute-done.3.refs_6_), channel_id=1, source_target_pairs={{0,32},{8,40},{16,48},{24,56},{32,64},{40,72},{48,80},{56,88},{64,... | collective-permute-start | bytes 589832 | tf_op jit(solution)/shard_map/ppermute | solution.py:240
  19.8 47.7 %collective-permute-start.14 = (bf16[256,384]{1,0:T(8,128)(2,1)S(1)}, bf16[256,384]{1,0:T(8,128)(2,1)S(1)}, u32[]{:S(2)}, u32[]{:S(2)}) collective-permute-start(bf16[256,384]{1,0:T(8,128)(2,1)S(1)} %collective-permute-done.6.refs_9_), channel_id=1, source_target_pairs={{0,224},{8,232},{16,240},{24,248},{32,0},{40,8},{48,16},{56,24},{6... | collective-permute-start | bytes 589832 | tf_op jit(solution)/shard_map/ppermute | solution.py:244
  60.4 10.5 %collective-permute-start.9 = (bf16[256,384]{1,0:T(8,128)(2,1)S(1)}, bf16[256,384]{1,0:T(8,128)(2,1)S(1)}, u32[]{:S(2)}, u32[]{:S(2)}) collective-permute-start(bf16[256,384]{1,0:T(8,128)(2,1)S(1)} %collective-permute-done.4.refs_7_), channel_id=1, source_target_pairs={{0,224},{8,232},{16,240},{24,248},{32,0},{40,8},{48,16},{56,24},{6... | collective-permute-start | bytes 589832 | tf_op jit(solution)/shard_map/ppermute | solution.py:242
  66.9 9.0 %collective-permute-start.12 = (bf16[256,384]{1,0:T(8,128)(2,1)S(1)}, bf16[256,384]{1,0:T(8,128)(2,1)S(1)}, u32[]{:S(2)}, u32[]{:S(2)}) collective-permute-start(bf16[256,384]{1,0:T(8,128)(2,1)S(1)} %collective-permute-done.5.refs_8_), channel_id=1, source_target_pairs={{0,32},{8,40},{16,48},{24,56},{32,64},{40,72},{48,80},{56,88},{64,... | collective-permute-start | bytes 589832 | tf_op jit(solution)/shard_map/ppermute | solution.py:243
  67.6 12.5 %collective-permute-start.8 = (bf16[256,384]{1,0:T(8,128)(2,1)S(1)}, bf16[256,384]{1,0:T(8,128)(2,1)S(1)}, u32[]{:S(2)}, u32[]{:S(2)}) collective-permute-start(bf16[256,384]{1,0:T(8,128)(2,1)S(1)} %collective-permute-done.7.refs_3_), channel_id=1, source_target_pairs={{0,32},{8,40},{16,48},{24,56},{32,64},{40,72},{48,80},{56,88},{64,... | collective-permute-start | bytes 589832 | tf_op jit(solution)/shard_map/ppermute | solution.py:240
  67.6 12.5 %collective-permute-start.15 = (bf16[256,384]{1,0:T(8,128)(2,1)S(1)}, bf16[256,384]{1,0:T(8,128)(2,1)S(1)}, u32[]{:S(2)}, u32[]{:S(2)}) collective-permute-start(bf16[256,384]{1,0:T(8,128)(2,1)S(1)} %collective-permute-done.14.refs_9_), channel_id=1, source_target_pairs={{0,224},{8,232},{16,240},{24,248},{32,0},{40,8},{48,16},{56,24},{6... | collective-permute-start | bytes 589832 | tf_op jit(solution)/shard_map/ppermute | solution.py:244
  70.9 23.1 %collective-permute-start.10 = (bf16[256,384]{1,0:T(8,128)(2,1)S(1)}, bf16[256,384]{1,0:T(8,128)(2,1)S(1)}, u32[]{:S(2)}, u32[]{:S(2)}) collective-permute-start(bf16[256,384]{1,0:T(8,128)(2,1)S(1)} %collective-permute-done.9.refs_4_), channel_id=1, source_target_pairs={{0,224},{8,232},{16,240},{24,248},{32,0},{40,8},{48,16},{56,24},{6... | collective-permute-start | bytes 589832 | tf_op jit(solution)/shard_map/ppermute | solution.py:242
  75.9 18.7 %collective-permute-start.13 = (bf16[256,384]{1,0:T(8,128)(2,1)S(1)}, bf16[256,384]{1,0:T(8,128)(2,1)S(1)}, u32[]{:S(2)}, u32[]{:S(2)}) collective-permute-start(bf16[256,384]{1,0:T(8,128)(2,1)S(1)} %collective-permute-done.12.refs_8_), channel_id=1, source_target_pairs={{0,32},{8,40},{16,48},{24,56},{32,64},{40,72},{48,80},{56,88},{64,... | collective-permute-start | bytes 589832 | tf_op jit(solution)/shard_map/ppermute | solution.py:243
  80.1 15.3 %collective-permute-start.11 = (bf16[256,384]{1,0:T(8,128)(2,1)S(1)}, bf16[256,384]{1,0:T(8,128)(2,1)S(1)}, u32[]{:S(2)}, u32[]{:S(2)}) collective-permute-start(bf16[256,384]{1,0:T(8,128)(2,1)S(1)} %collective-permute-done.8.refs_0_), channel_id=1, source_target_pairs={{0,32},{8,40},{16,48},{24,56},{32,64},{40,72},{48,80},{56,88},{64,... | collective-permute-start | bytes 589832 | tf_op jit(solution)/shard_map/ppermute | solution.py:240
  80.1 16.0 %collective-permute-start.16 = (bf16[256,384]{1,0:T(8,128)(2,1)S(1)}, bf16[256,384]{1,0:T(8,128)(2,1)S(1)}, u32[]{:S(2)}, u32[]{:S(2)}) collective-permute-start(bf16[256,384]{1,0:T(8,128)(2,1)S(1)} %collective-permute-done.15.refs_6_), channel_id=1, source_target_pairs={{0,224},{8,232},{16,240},{24,248},{32,0},{40,8},{48,16},{56,24},{6... | collective-permute-start | bytes 589832 | tf_op jit(solution)/shard_map/ppermute | solution.py:244
  83.3 0.9 copy-start.9
  84.2 0.9 copy-start.10
  85.2 0.9 copy-start.12
  86.1 0.9 copy-start.14
  87.0 0.9 copy-start.16
  96.0 0.7 copy-start.7
  96.7 0.9 copy-start.2
  97.7 0.9 copy-start.4
  98.6 0.9 copy-start.6
  99.5 0.9 copy-start.8
  100.4 21.6 %copy-start = (bf16[384,3072]{1,0:T(8,128)(2,1)S(1)}, bf16[384,3072]{1,0:T(8,128)(2,1)}, u32[]{:S(2)}) copy-start(bf16[384,3072]{1,0:T(8,128)(2,1)} %weight_ref.1) | copy-start | bytes 7077892
  104.7 1.9 %collective-permute-start.17 = (bf16[2,416,256]{2,1,0:T(8,128)(2,1)S(1)}, bf16[2,416,256]{2,1,0:T(8,128)(2,1)S(1)}, u32[]{:S(2)}, u32[]{:S(2)}) collective-permute-start(bf16[2,416,256]{2,1,0:T(8,128)(2,1)S(1)} %get-tuple-element.23), channel_id=1, source_target_pairs={{0,8},{8,0},{16,24},{24,16},{32,40},{40,32},{48,56},{56,48},{64,72... | collective-permute-start | bytes 1277960 | tf_op jit(solution)/shard_map/ppermute | solution.py:304
  106.7 7.4 %collective-permute-start.18 = (bf16[1,416,256]{2,1,0:T(8,128)(2,1)S(1)}, bf16[1,416,256]{2,1,0:T(8,128)(2,1)S(1)}, u32[]{:S(2)}, u32[]{:S(2)}) collective-permute-start(bf16[1,416,256]{2,1,0:T(8,128)(2,1)S(1)} %get-tuple-element.26), channel_id=1, source_target_pairs={{0,16},{8,24},{16,0},{24,8},{32,48},{40,56},{48,32},{56,40},{64,80... | collective-permute-start | bytes 638984 | tf_op jit(solution)/shard_map/ppermute | solution.py:317
  114.3 7.7 %collective-permute-start.19 = (bf16[256,384]{1,0:T(8,128)(2,1)S(1)}, bf16[256,384]{1,0:T(8,128)(2,1)S(1)}, u32[]{:S(2)}, u32[]{:S(2)}) collective-permute-start(bf16[256,384]{1,0:T(8,128)(2,1)S(1)} %finish.1.mine_ref), channel_id=1, source_target_pairs={{0,1},{1,0},{2,3},{3,2},{4,5},{5,4},{6,7},{7,6},{8,9},{9,8},{10,11... | collective-permute-start | bytes 589832 | tf_op jit(solution)/shard_map/ppermute | solution.py:333
  (7 other events, 4.7 us)

commit v11 on v9

--- a/solution.py
+++ b/solution.py
@@ -131,8 +131,9 @@
     lax.fori_loop(0, q_ref.shape[0], visit, 0)
 
 
-def list_wanted(seq_size, order, place_ref, q_refs, need_ref):
-    slots = [lax.rem(place_ref[0] + (GROUP * plane + seq_size), seq_size) for plane in order]
+def list_wanted(seq_size, order, text_ref, q_refs, need_ref):
+    me = lax.axis_index("seq")
+    slots = [lax.rem(me + (GROUP * plane + seq_size), seq_size) for plane in order]
     for t, q_ref in enumerate(q_refs):
         row = q_ref[TILE:TILE + PART_ROWS, 0:HD].astype(jnp.float32)
         bits = jnp.zeros_like(row)
@@ -141,21 +142,21 @@
         code = jnp.sum(bits).astype(jnp.int32)
         for j, slot in enumerate(slots):
             wanted = (code >> j) & 1
-            for i in range(1, place_ref.shape[0]):
-                wanted = jnp.where(slot == place_ref[i], 1, wanted)
+            for i in range(text_ref.shape[0]):
+                wanted = jnp.where(slot == text_ref[i], 1, wanted)
             need_ref[t, j] = wanted
 
 
-def near_kernel(factor, seq_size, order, place_ref, *refs):
-    q_refs, (own_ref, k_low, k_high, v_low, v_high) = refs[:GROUP], refs[GROUP:GROUP + 5]
-    need_ref, stacked_ref, acc_ref, peak_ref, total_ref, k_ref, vt_ref = refs[GROUP + 5:]
-    list_wanted(seq_size, order, place_ref, q_refs, need_ref)
+def near_kernel(factor, seq_size, order, text_ref, *refs):
+    q_refs, (k_own, v_own, k_low, k_high, v_low, v_high) = refs[:GROUP], refs[GROUP:GROUP + 6]
+    need_ref, stacked_ref, acc_ref, peak_ref, total_ref, k_ref, vt_ref = refs[GROUP + 6:]
+    list_wanted(seq_size, order, text_ref, q_refs, need_ref)
     acc_ref[...] = jnp.zeros_like(acc_ref)
     peak_ref[...] = jnp.full_like(peak_ref, LOWEST)
     total_ref[...] = jnp.zeros_like(total_ref)
     for t, q_ref in enumerate(q_refs):
         stacked_ref[t] = q_ref[0:TILE, :]
-    shards = [(own_ref.at[0:TILE], own_ref.at[TILE:2 * TILE]), (k_low, v_low), (k_high, v_high)]
+    shards = [(k_own, v_own), (k_low, v_low), (k_high, v_high)]
     load_shards(need_ref, 0, shards, k_ref, vt_ref)
     visit_shards(factor, need_ref, 0, 3, stacked_ref, k_ref, vt_ref, (acc_ref, peak_ref, total_ref))
 
@@ -204,17 +205,19 @@
         out_ref[:, h * HD:(h + 1) * HD] = outs[h].T.astype(jnp.bfloat16)
 
 
-def pick_kernel(side_ref, weight_ref, out_ref):
+def pick_kernel(weight_ref, out_ref):
     width = weight_ref.shape[0]
+    side = lax.rem(lax.axis_index("head"), 2)
     for j in range(out_ref.shape[1] // width):
-        begin = pl.multiple_of((2 * j + 1 - side_ref[0]) * width, HD)
+        begin = pl.multiple_of((2 * j + 1 - side) * width, HD)
         out_ref[:, j * width:(j + 1) * width] = weight_ref[:, pl.ds(begin, width)]
 
 
-def project_kernel(side_ref, mine_ref, other_ref, weight_ref, other_weight_ref, out_ref):
+def project_kernel(mine_ref, other_ref, weight_ref, other_weight_ref, out_ref):
     shares, _, width = out_ref.shape
+    side = lax.rem(lax.axis_index("head"), 2)
     for j in range(shares):
-        begin = pl.multiple_of((2 * j + side_ref[0]) * width, HD)
+        begin = pl.multiple_of((2 * j + side) * width, HD)
         mixed = jnp.dot(mine_ref[...], weight_ref[:, pl.ds(begin, width)], preferred_element_type=jnp.float32)
         mixed = mixed + jnp.dot(
             other_ref[...], other_weight_ref[:, j * width:(j + 1) * width], preferred_element_type=jnp.float32
@@ -239,7 +242,6 @@
     width = queries.shape[1]
     heads = width // HD
     planes = seq_size // GROUP
-    me = lax.axis_index("seq")
     up = [(s, (s + GROUP) % seq_size) for s in range(seq_size)]
     down = [(s, (s - GROUP) % seq_size) for s in range(seq_size)]
 
@@ -252,15 +254,14 @@
             v_up.append(lax.ppermute(v_up[-1], "seq", up))
         v_down.append(lax.ppermute(v_down[-1], "seq", down))
 
-    side = lax.axis_index("head") % 2
     picked = pl.pallas_call(
         pick_kernel,
         out_shape=jax.ShapeDtypeStruct((width, head_size // 2 * width), out_weight.dtype),
-        in_specs=[pl.BlockSpec(memory_space=pltpu.SMEM)] + vmem_specs(1),
+        in_specs=vmem_specs(1),
         out_specs=pl.BlockSpec(memory_space=pltpu.VMEM),
         compiler_params=PARAMS,
         name="pick",
-    )(side[None], out_weight)
+    )(out_weight)
     other_weight = lax.ppermute(picked, "head", [(h, h ^ 1) for h in range(head_size)])
 
     listed = jnp.pad(
@@ -271,7 +272,6 @@
         lax.ppermute(packed, "seq", [(s, s ^ k) for s in range(seq_size)]) for k in range(1, GROUP)
     ]
     order = (0, -1, 1, -3, 3, 4, -2, 2)
-    place = jnp.concatenate([me.astype(jnp.int32)[None], text_slots])
 
     rows = GROUP * heads
     state = (
@@ -288,7 +288,6 @@
             pltpu.VMEM((count, heads, HD, TILE), jnp.bfloat16),
         ]
 
-    own = jnp.concatenate([key_states, value_states], axis=0)
     need, stacked, *held = pl.pallas_call(
         functools.partial(near_kernel, factor, seq_size, order),
         out_shape=(
@@ -296,13 +295,13 @@
             jax.ShapeDtypeStruct((GROUP, TILE, width), jnp.bfloat16),
         )
         + state,
-        in_specs=smem + vmem_specs(GROUP + 5),
+        in_specs=smem + vmem_specs(GROUP + 6),
         out_specs=tuple(smem + vmem_specs(4)),
         scratch_shapes=scratch(3),
         compiler_params=PARAMS,
         cost_estimate=attend_cost(27),
         name="attend_near",
-    )(place, *tiles, own, k_up[1], k_down[1], v_up[1], v_down[1])
+    )(text_slots, *tiles, key_states, value_states, k_up[1], k_down[1], v_up[1], v_down[1])
     far = [(k_up[3], v_up[3]), (k_down[3], v_down[3]), (k_up[4], v_down[4]), (k_up[2], v_up[2]), (k_down[2], v_down[2])]
     keep, keep_sum, send = pl.pallas_call(
         functools.partial(far_kernel, factor, 3, len(far)),
@@ -345,11 +344,11 @@
     shares = pl.pallas_call(
         project_kernel,
         out_shape=jax.ShapeDtypeStruct((head_size // 2, TILE, width), jnp.bfloat16),
-        in_specs=smem + vmem_specs(4),
+        in_specs=vmem_specs(4),
         out_specs=pl.BlockSpec(memory_space=pltpu.VMEM),
         compiler_params=PARAMS,
         name="project",
-    )(side[None], attended, lax.ppermute(attended, "head", swap_side), out_weight, other_weight)
+    )(attended, lax.ppermute(attended, "head", swap_side), out_weight, other_weight)
     sides = [list(range(k, head_size, 2)) for k in range(2)]
     shares = lax.all_to_all(shares, "head", 0, 0, axis_index_groups=sides, tiled=True)
     return jnp.sum(shares.astype(jnp.float32), axis=0).astype(jnp.bfloat16)

time: 87.7 us -> 82.9 us (0.945)
  local copies, waits for them, and re-layouts: 9.71 us -> 1.68 us
  waiting for transfers between devices: 20.1 us -> 28.1 us
  Pallas kernels: 11.8 us -> 10.2 us
  blocking collectives: 15.2 us -> 13.8 us
  starting transfers between devices: 27.7 us -> 26.5 us
    unnamed x30 -> x10, local copies, waits for them, and re-layouts: 9.71 us -> 1.68 us
    ppermute x1, waiting for transfers between devices: 7.82 us -> 12.3 us  [per_device(): other = lax.ppermute(send, 'seq', [(s, s ^ 2) for s in range(seq_size)])]
    ppermute x4, waiting for transfers between devices: 1.93 us -> 5.77 us  [per_device(): v_down.append(lax.ppermute(v_down[-1], 'seq', down))]
    all_to_all x1, blocking collectives: 15.2 us -> 13.8 us  [per_device(): lax.all_to_all(shares, 'head', 0, 0, axis_index_groups=sides, tiled=True)]
    ppermute x1, starting transfers between devices: 1.97 us -> 0.7 us  [per_device(): lax.ppermute(attended, 'head', swap_side)]
    ppermute x4, waiting for transfers between devices: 2.76 us -> 1.67 us  [per_device(): k_up.append(lax.ppermute(k_up[-1], 'seq', up))]
    pallas_call x1, Pallas kernels: 5.29 us -> 4.35 us  [per_device(): pl.pallas_call(functools.partial(near_kernel, factor, seq_size, order), o...]
  transfers between devices with their start and end apart: 21 -> 21, of which waited for: 6 -> 7; matrix products, arithmetic and copies ran while one was open for 2% -> 2% of each run, Pallas kernels for 12% -> 11%
where the time goes in v11:
time: 82.9 us; the launch traced here: 82.8 us
  waiting for transfers between devices  28.1 us (34%)
  starting transfers between devices  26.5 us (32%)
  blocking collectives  13.8 us (17%)
  Pallas kernels  10.2 us (12%)
  other arithmetic  2.48 us (3%)
  local copies, waits for them, and re-layouts  1.68 us (2%)
    all_to_all x1, blocking collectives, per_device(): lax.all_to_all(shares, 'head', 0, 0, axis_index_groups=sides, tiled=True)  13.8 us
    ppermute x1, waiting for transfers between devices, per_device(): other = lax.ppermute(send, 'seq', [(s, s ^ 2) for s in range(seq_size)])  12.3 us
    ppermute x4, starting transfers between devices, per_device(): v_down.append(lax.ppermute(v_down[-1], 'seq', down))  12.3 us
    ppermute x1, waiting for transfers between devices, per_device(): lax.ppermute(attended, 'head', swap_side)  6.55 us
    ppermute x4, waiting for transfers between devices, per_device(): v_down.append(lax.ppermute(v_down[-1], 'seq', down))  5.77 us
    ppermute x3, starting transfers between devices, per_device(): k_down.append(lax.ppermute(k_down[-1], 'seq', down))  4.98 us
    pallas_call x1, Pallas kernels, per_device(): pl.pallas_call(functools.partial(near_kernel, factor, seq_size, order), o...  4.35 us
    pallas_call x1, Pallas kernels, per_device(): pl.pallas_call(functools.partial(far_kernel, factor, 3, len(far)), out_sh...  4.24 us
  transfers between devices with their start and end apart: 21, of which 7 were waited for; matrix products, arithmetic and copies ran while one was open for 2% of the time, Pallas kernels for 11%

profile of v11, /device:TPU:2, one launch (start us, length us, event | category | flops | bytes accessed | tf_op | source)
XLA Modules:
  0.0 82.8 jit_solution(16253366740431723961)
XLA Ops:
  0.0 1.9 %collective-permute-start.3 = (bf16[256,384]{1,0:T(8,128)(2,1)}, bf16[256,384]{1,0:T(8,128)(2,1)S(1)}, u32[]{:S(2)}, u32[]{:S(2)}) collective-permute-start(bf16[256,384]{1,0:T(8,128)(2,1)} %refs_4_.1), channel_id=1, source_target_pairs={{0,32},{8,40},{16,48},{24,56},{32,64},{40,72},{48,80},{56,88},{64,... | collective-permute-start | bytes 589832 | tf_op jit(solution)/shard_map/ppermute | solution.py:251
  1.9 3.9 %collective-permute-start.4 = (bf16[256,384]{1,0:T(8,128)(2,1)}, bf16[256,384]{1,0:T(8,128)(2,1)S(1)}, u32[]{:S(2)}, u32[]{:S(2)}) collective-permute-start(bf16[256,384]{1,0:T(8,128)(2,1)} %refs_4_.1), channel_id=1, source_target_pairs={{0,224},{8,232},{16,240},{24,248},{32,0},{40,8},{48,16},{56,24},{6... | collective-permute-start | bytes 589832 | tf_op jit(solution)/shard_map/ppermute | solution.py:253
  5.9 2.0 %collective-permute-start.6 = (bf16[256,384]{1,0:T(8,128)(2,1)}, bf16[256,384]{1,0:T(8,128)(2,1)S(1)}, u32[]{:S(2)}, u32[]{:S(2)}) collective-permute-start(bf16[256,384]{1,0:T(8,128)(2,1)} %refs_5_.1), channel_id=1, source_target_pairs={{0,224},{8,232},{16,240},{24,248},{32,0},{40,8},{48,16},{56,24},{6... | collective-permute-start | bytes 589832 | tf_op jit(solution)/shard_map/ppermute | solution.py:255
  7.9 0.7 convert.5
  8.6 1.0 %fusion.1.refs_0_ = bf16[272,384]{1,0:T(8,128)(2,1)S(1)} fusion(bf16[1,27]{1,0:T(2,128)(2,1)S(1)} %convert.5, bf16[256,384]{1,0:T(8,128)(2,1)} %param.6), kind=kLoop, calls=%fused_computation.2 | loop fusion | flops 626688 | bytes 405558 | tf_op jit(solution)/shard_map/concatenate | solution.py:270
  9.7 1.3 %collective-permute-done.3.refs_6_ = bf16[256,384]{1,0:T(8,128)(2,1)S(1)} collective-permute-done((bf16[256,384]{1,0:T(8,128)(2,1)}, bf16[256,384]{1,0:T(8,128)(2,1)S(1)}, u32[]{:S(2)}, u32[]{:S(2)}) %collective-permute-start.3) | collective-permute-done | bytes 196640 | tf_op jit(solution)/shard_map/ppermute | solution.py:251
  11.0 0.5 collective-permute-start.1
  11.5 0.3 collective-permute-start.7
  11.8 2.7 %collective-permute-done.6.refs_9_ = bf16[256,384]{1,0:T(8,128)(2,1)S(1)} collective-permute-done((bf16[256,384]{1,0:T(8,128)(2,1)}, bf16[256,384]{1,0:T(8,128)(2,1)S(1)}, u32[]{:S(2)}, u32[]{:S(2)}) %collective-permute-start.6) | collective-permute-done | bytes 196640 | tf_op jit(solution)/shard_map/ppermute | solution.py:255
  14.6 3.6 %collective-permute-start.14 = (bf16[256,384]{1,0:T(8,128)(2,1)S(1)}, bf16[256,384]{1,0:T(8,128)(2,1)S(1)}, u32[]{:S(2)}, u32[]{:S(2)}) collective-permute-start(bf16[256,384]{1,0:T(8,128)(2,1)S(1)} %collective-permute-done.6.refs_9_), channel_id=1, source_target_pairs={{0,224},{8,232},{16,240},{24,248},{32,0},{40,8},{48,16},{56,24},{6... | collective-permute-start | bytes 589832 | tf_op jit(solution)/shard_map/ppermute | solution.py:255
  18.1 0.6 collective-permute-start.9
  18.8 1.5 %collective-permute-start.12 = (bf16[256,384]{1,0:T(8,128)(2,1)S(1)}, bf16[256,384]{1,0:T(8,128)(2,1)S(1)}, u32[]{:S(2)}, u32[]{:S(2)}) collective-permute-start(bf16[256,384]{1,0:T(8,128)(2,1)S(1)} %collective-permute-done.5.refs_8_), channel_id=1, source_target_pairs={{0,32},{8,40},{16,48},{24,56},{32,64},{40,72},{48,80},{56,88},{64,... | collective-permute-start | bytes 589832 | tf_op jit(solution)/shard_map/ppermute | solution.py:254
  20.3 3.1 %collective-permute-done.14.refs_9_ = bf16[256,384]{1,0:T(8,128)(2,1)S(1)} collective-permute-done((bf16[256,384]{1,0:T(8,128)(2,1)S(1)}, bf16[256,384]{1,0:T(8,128)(2,1)S(1)}, u32[]{:S(2)}, u32[]{:S(2)}) %collective-permute-start.14) | collective-permute-done | bytes 196640 | tf_op jit(solution)/shard_map/ppermute | solution.py:255
  23.4 3.7 %collective-permute-start.15 = (bf16[256,384]{1,0:T(8,128)(2,1)S(1)}, bf16[256,384]{1,0:T(8,128)(2,1)S(1)}, u32[]{:S(2)}, u32[]{:S(2)}) collective-permute-start(bf16[256,384]{1,0:T(8,128)(2,1)S(1)} %collective-permute-done.14.refs_9_), channel_id=1, source_target_pairs={{0,224},{8,232},{16,240},{24,248},{32,0},{40,8},{48,16},{56,24},{6... | collective-permute-start | bytes 589832 | tf_op jit(solution)/shard_map/ppermute | solution.py:255
  27.1 1.7 %copy-done = bf16[384,3072]{1,0:T(8,128)(2,1)S(1)} copy-done((bf16[384,3072]{1,0:T(8,128)(2,1)S(1)}, bf16[384,3072]{1,0:T(8,128)(2,1)}, u32[]{:S(2)}) %copy-start) | copy-done | bytes 2359320
  28.9 2.0 %collective-permute-start.20 = (bf16[384,1536]{1,0:T(8,128)(2,1)S(1)}, bf16[384,1536]{1,0:T(8,128)(2,1)S(1)}, u32[]{:S(2)}, u32[]{:S(2)}) collective-permute-start(bf16[384,1536]{1,0:T(8,128)(2,1)S(1)} %pick.1), channel_id=1, source_target_pairs={{0,1},{1,0},{2,3},{3,2},{4,5},{5,4},{6,7},{7,6},{8,9},{9,8},{10,11... | collective-permute-start | bytes 3538952 | tf_op jit(solution)/shard_map/ppermute | solution.py:265
  30.9 0.4 collective-permute-start.10
  31.3 1.6 %collective-permute-start.13 = (bf16[256,384]{1,0:T(8,128)(2,1)S(1)}, bf16[256,384]{1,0:T(8,128)(2,1)S(1)}, u32[]{:S(2)}, u32[]{:S(2)}) collective-permute-start(bf16[256,384]{1,0:T(8,128)(2,1)S(1)} %collective-permute-done.12.refs_8_), channel_id=1, source_target_pairs={{0,32},{8,40},{16,48},{24,56},{32,64},{40,72},{48,80},{56,88},{64,... | collective-permute-start | bytes 589832 | tf_op jit(solution)/shard_map/ppermute | solution.py:254
  32.9 0.3 collective-permute-start.11
  33.2 3.0 %collective-permute-start.16 = (bf16[256,384]{1,0:T(8,128)(2,1)S(1)}, bf16[256,384]{1,0:T(8,128)(2,1)S(1)}, u32[]{:S(2)}, u32[]{:S(2)}) collective-permute-start(bf16[256,384]{1,0:T(8,128)(2,1)S(1)} %collective-permute-done.15.refs_6_), channel_id=1, source_target_pairs={{0,224},{8,232},{16,240},{24,248},{32,0},{40,8},{48,16},{56,24},{6... | collective-permute-start | bytes 589832 | tf_op jit(solution)/shard_map/ppermute | solution.py:255
  36.2 4.3 %attend_near.1 = (s32[4,8]{1,0:T(4,128)S(1)}, bf16[4,256,384]{2,1,0:T(8,128)(2,1)S(1)}, f32[12,128,256]{2,1,0:T(8,128)S(1)}, f32[12,1,256]{2,1,0:T(1,128)S(1)}, f32[12,1,256]{2,1,0:T(1,128)S(1)}) custom-call(s32[2]{0:T(128)S(1)} %copy-done.4, bf16[272,384]{1,0:T(8,128)(2,1)S(1)} %fusion.1.refs_0_, bf16[272,384]{1,0:T(8,128)(2,1)S(1)} %collective-permute-done.refs_1_, ...), custom_call_target="tpu_custom_call" | custom-call | flops 905969664 | bytes 4194304 | tf_op jit(solution)/shard_map/attend_near/pallas_call | solution.py:291
  40.5 0.3 collective-permute-done.11.refs_2_
  40.9 4.2 %attend_far.1 = (f32[2,384,256]{2,1,0:T(8,128)S(1)}, f32[2,8,256]{2,1,0:T(8,128)S(1)}, bf16[2,416,256]{2,1,0:T(8,128)(2,1)S(1)}) custom-call(s32[4,8]{1,0:T(4,128)S(1)} %get-tuple-element.16.need_ref, bf16[4,256,384]{2,1,0:T(8,128)(2,1)S(1)} %get-tuple-element.17.stacked_ref, bf16[256,384]{1,0:T(8,128)(2,1)S(1)} %collective-permute-done.8.refs_0_, ...), custom_call_target="tpu_custom_call" | custom-call | flops 905969664 | bytes 4194304 | tf_op jit(solution)/shard_map/attend_far/pallas_call | solution.py:306
  45.2 1.8 %collective-permute-done.17.other_ref = bf16[2,416,256]{2,1,0:T(8,128)(2,1)S(1)} collective-permute-done((bf16[2,416,256]{2,1,0:T(8,128)(2,1)S(1)}, bf16[2,416,256]{2,1,0:T(8,128)(2,1)S(1)}, u32[]{:S(2)}, u32[]{:S(2)}) %collective-permute-start.17) | collective-permute-done | bytes 426016 | tf_op jit(solution)/shard_map/ppermute | solution.py:321
  47.0 0.2 merge.1
  47.3 12.3 %collective-permute-done.18.other_ref = bf16[1,416,256]{2,1,0:T(8,128)(2,1)S(1)} collective-permute-done((bf16[1,416,256]{2,1,0:T(8,128)(2,1)S(1)}, bf16[1,416,256]{2,1,0:T(8,128)(2,1)S(1)}, u32[]{:S(2)}, u32[]{:S(2)}) %collective-permute-start.18) | collective-permute-done | bytes 213024 | tf_op jit(solution)/shard_map/ppermute | solution.py:334
  59.6 0.2 finish.1.mine_ref
  59.8 0.7 collective-permute-start.19
  60.5 6.6 %collective-permute-done.19.other_ref = bf16[256,384]{1,0:T(8,128)(2,1)S(1)} collective-permute-done((bf16[256,384]{1,0:T(8,128)(2,1)S(1)}, bf16[256,384]{1,0:T(8,128)(2,1)S(1)}, u32[]{:S(2)}, u32[]{:S(2)}) %collective-permute-start.19) | collective-permute-done | bytes 196640 | tf_op jit(solution)/shard_map/ppermute | solution.py:351
  67.1 1.1 %project.1 = bf16[4,256,384]{2,1,0:T(8,128)(2,1)S(1)} custom-call(bf16[256,384]{1,0:T(8,128)(2,1)S(1)} %finish.1.mine_ref, bf16[256,384]{1,0:T(8,128)(2,1)S(1)} %collective-permute-done.19.other_ref, bf16[384,3072]{1,0:T(8,128)(2,1)S(1)} %copy-done.1, bf16[384,1536]{1,0:T(8,128)(2,1)S(1)} %collective-permute-done.20.other_weight_ref), custom_call_target="tpu_custom_call" | custom-call | tf_op jit(solution)/shard_map/project/pallas_call | solution.py:344
  68.2 13.8 %all_to_all.5 = bf16[4,256,384]{2,1,0:T(8,128)(2,1)S(1)} all-to-all(bf16[4,256,384]{2,1,0:T(8,128)(2,1)S(1)} %project.1), channel_id=1, replica_groups={{0,2,4,6},{1,3,5,7},{8,10,12,14},{9,11,13,15},{16,18,20,22},{17,19,21,2..., dimensions={0} | all-to-all | bytes 1572864 | tf_op jit(solution)/shard_map/all_to_all | solution.py:353
  82.0 0.8 reduce_sum.12
  (30 shorter events, 0.5 us)
Async XLA Ops:
  0.0 11.0 %collective-permute-start.3 = (bf16[256,384]{1,0:T(8,128)(2,1)}, bf16[256,384]{1,0:T(8,128)(2,1)S(1)}, u32[]{:S(2)}, u32[]{:S(2)}) collective-permute-start(bf16[256,384]{1,0:T(8,128)(2,1)} %refs_4_.1), channel_id=1, source_target_pairs={{0,32},{8,40},{16,48},{24,56},{32,64},{40,72},{48,80},{56,88},{64,... | collective-permute-start | bytes 589832 | tf_op jit(solution)/shard_map/ppermute | solution.py:251
  1.9 9.6 %collective-permute-start.4 = (bf16[256,384]{1,0:T(8,128)(2,1)}, bf16[256,384]{1,0:T(8,128)(2,1)S(1)}, u32[]{:S(2)}, u32[]{:S(2)}) collective-permute-start(bf16[256,384]{1,0:T(8,128)(2,1)} %refs_4_.1), channel_id=1, source_target_pairs={{0,224},{8,232},{16,240},{24,248},{32,0},{40,8},{48,16},{56,24},{6... | collective-permute-start | bytes 589832 | tf_op jit(solution)/shard_map/ppermute | solution.py:253
  5.9 8.7 %collective-permute-start.6 = (bf16[256,384]{1,0:T(8,128)(2,1)}, bf16[256,384]{1,0:T(8,128)(2,1)S(1)}, u32[]{:S(2)}, u32[]{:S(2)}) collective-permute-start(bf16[256,384]{1,0:T(8,128)(2,1)} %refs_5_.1), channel_id=1, source_target_pairs={{0,224},{8,232},{16,240},{24,248},{32,0},{40,8},{48,16},{56,24},{6... | collective-permute-start | bytes 589832 | tf_op jit(solution)/shard_map/ppermute | solution.py:255
  7.9 10.3 %collective-permute-start.5 = (bf16[256,384]{1,0:T(8,128)(2,1)}, bf16[256,384]{1,0:T(8,128)(2,1)S(1)}, u32[]{:S(2)}, u32[]{:S(2)}) collective-permute-start(bf16[256,384]{1,0:T(8,128)(2,1)} %refs_5_.1), channel_id=1, source_target_pairs={{0,32},{8,40},{16,48},{24,56},{32,64},{40,72},{48,80},{56,88},{64,... | collective-permute-start | bytes 589832 | tf_op jit(solution)/shard_map/ppermute | solution.py:254
  8.5 27.6 %copy-start.2 = (bf16[256,384]{1,0:T(8,128)(2,1)S(1)}, bf16[256,384]{1,0:T(8,128)(2,1)}, u32[]{:S(2)}) copy-start(bf16[256,384]{1,0:T(8,128)(2,1)} %refs_4_.1) | copy-start | bytes 589828
  8.5 27.6 %copy-start.3 = (bf16[256,384]{1,0:T(8,128)(2,1)S(1)}, bf16[256,384]{1,0:T(8,128)(2,1)}, u32[]{:S(2)}) copy-start(bf16[256,384]{1,0:T(8,128)(2,1)} %refs_5_.1) | copy-start | bytes 589828
  8.6 27.6 %copy-start.4 = (s32[2]{0:T(128)S(1)}, s32[2]{0:T(128)}, u32[]{:S(2)}) copy-start(s32[2]{0:T(128)} %text_ref.1) | copy-start | bytes 28
  9.6 8.6 %collective-permute-start = (bf16[272,384]{1,0:T(8,128)(2,1)S(1)}, bf16[272,384]{1,0:T(8,128)(2,1)S(1)}, u32[]{:S(2)}, u32[]{:S(2)}) collective-permute-start(bf16[272,384]{1,0:T(8,128)(2,1)S(1)} %fusion.1.refs_0_), channel_id=1, source_target_pairs={{0,8},{8,0},{16,24},{24,16},{32,40},{40,32},{48,56},{56,48},{64,72... | collective-permute-start | bytes 626696 | tf_op jit(solution)/shard_map/ppermute | solution.py:272
  11.0 7.8 %collective-permute-start.1 = (bf16[272,384]{1,0:T(8,128)(2,1)S(1)}, bf16[272,384]{1,0:T(8,128)(2,1)S(1)}, u32[]{:S(2)}, u32[]{:S(2)}) collective-permute-start(bf16[272,384]{1,0:T(8,128)(2,1)S(1)} %fusion.1.refs_0_), channel_id=1, source_target_pairs={{0,16},{8,24},{16,0},{24,8},{32,48},{40,56},{48,32},{56,40},{64,80... | collective-permute-start | bytes 626696 | tf_op jit(solution)/shard_map/ppermute | solution.py:272
  11.5 8.8 %collective-permute-start.7 = (bf16[256,384]{1,0:T(8,128)(2,1)S(1)}, bf16[256,384]{1,0:T(8,128)(2,1)S(1)}, u32[]{:S(2)}, u32[]{:S(2)}) collective-permute-start(bf16[256,384]{1,0:T(8,128)(2,1)S(1)} %collective-permute-done.3.refs_6_), channel_id=1, source_target_pairs={{0,32},{8,40},{16,48},{24,56},{32,64},{40,72},{48,80},{56,88},{64,... | collective-permute-start | bytes 589832 | tf_op jit(solution)/shard_map/ppermute | solution.py:251
  14.6 8.9 %collective-permute-start.14 = (bf16[256,384]{1,0:T(8,128)(2,1)S(1)}, bf16[256,384]{1,0:T(8,128)(2,1)S(1)}, u32[]{:S(2)}, u32[]{:S(2)}) collective-permute-start(bf16[256,384]{1,0:T(8,128)(2,1)S(1)} %collective-permute-done.6.refs_9_), channel_id=1, source_target_pairs={{0,224},{8,232},{16,240},{24,248},{32,0},{40,8},{48,16},{56,24},{6... | collective-permute-start | bytes 589832 | tf_op jit(solution)/shard_map/ppermute | solution.py:255
  18.1 10.7 %collective-permute-start.2 = (bf16[272,384]{1,0:T(8,128)(2,1)S(1)}, bf16[272,384]{1,0:T(8,128)(2,1)S(1)}, u32[]{:S(2)}, u32[]{:S(2)}) collective-permute-start(bf16[272,384]{1,0:T(8,128)(2,1)S(1)} %fusion.1.refs_0_), channel_id=1, source_target_pairs={{0,24},{8,16},{16,8},{24,0},{32,56},{40,48},{48,40},{56,32},{64,88... | collective-permute-start | bytes 626696 | tf_op jit(solution)/shard_map/ppermute | solution.py:272
  18.1 12.7 %collective-permute-start.9 = (bf16[256,384]{1,0:T(8,128)(2,1)S(1)}, bf16[256,384]{1,0:T(8,128)(2,1)S(1)}, u32[]{:S(2)}, u32[]{:S(2)}) collective-permute-start(bf16[256,384]{1,0:T(8,128)(2,1)S(1)} %collective-permute-done.4.refs_7_), channel_id=1, source_target_pairs={{0,224},{8,232},{16,240},{24,248},{32,0},{40,8},{48,16},{56,24},{6... | collective-permute-start | bytes 589832 | tf_op jit(solution)/shard_map/ppermute | solution.py:253
  18.8 12.6 %collective-permute-start.12 = (bf16[256,384]{1,0:T(8,128)(2,1)S(1)}, bf16[256,384]{1,0:T(8,128)(2,1)S(1)}, u32[]{:S(2)}, u32[]{:S(2)}) collective-permute-start(bf16[256,384]{1,0:T(8,128)(2,1)S(1)} %collective-permute-done.5.refs_8_), channel_id=1, source_target_pairs={{0,32},{8,40},{16,48},{24,56},{32,64},{40,72},{48,80},{56,88},{64,... | collective-permute-start | bytes 589832 | tf_op jit(solution)/shard_map/ppermute | solution.py:254
  20.3 12.6 %collective-permute-start.8 = (bf16[256,384]{1,0:T(8,128)(2,1)S(1)}, bf16[256,384]{1,0:T(8,128)(2,1)S(1)}, u32[]{:S(2)}, u32[]{:S(2)}) collective-permute-start(bf16[256,384]{1,0:T(8,128)(2,1)S(1)} %collective-permute-done.7.refs_3_), channel_id=1, source_target_pairs={{0,32},{8,40},{16,48},{24,56},{32,64},{40,72},{48,80},{56,88},{64,... | collective-permute-start | bytes 589832 | tf_op jit(solution)/shard_map/ppermute | solution.py:251
  23.4 9.8 %collective-permute-start.15 = (bf16[256,384]{1,0:T(8,128)(2,1)S(1)}, bf16[256,384]{1,0:T(8,128)(2,1)S(1)}, u32[]{:S(2)}, u32[]{:S(2)}) collective-permute-start(bf16[256,384]{1,0:T(8,128)(2,1)S(1)} %collective-permute-done.14.refs_9_), channel_id=1, source_target_pairs={{0,224},{8,232},{16,240},{24,248},{32,0},{40,8},{48,16},{56,24},{6... | collective-permute-start | bytes 589832 | tf_op jit(solution)/shard_map/ppermute | solution.py:255
  27.1 1.7 %copy-start = (bf16[384,3072]{1,0:T(8,128)(2,1)S(1)}, bf16[384,3072]{1,0:T(8,128)(2,1)}, u32[]{:S(2)}) copy-start(bf16[384,3072]{1,0:T(8,128)(2,1)} %weight_ref.3) | copy-start | bytes 7077892
  28.9 31.6 %collective-permute-start.20 = (bf16[384,1536]{1,0:T(8,128)(2,1)S(1)}, bf16[384,1536]{1,0:T(8,128)(2,1)S(1)}, u32[]{:S(2)}, u32[]{:S(2)}) collective-permute-start(bf16[384,1536]{1,0:T(8,128)(2,1)S(1)} %pick.1), channel_id=1, source_target_pairs={{0,1},{1,0},{2,3},{3,2},{4,5},{5,4},{6,7},{7,6},{8,9},{9,8},{10,11... | collective-permute-start | bytes 3538952 | tf_op jit(solution)/shard_map/ppermute | solution.py:265
  30.9 9.6 %collective-permute-start.10 = (bf16[256,384]{1,0:T(8,128)(2,1)S(1)}, bf16[256,384]{1,0:T(8,128)(2,1)S(1)}, u32[]{:S(2)}, u32[]{:S(2)}) collective-permute-start(bf16[256,384]{1,0:T(8,128)(2,1)S(1)} %collective-permute-done.9.refs_4_), channel_id=1, source_target_pairs={{0,224},{8,232},{16,240},{24,248},{32,0},{40,8},{48,16},{56,24},{6... | collective-permute-start | bytes 589832 | tf_op jit(solution)/shard_map/ppermute | solution.py:253
  31.3 9.2 %collective-permute-start.13 = (bf16[256,384]{1,0:T(8,128)(2,1)S(1)}, bf16[256,384]{1,0:T(8,128)(2,1)S(1)}, u32[]{:S(2)}, u32[]{:S(2)}) collective-permute-start(bf16[256,384]{1,0:T(8,128)(2,1)S(1)} %collective-permute-done.12.refs_8_), channel_id=1, source_target_pairs={{0,32},{8,40},{16,48},{24,56},{32,64},{40,72},{48,80},{56,88},{64,... | collective-permute-start | bytes 589832 | tf_op jit(solution)/shard_map/ppermute | solution.py:254
  32.9 8.0 %collective-permute-start.11 = (bf16[256,384]{1,0:T(8,128)(2,1)S(1)}, bf16[256,384]{1,0:T(8,128)(2,1)S(1)}, u32[]{:S(2)}, u32[]{:S(2)}) collective-permute-start(bf16[256,384]{1,0:T(8,128)(2,1)S(1)} %collective-permute-done.8.refs_0_), channel_id=1, source_target_pairs={{0,32},{8,40},{16,48},{24,56},{32,64},{40,72},{48,80},{56,88},{64,... | collective-permute-start | bytes 589832 | tf_op jit(solution)/shard_map/ppermute | solution.py:251
  33.2 7.7 %collective-permute-start.16 = (bf16[256,384]{1,0:T(8,128)(2,1)S(1)}, bf16[256,384]{1,0:T(8,128)(2,1)S(1)}, u32[]{:S(2)}, u32[]{:S(2)}) collective-permute-start(bf16[256,384]{1,0:T(8,128)(2,1)S(1)} %collective-permute-done.15.refs_6_), channel_id=1, source_target_pairs={{0,224},{8,232},{16,240},{24,248},{32,0},{40,8},{48,16},{56,24},{6... | collective-permute-start | bytes 589832 | tf_op jit(solution)/shard_map/ppermute | solution.py:255
  40.9 26.2 %copy-start.1 = (bf16[384,3072]{1,0:T(8,128)(2,1)S(1)}, bf16[384,3072]{1,0:T(8,128)(2,1)}, u32[]{:S(2)}) copy-start(bf16[384,3072]{1,0:T(8,128)(2,1)} %weight_ref.3) | copy-start | bytes 7077892
  45.1 1.9 %collective-permute-start.17 = (bf16[2,416,256]{2,1,0:T(8,128)(2,1)S(1)}, bf16[2,416,256]{2,1,0:T(8,128)(2,1)S(1)}, u32[]{:S(2)}, u32[]{:S(2)}) collective-permute-start(bf16[2,416,256]{2,1,0:T(8,128)(2,1)S(1)} %get-tuple-element.23), channel_id=1, source_target_pairs={{0,8},{8,0},{16,24},{24,16},{32,40},{40,32},{48,56},{56,48},{64,72... | collective-permute-start | bytes 1277960 | tf_op jit(solution)/shard_map/ppermute | solution.py:321
  47.2 12.4 %collective-permute-start.18 = (bf16[1,416,256]{2,1,0:T(8,128)(2,1)S(1)}, bf16[1,416,256]{2,1,0:T(8,128)(2,1)S(1)}, u32[]{:S(2)}, u32[]{:S(2)}) collective-permute-start(bf16[1,416,256]{2,1,0:T(8,128)(2,1)S(1)} %get-tuple-element.26), channel_id=1, source_target_pairs={{0,16},{8,24},{16,0},{24,8},{32,48},{40,56},{48,32},{56,40},{64,80... | collective-permute-start | bytes 638984 | tf_op jit(solution)/shard_map/ppermute | solution.py:334
  59.8 7.3 %collective-permute-start.19 = (bf16[256,384]{1,0:T(8,128)(2,1)S(1)}, bf16[256,384]{1,0:T(8,128)(2,1)S(1)}, u32[]{:S(2)}, u32[]{:S(2)}) collective-permute-start(bf16[256,384]{1,0:T(8,128)(2,1)S(1)} %finish.1.mine_ref), channel_id=1, source_target_pairs={{0,1},{1,0},{2,3},{3,2},{4,5},{5,4},{6,7},{7,6},{8,9},{9,8},{10,11... | collective-permute-start | bytes 589832 | tf_op jit(solution)/shard_map/ppermute | solution.py:351

commit v12 on v11

--- a/solution.py
+++ b/solution.py
@@ -207,20 +207,26 @@
 
 def pick_kernel(weight_ref, out_ref):
     width = weight_ref.shape[0]
+    count = out_ref.shape[1] // width
     side = lax.rem(lax.axis_index("head"), 2)
-    for j in range(out_ref.shape[1] // width):
-        begin = pl.multiple_of((2 * j + 1 - side) * width, HD)
+    core = lax.rem(lax.axis_index("seq"), 2)
+    for j in range(count):
+        begin = pl.multiple_of((2 * (core * count + j) + 1 - side) * width, HD)
         out_ref[:, j * width:(j + 1) * width] = weight_ref[:, pl.ds(begin, width)]
 
 
-def project_kernel(mine_ref, other_ref, weight_ref, other_weight_ref, out_ref):
+def project_kernel(mine_ref, other_ref, weight_ref, half_ref, swapped_ref, out_ref, blocks_ref):
     shares, _, width = out_ref.shape
     side = lax.rem(lax.axis_index("head"), 2)
+    core = lax.rem(lax.axis_index("seq"), 2)
+    half = half_ref.shape[1]
+    blocks_ref[:, pl.ds(pl.multiple_of(core * half, HD), half)] = half_ref[...]
+    blocks_ref[:, pl.ds(pl.multiple_of((1 - core) * half, HD), half)] = swapped_ref[...]
     for j in range(shares):
         begin = pl.multiple_of((2 * j + side) * width, HD)
         mixed = jnp.dot(mine_ref[...], weight_ref[:, pl.ds(begin, width)], preferred_element_type=jnp.float32)
         mixed = mixed + jnp.dot(
-            other_ref[...], other_weight_ref[:, j * width:(j + 1) * width], preferred_element_type=jnp.float32
+            other_ref[...], blocks_ref[:, j * width:(j + 1) * width], preferred_element_type=jnp.float32
         )
         out_ref[j] = mixed.astype(jnp.bfloat16)
 
@@ -256,13 +262,14 @@
 
     picked = pl.pallas_call(
         pick_kernel,
-        out_shape=jax.ShapeDtypeStruct((width, head_size // 2 * width), out_weight.dtype),
+        out_shape=jax.ShapeDtypeStruct((width, head_size // 4 * width), out_weight.dtype),
         in_specs=vmem_specs(1),
         out_specs=pl.BlockSpec(memory_space=pltpu.VMEM),
         compiler_params=PARAMS,
         name="pick",
     )(out_weight)
-    other_weight = lax.ppermute(picked, "head", [(h, h ^ 1) for h in range(head_size)])
+    other_half = lax.ppermute(picked, "head", [(h, h ^ 1) for h in range(head_size)])
+    other_swapped = lax.ppermute(other_half, "seq", [(s, s ^ 1) for s in range(seq_size)])
 
     listed = jnp.pad(
         block_list, ((0, PART_ROWS - 1), (0, width - block_list.shape[1])), constant_values=-1
@@ -344,11 +351,12 @@
     shares = pl.pallas_call(
         project_kernel,
         out_shape=jax.ShapeDtypeStruct((head_size // 2, TILE, width), jnp.bfloat16),
-        in_specs=vmem_specs(4),
+        in_specs=vmem_specs(5),
         out_specs=pl.BlockSpec(memory_space=pltpu.VMEM),
+        scratch_shapes=[pltpu.VMEM((width, head_size // 2 * width), out_weight.dtype)],
         compiler_params=PARAMS,
         name="project",
-    )(attended, lax.ppermute(attended, "head", swap_side), out_weight, other_weight)
+    )(attended, lax.ppermute(attended, "head", swap_side), out_weight, other_half, other_swapped)
     sides = [list(range(k, head_size, 2)) for k in range(2)]
     shares = lax.all_to_all(shares, "head", 0, 0, axis_index_groups=sides, tiled=True)
     return jnp.sum(shares.astype(jnp.float32), axis=0).astype(jnp.bfloat16)

time: 82.9 us -> 80.6 us (0.972)
  waiting for transfers between devices: 28.1 us -> 20.9 us
  starting transfers between devices: 26.5 us -> 28.9 us
  blocking collectives: 13.8 us -> 15.1 us
    ppermute x1, waiting for transfers between devices: 12.3 us -> 7.28 us  [per_device(): other = lax.ppermute(send, 'seq', [(s, s ^ 2) for s in range(seq_size)])]
    ppermute x1, starting transfers between devices: 0.7 us -> 2.65 us  [per_device(): lax.ppermute(attended, 'head', swap_side)]
    ppermute x1, waiting for transfers between devices: 6.55 us -> 5.06 us  [per_device(): lax.ppermute(attended, 'head', swap_side)]
    all_to_all x1, blocking collectives: 13.8 us -> 15.1 us  [per_device(): lax.all_to_all(shares, 'head', 0, 0, axis_index_groups=sides, tiled=True)]
  transfers between devices with their start and end apart: 21 -> 22, of which waited for: 7 -> 7; matrix products, arithmetic and copies ran while one was open for 2% -> 2% of each run, Pallas kernels for 11% -> 12%
where the time goes in v12:
time: 80.6 us; the launch traced here: 79.9 us
  starting transfers between devices  28.9 us (36%)
  waiting for transfers between devices  20.9 us (26%)
  blocking collectives  15.1 us (19%)
  Pallas kernels  10.7 us (13%)
  other arithmetic  2.42 us (3%)
  local copies, waits for them, and re-layouts  1.68 us (2%)
    all_to_all x1, blocking collectives, per_device(): lax.all_to_all(shares, 'head', 0, 0, axis_index_groups=sides, tiled=True)  15.1 us
    ppermute x4, starting transfers between devices, per_device(): v_down.append(lax.ppermute(v_down[-1], 'seq', down))  12.2 us
    ppermute x1, waiting for transfers between devices, per_device(): other = lax.ppermute(send, 'seq', [(s, s ^ 2) for s in range(seq_size)])  7.28 us
    ppermute x4, waiting for transfers between devices, per_device(): v_down.append(lax.ppermute(v_down[-1], 'seq', down))  5.94 us
    ppermute x3, starting transfers between devices, per_device(): k_down.append(lax.ppermute(k_down[-1], 'seq', down))  5.11 us
    ppermute x1, waiting for transfers between devices, per_device(): lax.ppermute(attended, 'head', swap_side)  5.06 us
    pallas_call x1, Pallas kernels, per_device(): pl.pallas_call(functools.partial(near_kernel, factor, seq_size, order), o...  4.8 us
    pallas_call x1, Pallas kernels, per_device(): pl.pallas_call(functools.partial(far_kernel, factor, 3, len(far)), out_sh...  4.25 us
  transfers between devices with their start and end apart: 22, of which 7 were waited for; matrix products, arithmetic and copies ran while one was open for 2% of the time, Pallas kernels for 12%

profile of v12, /device:TPU:2, one launch (start us, length us, event | category | flops | bytes accessed | tf_op | source)
XLA Modules:
  0.0 79.9 jit_solution(5884625735272450527)
XLA Ops:
  0.0 2.0 %collective-permute-start.3 = (bf16[256,384]{1,0:T(8,128)(2,1)}, bf16[256,384]{1,0:T(8,128)(2,1)S(1)}, u32[]{:S(2)}, u32[]{:S(2)}) collective-permute-start(bf16[256,384]{1,0:T(8,128)(2,1)} %refs_4_.1), channel_id=1, source_target_pairs={{0,32},{8,40},{16,48},{24,56},{32,64},{40,72},{48,80},{56,88},{64,... | collective-permute-start | bytes 589832 | tf_op jit(solution)/shard_map/ppermute | solution.py:257
  2.0 4.0 %collective-permute-start.4 = (bf16[256,384]{1,0:T(8,128)(2,1)}, bf16[256,384]{1,0:T(8,128)(2,1)S(1)}, u32[]{:S(2)}, u32[]{:S(2)}) collective-permute-start(bf16[256,384]{1,0:T(8,128)(2,1)} %refs_4_.1), channel_id=1, source_target_pairs={{0,224},{8,232},{16,240},{24,248},{32,0},{40,8},{48,16},{56,24},{6... | collective-permute-start | bytes 589832 | tf_op jit(solution)/shard_map/ppermute | solution.py:259
  6.0 1.9 %collective-permute-start.6 = (bf16[256,384]{1,0:T(8,128)(2,1)}, bf16[256,384]{1,0:T(8,128)(2,1)S(1)}, u32[]{:S(2)}, u32[]{:S(2)}) collective-permute-start(bf16[256,384]{1,0:T(8,128)(2,1)} %refs_5_.1), channel_id=1, source_target_pairs={{0,224},{8,232},{16,240},{24,248},{32,0},{40,8},{48,16},{56,24},{6... | collective-permute-start | bytes 589832 | tf_op jit(solution)/shard_map/ppermute | solution.py:261
  8.1 0.7 convert.5
  8.7 0.9 %fusion.1.refs_0_ = bf16[272,384]{1,0:T(8,128)(2,1)S(1)} fusion(bf16[1,27]{1,0:T(2,128)(2,1)S(1)} %convert.5, bf16[256,384]{1,0:T(8,128)(2,1)} %param.6), kind=kLoop, calls=%fused_computation.2 | loop fusion | flops 626688 | bytes 405558 | tf_op jit(solution)/shard_map/concatenate | solution.py:277
  9.8 1.3 %collective-permute-done.3.refs_6_ = bf16[256,384]{1,0:T(8,128)(2,1)S(1)} collective-permute-done((bf16[256,384]{1,0:T(8,128)(2,1)}, bf16[256,384]{1,0:T(8,128)(2,1)S(1)}, u32[]{:S(2)}, u32[]{:S(2)}) %collective-permute-start.3) | collective-permute-done | bytes 196640 | tf_op jit(solution)/shard_map/ppermute | solution.py:257
  11.1 0.5 collective-permute-start.1
  11.7 0.3 collective-permute-start.7
  11.9 2.8 %collective-permute-done.6.refs_9_ = bf16[256,384]{1,0:T(8,128)(2,1)S(1)} collective-permute-done((bf16[256,384]{1,0:T(8,128)(2,1)}, bf16[256,384]{1,0:T(8,128)(2,1)S(1)}, u32[]{:S(2)}, u32[]{:S(2)}) %collective-permute-start.6) | collective-permute-done | bytes 196640 | tf_op jit(solution)/shard_map/ppermute | solution.py:261
  14.7 3.6 %collective-permute-start.14 = (bf16[256,384]{1,0:T(8,128)(2,1)S(1)}, bf16[256,384]{1,0:T(8,128)(2,1)S(1)}, u32[]{:S(2)}, u32[]{:S(2)}) collective-permute-start(bf16[256,384]{1,0:T(8,128)(2,1)S(1)} %collective-permute-done.6.refs_9_), channel_id=1, source_target_pairs={{0,224},{8,232},{16,240},{24,248},{32,0},{40,8},{48,16},{56,24},{6... | collective-permute-start | bytes 589832 | tf_op jit(solution)/shard_map/ppermute | solution.py:261
  18.3 0.5 collective-permute-start.9
  18.8 1.6 %collective-permute-start.12 = (bf16[256,384]{1,0:T(8,128)(2,1)S(1)}, bf16[256,384]{1,0:T(8,128)(2,1)S(1)}, u32[]{:S(2)}, u32[]{:S(2)}) collective-permute-start(bf16[256,384]{1,0:T(8,128)(2,1)S(1)} %collective-permute-done.5.refs_8_), channel_id=1, source_target_pairs={{0,32},{8,40},{16,48},{24,56},{32,64},{40,72},{48,80},{56,88},{64,... | collective-permute-start | bytes 589832 | tf_op jit(solution)/shard_map/ppermute | solution.py:260
  20.5 3.2 %collective-permute-done.14.refs_9_ = bf16[256,384]{1,0:T(8,128)(2,1)S(1)} collective-permute-done((bf16[256,384]{1,0:T(8,128)(2,1)S(1)}, bf16[256,384]{1,0:T(8,128)(2,1)S(1)}, u32[]{:S(2)}, u32[]{:S(2)}) %collective-permute-start.14) | collective-permute-done | bytes 196640 | tf_op jit(solution)/shard_map/ppermute | solution.py:261
  23.7 3.7 %collective-permute-start.15 = (bf16[256,384]{1,0:T(8,128)(2,1)S(1)}, bf16[256,384]{1,0:T(8,128)(2,1)S(1)}, u32[]{:S(2)}, u32[]{:S(2)}) collective-permute-start(bf16[256,384]{1,0:T(8,128)(2,1)S(1)} %collective-permute-done.14.refs_9_), channel_id=1, source_target_pairs={{0,224},{8,232},{16,240},{24,248},{32,0},{40,8},{48,16},{56,24},{6... | collective-permute-start | bytes 589832 | tf_op jit(solution)/shard_map/ppermute | solution.py:261
  27.4 1.7 %copy-done = bf16[384,3072]{1,0:T(8,128)(2,1)S(1)} copy-done((bf16[384,3072]{1,0:T(8,128)(2,1)S(1)}, bf16[384,3072]{1,0:T(8,128)(2,1)}, u32[]{:S(2)}) %copy-start) | copy-done | bytes 2359320
  29.1 1.9 %collective-permute-start.20 = (bf16[384,768]{1,0:T(8,128)(2,1)S(1)}, bf16[384,768]{1,0:T(8,128)(2,1)S(1)}, u32[]{:S(2)}, u32[]{:S(2)}) collective-permute-start(bf16[384,768]{1,0:T(8,128)(2,1)S(1)} %pick.1), channel_id=1, source_target_pairs={{0,1},{1,0},{2,3},{3,2},{4,5},{5,4},{6,7},{7,6},{8,9},{9,8},{10,11... | collective-permute-start | bytes 1769480 | tf_op jit(solution)/shard_map/ppermute | solution.py:271
  31.0 0.6 collective-permute-start.10
  31.6 1.5 %collective-permute-start.13 = (bf16[256,384]{1,0:T(8,128)(2,1)S(1)}, bf16[256,384]{1,0:T(8,128)(2,1)S(1)}, u32[]{:S(2)}, u32[]{:S(2)}) collective-permute-start(bf16[256,384]{1,0:T(8,128)(2,1)S(1)} %collective-permute-done.12.refs_8_), channel_id=1, source_target_pairs={{0,32},{8,40},{16,48},{24,56},{32,64},{40,72},{48,80},{56,88},{64,... | collective-permute-start | bytes 589832 | tf_op jit(solution)/shard_map/ppermute | solution.py:260
  33.0 0.3 collective-permute-start.11
  33.3 3.0 %collective-permute-start.16 = (bf16[256,384]{1,0:T(8,128)(2,1)S(1)}, bf16[256,384]{1,0:T(8,128)(2,1)S(1)}, u32[]{:S(2)}, u32[]{:S(2)}) collective-permute-start(bf16[256,384]{1,0:T(8,128)(2,1)S(1)} %collective-permute-done.15.refs_6_), channel_id=1, source_target_pairs={{0,224},{8,232},{16,240},{24,248},{32,0},{40,8},{48,16},{56,24},{6... | collective-permute-start | bytes 589832 | tf_op jit(solution)/shard_map/ppermute | solution.py:261
  36.3 4.8 %attend_near.1 = (s32[4,8]{1,0:T(4,128)S(1)}, bf16[4,256,384]{2,1,0:T(8,128)(2,1)S(1)}, f32[12,128,256]{2,1,0:T(8,128)S(1)}, f32[12,1,256]{2,1,0:T(1,128)S(1)}, f32[12,1,256]{2,1,0:T(1,128)S(1)}) custom-call(s32[2]{0:T(128)S(1)} %copy-done.4, bf16[272,384]{1,0:T(8,128)(2,1)S(1)} %fusion.1.refs_0_, bf16[272,384]{1,0:T(8,128)(2,1)S(1)} %collective-permute-done.refs_1_, ...), custom_call_target="tpu_custom_call" | custom-call | flops 905969664 | bytes 4194304 | tf_op jit(solution)/shard_map/attend_near/pallas_call | solution.py:298
  41.2 4.2 %attend_far.1 = (f32[2,384,256]{2,1,0:T(8,128)S(1)}, f32[2,8,256]{2,1,0:T(8,128)S(1)}, bf16[2,416,256]{2,1,0:T(8,128)(2,1)S(1)}) custom-call(s32[4,8]{1,0:T(4,128)S(1)} %get-tuple-element.16.need_ref, bf16[4,256,384]{2,1,0:T(8,128)(2,1)S(1)} %get-tuple-element.17.stacked_ref, bf16[256,384]{1,0:T(8,128)(2,1)S(1)} %collective-permute-done.8.refs_0_, ...), custom_call_target="tpu_custom_call" | custom-call | flops 905969664 | bytes 4194304 | tf_op jit(solution)/shard_map/attend_far/pallas_call | solution.py:313
  45.5 0.5 collective-permute-start.21
  46.0 1.3 %collective-permute-done.17.other_ref = bf16[2,416,256]{2,1,0:T(8,128)(2,1)S(1)} collective-permute-done((bf16[2,416,256]{2,1,0:T(8,128)(2,1)S(1)}, bf16[2,416,256]{2,1,0:T(8,128)(2,1)S(1)}, u32[]{:S(2)}, u32[]{:S(2)}) %collective-permute-start.17) | collective-permute-done | bytes 426016 | tf_op jit(solution)/shard_map/ppermute | solution.py:328
  47.3 0.2 merge.1
  47.6 7.3 %collective-permute-done.18.other_ref = bf16[1,416,256]{2,1,0:T(8,128)(2,1)S(1)} collective-permute-done((bf16[1,416,256]{2,1,0:T(8,128)(2,1)S(1)}, bf16[1,416,256]{2,1,0:T(8,128)(2,1)S(1)}, u32[]{:S(2)}, u32[]{:S(2)}) %collective-permute-start.18) | collective-permute-done | bytes 213024 | tf_op jit(solution)/shard_map/ppermute | solution.py:341
  54.8 0.2 finish.1.mine_ref
  55.0 2.6 %collective-permute-start.19 = (bf16[256,384]{1,0:T(8,128)(2,1)S(1)}, bf16[256,384]{1,0:T(8,128)(2,1)S(1)}, u32[]{:S(2)}, u32[]{:S(2)}) collective-permute-start(bf16[256,384]{1,0:T(8,128)(2,1)S(1)} %finish.1.mine_ref), channel_id=1, source_target_pairs={{0,1},{1,0},{2,3},{3,2},{4,5},{5,4},{6,7},{7,6},{8,9},{9,8},{10,11... | collective-permute-start | bytes 589832 | tf_op jit(solution)/shard_map/ppermute | solution.py:359
  57.7 5.1 %collective-permute-done.19.other_ref = bf16[256,384]{1,0:T(8,128)(2,1)S(1)} collective-permute-done((bf16[256,384]{1,0:T(8,128)(2,1)S(1)}, bf16[256,384]{1,0:T(8,128)(2,1)S(1)}, u32[]{:S(2)}, u32[]{:S(2)}) %collective-permute-start.19) | collective-permute-done | bytes 196640 | tf_op jit(solution)/shard_map/ppermute | solution.py:359
  62.7 1.2 %project.1 = bf16[4,256,384]{2,1,0:T(8,128)(2,1)S(1)} custom-call(bf16[256,384]{1,0:T(8,128)(2,1)S(1)} %finish.1.mine_ref, bf16[256,384]{1,0:T(8,128)(2,1)S(1)} %collective-permute-done.19.other_ref, bf16[384,3072]{1,0:T(8,128)(2,1)S(1)} %copy-done.1, bf16[384,768]{1,0:T(8,128)(2,1)S(1)} %collective-permute-done.20.half_ref, ...), custom_call_target="tpu_custom_call" | custom-call | tf_op jit(solution)/shard_map/project/pallas_call | solution.py:351
  64.0 15.1 %all_to_all.5 = bf16[4,256,384]{2,1,0:T(8,128)(2,1)S(1)} all-to-all(bf16[4,256,384]{2,1,0:T(8,128)(2,1)S(1)} %project.1), channel_id=1, replica_groups={{0,2,4,6},{1,3,5,7},{8,10,12,14},{9,11,13,15},{16,18,20,22},{17,19,21,2..., dimensions={0} | all-to-all | bytes 1572864 | tf_op jit(solution)/shard_map/all_to_all | solution.py:361
  79.1 0.8 %reduce_sum.12 = bf16[256,384]{1,0:T(8,128)(2,1)} reduce(bf16[4,256,384]{2,1,0:T(8,128)(2,1)S(1)} %all_to_all.5, bf16[]{:T(256)} %constant.5.clone.1), dimensions={0}, to_apply=%region_0.1 | reduce | flops 294912 | bytes 983042 | tf_op jit(solution)/shard_map/reduce_sum | solution.py:362
  (32 shorter events, 0.6 us)
Async XLA Ops:
  0.0 36.3 %copy-start.2 = (bf16[256,384]{1,0:T(8,128)(2,1)S(1)}, bf16[256,384]{1,0:T(8,128)(2,1)}, u32[]{:S(2)}) copy-start(bf16[256,384]{1,0:T(8,128)(2,1)} %refs_4_.1) | copy-start | bytes 589828
  0.0 36.3 %copy-start.3 = (bf16[256,384]{1,0:T(8,128)(2,1)S(1)}, bf16[256,384]{1,0:T(8,128)(2,1)}, u32[]{:S(2)}) copy-start(bf16[256,384]{1,0:T(8,128)(2,1)} %refs_5_.1) | copy-start | bytes 589828
  0.0 36.3 %copy-start.4 = (s32[2]{0:T(128)S(1)}, s32[2]{0:T(128)}, u32[]{:S(2)}) copy-start(s32[2]{0:T(128)} %text_ref.1) | copy-start | bytes 28
  0.0 11.0 %collective-permute-start.3 = (bf16[256,384]{1,0:T(8,128)(2,1)}, bf16[256,384]{1,0:T(8,128)(2,1)S(1)}, u32[]{:S(2)}, u32[]{:S(2)}) collective-permute-start(bf16[256,384]{1,0:T(8,128)(2,1)} %refs_4_.1), channel_id=1, source_target_pairs={{0,32},{8,40},{16,48},{24,56},{32,64},{40,72},{48,80},{56,88},{64,... | collective-permute-start | bytes 589832 | tf_op jit(solution)/shard_map/ppermute | solution.py:257
  2.0 9.6 %collective-permute-start.4 = (bf16[256,384]{1,0:T(8,128)(2,1)}, bf16[256,384]{1,0:T(8,128)(2,1)S(1)}, u32[]{:S(2)}, u32[]{:S(2)}) collective-permute-start(bf16[256,384]{1,0:T(8,128)(2,1)} %refs_4_.1), channel_id=1, source_target_pairs={{0,224},{8,232},{16,240},{24,248},{32,0},{40,8},{48,16},{56,24},{6... | collective-permute-start | bytes 589832 | tf_op jit(solution)/shard_map/ppermute | solution.py:259
  6.0 8.7 %collective-permute-start.6 = (bf16[256,384]{1,0:T(8,128)(2,1)}, bf16[256,384]{1,0:T(8,128)(2,1)S(1)}, u32[]{:S(2)}, u32[]{:S(2)}) collective-permute-start(bf16[256,384]{1,0:T(8,128)(2,1)} %refs_5_.1), channel_id=1, source_target_pairs={{0,224},{8,232},{16,240},{24,248},{32,0},{40,8},{48,16},{56,24},{6... | collective-permute-start | bytes 589832 | tf_op jit(solution)/shard_map/ppermute | solution.py:261
  8.0 10.3 %collective-permute-start.5 = (bf16[256,384]{1,0:T(8,128)(2,1)}, bf16[256,384]{1,0:T(8,128)(2,1)S(1)}, u32[]{:S(2)}, u32[]{:S(2)}) collective-permute-start(bf16[256,384]{1,0:T(8,128)(2,1)} %refs_5_.1), channel_id=1, source_target_pairs={{0,32},{8,40},{16,48},{24,56},{32,64},{40,72},{48,80},{56,88},{64,... | collective-permute-start | bytes 589832 | tf_op jit(solution)/shard_map/ppermute | solution.py:260
  9.7 8.6 %collective-permute-start = (bf16[272,384]{1,0:T(8,128)(2,1)S(1)}, bf16[272,384]{1,0:T(8,128)(2,1)S(1)}, u32[]{:S(2)}, u32[]{:S(2)}) collective-permute-start(bf16[272,384]{1,0:T(8,128)(2,1)S(1)} %fusion.1.refs_0_), channel_id=1, source_target_pairs={{0,8},{8,0},{16,24},{24,16},{32,40},{40,32},{48,56},{56,48},{64,72... | collective-permute-start | bytes 626696 | tf_op jit(solution)/shard_map/ppermute | solution.py:279
  11.1 7.8 %collective-permute-start.1 = (bf16[272,384]{1,0:T(8,128)(2,1)S(1)}, bf16[272,384]{1,0:T(8,128)(2,1)S(1)}, u32[]{:S(2)}, u32[]{:S(2)}) collective-permute-start(bf16[272,384]{1,0:T(8,128)(2,1)S(1)} %fusion.1.refs_0_), channel_id=1, source_target_pairs={{0,16},{8,24},{16,0},{24,8},{32,48},{40,56},{48,32},{56,40},{64,80... | collective-permute-start | bytes 626696 | tf_op jit(solution)/shard_map/ppermute | solution.py:279
  11.7 8.8 %collective-permute-start.7 = (bf16[256,384]{1,0:T(8,128)(2,1)S(1)}, bf16[256,384]{1,0:T(8,128)(2,1)S(1)}, u32[]{:S(2)}, u32[]{:S(2)}) collective-permute-start(bf16[256,384]{1,0:T(8,128)(2,1)S(1)} %collective-permute-done.3.refs_6_), channel_id=1, source_target_pairs={{0,32},{8,40},{16,48},{24,56},{32,64},{40,72},{48,80},{56,88},{64,... | collective-permute-start | bytes 589832 | tf_op jit(solution)/shard_map/ppermute | solution.py:257
  14.7 8.9 %collective-permute-start.14 = (bf16[256,384]{1,0:T(8,128)(2,1)S(1)}, bf16[256,384]{1,0:T(8,128)(2,1)S(1)}, u32[]{:S(2)}, u32[]{:S(2)}) collective-permute-start(bf16[256,384]{1,0:T(8,128)(2,1)S(1)} %collective-permute-done.6.refs_9_), channel_id=1, source_target_pairs={{0,224},{8,232},{16,240},{24,248},{32,0},{40,8},{48,16},{56,24},{6... | collective-permute-start | bytes 589832 | tf_op jit(solution)/shard_map/ppermute | solution.py:261
  18.3 10.8 %collective-permute-start.2 = (bf16[272,384]{1,0:T(8,128)(2,1)S(1)}, bf16[272,384]{1,0:T(8,128)(2,1)S(1)}, u32[]{:S(2)}, u32[]{:S(2)}) collective-permute-start(bf16[272,384]{1,0:T(8,128)(2,1)S(1)} %fusion.1.refs_0_), channel_id=1, source_target_pairs={{0,24},{8,16},{16,8},{24,0},{32,56},{40,48},{48,40},{56,32},{64,88... | collective-permute-start | bytes 626696 | tf_op jit(solution)/shard_map/ppermute | solution.py:279
  18.3 12.7 %collective-permute-start.9 = (bf16[256,384]{1,0:T(8,128)(2,1)S(1)}, bf16[256,384]{1,0:T(8,128)(2,1)S(1)}, u32[]{:S(2)}, u32[]{:S(2)}) collective-permute-start(bf16[256,384]{1,0:T(8,128)(2,1)S(1)} %collective-permute-done.4.refs_7_), channel_id=1, source_target_pairs={{0,224},{8,232},{16,240},{24,248},{32,0},{40,8},{48,16},{56,24},{6... | collective-permute-start | bytes 589832 | tf_op jit(solution)/shard_map/ppermute | solution.py:259
  18.8 12.7 %collective-permute-start.12 = (bf16[256,384]{1,0:T(8,128)(2,1)S(1)}, bf16[256,384]{1,0:T(8,128)(2,1)S(1)}, u32[]{:S(2)}, u32[]{:S(2)}) collective-permute-start(bf16[256,384]{1,0:T(8,128)(2,1)S(1)} %collective-permute-done.5.refs_8_), channel_id=1, source_target_pairs={{0,32},{8,40},{16,48},{24,56},{32,64},{40,72},{48,80},{56,88},{64,... | collective-permute-start | bytes 589832 | tf_op jit(solution)/shard_map/ppermute | solution.py:260
  20.4 12.6 %collective-permute-start.8 = (bf16[256,384]{1,0:T(8,128)(2,1)S(1)}, bf16[256,384]{1,0:T(8,128)(2,1)S(1)}, u32[]{:S(2)}, u32[]{:S(2)}) collective-permute-start(bf16[256,384]{1,0:T(8,128)(2,1)S(1)} %collective-permute-done.7.refs_3_), channel_id=1, source_target_pairs={{0,32},{8,40},{16,48},{24,56},{32,64},{40,72},{48,80},{56,88},{64,... | collective-permute-start | bytes 589832 | tf_op jit(solution)/shard_map/ppermute | solution.py:257
  23.7 9.6 %collective-permute-start.15 = (bf16[256,384]{1,0:T(8,128)(2,1)S(1)}, bf16[256,384]{1,0:T(8,128)(2,1)S(1)}, u32[]{:S(2)}, u32[]{:S(2)}) collective-permute-start(bf16[256,384]{1,0:T(8,128)(2,1)S(1)} %collective-permute-done.14.refs_9_), channel_id=1, source_target_pairs={{0,224},{8,232},{16,240},{24,248},{32,0},{40,8},{48,16},{56,24},{6... | collective-permute-start | bytes 589832 | tf_op jit(solution)/shard_map/ppermute | solution.py:261
  27.4 1.7 %copy-start = (bf16[384,3072]{1,0:T(8,128)(2,1)S(1)}, bf16[384,3072]{1,0:T(8,128)(2,1)}, u32[]{:S(2)}) copy-start(bf16[384,3072]{1,0:T(8,128)(2,1)} %weight_ref.3) | copy-start | bytes 7077892
  29.1 16.4 %collective-permute-start.20 = (bf16[384,768]{1,0:T(8,128)(2,1)S(1)}, bf16[384,768]{1,0:T(8,128)(2,1)S(1)}, u32[]{:S(2)}, u32[]{:S(2)}) collective-permute-start(bf16[384,768]{1,0:T(8,128)(2,1)S(1)} %pick.1), channel_id=1, source_target_pairs={{0,1},{1,0},{2,3},{3,2},{4,5},{5,4},{6,7},{7,6},{8,9},{9,8},{10,11... | collective-permute-start | bytes 1769480 | tf_op jit(solution)/shard_map/ppermute | solution.py:271
  31.0 10.1 %collective-permute-start.10 = (bf16[256,384]{1,0:T(8,128)(2,1)S(1)}, bf16[256,384]{1,0:T(8,128)(2,1)S(1)}, u32[]{:S(2)}, u32[]{:S(2)}) collective-permute-start(bf16[256,384]{1,0:T(8,128)(2,1)S(1)} %collective-permute-done.9.refs_4_), channel_id=1, source_target_pairs={{0,224},{8,232},{16,240},{24,248},{32,0},{40,8},{48,16},{56,24},{6... | collective-permute-start | bytes 589832 | tf_op jit(solution)/shard_map/ppermute | solution.py:259
  31.6 9.5 %collective-permute-start.13 = (bf16[256,384]{1,0:T(8,128)(2,1)S(1)}, bf16[256,384]{1,0:T(8,128)(2,1)S(1)}, u32[]{:S(2)}, u32[]{:S(2)}) collective-permute-start(bf16[256,384]{1,0:T(8,128)(2,1)S(1)} %collective-permute-done.12.refs_8_), channel_id=1, source_target_pairs={{0,32},{8,40},{16,48},{24,56},{32,64},{40,72},{48,80},{56,88},{64,... | collective-permute-start | bytes 589832 | tf_op jit(solution)/shard_map/ppermute | solution.py:260
  33.0 8.1 %collective-permute-start.11 = (bf16[256,384]{1,0:T(8,128)(2,1)S(1)}, bf16[256,384]{1,0:T(8,128)(2,1)S(1)}, u32[]{:S(2)}, u32[]{:S(2)}) collective-permute-start(bf16[256,384]{1,0:T(8,128)(2,1)S(1)} %collective-permute-done.8.refs_0_), channel_id=1, source_target_pairs={{0,32},{8,40},{16,48},{24,56},{32,64},{40,72},{48,80},{56,88},{64,... | collective-permute-start | bytes 589832 | tf_op jit(solution)/shard_map/ppermute | solution.py:257
  33.3 7.8 %collective-permute-start.16 = (bf16[256,384]{1,0:T(8,128)(2,1)S(1)}, bf16[256,384]{1,0:T(8,128)(2,1)S(1)}, u32[]{:S(2)}, u32[]{:S(2)}) collective-permute-start(bf16[256,384]{1,0:T(8,128)(2,1)S(1)} %collective-permute-done.15.refs_6_), channel_id=1, source_target_pairs={{0,224},{8,232},{16,240},{24,248},{32,0},{40,8},{48,16},{56,24},{6... | collective-permute-start | bytes 589832 | tf_op jit(solution)/shard_map/ppermute | solution.py:261
  41.1 21.6 %copy-start.1 = (bf16[384,3072]{1,0:T(8,128)(2,1)S(1)}, bf16[384,3072]{1,0:T(8,128)(2,1)}, u32[]{:S(2)}) copy-start(bf16[384,3072]{1,0:T(8,128)(2,1)} %weight_ref.3) | copy-start | bytes 7077892
  45.4 1.9 %collective-permute-start.17 = (bf16[2,416,256]{2,1,0:T(8,128)(2,1)S(1)}, bf16[2,416,256]{2,1,0:T(8,128)(2,1)S(1)}, u32[]{:S(2)}, u32[]{:S(2)}) collective-permute-start(bf16[2,416,256]{2,1,0:T(8,128)(2,1)S(1)} %get-tuple-element.23), channel_id=1, source_target_pairs={{0,8},{8,0},{16,24},{24,16},{32,40},{40,32},{48,56},{56,48},{64,72... | collective-permute-start | bytes 1277960 | tf_op jit(solution)/shard_map/ppermute | solution.py:328
  45.5 12.1 %collective-permute-start.21 = (bf16[384,768]{1,0:T(8,128)(2,1)S(1)}, bf16[384,768]{1,0:T(8,128)(2,1)S(1)}, u32[]{:S(2)}, u32[]{:S(2)}) collective-permute-start(bf16[384,768]{1,0:T(8,128)(2,1)S(1)} %collective-permute-done.20.half_ref), channel_id=1, source_target_pairs={{0,8},{8,0},{16,24},{24,16},{32,40},{40,32},{48,56},{56,48},{64,72... | collective-permute-start | bytes 1769480 | tf_op jit(solution)/shard_map/ppermute | solution.py:272
  47.5 7.4 %collective-permute-start.18 = (bf16[1,416,256]{2,1,0:T(8,128)(2,1)S(1)}, bf16[1,416,256]{2,1,0:T(8,128)(2,1)S(1)}, u32[]{:S(2)}, u32[]{:S(2)}) collective-permute-start(bf16[1,416,256]{2,1,0:T(8,128)(2,1)S(1)} %get-tuple-element.26), channel_id=1, source_target_pairs={{0,16},{8,24},{16,0},{24,8},{32,48},{40,56},{48,32},{56,40},{64,80... | collective-permute-start | bytes 638984 | tf_op jit(solution)/shard_map/ppermute | solution.py:341
  55.0 7.7 %collective-permute-start.19 = (bf16[256,384]{1,0:T(8,128)(2,1)S(1)}, bf16[256,384]{1,0:T(8,128)(2,1)S(1)}, u32[]{:S(2)}, u32[]{:S(2)}) collective-permute-start(bf16[256,384]{1,0:T(8,128)(2,1)S(1)} %finish.1.mine_ref), channel_id=1, source_target_pairs={{0,1},{1,0},{2,3},{3,2},{4,5},{5,4},{6,7},{7,6},{8,9},{9,8},{10,11... | collective-permute-start | bytes 589832 | tf_op jit(solution)/shard_map/ppermute | solution.py:359

commit v13 on v12

--- a/solution.py
+++ b/solution.py
@@ -215,8 +215,8 @@
         out_ref[:, j * width:(j + 1) * width] = weight_ref[:, pl.ds(begin, width)]
 
 
-def project_kernel(mine_ref, other_ref, weight_ref, half_ref, swapped_ref, out_ref, blocks_ref):
-    shares, _, width = out_ref.shape
+def project_own_kernel(mine_ref, weight_ref, half_ref, swapped_ref, sum_ref, blocks_ref):
+    shares, _, width = sum_ref.shape
     side = lax.rem(lax.axis_index("head"), 2)
     core = lax.rem(lax.axis_index("seq"), 2)
     half = half_ref.shape[1]
@@ -224,8 +224,13 @@
     blocks_ref[:, pl.ds(pl.multiple_of((1 - core) * half, HD), half)] = swapped_ref[...]
     for j in range(shares):
         begin = pl.multiple_of((2 * j + side) * width, HD)
-        mixed = jnp.dot(mine_ref[...], weight_ref[:, pl.ds(begin, width)], preferred_element_type=jnp.float32)
-        mixed = mixed + jnp.dot(
+        sum_ref[j] = jnp.dot(mine_ref[...], weight_ref[:, pl.ds(begin, width)], preferred_element_type=jnp.float32)
+
+
+def project_other_kernel(other_ref, sum_ref, blocks_ref, out_ref):
+    shares, _, width = out_ref.shape
+    for j in range(shares):
+        mixed = sum_ref[j] + jnp.dot(
             other_ref[...], blocks_ref[:, j * width:(j + 1) * width], preferred_element_type=jnp.float32
         )
         out_ref[j] = mixed.astype(jnp.bfloat16)
@@ -348,15 +353,26 @@
         name="finish",
     )(keep, keep_sum, other)
     swap_side = [(h, h ^ 1) for h in range(head_size)]
+    other = lax.ppermute(attended, "head", swap_side)
+    sums, blocks = pl.pallas_call(
+        project_own_kernel,
+        out_shape=(
+            jax.ShapeDtypeStruct((head_size // 2, TILE, width), jnp.float32),
+            jax.ShapeDtypeStruct((width, head_size // 2 * width), out_weight.dtype),
+        ),
+        in_specs=vmem_specs(4),
+        out_specs=tuple(vmem_specs(2)),
+        compiler_params=PARAMS,
+        name="project_own",
+    )(attended, out_weight, other_half, other_swapped)
     shares = pl.pallas_call(
-        project_kernel,
+        project_other_kernel,
         out_shape=jax.ShapeDtypeStruct((head_size // 2, TILE, width), jnp.bfloat16),
-        in_specs=vmem_specs(5),
+        in_specs=vmem_specs(3),
         out_specs=pl.BlockSpec(memory_space=pltpu.VMEM),
-        scratch_shapes=[pltpu.VMEM((width, head_size // 2 * width), out_weight.dtype)],
-        compiler_params=PARAMS,
-        name="project",
-    )(attended, lax.ppermute(attended, "head", swap_side), out_weight, other_half, other_swapped)
+        compiler_params=PARAMS,
+        name="project_other",
+    )(other, sums, blocks)
     sides = [list(range(k, head_size, 2)) for k in range(2)]
     shares = lax.all_to_all(shares, "head", 0, 0, axis_index_groups=sides, tiled=True)
     return jnp.sum(shares.astype(jnp.float32), axis=0).astype(jnp.bfloat16)

time: 80.6 us -> 80.5 us (level)
  waiting for transfers between devices: 20.9 us -> 19.1 us
  starting transfers between devices: 28.9 us -> 29.8 us
    ppermute x1, starting transfers between devices: 0.09 us -> 0.99 us  [per_device(): other = lax.ppermute(send, 'seq', [(s, s ^ 2) for s in range(seq_size)])]
    ppermute x1, waiting for transfers between devices: 7.28 us -> 6.4 us  [per_device(): other = lax.ppermute(send, 'seq', [(s, s ^ 2) for s in range(seq_size)])]
  transfers between devices with their start and end apart: 22 -> 22, of which waited for: 7 -> 6; matrix products, arithmetic and copies ran while one was open for 2% -> 2% of each run, Pallas kernels for 12% -> 13%
where the time goes in v13:
time: 80.5 us; the launch traced here: 79.2 us
  starting transfers between devices  29.8 us (37%)
  waiting for transfers between devices  19.1 us (24%)
  blocking collectives  15.1 us (19%)
  Pallas kernels  10.9 us (14%)
  other arithmetic  2.48 us (3%)
  local copies, waits for them, and re-layouts  1.68 us (2%)
    all_to_all x1, blocking collectives, per_device(): lax.all_to_all(shares, 'head', 0, 0, axis_index_groups=sides, tiled=True)  15.1 us
    ppermute x4, starting transfers between devices, per_device(): v_down.append(lax.ppermute(v_down[-1], 'seq', down))  12.3 us
    ppermute x1, waiting for transfers between devices, per_device(): other = lax.ppermute(send, 'seq', [(s, s ^ 2) for s in range(seq_size)])  6.4 us
    ppermute x4, waiting for transfers between devices, per_device(): v_down.append(lax.ppermute(v_down[-1], 'seq', down))  5.77 us
    ppermute x3, starting transfers between devices, per_device(): k_down.append(lax.ppermute(k_down[-1], 'seq', down))  5.04 us
    pallas_call x1, Pallas kernels, per_device(): pl.pallas_call(functools.partial(near_kernel, factor, seq_size, order), o...  4.92 us
    ppermute x1, waiting for transfers between devices, per_device(): other = lax.ppermute(attended, 'head', swap_side)  4.33 us
    pallas_call x1, Pallas kernels, per_device(): pl.pallas_call(functools.partial(far_kernel, factor, 3, len(far)), out_sh...  4.24 us
  transfers between devices with their start and end apart: 22, of which 6 were waited for; matrix products, arithmetic and copies ran while one was open for 2% of the time, Pallas kernels for 13%

profile of v13, /device:TPU:2, one launch (start us, length us, event | category | flops | bytes accessed | tf_op | source)
XLA Modules:
  0.0 79.2 jit_solution(16537437626879649163)
XLA Ops:
  0.0 1.9 %collective-permute-start.3 = (bf16[256,384]{1,0:T(8,128)(2,1)}, bf16[256,384]{1,0:T(8,128)(2,1)S(1)}, u32[]{:S(2)}, u32[]{:S(2)}) collective-permute-start(bf16[256,384]{1,0:T(8,128)(2,1)} %refs_4_.1), channel_id=1, source_target_pairs={{0,32},{8,40},{16,48},{24,56},{32,64},{40,72},{48,80},{56,88},{64,... | collective-permute-start | bytes 589832 | tf_op jit(solution)/shard_map/ppermute | solution.py:262
  1.9 3.9 %collective-permute-start.4 = (bf16[256,384]{1,0:T(8,128)(2,1)}, bf16[256,384]{1,0:T(8,128)(2,1)S(1)}, u32[]{:S(2)}, u32[]{:S(2)}) collective-permute-start(bf16[256,384]{1,0:T(8,128)(2,1)} %refs_4_.1), channel_id=1, source_target_pairs={{0,224},{8,232},{16,240},{24,248},{32,0},{40,8},{48,16},{56,24},{6... | collective-permute-start | bytes 589832 | tf_op jit(solution)/shard_map/ppermute | solution.py:264
  5.9 2.0 %collective-permute-start.6 = (bf16[256,384]{1,0:T(8,128)(2,1)}, bf16[256,384]{1,0:T(8,128)(2,1)S(1)}, u32[]{:S(2)}, u32[]{:S(2)}) collective-permute-start(bf16[256,384]{1,0:T(8,128)(2,1)} %refs_5_.1), channel_id=1, source_target_pairs={{0,224},{8,232},{16,240},{24,248},{32,0},{40,8},{48,16},{56,24},{6... | collective-permute-start | bytes 589832 | tf_op jit(solution)/shard_map/ppermute | solution.py:266
  7.9 0.7 convert.5
  8.6 1.0 %fusion.1.refs_0_ = bf16[272,384]{1,0:T(8,128)(2,1)S(1)} fusion(bf16[1,27]{1,0:T(2,128)(2,1)S(1)} %convert.5, bf16[256,384]{1,0:T(8,128)(2,1)} %param.6), kind=kLoop, calls=%fused_computation.2 | loop fusion | flops 626688 | bytes 405558 | tf_op jit(solution)/shard_map/concatenate | solution.py:282
  9.7 1.3 %collective-permute-done.3.refs_6_ = bf16[256,384]{1,0:T(8,128)(2,1)S(1)} collective-permute-done((bf16[256,384]{1,0:T(8,128)(2,1)}, bf16[256,384]{1,0:T(8,128)(2,1)S(1)}, u32[]{:S(2)}, u32[]{:S(2)}) %collective-permute-start.3) | collective-permute-done | bytes 196640 | tf_op jit(solution)/shard_map/ppermute | solution.py:262
  11.0 0.5 collective-permute-start.1
  11.5 0.3 collective-permute-start.7
  11.8 2.7 %collective-permute-done.6.refs_9_ = bf16[256,384]{1,0:T(8,128)(2,1)S(1)} collective-permute-done((bf16[256,384]{1,0:T(8,128)(2,1)}, bf16[256,384]{1,0:T(8,128)(2,1)S(1)}, u32[]{:S(2)}, u32[]{:S(2)}) %collective-permute-start.6) | collective-permute-done | bytes 196640 | tf_op jit(solution)/shard_map/ppermute | solution.py:266
  14.6 3.6 %collective-permute-start.14 = (bf16[256,384]{1,0:T(8,128)(2,1)S(1)}, bf16[256,384]{1,0:T(8,128)(2,1)S(1)}, u32[]{:S(2)}, u32[]{:S(2)}) collective-permute-start(bf16[256,384]{1,0:T(8,128)(2,1)S(1)} %collective-permute-done.6.refs_9_), channel_id=1, source_target_pairs={{0,224},{8,232},{16,240},{24,248},{32,0},{40,8},{48,16},{56,24},{6... | collective-permute-start | bytes 589832 | tf_op jit(solution)/shard_map/ppermute | solution.py:266
  18.1 0.6 collective-permute-start.9
  18.8 1.5 %collective-permute-start.12 = (bf16[256,384]{1,0:T(8,128)(2,1)S(1)}, bf16[256,384]{1,0:T(8,128)(2,1)S(1)}, u32[]{:S(2)}, u32[]{:S(2)}) collective-permute-start(bf16[256,384]{1,0:T(8,128)(2,1)S(1)} %collective-permute-done.5.refs_8_), channel_id=1, source_target_pairs={{0,32},{8,40},{16,48},{24,56},{32,64},{40,72},{48,80},{56,88},{64,... | collective-permute-start | bytes 589832 | tf_op jit(solution)/shard_map/ppermute | solution.py:265
  20.3 3.1 %collective-permute-done.14.refs_9_ = bf16[256,384]{1,0:T(8,128)(2,1)S(1)} collective-permute-done((bf16[256,384]{1,0:T(8,128)(2,1)S(1)}, bf16[256,384]{1,0:T(8,128)(2,1)S(1)}, u32[]{:S(2)}, u32[]{:S(2)}) %collective-permute-start.14) | collective-permute-done | bytes 196640 | tf_op jit(solution)/shard_map/ppermute | solution.py:266
  23.4 3.7 %collective-permute-start.15 = (bf16[256,384]{1,0:T(8,128)(2,1)S(1)}, bf16[256,384]{1,0:T(8,128)(2,1)S(1)}, u32[]{:S(2)}, u32[]{:S(2)}) collective-permute-start(bf16[256,384]{1,0:T(8,128)(2,1)S(1)} %collective-permute-done.14.refs_9_), channel_id=1, source_target_pairs={{0,224},{8,232},{16,240},{24,248},{32,0},{40,8},{48,16},{56,24},{6... | collective-permute-start | bytes 589832 | tf_op jit(solution)/shard_map/ppermute | solution.py:266
  27.1 1.7 %copy-done = bf16[384,3072]{1,0:T(8,128)(2,1)S(1)} copy-done((bf16[384,3072]{1,0:T(8,128)(2,1)S(1)}, bf16[384,3072]{1,0:T(8,128)(2,1)}, u32[]{:S(2)}) %copy-start) | copy-done | bytes 2359320
  28.8 2.0 %collective-permute-start.20 = (bf16[384,768]{1,0:T(8,128)(2,1)S(1)}, bf16[384,768]{1,0:T(8,128)(2,1)S(1)}, u32[]{:S(2)}, u32[]{:S(2)}) collective-permute-start(bf16[384,768]{1,0:T(8,128)(2,1)S(1)} %pick.1), channel_id=1, source_target_pairs={{0,1},{1,0},{2,3},{3,2},{4,5},{5,4},{6,7},{7,6},{8,9},{9,8},{10,11... | collective-permute-start | bytes 1769480 | tf_op jit(solution)/shard_map/ppermute | solution.py:276
  30.8 0.5 collective-permute-start.10
  31.3 1.5 %collective-permute-start.13 = (bf16[256,384]{1,0:T(8,128)(2,1)S(1)}, bf16[256,384]{1,0:T(8,128)(2,1)S(1)}, u32[]{:S(2)}, u32[]{:S(2)}) collective-permute-start(bf16[256,384]{1,0:T(8,128)(2,1)S(1)} %collective-permute-done.12.refs_8_), channel_id=1, source_target_pairs={{0,32},{8,40},{16,48},{24,56},{32,64},{40,72},{48,80},{56,88},{64,... | collective-permute-start | bytes 589832 | tf_op jit(solution)/shard_map/ppermute | solution.py:265
  32.9 0.3 collective-permute-start.11
  33.1 3.0 %collective-permute-start.16 = (bf16[256,384]{1,0:T(8,128)(2,1)S(1)}, bf16[256,384]{1,0:T(8,128)(2,1)S(1)}, u32[]{:S(2)}, u32[]{:S(2)}) collective-permute-start(bf16[256,384]{1,0:T(8,128)(2,1)S(1)} %collective-permute-done.15.refs_6_), channel_id=1, source_target_pairs={{0,224},{8,232},{16,240},{24,248},{32,0},{40,8},{48,16},{56,24},{6... | collective-permute-start | bytes 589832 | tf_op jit(solution)/shard_map/ppermute | solution.py:266
  36.1 4.9 %attend_near.1 = (s32[4,8]{1,0:T(4,128)S(1)}, bf16[4,256,384]{2,1,0:T(8,128)(2,1)S(1)}, f32[12,128,256]{2,1,0:T(8,128)S(1)}, f32[12,1,256]{2,1,0:T(1,128)S(1)}, f32[12,1,256]{2,1,0:T(1,128)S(1)}) custom-call(s32[2]{0:T(128)S(1)} %copy-done.4, bf16[272,384]{1,0:T(8,128)(2,1)S(1)} %fusion.1.refs_0_, bf16[272,384]{1,0:T(8,128)(2,1)S(1)} %collective-permute-done.refs_1_, ...), custom_call_target="tpu_custom_call" | custom-call | flops 905969664 | bytes 4194304 | tf_op jit(solution)/shard_map/attend_near/pallas_call | solution.py:303
  41.1 4.2 %attend_far.1 = (f32[2,384,256]{2,1,0:T(8,128)S(1)}, f32[2,8,256]{2,1,0:T(8,128)S(1)}, bf16[2,416,256]{2,1,0:T(8,128)(2,1)S(1)}) custom-call(s32[4,8]{1,0:T(4,128)S(1)} %get-tuple-element.18.need_ref, bf16[4,256,384]{2,1,0:T(8,128)(2,1)S(1)} %get-tuple-element.19.stacked_ref, bf16[256,384]{1,0:T(8,128)(2,1)S(1)} %collective-permute-done.8.refs_0_, ...), custom_call_target="tpu_custom_call" | custom-call | flops 905969664 | bytes 4194304 | tf_op jit(solution)/shard_map/attend_far/pallas_call | solution.py:318
  45.4 0.5 collective-permute-start.21
  45.9 1.3 %collective-permute-done.17.other_ref = bf16[2,416,256]{2,1,0:T(8,128)(2,1)S(1)} collective-permute-done((bf16[2,416,256]{2,1,0:T(8,128)(2,1)S(1)}, bf16[2,416,256]{2,1,0:T(8,128)(2,1)S(1)}, u32[]{:S(2)}, u32[]{:S(2)}) %collective-permute-start.17) | collective-permute-done | bytes 426016 | tf_op jit(solution)/shard_map/ppermute | solution.py:333
  47.4 1.0 %collective-permute-start.18 = (bf16[1,416,256]{2,1,0:T(8,128)(2,1)S(1)}, bf16[1,416,256]{2,1,0:T(8,128)(2,1)S(1)}, u32[]{:S(2)}, u32[]{:S(2)}) collective-permute-start(bf16[1,416,256]{2,1,0:T(8,128)(2,1)S(1)} %get-tuple-element.28), channel_id=1, source_target_pairs={{0,16},{8,24},{16,0},{24,8},{32,48},{40,56},{48,32},{56,40},{64,80... | collective-permute-start | bytes 638984 | tf_op jit(solution)/shard_map/ppermute | solution.py:346
  48.4 6.4 %collective-permute-done.18.other_ref = bf16[1,416,256]{2,1,0:T(8,128)(2,1)S(1)} collective-permute-done((bf16[1,416,256]{2,1,0:T(8,128)(2,1)S(1)}, bf16[1,416,256]{2,1,0:T(8,128)(2,1)S(1)}, u32[]{:S(2)}, u32[]{:S(2)}) %collective-permute-start.18) | collective-permute-done | bytes 213024 | tf_op jit(solution)/shard_map/ppermute | solution.py:346
  54.9 2.6 %collective-permute-start.19 = (bf16[256,384]{1,0:T(8,128)(2,1)S(1)}, bf16[256,384]{1,0:T(8,128)(2,1)S(1)}, u32[]{:S(2)}, u32[]{:S(2)}) collective-permute-start(bf16[256,384]{1,0:T(8,128)(2,1)S(1)} %finish.1.mine_ref), channel_id=1, source_target_pairs={{0,1},{1,0},{2,3},{3,2},{4,5},{5,4},{6,7},{7,6},{8,9},{9,8},{10,11... | collective-permute-start | bytes 589832 | tf_op jit(solution)/shard_map/ppermute | solution.py:356
  57.6 0.7 project_own.1
  58.3 4.3 %collective-permute-done.19.other_ref = bf16[256,384]{1,0:T(8,128)(2,1)S(1)} collective-permute-done((bf16[256,384]{1,0:T(8,128)(2,1)S(1)}, bf16[256,384]{1,0:T(8,128)(2,1)S(1)}, u32[]{:S(2)}, u32[]{:S(2)}) %collective-permute-start.19) | collective-permute-done | bytes 196640 | tf_op jit(solution)/shard_map/ppermute | solution.py:356
  62.6 0.6 project_other.1
  63.3 15.1 %all_to_all.5 = bf16[4,256,384]{2,1,0:T(8,128)(2,1)S(1)} all-to-all(bf16[4,256,384]{2,1,0:T(8,128)(2,1)S(1)} %project_other.1), channel_id=1, replica_groups={{0,2,4,6},{1,3,5,7},{8,10,12,14},{9,11,13,15},{16,18,20,22},{17,19,21,2..., dimensions={0} | all-to-all | bytes 1572864 | tf_op jit(solution)/shard_map/all_to_all | solution.py:377
  78.4 0.8 %reduce_sum.12 = bf16[256,384]{1,0:T(8,128)(2,1)} reduce(bf16[4,256,384]{2,1,0:T(8,128)(2,1)S(1)} %all_to_all.5, bf16[]{:T(256)} %constant.5.clone.1), dimensions={0}, to_apply=%region_0.1 | reduce | flops 294912 | bytes 983042 | tf_op jit(solution)/shard_map/reduce_sum | solution.py:378
  (33 shorter events, 0.7 us)
Async XLA Ops:
  0.0 11.0 %collective-permute-start.3 = (bf16[256,384]{1,0:T(8,128)(2,1)}, bf16[256,384]{1,0:T(8,128)(2,1)S(1)}, u32[]{:S(2)}, u32[]{:S(2)}) collective-permute-start(bf16[256,384]{1,0:T(8,128)(2,1)} %refs_4_.1), channel_id=1, source_target_pairs={{0,32},{8,40},{16,48},{24,56},{32,64},{40,72},{48,80},{56,88},{64,... | collective-permute-start | bytes 589832 | tf_op jit(solution)/shard_map/ppermute | solution.py:262
  1.9 9.6 %collective-permute-start.4 = (bf16[256,384]{1,0:T(8,128)(2,1)}, bf16[256,384]{1,0:T(8,128)(2,1)S(1)}, u32[]{:S(2)}, u32[]{:S(2)}) collective-permute-start(bf16[256,384]{1,0:T(8,128)(2,1)} %refs_4_.1), channel_id=1, source_target_pairs={{0,224},{8,232},{16,240},{24,248},{32,0},{40,8},{48,16},{56,24},{6... | collective-permute-start | bytes 589832 | tf_op jit(solution)/shard_map/ppermute | solution.py:264
  5.9 8.7 %collective-permute-start.6 = (bf16[256,384]{1,0:T(8,128)(2,1)}, bf16[256,384]{1,0:T(8,128)(2,1)S(1)}, u32[]{:S(2)}, u32[]{:S(2)}) collective-permute-start(bf16[256,384]{1,0:T(8,128)(2,1)} %refs_5_.1), channel_id=1, source_target_pairs={{0,224},{8,232},{16,240},{24,248},{32,0},{40,8},{48,16},{56,24},{6... | collective-permute-start | bytes 589832 | tf_op jit(solution)/shard_map/ppermute | solution.py:266
  7.9 10.3 %collective-permute-start.5 = (bf16[256,384]{1,0:T(8,128)(2,1)}, bf16[256,384]{1,0:T(8,128)(2,1)S(1)}, u32[]{:S(2)}, u32[]{:S(2)}) collective-permute-start(bf16[256,384]{1,0:T(8,128)(2,1)} %refs_5_.1), channel_id=1, source_target_pairs={{0,32},{8,40},{16,48},{24,56},{32,64},{40,72},{48,80},{56,88},{64,... | collective-permute-start | bytes 589832 | tf_op jit(solution)/shard_map/ppermute | solution.py:265
  8.5 27.6 %copy-start.2 = (bf16[256,384]{1,0:T(8,128)(2,1)S(1)}, bf16[256,384]{1,0:T(8,128)(2,1)}, u32[]{:S(2)}) copy-start(bf16[256,384]{1,0:T(8,128)(2,1)} %refs_4_.1) | copy-start | bytes 589828
  8.5 27.6 %copy-start.3 = (bf16[256,384]{1,0:T(8,128)(2,1)S(1)}, bf16[256,384]{1,0:T(8,128)(2,1)}, u32[]{:S(2)}) copy-start(bf16[256,384]{1,0:T(8,128)(2,1)} %refs_5_.1) | copy-start | bytes 589828
  8.6 27.6 %copy-start.4 = (s32[2]{0:T(128)S(1)}, s32[2]{0:T(128)}, u32[]{:S(2)}) copy-start(s32[2]{0:T(128)} %text_ref.1) | copy-start | bytes 28
  9.6 8.6 %collective-permute-start = (bf16[272,384]{1,0:T(8,128)(2,1)S(1)}, bf16[272,384]{1,0:T(8,128)(2,1)S(1)}, u32[]{:S(2)}, u32[]{:S(2)}) collective-permute-start(bf16[272,384]{1,0:T(8,128)(2,1)S(1)} %fusion.1.refs_0_), channel_id=1, source_target_pairs={{0,8},{8,0},{16,24},{24,16},{32,40},{40,32},{48,56},{56,48},{64,72... | collective-permute-start | bytes 626696 | tf_op jit(solution)/shard_map/ppermute | solution.py:284
  11.0 7.8 %collective-permute-start.1 = (bf16[272,384]{1,0:T(8,128)(2,1)S(1)}, bf16[272,384]{1,0:T(8,128)(2,1)S(1)}, u32[]{:S(2)}, u32[]{:S(2)}) collective-permute-start(bf16[272,384]{1,0:T(8,128)(2,1)S(1)} %fusion.1.refs_0_), channel_id=1, source_target_pairs={{0,16},{8,24},{16,0},{24,8},{32,48},{40,56},{48,32},{56,40},{64,80... | collective-permute-start | bytes 626696 | tf_op jit(solution)/shard_map/ppermute | solution.py:284
  11.5 8.8 %collective-permute-start.7 = (bf16[256,384]{1,0:T(8,128)(2,1)S(1)}, bf16[256,384]{1,0:T(8,128)(2,1)S(1)}, u32[]{:S(2)}, u32[]{:S(2)}) collective-permute-start(bf16[256,384]{1,0:T(8,128)(2,1)S(1)} %collective-permute-done.3.refs_6_), channel_id=1, source_target_pairs={{0,32},{8,40},{16,48},{24,56},{32,64},{40,72},{48,80},{56,88},{64,... | collective-permute-start | bytes 589832 | tf_op jit(solution)/shard_map/ppermute | solution.py:262
  14.6 8.9 %collective-permute-start.14 = (bf16[256,384]{1,0:T(8,128)(2,1)S(1)}, bf16[256,384]{1,0:T(8,128)(2,1)S(1)}, u32[]{:S(2)}, u32[]{:S(2)}) collective-permute-start(bf16[256,384]{1,0:T(8,128)(2,1)S(1)} %collective-permute-done.6.refs_9_), channel_id=1, source_target_pairs={{0,224},{8,232},{16,240},{24,248},{32,0},{40,8},{48,16},{56,24},{6... | collective-permute-start | bytes 589832 | tf_op jit(solution)/shard_map/ppermute | solution.py:266
  18.1 10.7 %collective-permute-start.2 = (bf16[272,384]{1,0:T(8,128)(2,1)S(1)}, bf16[272,384]{1,0:T(8,128)(2,1)S(1)}, u32[]{:S(2)}, u32[]{:S(2)}) collective-permute-start(bf16[272,384]{1,0:T(8,128)(2,1)S(1)} %fusion.1.refs_0_), channel_id=1, source_target_pairs={{0,24},{8,16},{16,8},{24,0},{32,56},{40,48},{48,40},{56,32},{64,88... | collective-permute-start | bytes 626696 | tf_op jit(solution)/shard_map/ppermute | solution.py:284
  18.1 12.7 %collective-permute-start.9 = (bf16[256,384]{1,0:T(8,128)(2,1)S(1)}, bf16[256,384]{1,0:T(8,128)(2,1)S(1)}, u32[]{:S(2)}, u32[]{:S(2)}) collective-permute-start(bf16[256,384]{1,0:T(8,128)(2,1)S(1)} %collective-permute-done.4.refs_7_), channel_id=1, source_target_pairs={{0,224},{8,232},{16,240},{24,248},{32,0},{40,8},{48,16},{56,24},{6... | collective-permute-start | bytes 589832 | tf_op jit(solution)/shard_map/ppermute | solution.py:264
  18.8 12.6 %collective-permute-start.12 = (bf16[256,384]{1,0:T(8,128)(2,1)S(1)}, bf16[256,384]{1,0:T(8,128)(2,1)S(1)}, u32[]{:S(2)}, u32[]{:S(2)}) collective-permute-start(bf16[256,384]{1,0:T(8,128)(2,1)S(1)} %collective-permute-done.5.refs_8_), channel_id=1, source_target_pairs={{0,32},{8,40},{16,48},{24,56},{32,64},{40,72},{48,80},{56,88},{64,... | collective-permute-start | bytes 589832 | tf_op jit(solution)/shard_map/ppermute | solution.py:265
  20.3 12.6 %collective-permute-start.8 = (bf16[256,384]{1,0:T(8,128)(2,1)S(1)}, bf16[256,384]{1,0:T(8,128)(2,1)S(1)}, u32[]{:S(2)}, u32[]{:S(2)}) collective-permute-start(bf16[256,384]{1,0:T(8,128)(2,1)S(1)} %collective-permute-done.7.refs_3_), channel_id=1, source_target_pairs={{0,32},{8,40},{16,48},{24,56},{32,64},{40,72},{48,80},{56,88},{64,... | collective-permute-start | bytes 589832 | tf_op jit(solution)/shard_map/ppermute | solution.py:262
  23.4 9.7 %collective-permute-start.15 = (bf16[256,384]{1,0:T(8,128)(2,1)S(1)}, bf16[256,384]{1,0:T(8,128)(2,1)S(1)}, u32[]{:S(2)}, u32[]{:S(2)}) collective-permute-start(bf16[256,384]{1,0:T(8,128)(2,1)S(1)} %collective-permute-done.14.refs_9_), channel_id=1, source_target_pairs={{0,224},{8,232},{16,240},{24,248},{32,0},{40,8},{48,16},{56,24},{6... | collective-permute-start | bytes 589832 | tf_op jit(solution)/shard_map/ppermute | solution.py:266
  27.1 1.7 %copy-start = (bf16[384,3072]{1,0:T(8,128)(2,1)S(1)}, bf16[384,3072]{1,0:T(8,128)(2,1)}, u32[]{:S(2)}) copy-start(bf16[384,3072]{1,0:T(8,128)(2,1)} %weight_ref.3) | copy-start | bytes 7077892
  28.8 16.6 %collective-permute-start.20 = (bf16[384,768]{1,0:T(8,128)(2,1)S(1)}, bf16[384,768]{1,0:T(8,128)(2,1)S(1)}, u32[]{:S(2)}, u32[]{:S(2)}) collective-permute-start(bf16[384,768]{1,0:T(8,128)(2,1)S(1)} %pick.1), channel_id=1, source_target_pairs={{0,1},{1,0},{2,3},{3,2},{4,5},{5,4},{6,7},{7,6},{8,9},{9,8},{10,11... | collective-permute-start | bytes 1769480 | tf_op jit(solution)/shard_map/ppermute | solution.py:276
  30.8 10.2 %collective-permute-start.10 = (bf16[256,384]{1,0:T(8,128)(2,1)S(1)}, bf16[256,384]{1,0:T(8,128)(2,1)S(1)}, u32[]{:S(2)}, u32[]{:S(2)}) collective-permute-start(bf16[256,384]{1,0:T(8,128)(2,1)S(1)} %collective-permute-done.9.refs_4_), channel_id=1, source_target_pairs={{0,224},{8,232},{16,240},{24,248},{32,0},{40,8},{48,16},{56,24},{6... | collective-permute-start | bytes 589832 | tf_op jit(solution)/shard_map/ppermute | solution.py:264
  31.3 9.7 %collective-permute-start.13 = (bf16[256,384]{1,0:T(8,128)(2,1)S(1)}, bf16[256,384]{1,0:T(8,128)(2,1)S(1)}, u32[]{:S(2)}, u32[]{:S(2)}) collective-permute-start(bf16[256,384]{1,0:T(8,128)(2,1)S(1)} %collective-permute-done.12.refs_8_), channel_id=1, source_target_pairs={{0,32},{8,40},{16,48},{24,56},{32,64},{40,72},{48,80},{56,88},{64,... | collective-permute-start | bytes 589832 | tf_op jit(solution)/shard_map/ppermute | solution.py:265
  32.9 8.2 %collective-permute-start.11 = (bf16[256,384]{1,0:T(8,128)(2,1)S(1)}, bf16[256,384]{1,0:T(8,128)(2,1)S(1)}, u32[]{:S(2)}, u32[]{:S(2)}) collective-permute-start(bf16[256,384]{1,0:T(8,128)(2,1)S(1)} %collective-permute-done.8.refs_0_), channel_id=1, source_target_pairs={{0,32},{8,40},{16,48},{24,56},{32,64},{40,72},{48,80},{56,88},{64,... | collective-permute-start | bytes 589832 | tf_op jit(solution)/shard_map/ppermute | solution.py:262
  33.1 7.9 %collective-permute-start.16 = (bf16[256,384]{1,0:T(8,128)(2,1)S(1)}, bf16[256,384]{1,0:T(8,128)(2,1)S(1)}, u32[]{:S(2)}, u32[]{:S(2)}) collective-permute-start(bf16[256,384]{1,0:T(8,128)(2,1)S(1)} %collective-permute-done.15.refs_6_), channel_id=1, source_target_pairs={{0,224},{8,232},{16,240},{24,248},{32,0},{40,8},{48,16},{56,24},{6... | collective-permute-start | bytes 589832 | tf_op jit(solution)/shard_map/ppermute | solution.py:266
  41.1 16.5 %copy-start.1 = (bf16[384,3072]{1,0:T(8,128)(2,1)S(1)}, bf16[384,3072]{1,0:T(8,128)(2,1)}, u32[]{:S(2)}) copy-start(bf16[384,3072]{1,0:T(8,128)(2,1)} %weight_ref.3) | copy-start | bytes 7077892
  45.3 1.9 %collective-permute-start.17 = (bf16[2,416,256]{2,1,0:T(8,128)(2,1)S(1)}, bf16[2,416,256]{2,1,0:T(8,128)(2,1)S(1)}, u32[]{:S(2)}, u32[]{:S(2)}) collective-permute-start(bf16[2,416,256]{2,1,0:T(8,128)(2,1)S(1)} %get-tuple-element.25), channel_id=1, source_target_pairs={{0,8},{8,0},{16,24},{24,16},{32,40},{40,32},{48,56},{56,48},{64,72... | collective-permute-start | bytes 1277960 | tf_op jit(solution)/shard_map/ppermute | solution.py:333
  45.4 12.1 %collective-permute-start.21 = (bf16[384,768]{1,0:T(8,128)(2,1)S(1)}, bf16[384,768]{1,0:T(8,128)(2,1)S(1)}, u32[]{:S(2)}, u32[]{:S(2)}) collective-permute-start(bf16[384,768]{1,0:T(8,128)(2,1)S(1)} %collective-permute-done.20.half_ref), channel_id=1, source_target_pairs={{0,8},{8,0},{16,24},{24,16},{32,40},{40,32},{48,56},{56,48},{64,72... | collective-permute-start | bytes 1769480 | tf_op jit(solution)/shard_map/ppermute | solution.py:277
  47.4 7.4 %collective-permute-start.18 = (bf16[1,416,256]{2,1,0:T(8,128)(2,1)S(1)}, bf16[1,416,256]{2,1,0:T(8,128)(2,1)S(1)}, u32[]{:S(2)}, u32[]{:S(2)}) collective-permute-start(bf16[1,416,256]{2,1,0:T(8,128)(2,1)S(1)} %get-tuple-element.28), channel_id=1, source_target_pairs={{0,16},{8,24},{16,0},{24,8},{32,48},{40,56},{48,32},{56,40},{64,80... | collective-permute-start | bytes 638984 | tf_op jit(solution)/shard_map/ppermute | solution.py:346
  54.9 7.7 %collective-permute-start.19 = (bf16[256,384]{1,0:T(8,128)(2,1)S(1)}, bf16[256,384]{1,0:T(8,128)(2,1)S(1)}, u32[]{:S(2)}, u32[]{:S(2)}) collective-permute-start(bf16[256,384]{1,0:T(8,128)(2,1)S(1)} %finish.1.mine_ref), channel_id=1, source_target_pairs={{0,1},{1,0},{2,3},{3,2},{4,5},{5,4},{6,7},{7,6},{8,9},{9,8},{10,11... | collective-permute-start | bytes 589832 | tf_op jit(solution)/shard_map/ppermute | solution.py:356

commit v14 on v13

--- a/solution.py
+++ b/solution.py
@@ -20,20 +20,20 @@
     heads = len(outs)
     for h in range(heads):
         ref[index, h * HD:(h + 1) * HD, :] = outs[h].astype(jnp.bfloat16)
-    rows = jnp.concatenate(sums + [jnp.zeros((8 - heads, TILE), jnp.float32)], axis=0)
+    rows = jnp.concatenate(sums, axis=0)
     high = rows.astype(jnp.bfloat16).astype(jnp.float32)
     middle = (rows - high).astype(jnp.bfloat16).astype(jnp.float32)
     low = rows - high - middle
+    unused = jnp.zeros((PART_ROWS - 3 * heads, TILE), jnp.float32)
     base = heads * HD
-    ref[index, base:base + 16, :] = jnp.concatenate([high, middle], axis=0).astype(jnp.bfloat16)
-    ref[index, base + 16:base + 32, :] = jnp.concatenate([low, jnp.zeros_like(low)], axis=0).astype(jnp.bfloat16)
+    block = jnp.concatenate([high, middle, low, unused], axis=0)
+    ref[index, base:base + PART_ROWS, :] = block.astype(jnp.bfloat16)
 
 
 def unpack_sums(ref, index, heads):
     base = heads * HD
-    block = ref[index, base:base + 16, :].astype(jnp.float32)
-    last = ref[index, base + 16:base + 32, :].astype(jnp.float32)
-    return block[0:8] + block[8:16] + last[0:8]
+    block = ref[index, base:base + PART_ROWS, :].astype(jnp.float32)
+    return block[0:heads] + block[heads:2 * heads] + block[2 * heads:3 * heads]
 
 
 def merged(mine_ref, mine_sum_ref, mine, other_ref, other, heads):
@@ -320,7 +320,7 @@
         out_shape=(
             jax.ShapeDtypeStruct((2, width, TILE), jnp.float32),
             jax.ShapeDtypeStruct((2, 8, TILE), jnp.float32),
-            jax.ShapeDtypeStruct((2, width + 2 * PART_ROWS, TILE), jnp.bfloat16),
+            jax.ShapeDtypeStruct((2, width + PART_ROWS, TILE), jnp.bfloat16),
         ),
         in_specs=smem + vmem_specs(1 + 2 * len(far) + 3),
         out_specs=tuple(vmem_specs(3)),
@@ -336,7 +336,7 @@
         out_shape=(
             jax.ShapeDtypeStruct((1, width, TILE), jnp.float32),
             jax.ShapeDtypeStruct((1, 8, TILE), jnp.float32),
-            jax.ShapeDtypeStruct((1, width + 2 * PART_ROWS, TILE), jnp.bfloat16),
+            jax.ShapeDtypeStruct((1, width + PART_ROWS, TILE), jnp.bfloat16),
         ),
         in_specs=vmem_specs(3),
         out_specs=tuple(vmem_specs(3)),

time: 80.5 us -> 79.6 us (0.989)
  no operation moved by 1% of the time
where the time goes in v14:
time: 79.6 us; the launch traced here: 78.9 us
  starting transfers between devices  30 us (38%)
  waiting for transfers between devices  18.7 us (23%)
  blocking collectives  15.1 us (19%)
  Pallas kernels  10.8 us (14%)
  other arithmetic  2.48 us (3%)
  local copies, waits for them, and re-layouts  1.68 us (2%)
    all_to_all x1, blocking collectives, per_device(): lax.all_to_all(shares, 'head', 0, 0, axis_index_groups=sides, tiled=True)  15.1 us
    ppermute x4, starting transfers between devices, per_device(): v_down.append(lax.ppermute(v_down[-1], 'seq', down))  12.3 us
    ppermute x1, waiting for transfers between devices, per_device(): other = lax.ppermute(send, 'seq', [(s, s ^ 2) for s in range(seq_size)])  6.1 us
    ppermute x4, waiting for transfers between devices, per_device(): v_down.append(lax.ppermute(v_down[-1], 'seq', down))  5.77 us
    ppermute x3, starting transfers between devices, per_device(): k_down.append(lax.ppermute(k_down[-1], 'seq', down))  5.04 us
    pallas_call x1, Pallas kernels, per_device(): pl.pallas_call(functools.partial(near_kernel, factor, seq_size, order), o...  4.79 us
    pallas_call x1, Pallas kernels, per_device(): pl.pallas_call(functools.partial(far_kernel, factor, 3, len(far)), out_sh...  4.26 us
    ppermute x1, waiting for transfers between devices, per_device(): other = lax.ppermute(attended, 'head', swap_side)  4.22 us
  transfers between devices with their start and end apart: 22, of which 6 were waited for; matrix products, arithmetic and copies ran while one was open for 2% of the time, Pallas kernels for 13%

profile of v14, /device:TPU:2, one launch (start us, length us, event | category | flops | bytes accessed | tf_op | source)
XLA Modules:
  0.0 78.9 jit_solution(17323263651290509404)
XLA Ops:
  0.0 1.9 %collective-permute-start.3 = (bf16[256,384]{1,0:T(8,128)(2,1)}, bf16[256,384]{1,0:T(8,128)(2,1)S(1)}, u32[]{:S(2)}, u32[]{:S(2)}) collective-permute-start(bf16[256,384]{1,0:T(8,128)(2,1)} %refs_4_.1), channel_id=1, source_target_pairs={{0,32},{8,40},{16,48},{24,56},{32,64},{40,72},{48,80},{56,88},{64,... | collective-permute-start | bytes 589832 | tf_op jit(solution)/shard_map/ppermute | solution.py:262
  1.9 3.9 %collective-permute-start.4 = (bf16[256,384]{1,0:T(8,128)(2,1)}, bf16[256,384]{1,0:T(8,128)(2,1)S(1)}, u32[]{:S(2)}, u32[]{:S(2)}) collective-permute-start(bf16[256,384]{1,0:T(8,128)(2,1)} %refs_4_.1), channel_id=1, source_target_pairs={{0,224},{8,232},{16,240},{24,248},{32,0},{40,8},{48,16},{56,24},{6... | collective-permute-start | bytes 589832 | tf_op jit(solution)/shard_map/ppermute | solution.py:264
  5.9 2.0 %collective-permute-start.6 = (bf16[256,384]{1,0:T(8,128)(2,1)}, bf16[256,384]{1,0:T(8,128)(2,1)S(1)}, u32[]{:S(2)}, u32[]{:S(2)}) collective-permute-start(bf16[256,384]{1,0:T(8,128)(2,1)} %refs_5_.1), channel_id=1, source_target_pairs={{0,224},{8,232},{16,240},{24,248},{32,0},{40,8},{48,16},{56,24},{6... | collective-permute-start | bytes 589832 | tf_op jit(solution)/shard_map/ppermute | solution.py:266
  7.9 0.7 convert.5
  8.6 1.0 %fusion.1.refs_0_ = bf16[272,384]{1,0:T(8,128)(2,1)S(1)} fusion(bf16[1,27]{1,0:T(2,128)(2,1)S(1)} %convert.5, bf16[256,384]{1,0:T(8,128)(2,1)} %param.6), kind=kLoop, calls=%fused_computation.2 | loop fusion | flops 626688 | bytes 405558 | tf_op jit(solution)/shard_map/concatenate | solution.py:282
  9.7 1.3 %collective-permute-done.3.refs_6_ = bf16[256,384]{1,0:T(8,128)(2,1)S(1)} collective-permute-done((bf16[256,384]{1,0:T(8,128)(2,1)}, bf16[256,384]{1,0:T(8,128)(2,1)S(1)}, u32[]{:S(2)}, u32[]{:S(2)}) %collective-permute-start.3) | collective-permute-done | bytes 196640 | tf_op jit(solution)/shard_map/ppermute | solution.py:262
  11.0 0.5 collective-permute-start.1
  11.5 0.3 collective-permute-start.7
  11.8 2.7 %collective-permute-done.6.refs_9_ = bf16[256,384]{1,0:T(8,128)(2,1)S(1)} collective-permute-done((bf16[256,384]{1,0:T(8,128)(2,1)}, bf16[256,384]{1,0:T(8,128)(2,1)S(1)}, u32[]{:S(2)}, u32[]{:S(2)}) %collective-permute-start.6) | collective-permute-done | bytes 196640 | tf_op jit(solution)/shard_map/ppermute | solution.py:266
  14.6 3.6 %collective-permute-start.14 = (bf16[256,384]{1,0:T(8,128)(2,1)S(1)}, bf16[256,384]{1,0:T(8,128)(2,1)S(1)}, u32[]{:S(2)}, u32[]{:S(2)}) collective-permute-start(bf16[256,384]{1,0:T(8,128)(2,1)S(1)} %collective-permute-done.6.refs_9_), channel_id=1, source_target_pairs={{0,224},{8,232},{16,240},{24,248},{32,0},{40,8},{48,16},{56,24},{6... | collective-permute-start | bytes 589832 | tf_op jit(solution)/shard_map/ppermute | solution.py:266
  18.1 0.6 collective-permute-start.9
  18.8 1.5 %collective-permute-start.12 = (bf16[256,384]{1,0:T(8,128)(2,1)S(1)}, bf16[256,384]{1,0:T(8,128)(2,1)S(1)}, u32[]{:S(2)}, u32[]{:S(2)}) collective-permute-start(bf16[256,384]{1,0:T(8,128)(2,1)S(1)} %collective-permute-done.5.refs_8_), channel_id=1, source_target_pairs={{0,32},{8,40},{16,48},{24,56},{32,64},{40,72},{48,80},{56,88},{64,... | collective-permute-start | bytes 589832 | tf_op jit(solution)/shard_map/ppermute | solution.py:265
  20.3 3.1 %collective-permute-done.14.refs_9_ = bf16[256,384]{1,0:T(8,128)(2,1)S(1)} collective-permute-done((bf16[256,384]{1,0:T(8,128)(2,1)S(1)}, bf16[256,384]{1,0:T(8,128)(2,1)S(1)}, u32[]{:S(2)}, u32[]{:S(2)}) %collective-permute-start.14) | collective-permute-done | bytes 196640 | tf_op jit(solution)/shard_map/ppermute | solution.py:266
  23.4 3.7 %collective-permute-start.15 = (bf16[256,384]{1,0:T(8,128)(2,1)S(1)}, bf16[256,384]{1,0:T(8,128)(2,1)S(1)}, u32[]{:S(2)}, u32[]{:S(2)}) collective-permute-start(bf16[256,384]{1,0:T(8,128)(2,1)S(1)} %collective-permute-done.14.refs_9_), channel_id=1, source_target_pairs={{0,224},{8,232},{16,240},{24,248},{32,0},{40,8},{48,16},{56,24},{6... | collective-permute-start | bytes 589832 | tf_op jit(solution)/shard_map/ppermute | solution.py:266
  27.1 1.7 %copy-done = bf16[384,3072]{1,0:T(8,128)(2,1)S(1)} copy-done((bf16[384,3072]{1,0:T(8,128)(2,1)S(1)}, bf16[384,3072]{1,0:T(8,128)(2,1)}, u32[]{:S(2)}) %copy-start) | copy-done | bytes 2359320
  28.8 2.0 %collective-permute-start.20 = (bf16[384,768]{1,0:T(8,128)(2,1)S(1)}, bf16[384,768]{1,0:T(8,128)(2,1)S(1)}, u32[]{:S(2)}, u32[]{:S(2)}) collective-permute-start(bf16[384,768]{1,0:T(8,128)(2,1)S(1)} %pick.1), channel_id=1, source_target_pairs={{0,1},{1,0},{2,3},{3,2},{4,5},{5,4},{6,7},{7,6},{8,9},{9,8},{10,11... | collective-permute-start | bytes 1769480 | tf_op jit(solution)/shard_map/ppermute | solution.py:276
  30.8 0.5 collective-permute-start.10
  31.3 1.5 %collective-permute-start.13 = (bf16[256,384]{1,0:T(8,128)(2,1)S(1)}, bf16[256,384]{1,0:T(8,128)(2,1)S(1)}, u32[]{:S(2)}, u32[]{:S(2)}) collective-permute-start(bf16[256,384]{1,0:T(8,128)(2,1)S(1)} %collective-permute-done.12.refs_8_), channel_id=1, source_target_pairs={{0,32},{8,40},{16,48},{24,56},{32,64},{40,72},{48,80},{56,88},{64,... | collective-permute-start | bytes 589832 | tf_op jit(solution)/shard_map/ppermute | solution.py:265
  32.9 0.3 collective-permute-start.11
  33.1 3.0 %collective-permute-start.16 = (bf16[256,384]{1,0:T(8,128)(2,1)S(1)}, bf16[256,384]{1,0:T(8,128)(2,1)S(1)}, u32[]{:S(2)}, u32[]{:S(2)}) collective-permute-start(bf16[256,384]{1,0:T(8,128)(2,1)S(1)} %collective-permute-done.15.refs_6_), channel_id=1, source_target_pairs={{0,224},{8,232},{16,240},{24,248},{32,0},{40,8},{48,16},{56,24},{6... | collective-permute-start | bytes 589832 | tf_op jit(solution)/shard_map/ppermute | solution.py:266
  36.1 4.8 %attend_near.1 = (s32[4,8]{1,0:T(4,128)S(1)}, bf16[4,256,384]{2,1,0:T(8,128)(2,1)S(1)}, f32[12,128,256]{2,1,0:T(8,128)S(1)}, f32[12,1,256]{2,1,0:T(1,128)S(1)}, f32[12,1,256]{2,1,0:T(1,128)S(1)}) custom-call(s32[2]{0:T(128)S(1)} %copy-done.4, bf16[272,384]{1,0:T(8,128)(2,1)S(1)} %fusion.1.refs_0_, bf16[272,384]{1,0:T(8,128)(2,1)S(1)} %collective-permute-done.refs_1_, ...), custom_call_target="tpu_custom_call" | custom-call | flops 905969664 | bytes 4194304 | tf_op jit(solution)/shard_map/attend_near/pallas_call | solution.py:303
  41.0 4.3 %attend_far.1 = (f32[2,384,256]{2,1,0:T(8,128)S(1)}, f32[2,8,256]{2,1,0:T(8,128)S(1)}, bf16[2,400,256]{2,1,0:T(8,128)(2,1)S(1)}) custom-call(s32[4,8]{1,0:T(4,128)S(1)} %get-tuple-element.18.need_ref, bf16[4,256,384]{2,1,0:T(8,128)(2,1)S(1)} %get-tuple-element.19.stacked_ref, bf16[256,384]{1,0:T(8,128)(2,1)S(1)} %collective-permute-done.8.refs_0_, ...), custom_call_target="tpu_custom_call" | custom-call | flops 905969664 | bytes 4194304 | tf_op jit(solution)/shard_map/attend_far/pallas_call | solution.py:318
  45.3 0.5 collective-permute-start.21
  45.8 1.2 %collective-permute-done.17.other_ref = bf16[2,400,256]{2,1,0:T(8,128)(2,1)S(1)} collective-permute-done((bf16[2,400,256]{2,1,0:T(8,128)(2,1)S(1)}, bf16[2,400,256]{2,1,0:T(8,128)(2,1)S(1)}, u32[]{:S(2)}, u32[]{:S(2)}) %collective-permute-start.17) | collective-permute-done | bytes 409632 | tf_op jit(solution)/shard_map/ppermute | solution.py:333
  47.2 1.1 %collective-permute-start.18 = (bf16[1,400,256]{2,1,0:T(8,128)(2,1)S(1)}, bf16[1,400,256]{2,1,0:T(8,128)(2,1)S(1)}, u32[]{:S(2)}, u32[]{:S(2)}) collective-permute-start(bf16[1,400,256]{2,1,0:T(8,128)(2,1)S(1)} %get-tuple-element.28), channel_id=1, source_target_pairs={{0,16},{8,24},{16,0},{24,8},{32,48},{40,56},{48,32},{56,40},{64,80... | collective-permute-start | bytes 614408 | tf_op jit(solution)/shard_map/ppermute | solution.py:346
  48.3 6.1 %collective-permute-done.18.other_ref = bf16[1,400,256]{2,1,0:T(8,128)(2,1)S(1)} collective-permute-done((bf16[1,400,256]{2,1,0:T(8,128)(2,1)S(1)}, bf16[1,400,256]{2,1,0:T(8,128)(2,1)S(1)}, u32[]{:S(2)}, u32[]{:S(2)}) %collective-permute-start.18) | collective-permute-done | bytes 204832 | tf_op jit(solution)/shard_map/ppermute | solution.py:346
  54.6 2.8 %collective-permute-start.19 = (bf16[256,384]{1,0:T(8,128)(2,1)S(1)}, bf16[256,384]{1,0:T(8,128)(2,1)S(1)}, u32[]{:S(2)}, u32[]{:S(2)}) collective-permute-start(bf16[256,384]{1,0:T(8,128)(2,1)S(1)} %finish.1.mine_ref), channel_id=1, source_target_pairs={{0,1},{1,0},{2,3},{3,2},{4,5},{5,4},{6,7},{7,6},{8,9},{9,8},{10,11... | collective-permute-start | bytes 589832 | tf_op jit(solution)/shard_map/ppermute | solution.py:356
  57.4 0.7 project_own.1
  58.1 4.2 %collective-permute-done.19.other_ref = bf16[256,384]{1,0:T(8,128)(2,1)S(1)} collective-permute-done((bf16[256,384]{1,0:T(8,128)(2,1)S(1)}, bf16[256,384]{1,0:T(8,128)(2,1)S(1)}, u32[]{:S(2)}, u32[]{:S(2)}) %collective-permute-start.19) | collective-permute-done | bytes 196640 | tf_op jit(solution)/shard_map/ppermute | solution.py:356
  62.3 0.6 project_other.1
  63.0 15.1 %all_to_all.5 = bf16[4,256,384]{2,1,0:T(8,128)(2,1)S(1)} all-to-all(bf16[4,256,384]{2,1,0:T(8,128)(2,1)S(1)} %project_other.1), channel_id=1, replica_groups={{0,2,4,6},{1,3,5,7},{8,10,12,14},{9,11,13,15},{16,18,20,22},{17,19,21,2..., dimensions={0} | all-to-all | bytes 1572864 | tf_op jit(solution)/shard_map/all_to_all | solution.py:377
  78.1 0.8 %reduce_sum.12 = bf16[256,384]{1,0:T(8,128)(2,1)} reduce(bf16[4,256,384]{2,1,0:T(8,128)(2,1)S(1)} %all_to_all.5, bf16[]{:T(256)} %constant.5.clone.1), dimensions={0}, to_apply=%region_0.1 | reduce | flops 294912 | bytes 983042 | tf_op jit(solution)/shard_map/reduce_sum | solution.py:378
  (33 shorter events, 0.7 us)
Async XLA Ops:
  0.0 11.0 %collective-permute-start.3 = (bf16[256,384]{1,0:T(8,128)(2,1)}, bf16[256,384]{1,0:T(8,128)(2,1)S(1)}, u32[]{:S(2)}, u32[]{:S(2)}) collective-permute-start(bf16[256,384]{1,0:T(8,128)(2,1)} %refs_4_.1), channel_id=1, source_target_pairs={{0,32},{8,40},{16,48},{24,56},{32,64},{40,72},{48,80},{56,88},{64,... | collective-permute-start | bytes 589832 | tf_op jit(solution)/shard_map/ppermute | solution.py:262
  1.9 9.6 %collective-permute-start.4 = (bf16[256,384]{1,0:T(8,128)(2,1)}, bf16[256,384]{1,0:T(8,128)(2,1)S(1)}, u32[]{:S(2)}, u32[]{:S(2)}) collective-permute-start(bf16[256,384]{1,0:T(8,128)(2,1)} %refs_4_.1), channel_id=1, source_target_pairs={{0,224},{8,232},{16,240},{24,248},{32,0},{40,8},{48,16},{56,24},{6... | collective-permute-start | bytes 589832 | tf_op jit(solution)/shard_map/ppermute | solution.py:264
  5.9 8.7 %collective-permute-start.6 = (bf16[256,384]{1,0:T(8,128)(2,1)}, bf16[256,384]{1,0:T(8,128)(2,1)S(1)}, u32[]{:S(2)}, u32[]{:S(2)}) collective-permute-start(bf16[256,384]{1,0:T(8,128)(2,1)} %refs_5_.1), channel_id=1, source_target_pairs={{0,224},{8,232},{16,240},{24,248},{32,0},{40,8},{48,16},{56,24},{6... | collective-permute-start | bytes 589832 | tf_op jit(solution)/shard_map/ppermute | solution.py:266
  7.9 10.3 %collective-permute-start.5 = (bf16[256,384]{1,0:T(8,128)(2,1)}, bf16[256,384]{1,0:T(8,128)(2,1)S(1)}, u32[]{:S(2)}, u32[]{:S(2)}) collective-permute-start(bf16[256,384]{1,0:T(8,128)(2,1)} %refs_5_.1), channel_id=1, source_target_pairs={{0,32},{8,40},{16,48},{24,56},{32,64},{40,72},{48,80},{56,88},{64,... | collective-permute-start | bytes 589832 | tf_op jit(solution)/shard_map/ppermute | solution.py:265
  8.5 27.6 %copy-start.2 = (bf16[256,384]{1,0:T(8,128)(2,1)S(1)}, bf16[256,384]{1,0:T(8,128)(2,1)}, u32[]{:S(2)}) copy-start(bf16[256,384]{1,0:T(8,128)(2,1)} %refs_4_.1) | copy-start | bytes 589828
  8.5 27.6 %copy-start.3 = (bf16[256,384]{1,0:T(8,128)(2,1)S(1)}, bf16[256,384]{1,0:T(8,128)(2,1)}, u32[]{:S(2)}) copy-start(bf16[256,384]{1,0:T(8,128)(2,1)} %refs_5_.1) | copy-start | bytes 589828
  8.6 27.6 %copy-start.4 = (s32[2]{0:T(128)S(1)}, s32[2]{0:T(128)}, u32[]{:S(2)}) copy-start(s32[2]{0:T(128)} %text_ref.1) | copy-start | bytes 28
  9.6 8.6 %collective-permute-start = (bf16[272,384]{1,0:T(8,128)(2,1)S(1)}, bf16[272,384]{1,0:T(8,128)(2,1)S(1)}, u32[]{:S(2)}, u32[]{:S(2)}) collective-permute-start(bf16[272,384]{1,0:T(8,128)(2,1)S(1)} %fusion.1.refs_0_), channel_id=1, source_target_pairs={{0,8},{8,0},{16,24},{24,16},{32,40},{40,32},{48,56},{56,48},{64,72... | collective-permute-start | bytes 626696 | tf_op jit(solution)/shard_map/ppermute | solution.py:284
  11.0 7.8 %collective-permute-start.1 = (bf16[272,384]{1,0:T(8,128)(2,1)S(1)}, bf16[272,384]{1,0:T(8,128)(2,1)S(1)}, u32[]{:S(2)}, u32[]{:S(2)}) collective-permute-start(bf16[272,384]{1,0:T(8,128)(2,1)S(1)} %fusion.1.refs_0_), channel_id=1, source_target_pairs={{0,16},{8,24},{16,0},{24,8},{32,48},{40,56},{48,32},{56,40},{64,80... | collective-permute-start | bytes 626696 | tf_op jit(solution)/shard_map/ppermute | solution.py:284
  11.5 8.8 %collective-permute-start.7 = (bf16[256,384]{1,0:T(8,128)(2,1)S(1)}, bf16[256,384]{1,0:T(8,128)(2,1)S(1)}, u32[]{:S(2)}, u32[]{:S(2)}) collective-permute-start(bf16[256,384]{1,0:T(8,128)(2,1)S(1)} %collective-permute-done.3.refs_6_), channel_id=1, source_target_pairs={{0,32},{8,40},{16,48},{24,56},{32,64},{40,72},{48,80},{56,88},{64,... | collective-permute-start | bytes 589832 | tf_op jit(solution)/shard_map/ppermute | solution.py:262
  14.6 8.9 %collective-permute-start.14 = (bf16[256,384]{1,0:T(8,128)(2,1)S(1)}, bf16[256,384]{1,0:T(8,128)(2,1)S(1)}, u32[]{:S(2)}, u32[]{:S(2)}) collective-permute-start(bf16[256,384]{1,0:T(8,128)(2,1)S(1)} %collective-permute-done.6.refs_9_), channel_id=1, source_target_pairs={{0,224},{8,232},{16,240},{24,248},{32,0},{40,8},{48,16},{56,24},{6... | collective-permute-start | bytes 589832 | tf_op jit(solution)/shard_map/ppermute | solution.py:266
  18.1 10.7 %collective-permute-start.2 = (bf16[272,384]{1,0:T(8,128)(2,1)S(1)}, bf16[272,384]{1,0:T(8,128)(2,1)S(1)}, u32[]{:S(2)}, u32[]{:S(2)}) collective-permute-start(bf16[272,384]{1,0:T(8,128)(2,1)S(1)} %fusion.1.refs_0_), channel_id=1, source_target_pairs={{0,24},{8,16},{16,8},{24,0},{32,56},{40,48},{48,40},{56,32},{64,88... | collective-permute-start | bytes 626696 | tf_op jit(solution)/shard_map/ppermute | solution.py:284
  18.1 12.7 %collective-permute-start.9 = (bf16[256,384]{1,0:T(8,128)(2,1)S(1)}, bf16[256,384]{1,0:T(8,128)(2,1)S(1)}, u32[]{:S(2)}, u32[]{:S(2)}) collective-permute-start(bf16[256,384]{1,0:T(8,128)(2,1)S(1)} %collective-permute-done.4.refs_7_), channel_id=1, source_target_pairs={{0,224},{8,232},{16,240},{24,248},{32,0},{40,8},{48,16},{56,24},{6... | collective-permute-start | bytes 589832 | tf_op jit(solution)/shard_map/ppermute | solution.py:264
  18.8 12.6 %collective-permute-start.12 = (bf16[256,384]{1,0:T(8,128)(2,1)S(1)}, bf16[256,384]{1,0:T(8,128)(2,1)S(1)}, u32[]{:S(2)}, u32[]{:S(2)}) collective-permute-start(bf16[256,384]{1,0:T(8,128)(2,1)S(1)} %collective-permute-done.5.refs_8_), channel_id=1, source_target_pairs={{0,32},{8,40},{16,48},{24,56},{32,64},{40,72},{48,80},{56,88},{64,... | collective-permute-start | bytes 589832 | tf_op jit(solution)/shard_map/ppermute | solution.py:265
  20.3 12.6 %collective-permute-start.8 = (bf16[256,384]{1,0:T(8,128)(2,1)S(1)}, bf16[256,384]{1,0:T(8,128)(2,1)S(1)}, u32[]{:S(2)}, u32[]{:S(2)}) collective-permute-start(bf16[256,384]{1,0:T(8,128)(2,1)S(1)} %collective-permute-done.7.refs_3_), channel_id=1, source_target_pairs={{0,32},{8,40},{16,48},{24,56},{32,64},{40,72},{48,80},{56,88},{64,... | collective-permute-start | bytes 589832 | tf_op jit(solution)/shard_map/ppermute | solution.py:262
  23.4 9.7 %collective-permute-start.15 = (bf16[256,384]{1,0:T(8,128)(2,1)S(1)}, bf16[256,384]{1,0:T(8,128)(2,1)S(1)}, u32[]{:S(2)}, u32[]{:S(2)}) collective-permute-start(bf16[256,384]{1,0:T(8,128)(2,1)S(1)} %collective-permute-done.14.refs_9_), channel_id=1, source_target_pairs={{0,224},{8,232},{16,240},{24,248},{32,0},{40,8},{48,16},{56,24},{6... | collective-permute-start | bytes 589832 | tf_op jit(solution)/shard_map/ppermute | solution.py:266
  27.1 1.7 %copy-start = (bf16[384,3072]{1,0:T(8,128)(2,1)S(1)}, bf16[384,3072]{1,0:T(8,128)(2,1)}, u32[]{:S(2)}) copy-start(bf16[384,3072]{1,0:T(8,128)(2,1)} %weight_ref.3) | copy-start | bytes 7077892
  28.8 16.5 %collective-permute-start.20 = (bf16[384,768]{1,0:T(8,128)(2,1)S(1)}, bf16[384,768]{1,0:T(8,128)(2,1)S(1)}, u32[]{:S(2)}, u32[]{:S(2)}) collective-permute-start(bf16[384,768]{1,0:T(8,128)(2,1)S(1)} %pick.1), channel_id=1, source_target_pairs={{0,1},{1,0},{2,3},{3,2},{4,5},{5,4},{6,7},{7,6},{8,9},{9,8},{10,11... | collective-permute-start | bytes 1769480 | tf_op jit(solution)/shard_map/ppermute | solution.py:276
  30.8 10.1 %collective-permute-start.10 = (bf16[256,384]{1,0:T(8,128)(2,1)S(1)}, bf16[256,384]{1,0:T(8,128)(2,1)S(1)}, u32[]{:S(2)}, u32[]{:S(2)}) collective-permute-start(bf16[256,384]{1,0:T(8,128)(2,1)S(1)} %collective-permute-done.9.refs_4_), channel_id=1, source_target_pairs={{0,224},{8,232},{16,240},{24,248},{32,0},{40,8},{48,16},{56,24},{6... | collective-permute-start | bytes 589832 | tf_op jit(solution)/shard_map/ppermute | solution.py:264
  31.3 9.6 %collective-permute-start.13 = (bf16[256,384]{1,0:T(8,128)(2,1)S(1)}, bf16[256,384]{1,0:T(8,128)(2,1)S(1)}, u32[]{:S(2)}, u32[]{:S(2)}) collective-permute-start(bf16[256,384]{1,0:T(8,128)(2,1)S(1)} %collective-permute-done.12.refs_8_), channel_id=1, source_target_pairs={{0,32},{8,40},{16,48},{24,56},{32,64},{40,72},{48,80},{56,88},{64,... | collective-permute-start | bytes 589832 | tf_op jit(solution)/shard_map/ppermute | solution.py:265
  32.9 8.1 %collective-permute-start.11 = (bf16[256,384]{1,0:T(8,128)(2,1)S(1)}, bf16[256,384]{1,0:T(8,128)(2,1)S(1)}, u32[]{:S(2)}, u32[]{:S(2)}) collective-permute-start(bf16[256,384]{1,0:T(8,128)(2,1)S(1)} %collective-permute-done.8.refs_0_), channel_id=1, source_target_pairs={{0,32},{8,40},{16,48},{24,56},{32,64},{40,72},{48,80},{56,88},{64,... | collective-permute-start | bytes 589832 | tf_op jit(solution)/shard_map/ppermute | solution.py:262
  33.1 7.8 %collective-permute-start.16 = (bf16[256,384]{1,0:T(8,128)(2,1)S(1)}, bf16[256,384]{1,0:T(8,128)(2,1)S(1)}, u32[]{:S(2)}, u32[]{:S(2)}) collective-permute-start(bf16[256,384]{1,0:T(8,128)(2,1)S(1)} %collective-permute-done.15.refs_6_), channel_id=1, source_target_pairs={{0,224},{8,232},{16,240},{24,248},{32,0},{40,8},{48,16},{56,24},{6... | collective-permute-start | bytes 589832 | tf_op jit(solution)/shard_map/ppermute | solution.py:266
  41.0 16.4 %copy-start.1 = (bf16[384,3072]{1,0:T(8,128)(2,1)S(1)}, bf16[384,3072]{1,0:T(8,128)(2,1)}, u32[]{:S(2)}) copy-start(bf16[384,3072]{1,0:T(8,128)(2,1)} %weight_ref.3) | copy-start | bytes 7077892
  45.2 1.8 %collective-permute-start.17 = (bf16[2,400,256]{2,1,0:T(8,128)(2,1)S(1)}, bf16[2,400,256]{2,1,0:T(8,128)(2,1)S(1)}, u32[]{:S(2)}, u32[]{:S(2)}) collective-permute-start(bf16[2,400,256]{2,1,0:T(8,128)(2,1)S(1)} %get-tuple-element.25), channel_id=1, source_target_pairs={{0,8},{8,0},{16,24},{24,16},{32,40},{40,32},{48,56},{56,48},{64,72... | collective-permute-start | bytes 1228808 | tf_op jit(solution)/shard_map/ppermute | solution.py:333
  45.3 12.0 %collective-permute-start.21 = (bf16[384,768]{1,0:T(8,128)(2,1)S(1)}, bf16[384,768]{1,0:T(8,128)(2,1)S(1)}, u32[]{:S(2)}, u32[]{:S(2)}) collective-permute-start(bf16[384,768]{1,0:T(8,128)(2,1)S(1)} %collective-permute-done.20.half_ref), channel_id=1, source_target_pairs={{0,8},{8,0},{16,24},{24,16},{32,40},{40,32},{48,56},{56,48},{64,72... | collective-permute-start | bytes 1769480 | tf_op jit(solution)/shard_map/ppermute | solution.py:277
  47.2 7.2 %collective-permute-start.18 = (bf16[1,400,256]{2,1,0:T(8,128)(2,1)S(1)}, bf16[1,400,256]{2,1,0:T(8,128)(2,1)S(1)}, u32[]{:S(2)}, u32[]{:S(2)}) collective-permute-start(bf16[1,400,256]{2,1,0:T(8,128)(2,1)S(1)} %get-tuple-element.28), channel_id=1, source_target_pairs={{0,16},{8,24},{16,0},{24,8},{32,48},{40,56},{48,32},{56,40},{64,80... | collective-permute-start | bytes 614408 | tf_op jit(solution)/shard_map/ppermute | solution.py:346
  54.6 7.7 %collective-permute-start.19 = (bf16[256,384]{1,0:T(8,128)(2,1)S(1)}, bf16[256,384]{1,0:T(8,128)(2,1)S(1)}, u32[]{:S(2)}, u32[]{:S(2)}) collective-permute-start(bf16[256,384]{1,0:T(8,128)(2,1)S(1)} %finish.1.mine_ref), channel_id=1, source_target_pairs={{0,1},{1,0},{2,3},{3,2},{4,5},{5,4},{6,7},{7,6},{8,9},{9,8},{10,11... | collective-permute-start | bytes 589832 | tf_op jit(solution)/shard_map/ppermute | solution.py:356
